TPU v7x, 32 devices: a whole 2x2x4 slice. The times are simulated.
32 devices in a mesh: az: 16 (over z, x, core), rad: 2 (over y).
Axes of the slice: x: 2, y: 2, z: 4, core: 2. Of those that a mesh axis runs over, the one named last changes fastest.
Arguments:
- fields: float32 [5, 8, 128, 4096], P(None, None, 'rad', 'az'), may hold values from -6 to 6
- velocity: float32 [8, 128, 4096], P(None, 'rad', 'az'), may hold values from -0.5 to 0.5
- shifts: int32 [128], P('rad'), may hold values from 0 to 4095, as said below
- block_inverse: float32 [8, 128, 64], P(None, 'rad'), may hold values from -1 to 1, as said below
- coupling: float32 [8, 2], P(None, 'rad'), may hold values from 0.2 to 0.5
Outputs:
- updated: float32 [5, 8, 128, 4096], P(None, None, 'rad', 'az')
Inputs may be any that keep to these rules, and one draw needn't show every extreme that they name: `shifts`: each radius's shift; the values 0 and 4095 both occur in every draw. `block_inverse`: entries of the given block inverses.
All inputs are finite; a program needn't handle non-finite values.
Results may differ from a plain program's by a relative error of at most 0.000075.
Values sent between devices are 32-bit elements; how exact they have to be, the bound alone decides.
No kernel may reach another device: no remote copies, remote signals or barrier semaphores. Data moves between devices by JAX's collectives and lax.ppermute only.
A program may use at most 256 MiB of HBM per device.

v0:
```python
import jax
import jax.numpy as jnp
from jax import lax
from jax.sharding import PartitionSpec as P


def roll_rows(values, amounts):
    return jax.vmap(
        lambda one_row, amount: jnp.roll(one_row, amount, axis=-1), in_axes=(2, 0), out_axes=2
    )(values, amounts)


def interface_solve(first_row, last_row, top_left, top_right, low_left, low_right, link_rates):
    band_count = link_rates.shape[1]
    crossings = band_count - 1
    nothing = jnp.zeros_like(first_row[:, 0])
    flat_zero = jnp.zeros_like(link_rates[:, :1])
    carry_base = nothing
    carry_slope = flat_zero
    records = []
    for crossing in range(crossings):
        if crossing > 0:
            back_link = (link_rates[:, crossing - 1] * low_left[:, crossing])[:, None]
        else:
            back_link = flat_zero
        self_link = (link_rates[:, crossing] * low_right[:, crossing])[:, None]
        fore_link = (link_rates[:, crossing] * top_left[:, crossing + 1])[:, None]
        if crossing + 1 < crossings:
            next_link = (link_rates[:, crossing + 1] * top_right[:, crossing + 1])[:, None]
        else:
            next_link = flat_zero
        steepness = back_link * carry_slope + self_link
        offset = last_row[:, crossing] + back_link * carry_base
        denominator = 1.0 - fore_link * steepness
        upper_base = (first_row[:, crossing + 1] + fore_link * offset) / denominator
        upper_slope = next_link / denominator
        carry_base = offset + steepness * upper_base
        carry_slope = steepness * upper_slope
        records.append((carry_base, carry_slope, upper_base, upper_slope))
    lower_values = [nothing] * crossings
    upper_values = [nothing] * crossings
    follow = nothing
    for crossing in reversed(range(crossings)):
        carry_base, carry_slope, upper_base, upper_slope = records[crossing]
        lower_values[crossing] = carry_base + carry_slope * follow
        upper_values[crossing] = upper_base + upper_slope * follow
        follow = upper_values[crossing]
    before = jnp.stack([nothing] + lower_values, axis=1)
    beyond = jnp.stack(upper_values + [nothing], axis=1)
    return (before, beyond)


def periodic_transport(values, speed):
    ahead_cells = jnp.roll(values, -1, axis=3)
    outflow = jnp.maximum(speed, 0.0) * values + jnp.minimum(speed, 0.0) * ahead_cells
    return values - (outflow - jnp.roll(outflow, 1, axis=3))


def per_device(fields, velocity, shifts, block_inverse, coupling):
    stacked = jnp.concatenate([fields, velocity[None]], axis=0)
    grouped = lax.all_to_all(stacked, "az", split_axis=2, concat_axis=3, tiled=True)
    share = grouped.shape[2]
    own_shifts = lax.dynamic_slice_in_dim(shifts, lax.axis_index("az") * share, share)
    rotated = roll_rows(grouped[:5], own_shifts)
    moved_whole = periodic_transport(rotated, grouped[5:])
    transported = lax.all_to_all(moved_whole, "az", split_axis=3, concat_axis=2, tiled=True)
    energy = transported[4]
    local_part = jnp.einsum("zrl,zlp->zrp", block_inverse, energy, precision=lax.Precision.HIGHEST)
    corners = jnp.stack(
        [
            block_inverse[:, 0, 0],
            block_inverse[:, 0, -1],
            block_inverse[:, -1, 0],
            block_inverse[:, -1, -1],
        ],
        axis=1,
    )[:, None, :]
    first_all, last_all, corner_all, link_all = (
        lax.all_gather(local_part[:, :1, :], "rad", axis=1, tiled=True),
        lax.all_gather(local_part[:, -1:, :], "rad", axis=1, tiled=True),
        lax.all_gather(corners, "rad", axis=1, tiled=True),
        lax.all_gather(coupling, "rad", axis=1, tiled=True),
    )
    before, beyond = interface_solve(
        first_all,
        last_all,
        corner_all[..., 0],
        corner_all[..., 1],
        corner_all[..., 2],
        corner_all[..., 3],
        link_all,
    )
    band_index = lax.axis_index("rad")
    before_own = lax.dynamic_index_in_dim(before, band_index, 1, keepdims=False)
    beyond_own = lax.dynamic_index_in_dim(beyond, band_index, 1, keepdims=False)
    link_prev = jnp.concatenate([jnp.zeros_like(link_all[:, :1]), link_all[:, :-1]], axis=1)
    prev_own = lax.dynamic_index_in_dim(link_prev, band_index, 1, keepdims=False)
    link_own = coupling[:, 0]
    diffused = (
        local_part
        + (prev_own[:, None] * block_inverse[:, :, 0])[:, :, None] * before_own[:, None, :]
        + (link_own[:, None] * block_inverse[:, :, -1])[:, :, None] * beyond_own[:, None, :]
    )
    return jnp.concatenate([transported[:4], diffused[None]], axis=0)


def solution(mesh):
    placed = (
        P(None, None, "rad", "az"),
        P(None, "rad", "az"),
        P("rad"),
        P(None, "rad", None),
        P(None, "rad"),
    )
    return jax.shard_map(
        per_device,
        mesh=mesh,
        in_specs=placed,
        out_specs=P(None, None, "rad", "az"),
        check_vma=False,
    )
```

profile of v0, /device:TPU:20, one launch (start us, length us, event | category | flops | bytes accessed | tf_op | source)
XLA Modules:
  0.0 387.6 jit_solution(4056321155725466042)
XLA Ops:
  0.0 3.3 copy.57
  3.6 2.1 pad_maximum_fusion.1
  5.7 7.0 %all-to-all-start = ((f32[6,8,64,256]{3,1,0,2:T(8,128)}), f32[6,8,64,256]{3,1,0,2:T(8,128)}, u32[]{:S(2)}, u32[]{:S(2)}) async-start(f32[6,8,64,256]{3,1,0,2:T(8,128)} %pad_maximum_fusion.1), calls=%async_computation | async-start | bytes 6291456 | tf_op jit(solution)/shard_map/all_to_all | solution.py:61
  12.9 69.8 %all-to-all-done = f32[6,8,64,256]{3,1,0,2:T(8,128)} async-done(((f32[6,8,64,256]{3,1,0,2:T(8,128)}), f32[6,8,64,256]{3,1,0,2:T(8,128)}, u32[]{:S(2)}, u32[]{:S(2)}) %all-to-all-start) | async-done | bytes 3145760 | tf_op jit(solution)/shard_map/all_to_all | solution.py:61
  82.7 3.7 copy.77
  88.1 2.2 copy.59
  90.3 2.8 pad_maximum_fusion
  93.0 13.2 %while.1 = (s32[]{:T(128)}, f32[4,5,8,8192]{3,2,1,0:T(8,128)}, s32[4,4]{1,0:T(4,128)S(1)}, f32[4,5,8,4096]{3,2,0,1:T(8,128)S(1)}, s32[]{:T(128)}) while((s32[]{:T(128)}, f32[4,5,8,8192]{3,2,1,0:T(8,128)}, s32[4,4]{1,0:T(4,128)S(1)}, f32[4,5,8,4096]{3,2,0,1:T(8,128)S(1)}, s32[]{:T(128)}) %tuple.39), condition=%wide.while_cond, body=%wide.while_body.sunk | while | flops 2 | bytes 1310845 | solution.py:9
  93.7 2.6 bitcast_dynamic-update-slice_fusion.2
  97.0 2.6 bitcast_dynamic-update-slice_fusion.2
  100.3 2.6 bitcast_dynamic-update-slice_fusion.2
  103.6 2.6 bitcast_dynamic-update-slice_fusion.2
  106.3 2.2 slice.128
  108.5 2.2 slice_maximum_fusion
  111.9 1.9 min.12
  113.8 2.3 fusion
  116.2 2.3 fusion.1
  118.5 27.7 %copy.62 = f32[5,8,4,4096]{1,2,0,3:T(4,128)} copy(f32[5,8,4,4096]{3,1,2,0:T(8,128)} %fusion.1) | data formatting | bytes 5242880 | tf_op jit(solution)/shard_map/sub | solution.py:56
  146.2 50.9 %reshape.119 = f32[16,1,40960]{2,1,0:T(1,128)} reshape(f32[4096,5,4,8]{3,2,1,0:T(4,128)} %bitcast.83) | data formatting | bytes 5242880
  197.1 4.8 %all-to-all-start.1 = ((f32[16,1,40960]{2,1,0:T(1,128)}), f32[16,1,40960]{2,1,0:T(1,128)S(1)}, u32[]{:S(2)}, u32[]{:S(2)}) async-start(f32[16,1,40960]{2,1,0:T(1,128)} %reshape.119), calls=%async_computation.1 | async-start | bytes 5242880 | tf_op jit(solution)/shard_map/all_to_all | solution.py:66
  201.9 4.2 %all-gather.1 = f32[2,1,8]{2,1,0:T(1,128)S(1)} all-gather(f32[1,1,8]{2,1,0:T(1,128)S(1)} %bitcast.102), channel_id=1, replica_groups=mesh['az'=16,'rad'=2] {'rad'}, dimensions={0}, use_global_device_ids=true | all-gather | bytes 96 | tf_op jit(solution)/shard_map/all_gather | solution.py:82
  206.8 4.5 %all-gather.2 = f32[2,4,8]{2,1,0:T(4,128)S(1)} all-gather(f32[1,4,8]{2,1,0:T(4,128)S(1)} %maximum_bitcast_fusion), channel_id=2, replica_groups=mesh['az'=16,'rad'=2] {'rad'}, dimensions={0}, use_global_device_ids=true | all-gather | bytes 384 | tf_op jit(solution)/shard_map/all_gather | solution.py:81
  211.5 49.3 %all-to-all-done.1 = f32[16,1,40960]{2,1,0:T(1,128)S(1)} async-done(((f32[16,1,40960]{2,1,0:T(1,128)}), f32[16,1,40960]{2,1,0:T(1,128)S(1)}, u32[]{:S(2)}, u32[]{:S(2)}) %all-to-all-start.1) | async-done | bytes 2621472 | tf_op jit(solution)/shard_map/all_to_all | solution.py:66
  261.3 9.2 %reduce.8 = f32[16,40960]{1,0:T(8,128)} reduce(f32[16,1,40960]{2,1,0:T(1,128)S(1)} %all-to-all-done.1, f32[]{:T(128)} %broadcast.127), dimensions={1}, to_apply=%all_to_all.25.reduce_sub_computation | reduce | bytes 5242884 | tf_op jit(solution)/shard_map/all_to_all | solution.py:66
  270.5 70.8 %reshape.120 = f32[4096,5,4,8]{3,2,1,0:T(4,128)} reshape(f32[16,40960]{1,0:T(8,128)} %reduce.8) | data formatting | bytes 5242880
  341.3 29.0 %copy.63 = f32[5,8,4,16,256]{4,2,3,1,0:T(4,128)S(1)} copy(f32[5,8,4,16,256]{1,2,0,4,3:T(4,128)} %bitcast.84) | data formatting | bytes 5242880 | tf_op jit(solution)/shard_map/all_to_all | solution.py:66
  370.3 1.7 slice.132
  372.0 2.0 slice.91
  375.0 1.6 convolution_bitcast_fusion
  376.6 4.4 %all_gather.13 = f32[8,2,256]{2,0,1:T(8,128)S(1)} all-gather(f32[8,1,256]{2,0,1:T(8,128)S(1)} %copy.65), channel_id=1, replica_groups=mesh['az'=16,'rad'=2] {'rad'}, dimensions={1}, use_global_device_ids=true | all-gather | bytes 24576 | tf_op jit(solution)/shard_map/all_gather | solution.py:80
  381.0 4.4 %all_gather.15 = f32[8,2,256]{2,0,1:T(8,128)S(1)} all-gather(f32[8,1,256]{2,0,1:T(8,128)S(1)} %copy.66), channel_id=1, replica_groups=mesh['az'=16,'rad'=2] {'rad'}, dimensions={1}, use_global_device_ids=true | all-gather | bytes 24576 | tf_op jit(solution)/shard_map/all_gather | solution.py:79
  385.7 1.7 pad_maximum_fusion.2
  (48 shorter events, 8.7 us)
Async XLA Ops:
  0.0 3.3 copy-start.2
  5.7 7.0 %copy-start.4 = (s32[64]{0:T(128)S(1)}, s32[64]{0:T(128)}, u32[]{:S(2)}) copy-start(s32[64]{0:T(128)} %param.7) | copy-start | bytes 772
  5.7 77.0 %all-to-all-start = ((f32[6,8,64,256]{3,1,0,2:T(8,128)}), f32[6,8,64,256]{3,1,0,2:T(8,128)}, u32[]{:S(2)}, u32[]{:S(2)}) async-start(f32[6,8,64,256]{3,1,0,2:T(8,128)} %pad_maximum_fusion.1), calls=%async_computation | async-start | bytes 6291456 | tf_op jit(solution)/shard_map/all_to_all | solution.py:61
  86.5 1.7 copy-start
  197.1 4.8 %copy-start.3 = (f32[8,1]{0,1:T(1,128)S(1)}, f32[8,1]{0,1:T(1,128)}, u32[]{:S(2)}) copy-start(f32[8,1]{0,1:T(1,128)} %param.9) | copy-start | bytes 100
  197.1 9.0 %copy-start.1 = (f32[8,64,64]{2,1,0:T(8,128)S(1)}, f32[8,64,64]{2,1,0:T(8,128)}, u32[]{:S(2)}) copy-start(f32[8,64,64]{2,1,0:T(8,128)} %param.8) | copy-start | bytes 393220
  197.1 63.7 %all-to-all-start.1 = ((f32[16,1,40960]{2,1,0:T(1,128)}), f32[16,1,40960]{2,1,0:T(1,128)S(1)}, u32[]{:S(2)}, u32[]{:S(2)}) async-start(f32[16,1,40960]{2,1,0:T(1,128)} %reshape.119), calls=%async_computation.1 | async-start | bytes 5242880 | tf_op jit(solution)/shard_map/all_to_all | solution.py:66
where the time goes:
time: 393 us; the launch traced here: 388 us
  local copies, waits for them, and re-layouts  214 us (54%)
  waiting for transfers between devices  119 us (30%)
  other arithmetic  23 us (6%)
  blocking collectives  17.4 us (4%)
  starting transfers between devices  11.8 us (3%)
    unnamed x18, local copies, waits for them, and re-layouts  127 us
    all_to_all x1, waiting for transfers between devices, per_device(): lax.all_to_all(stacked, 'az', split_axis=2, concat_axis=3, tiled=True)  69.8 us
    all_to_all x1, waiting for transfers between devices, per_device(): lax.all_to_all(moved_whole, 'az', split_axis=3, concat_axis=2, tiled=True)  49.3 us
    all_to_all x2, local copies, waits for them, and re-layouts, per_device(): lax.all_to_all(moved_whole, 'az', split_axis=3, concat_axis=2, tiled=True)  29.5 us
    sub x1, local copies, waits for them, and re-layouts, periodic_transport(): return values - (outflow - jnp.roll(outflow, 1, axis=3))  27.7 us
    gather x12, local copies, waits for them, and re-layouts  13.1 us
    all_to_all x1, other arithmetic, per_device(): lax.all_to_all(moved_whole, 'az', split_axis=3, concat_axis=2, tiled=True)  9.16 us
  transfers between devices with their start and end apart: 2, of which 2 were waited for; matrix products, arithmetic and copies ran while one was open for 0% of the time, Pallas kernels for 0%

commit v1 on v0

--- a/solution.py
+++ b/solution.py
@@ -1,13 +1,14 @@
+import functools
+
 import jax
 import jax.numpy as jnp
 from jax import lax
+from jax.experimental import pallas as pl
+from jax.experimental.pallas import tpu as pltpu
 from jax.sharding import PartitionSpec as P
 
-
-def roll_rows(values, amounts):
-    return jax.vmap(
-        lambda one_row, amount: jnp.roll(one_row, amount, axis=-1), in_axes=(2, 0), out_axes=2
-    )(values, amounts)
+LANES = 128
+TILE_ROWS = 8
 
 
 def interface_solve(first_row, last_row, top_left, top_right, low_left, low_right, link_rates):
@@ -50,40 +51,188 @@
     return (before, beyond)
 
 
-def periodic_transport(values, speed):
-    ahead_cells = jnp.roll(values, -1, axis=3)
-    outflow = jnp.maximum(speed, 0.0) * values + jnp.minimum(speed, 0.0) * ahead_cells
-    return values - (outflow - jnp.roll(outflow, 1, axis=3))
+def turn_kernel(shift_ref, in_ref, out_ref):
+    n, nf, rows, width = in_ref.shape
+    per_block = width // LANES
+    tiles = n * per_block
+    groups = rows // TILE_ROWS
+    halo_row = nf * per_block * rows
+    lane = lax.broadcasted_iota(jnp.int32, (TILE_ROWS, LANES), 1)
+    for group in range(groups):
+        here = pl.ds(group * TILE_ROWS, TILE_ROWS)
+        shift = shift_ref[here, :]
+        cells = shift & (LANES - 1)
+        whole = shift >> 7
+        source = (lane - cells) & (LANES - 1)
+        own = lane >= cells
+
+        def one_field(field, _, group=group, here=here, whole=whole, source=source, own=own):
+            turned = []
+            for tile in range(tiles):
+                block, part = divmod(tile, per_block)
+                values = in_ref[block, field, here, part * LANES : (part + 1) * LANES]
+                turned.append(jnp.take_along_axis(values, source, axis=1, mode="promise_in_bounds"))
+            circle = [jnp.where(own, turned[tile], turned[tile - 1]) for tile in range(tiles)]
+            step = 1
+            while step < tiles:
+                wanted = (whole & step) != 0
+                circle = [
+                    jnp.where(wanted, circle[(tile - step) % tiles], circle[tile]) for tile in range(tiles)
+                ]
+                step *= 2
+            for tile in range(tiles):
+                block, part = divmod(tile, per_block)
+                row = (field * per_block + part) * rows + group * TILE_ROWS
+                out_ref[block, pl.ds(pl.multiple_of(row, TILE_ROWS), TILE_ROWS), :] = circle[tile]
+            place = (field * groups + group) * 2
+            edge = (lane == place) | (lane == place + 1)
+            for block in range(n):
+                left = circle[(block * per_block - 1) % tiles]
+                right = circle[((block + 1) * per_block) % tiles]
+                both = pltpu.roll(jnp.where(lane == 0, right, left), place + 1, 1)
+                target = out_ref.at[block, halo_row : halo_row + TILE_ROWS, :]
+                target[...] = jnp.where(edge, both, target[...])
+            return 0
+
+        if group == 0:
+            for block in range(n):
+                out_ref[block, halo_row : halo_row + TILE_ROWS, :] = jnp.zeros(
+                    (TILE_ROWS, LANES), jnp.float32
+                )
+        lax.fori_loop(0, nf, one_field, 0)
+
+
+def turn(shift_rows, gathered):
+    n, nf, rows, width = gathered.shape
+    out_rows = nf * (width // LANES) * rows + TILE_ROWS
+    size = gathered.size * 4
+    return pl.pallas_call(
+        turn_kernel,
+        out_shape=jax.ShapeDtypeStruct((n, out_rows, LANES), jnp.float32),
+        in_specs=[pl.BlockSpec(memory_space=pltpu.VMEM)] * 2,
+        out_specs=pl.BlockSpec(memory_space=pltpu.VMEM),
+        compiler_params=pltpu.CompilerParams(vmem_limit_bytes=32 * 1024 * 1024),
+        cost_estimate=pl.CostEstimate(flops=10 * gathered.size, bytes_accessed=2 * size, transcendentals=0),
+    )(shift_rows, gathered)
+
+
+def carry_kernel(nf, rows, recv_ref, speed_ref, back_ref, *rest):
+    out_ref = rest[-1]
+    pieces = recv_ref.shape[0]
+    width = speed_ref.shape[-1]
+    per_block = width // LANES
+    groups = rows // TILE_ROWS
+    halo_row = nf * per_block * rows
+    lane = lax.broadcasted_iota(jnp.int32, (TILE_ROWS, LANES), 1)
+    first = lane == 0
+    last = lane == LANES - 1
+    for piece in range(pieces):
+        halo = recv_ref[piece, halo_row : halo_row + TILE_ROWS, :]
+        for group in range(groups):
+            at = piece * rows + group * TILE_ROWS
+            fore = []
+            for part in range(per_block):
+                cut = (slice(at, at + TILE_ROWS), slice(part * LANES, (part + 1) * LANES))
+                speed = speed_ref[(0,) + cut]
+                back = back_ref[(0,) + cut]
+                fore.append(
+                    (
+                        jnp.maximum(speed, 0.0),
+                        jnp.minimum(speed, 0.0),
+                        jnp.maximum(back, 0.0),
+                        jnp.minimum(back, 0.0),
+                    )
+                )
+            for field in range(nf):
+                values = []
+                for part in range(per_block):
+                    row = (field * per_block + part) * rows + group * TILE_ROWS
+                    values.append(recv_ref[piece, row : row + TILE_ROWS, :])
+                place = (field * groups + group) * 2
+                up = [pltpu.roll(halo, (LANES - place) % LANES, 1)]
+                up += [pltpu.roll(one, 1, 1) for one in values]
+                down = [pltpu.roll(one, LANES - 1, 1) for one in values]
+                down.append(pltpu.roll(halo, (LANES - 2 - place) % LANES, 1))
+                for part in range(per_block):
+                    here = values[part]
+                    behind = jnp.where(first, up[part], up[part + 1])
+                    ahead = jnp.where(last, down[part + 1], down[part])
+                    plus, minus, back_plus, back_minus = fore[part]
+                    outflow = plus * here + minus * ahead
+                    inflow = back_plus * behind + back_minus * here
+                    out_ref[field, 0, at : at + TILE_ROWS, part * LANES : (part + 1) * LANES] = here - (
+                        outflow - inflow
+                    )
+    if len(rest) == 2:
+        out_ref[nf, 0] = rest[0][0]
+
+
+def carry(nf, received, speed, back_speed, *energy):
+    n, in_rows, _ = received.shape
+    levels, radii, width = speed.shape
+    rows = levels * radii // n
+    pieces = n // levels
+    plane = pl.BlockSpec((1, radii, width), lambda level: (level, 0, 0))
+    out_fields = nf + len(energy)
+    size = speed.size * 4
+    return pl.pallas_call(
+        functools.partial(carry_kernel, nf, rows),
+        grid=(levels,),
+        out_shape=jax.ShapeDtypeStruct((out_fields, levels, radii, width), jnp.float32),
+        in_specs=[
+            pl.BlockSpec((pieces, in_rows, LANES), lambda level: (level, 0, 0)),
+            plane,
+            plane,
+        ]
+        + [plane] * len(energy),
+        out_specs=pl.BlockSpec((out_fields, 1, radii, width), lambda level: (0, level, 0, 0)),
+        compiler_params=pltpu.CompilerParams(vmem_limit_bytes=32 * 1024 * 1024),
+        cost_estimate=pl.CostEstimate(
+            flops=10 * nf * speed.size, bytes_accessed=(2 * out_fields + 2) * size, transcendentals=0
+        ),
+    )(received, speed, back_speed, *energy)
+
+
+def exchange(blocks):
+    return lax.all_to_all(blocks, "az", split_axis=0, concat_axis=0, tiled=True)
 
 
 def per_device(fields, velocity, shifts, block_inverse, coupling):
-    stacked = jnp.concatenate([fields, velocity[None]], axis=0)
-    grouped = lax.all_to_all(stacked, "az", split_axis=2, concat_axis=3, tiled=True)
-    share = grouped.shape[2]
-    own_shifts = lax.dynamic_slice_in_dim(shifts, lax.axis_index("az") * share, share)
-    rotated = roll_rows(grouped[:5], own_shifts)
-    moved_whole = periodic_transport(rotated, grouped[5:])
-    transported = lax.all_to_all(moved_whole, "az", split_axis=3, concat_axis=2, tiled=True)
-    energy = transported[4]
-    local_part = jnp.einsum("zrl,zlp->zrp", block_inverse, energy, precision=lax.Precision.HIGHEST)
+    n = lax.axis_size("az")
+    nf, levels, radii, width = fields.shape
+    rows = levels * radii // n
+    me = lax.axis_index("az")
+
+    energy_blocks = exchange(fields[nf - 1].reshape(n, 1, rows, width))
+    rest_blocks = exchange(fields[: nf - 1].reshape(nf - 1, n, rows, width).transpose(1, 0, 2, 3))
+
+    own_shifts = lax.dynamic_slice_in_dim(shifts, (me * rows) % radii, rows)
+    shift_rows = jnp.broadcast_to(own_shifts[:, None], (rows, LANES))
+    edge_speed = lax.ppermute(velocity[:, :, -1], "az", [(i, (i + 1) % n) for i in range(n)])
+    back_speed = jnp.concatenate([edge_speed[:, :, None], velocity[:, :, :-1]], axis=2)
+
     corners = jnp.stack(
         [
             block_inverse[:, 0, 0],
             block_inverse[:, 0, -1],
             block_inverse[:, -1, 0],
             block_inverse[:, -1, -1],
+            coupling[:, 0],
         ],
         axis=1,
-    )[:, None, :]
-    first_all, last_all, corner_all, link_all = (
-        lax.all_gather(local_part[:, :1, :], "rad", axis=1, tiled=True),
-        lax.all_gather(local_part[:, -1:, :], "rad", axis=1, tiled=True),
-        lax.all_gather(corners, "rad", axis=1, tiled=True),
-        lax.all_gather(coupling, "rad", axis=1, tiled=True),
-    )
+    )
+    corner_all = lax.all_gather(corners, "rad", axis=1)
+
+    energy_turned = exchange(turn(shift_rows, energy_blocks))
+    rest_turned = exchange(turn(shift_rows, rest_blocks))
+
+    energy = carry(1, energy_turned, velocity, back_speed)[0]
+    local_part = jnp.einsum("zrl,zlp->zrp", block_inverse, energy, precision=lax.Precision.HIGHEST)
+    ends = lax.all_gather(jnp.stack([local_part[:, 0, :], local_part[:, -1, :]], axis=0), "rad", axis=2)
+    link_all = corner_all[..., 4]
     before, beyond = interface_solve(
-        first_all,
-        last_all,
+        ends[0],
+        ends[1],
         corner_all[..., 0],
         corner_all[..., 1],
         corner_all[..., 2],
@@ -101,7 +250,7 @@
         + (prev_own[:, None] * block_inverse[:, :, 0])[:, :, None] * before_own[:, None, :]
         + (link_own[:, None] * block_inverse[:, :, -1])[:, :, None] * beyond_own[:, None, :]
     )
-    return jnp.concatenate([transported[:4], diffused[None]], axis=0)
+    return carry(nf - 1, rest_turned, velocity, back_speed, diffused)
 
 
 def solution(mesh):

time: 393 us -> 166 us (0.42)
  the two profiles are of different devices: /device:TPU:20 before, /device:TPU:16 now
where the time goes in v1:
time: 166 us
  waiting for transfers between devices  107 us (64%)
  starting transfers between devices  20.4 us (12%)
  local copies, waits for them, and re-layouts  13.4 us (8%)
  Pallas kernels  9.49 us (6%)
  blocking collectives  8.77 us (5%)
  other arithmetic  5.79 us (3%)
    all_to_all x4, waiting for transfers between devices, exchange(): return lax.all_to_all(blocks, 'az', split_axis=0, concat_axis=0, tiled=True)  67.9 us
    ppermute x1, waiting for transfers between devices, per_device(): lax.ppermute(velocity[:, :, -1], 'az', [(i, (i + 1) % n) for i in range(n)])  39.1 us
    all_to_all x4, starting transfers between devices, exchange(): return lax.all_to_all(blocks, 'az', split_axis=0, concat_axis=0, tiled=True)  20.2 us
    unnamed x25, local copies, waits for them, and re-layouts  5.67 us
    pallas_call x2, Pallas kernels, carry(): pl.pallas_call(functools.partial(carry_kernel, nf, rows), grid=(levels,),...  5.08 us
    all_gather x1, blocking collectives, per_device(): lax.all_gather(jnp.stack([local_part[:, 0, :], local_part[:, -1, :]], axi...  4.44 us
    pallas_call x2, Pallas kernels, turn(): pl.pallas_call(turn_kernel, out_shape=jax.ShapeDtypeStruct((n, out_rows,...  4.41 us
    all_gather x1, blocking collectives, per_device(): corner_all = lax.all_gather(corners, 'rad', axis=1)  4.34 us
  transfers between devices with their start and end apart: 5, of which 4 were waited for; matrix products, arithmetic and copies ran while one was open for 7% of the time, Pallas kernels for 3%

profile of v1, /device:TPU:16, one launch (start us, length us, event | category | flops | bytes accessed | tf_op | source)
XLA Modules:
  0.0 165.6 jit_solution(10288134854876881490)
XLA Ops:
  0.0 1.9 %slice.71 = f32[1,8,64,256]{3,2,1,0:T(8,128)} slice(f32[5,8,64,256]{3,2,1,0:T(8,128)} %param.5), slice={[4:5], [0:8], [0:64], [0:256]} | slice | bytes 1048576 | tf_op jit(solution)/shard_map/slice | solution.py:206
  1.9 6.2 %all-to-all-start.2 = ((f32[16,1,32,256]{3,2,1,0:T(8,128)}), f32[16,1,32,256]{3,2,1,0:T(8,128)S(1)}, u32[]{:S(2)}, u32[]{:S(2)}) async-start(f32[16,1,32,256]{3,2,1,0:T(8,128)} %bitcast.4), calls=%async_computation.2 | async-start | bytes 1048576 | tf_op jit(solution)/shard_map/all_to_all | solution.py:197
  8.0 1.6 slice-done
  9.6 1.5 copy.60
  11.1 10.8 %all-to-all-done.2.in_ref = f32[16,1,32,256]{3,2,1,0:T(8,128)S(1)} async-done(((f32[16,1,32,256]{3,2,1,0:T(8,128)}), f32[16,1,32,256]{3,2,1,0:T(8,128)S(1)}, u32[]{:S(2)}, u32[]{:S(2)}) %all-to-all-start.2) | async-done | bytes 524320 | tf_op jit(solution)/shard_map/all_to_all | solution.py:197
  21.9 4.7 %all-to-all-start = ((f32[16,4,32,256]{3,2,1,0:T(8,128)}), f32[16,4,32,256]{3,2,1,0:T(8,128)S(1)}, u32[]{:S(2)}, u32[]{:S(2)}) async-start(f32[16,4,32,256]{3,2,1,0:T(8,128)} %bitcast.52), calls=%async_computation | async-start | bytes 4194304 | tf_op jit(solution)/shard_map/all_to_all | solution.py:197
  26.8 1.3 shard_map.56
  28.1 46.1 %all-to-all-done.in_ref = f32[16,4,32,256]{3,2,1,0:T(8,128)S(1)} async-done(((f32[16,4,32,256]{3,2,1,0:T(8,128)}), f32[16,4,32,256]{3,2,1,0:T(8,128)S(1)}, u32[]{:S(2)}, u32[]{:S(2)}) %all-to-all-start) | async-done | bytes 2097184 | tf_op jit(solution)/shard_map/all_to_all | solution.py:197
  74.2 4.7 %all-to-all-start.3 = ((f32[16,72,128]{2,1,0:T(8,128)}), f32[16,72,128]{2,1,0:T(8,128)S(1)}, u32[]{:S(2)}, u32[]{:S(2)}) async-start(f32[16,72,128]{2,1,0:T(8,128)} %shard_map.56), calls=%async_computation.3 | async-start | bytes 1179648 | tf_op jit(solution)/shard_map/all_to_all | solution.py:197
  78.9 3.1 %shard_map.55 = f32[16,264,128]{2,1,0:T(8,128)S(1)} custom-call(s32[32,128]{1,0:T(8,128)S(1)} %broadcast_in_dim.4.shift_ref, f32[16,4,32,256]{3,2,1,0:T(8,128)S(1)} %all-to-all-done.in_ref), custom_call_target="tpu_custom_call" | custom-call | flops 5242880 | bytes 4194304 | tf_op jit(solution)/shard_map/pallas_call | solution.py:109
  82.0 1.3 copy-done
  83.3 10.9 %all-to-all-done.3.recv_ref = f32[16,72,128]{2,1,0:T(8,128)S(1)} async-done(((f32[16,72,128]{2,1,0:T(8,128)}), f32[16,72,128]{2,1,0:T(8,128)S(1)}, u32[]{:S(2)}, u32[]{:S(2)}) %all-to-all-start.3) | async-done | bytes 589856 | tf_op jit(solution)/shard_map/all_to_all | solution.py:197
  94.2 4.7 %all-to-all-start.1 = ((f32[16,264,128]{2,1,0:T(8,128)}), f32[16,264,128]{2,1,0:T(8,128)S(1)}, u32[]{:S(2)}, u32[]{:S(2)}) async-start(f32[16,264,128]{2,1,0:T(8,128)} %copy-done), calls=%async_computation.1 | async-start | bytes 4325376 | tf_op jit(solution)/shard_map/all_to_all | solution.py:197
  98.9 0.8 slice.69
  99.8 1.1 copy.41
  101.0 0.2 slice_reduce_fusion.2
  101.3 4.3 %all-gather.2 = f32[2,5,8]{2,1,0:T(8,128)S(1)} all-gather(f32[1,5,8]{2,1,0:T(8,128)S(1)} %bitcast.55), channel_id=2, replica_groups=mesh['az'=16,'rad'=2] {'rad'}, dimensions={0}, use_global_device_ids=true | all-gather | bytes 480 | tf_op jit(solution)/shard_map/all_gather | solution.py:224
  106.5 0.6 multiply_bitcast_fusion.3
  107.2 0.7 multiply_bitcast_fusion
  108.0 0.5 multiply_bitcast_fusion.2
  108.5 39.1 %collective-permute-done = f32[8,64]{1,0:T(8,128)S(1)} collective-permute-done((f32[8,64]{1,0:T(8,128)S(1)}, f32[8,64]{1,0:T(8,128)S(1)}, u32[]{:S(2)}, u32[]{:S(2)}) %collective-permute-start) | collective-permute-done | bytes 2080 | tf_op jit(solution)/shard_map/ppermute | solution.py:211
  147.6 0.9 copy.31
  148.4 1.1 pad_maximum_fusion.back_ref
  149.6 1.1 copy-done.3
  150.7 1.0 shard_map.57
  151.6 0.6 convolution_bitcast_fusion
  152.2 0.8 copy-done.6
  153.1 4.4 %all-gather.1 = f32[2,8,512]{2,0,1:T(2,128)S(1)} all-gather(f32[2,8,256]{2,0,1:T(2,128)S(1)} %pad_maximum_fusion.1), channel_id=3, replica_groups=mesh['az'=16,'rad'=2] {'rad'}, dimensions={2}, use_global_device_ids=true | all-gather | bytes 49152 | tf_op jit(solution)/shard_map/all_gather | solution.py:231
  157.7 0.7 add_add_fusion
  158.4 2.0 %multiply_add_fusion.rest_0_ = f32[8,64,256]{2,1,0:T(8,128)} fusion(f32[8,64,256]{2,1,0:T(8,128)} %copy-done.6, f32[8,256]{1,0:T(8,128)S(1)} %get-tuple-element.27, f32[8,64]{1,0:T(8,128)S(1)} %multiply_bitcast_fusion, f32[8,256]{1,0:T(8,128)S(1)} %get-tuple-element.26, f32[8,64]{1,0:T(8,128)S(1)} %multiply_bitcast_fusion.1), kind=kLoop, calls=%fused_computation.4 | loop fusion | flops 524288 | bytes 1069056 | tf_op jit(solution)/shard_map/add | solution.py:249
  160.4 1.0 copy-done.4
  161.4 4.1 %shard_map.58 = f32[5,8,64,256]{3,2,1,0:T(8,128)} custom-call(f32[16,264,128]{2,1,0:T(8,128)S(1)} %all-to-all-done.1.recv_ref, f32[8,64,256]{2,1,0:T(8,128)S(1)} %copy-done.1, f32[8,64,256]{2,1,0:T(8,128)S(1)} %pad_maximum_fusion.back_ref, f32[8,64,256]{2,1,0:T(8,128)S(1)} %copy-done.4), custom_call_target="tpu_custom_call" | custom-call | flops 5242880 | bytes 6291456 | tf_op jit(solution)/shard_map/pallas_call | solution.py:178
  (42 shorter events, 1.6 us)
Async XLA Ops:
  1.9 20.1 %all-to-all-start.2 = ((f32[16,1,32,256]{3,2,1,0:T(8,128)}), f32[16,1,32,256]{3,2,1,0:T(8,128)S(1)}, u32[]{:S(2)}, u32[]{:S(2)}) async-start(f32[16,1,32,256]{3,2,1,0:T(8,128)} %bitcast.4), calls=%async_computation.2 | async-start | bytes 1048576 | tf_op jit(solution)/shard_map/all_to_all | solution.py:197
  8.0 1.6 slice-start
  11.1 15.5 %copy-start.9 = (s32[64]{0:T(128)S(1)}, s32[64]{0:T(128)}, u32[]{:S(2)}) copy-start(s32[64]{0:T(128)} %param.7) | copy-start | bytes 772
  21.9 52.3 %all-to-all-start = ((f32[16,4,32,256]{3,2,1,0:T(8,128)}), f32[16,4,32,256]{3,2,1,0:T(8,128)S(1)}, u32[]{:S(2)}, u32[]{:S(2)}) async-start(f32[16,4,32,256]{3,2,1,0:T(8,128)} %bitcast.52), calls=%async_computation | async-start | bytes 4194304 | tf_op jit(solution)/shard_map/all_to_all | solution.py:197
  74.2 20.0 %all-to-all-start.3 = ((f32[16,72,128]{2,1,0:T(8,128)}), f32[16,72,128]{2,1,0:T(8,128)S(1)}, u32[]{:S(2)}, u32[]{:S(2)}) async-start(f32[16,72,128]{2,1,0:T(8,128)} %shard_map.56), calls=%async_computation.3 | async-start | bytes 1179648 | tf_op jit(solution)/shard_map/all_to_all | solution.py:197
  82.0 1.3 copy-start
  83.3 15.6 %copy-start.1 = (f32[8,64,256]{2,1,0:T(8,128)S(1)}, f32[8,64,256]{2,1,0:T(8,128)}, u32[]{:S(2)}) copy-start(f32[8,64,256]{2,1,0:T(8,128)} %speed_ref.3) | copy-start | bytes 1572868
  83.3 17.7 %copy-start.5 = (f32[8,64,64]{2,1,0:T(8,128)S(1)}, f32[8,64,64]{2,1,0:T(8,128)}, u32[]{:S(2)}) copy-start(f32[8,64,64]{2,1,0:T(8,128)} %param.8) | copy-start | bytes 393220
  83.3 17.9 %copy-start.8 = (f32[8,1]{0,1:T(1,128)S(1)}, f32[8,1]{0,1:T(1,128)}, u32[]{:S(2)}) copy-start(f32[8,1]{0,1:T(1,128)} %param.9) | copy-start | bytes 100
  94.2 5.5 %copy-start.2 = (f32[16,72,128]{2,1,0:T(8,128)}, f32[16,72,128]{2,1,0:T(8,128)S(1)}, u32[]{:S(2)}) copy-start(f32[16,72,128]{2,1,0:T(8,128)S(1)} %all-to-all-done.3.recv_ref) | copy-start | bytes 1769476
  94.2 66.2 %all-to-all-start.1 = ((f32[16,264,128]{2,1,0:T(8,128)}), f32[16,264,128]{2,1,0:T(8,128)S(1)}, u32[]{:S(2)}, u32[]{:S(2)}) async-start(f32[16,264,128]{2,1,0:T(8,128)} %copy-done), calls=%async_computation.1 | async-start | bytes 4325376 | tf_op jit(solution)/shard_map/all_to_all | solution.py:197
  100.8 46.7 %collective-permute-start = (f32[8,64]{1,0:T(8,128)S(1)}, f32[8,64]{1,0:T(8,128)S(1)}, u32[]{:S(2)}, u32[]{:S(2)}) collective-permute-start(f32[8,64]{1,0:T(8,128)S(1)} %bitcast.56), channel_id=1, source_target_pairs={{0,2},{2,4},{4,6},{6,8},{8,10},{10,12},{12,14},{14,16},{16,18},{18... | collective-permute-start | bytes 6152 | tf_op jit(solution)/shard_map/ppermute | solution.py:211
  149.6 1.1 copy-start.3
  150.7 7.0 %copy-start.7 = (f32[8]{0:T(128)S(1)}, f32[8]{0:T(128)}, u32[]{:S(2)}) copy-start(f32[8]{0:T(128)} %get-tuple-element.24) | copy-start | bytes 100
  152.2 0.8 copy-start.6
  160.4 1.0 copy-start.4

commit v2 on v1

v2 whole, which is shorter than its diff:
```python
import functools

import jax
import jax.numpy as jnp
from jax import lax
from jax.experimental import pallas as pl
from jax.experimental.pallas import tpu as pltpu
from jax.sharding import PartitionSpec as P

LANES = 128
TILE_ROWS = 8


def interface_solve(first_row, last_row, top_left, top_right, low_left, low_right, link_rates):
    band_count = link_rates.shape[1]
    crossings = band_count - 1
    nothing = jnp.zeros_like(first_row[:, 0])
    flat_zero = jnp.zeros_like(link_rates[:, :1])
    carry_base = nothing
    carry_slope = flat_zero
    records = []
    for crossing in range(crossings):
        if crossing > 0:
            back_link = (link_rates[:, crossing - 1] * low_left[:, crossing])[:, None]
        else:
            back_link = flat_zero
        self_link = (link_rates[:, crossing] * low_right[:, crossing])[:, None]
        fore_link = (link_rates[:, crossing] * top_left[:, crossing + 1])[:, None]
        if crossing + 1 < crossings:
            next_link = (link_rates[:, crossing + 1] * top_right[:, crossing + 1])[:, None]
        else:
            next_link = flat_zero
        steepness = back_link * carry_slope + self_link
        offset = last_row[:, crossing] + back_link * carry_base
        denominator = 1.0 - fore_link * steepness
        upper_base = (first_row[:, crossing + 1] + fore_link * offset) / denominator
        upper_slope = next_link / denominator
        carry_base = offset + steepness * upper_base
        carry_slope = steepness * upper_slope
        records.append((carry_base, carry_slope, upper_base, upper_slope))
    lower_values = [nothing] * crossings
    upper_values = [nothing] * crossings
    follow = nothing
    for crossing in reversed(range(crossings)):
        carry_base, carry_slope, upper_base, upper_slope = records[crossing]
        lower_values[crossing] = carry_base + carry_slope * follow
        upper_values[crossing] = upper_base + upper_slope * follow
        follow = upper_values[crossing]
    before = jnp.stack([nothing] + lower_values, axis=1)
    beyond = jnp.stack(upper_values + [nothing], axis=1)
    return (before, beyond)


def turn_fields(shift_ref, blocks, outs, nf):
    n = len(blocks)
    rows, width = blocks[0].shape[-2:]
    per_block = width // LANES
    tiles = n * per_block
    groups = rows // TILE_ROWS
    halo_row = nf * per_block * rows
    lane = lax.broadcasted_iota(jnp.int32, (TILE_ROWS, LANES), 1)
    for block in range(n):
        outs[block][halo_row : halo_row + TILE_ROWS, :] = jnp.zeros((TILE_ROWS, LANES), jnp.float32)
    for group in range(groups):
        here = pl.ds(group * TILE_ROWS, TILE_ROWS)
        shift = shift_ref[here, :]
        cells = shift & (LANES - 1)
        whole = shift >> 7
        source = (lane - cells) & (LANES - 1)
        own = lane >= cells

        def one_field(field, _, group=group, here=here, whole=whole, source=source, own=own):
            turned = []
            for tile in range(tiles):
                block, part = divmod(tile, per_block)
                values = blocks[block][field, here, part * LANES : (part + 1) * LANES]
                turned.append(jnp.take_along_axis(values, source, axis=1, mode="promise_in_bounds"))
            circle = [jnp.where(own, turned[tile], turned[tile - 1]) for tile in range(tiles)]
            step = 1
            while step < tiles:
                wanted = (whole & step) != 0
                circle = [
                    jnp.where(wanted, circle[(tile - step) % tiles], circle[tile]) for tile in range(tiles)
                ]
                step *= 2
            for tile in range(tiles):
                block, part = divmod(tile, per_block)
                row = (field * per_block + part) * rows + group * TILE_ROWS
                outs[block][pl.ds(pl.multiple_of(row, TILE_ROWS), TILE_ROWS), :] = circle[tile]
            place = (field * groups + group) * 2
            edge = (lane == place) | (lane == place + 1)
            for block in range(n):
                left = circle[(block * per_block - 1) % tiles]
                right = circle[((block + 1) * per_block) % tiles]
                both = pltpu.roll(jnp.where(lane == 0, right, left), place + 1, 1)
                target = outs[block].at[halo_row : halo_row + TILE_ROWS, :]
                target[...] = jnp.where(edge, both, target[...])
            return 0

        lax.fori_loop(0, nf, one_field, 0)


def turn_kernel(shift_ref, in_ref, out_ref):
    n, nf = in_ref.shape[:2]
    turn_fields(shift_ref, [in_ref.at[i] for i in range(n)], [out_ref.at[i] for i in range(n)], nf)


def turn_apart_kernel(shift_ref, *refs):
    n = len(refs) // 2
    turn_fields(shift_ref, [refs[i].reshape((1,) + refs[i].shape) for i in range(n)], refs[n:], 1)


VMEM_SPEC = pl.BlockSpec(memory_space=pltpu.VMEM)
ROOMY = pltpu.CompilerParams(vmem_limit_bytes=32 * 1024 * 1024)


def turn(shift_rows, gathered):
    n, nf, rows, width = gathered.shape
    out_rows = nf * (width // LANES) * rows + TILE_ROWS
    size = gathered.size * 4
    return pl.pallas_call(
        turn_kernel,
        out_shape=jax.ShapeDtypeStruct((n, out_rows, LANES), jnp.float32),
        in_specs=[VMEM_SPEC] * 2,
        out_specs=VMEM_SPEC,
        compiler_params=ROOMY,
        cost_estimate=pl.CostEstimate(flops=10 * gathered.size, bytes_accessed=2 * size, transcendentals=0),
    )(shift_rows, gathered)


def turn_apart(shift_rows, blocks):
    n = len(blocks)
    rows, width = blocks[0].shape
    out_rows = (width // LANES) * rows + TILE_ROWS
    size = n * rows * width
    return pl.pallas_call(
        turn_apart_kernel,
        out_shape=[jax.ShapeDtypeStruct((out_rows, LANES), jnp.float32)] * n,
        in_specs=[VMEM_SPEC] * (n + 1),
        out_specs=[VMEM_SPEC] * n,
        compiler_params=ROOMY,
        cost_estimate=pl.CostEstimate(flops=10 * size, bytes_accessed=8 * size, transcendentals=0),
    )(shift_rows, *blocks)


def split_kernel(me_ref, in_ref, *rest):
    outs, sems = rest[:-1], rest[-1]
    n = len(outs)
    copies = []
    for distance in range(n):
        owner = lax.rem(me_ref[0] + distance, n)
        copies.append(
            pltpu.make_async_copy(
                in_ref.at[in_ref.shape[0] - 1, owner], outs[distance], sems.at[distance]
            )
        )
    for copy in copies:
        copy.start()
    for copy in copies:
        copy.wait()


def split(me, blocked):
    _, n, rows, width = blocked.shape
    return pl.pallas_call(
        split_kernel,
        out_shape=[jax.ShapeDtypeStruct((rows, width), jnp.float32)] * n,
        in_specs=[pl.BlockSpec(memory_space=pltpu.SMEM), pl.BlockSpec(memory_space=pl.ANY)],
        out_specs=[VMEM_SPEC] * n,
        scratch_shapes=[pltpu.SemaphoreType.DMA((n,))],
        compiler_params=ROOMY,
        cost_estimate=pl.CostEstimate(flops=0, bytes_accessed=8 * n * rows * width, transcendentals=0),
    )(me, blocked)


def send_apart(blocks):
    n = len(blocks)
    return [blocks[0]] + [
        lax.ppermute(blocks[distance], "az", [(i, (i + distance) % n) for i in range(n)])
        for distance in range(1, n)
    ]


def carry_piece(nf, recv, speed, back, store):
    rows, width = speed.shape
    per_block = width // LANES
    groups = rows // TILE_ROWS
    halo_row = nf * per_block * rows
    lane = lax.broadcasted_iota(jnp.int32, (TILE_ROWS, LANES), 1)
    first = lane == 0
    last = lane == LANES - 1
    halo = recv[halo_row : halo_row + TILE_ROWS, :]
    for group in range(groups):
        at = slice(group * TILE_ROWS, (group + 1) * TILE_ROWS)
        rates = []
        for part in range(per_block):
            cut = (at, slice(part * LANES, (part + 1) * LANES))
            ahead_speed = speed[cut]
            back_speed = back[cut]
            rates.append(
                (
                    jnp.maximum(ahead_speed, 0.0),
                    jnp.minimum(ahead_speed, 0.0),
                    jnp.maximum(back_speed, 0.0),
                    jnp.minimum(back_speed, 0.0),
                )
            )
        for field in range(nf):
            values = []
            for part in range(per_block):
                row = (field * per_block + part) * rows + group * TILE_ROWS
                values.append(recv[row : row + TILE_ROWS, :])
            place = (field * groups + group) * 2
            up = [pltpu.roll(halo, (LANES - place) % LANES, 1)]
            up += [pltpu.roll(one, 1, 1) for one in values]
            down = [pltpu.roll(one, LANES - 1, 1) for one in values]
            down.append(pltpu.roll(halo, (LANES - 2 - place) % LANES, 1))
            for part in range(per_block):
                here = values[part]
                behind = jnp.where(first, up[part], up[part + 1])
                ahead = jnp.where(last, down[part + 1], down[part])
                plus, minus, back_plus, back_minus = rates[part]
                outflow = plus * here + minus * ahead
                inflow = back_plus * behind + back_minus * here
                store(field, group * TILE_ROWS, part * LANES, here - (outflow - inflow))


def carry_kernel(nf, rows, recv_ref, speed_ref, back_ref, energy_ref, out_ref):
    for piece in range(recv_ref.shape[0]):
        here = pl.ds(piece * rows, rows)

        def store(field, row, cell, values, piece=piece):
            row += piece * rows
            out_ref[field, 0, row : row + TILE_ROWS, cell : cell + LANES] = values

        carry_piece(nf, recv_ref.at[piece], speed_ref.at[0, here], back_ref.at[0, here], store)
    out_ref[nf, 0] = energy_ref[0]


def carry(received, speed, back_speed, energy):
    n, in_rows, _ = received.shape
    levels, radii, width = speed.shape
    rows = levels * radii // n
    nf = (in_rows - TILE_ROWS) * LANES // (rows * width)
    pieces = n // levels
    plane = pl.BlockSpec((1, radii, width), lambda level: (level, 0, 0))
    size = speed.size * 4
    return pl.pallas_call(
        functools.partial(carry_kernel, nf, rows),
        grid=(levels,),
        out_shape=jax.ShapeDtypeStruct((nf + 1, levels, radii, width), jnp.float32),
        in_specs=[pl.BlockSpec((pieces, in_rows, LANES), lambda level: (level, 0, 0)), plane, plane, plane],
        out_specs=pl.BlockSpec((nf + 1, 1, radii, width), lambda level: (0, level, 0, 0)),
        compiler_params=ROOMY,
        cost_estimate=pl.CostEstimate(
            flops=10 * nf * speed.size, bytes_accessed=(2 * nf + 4) * size, transcendentals=0
        ),
    )(received, speed, back_speed, energy)


def carry_apart_kernel(me_ref, speed_ref, back_ref, *refs):
    out_ref = refs[-1]
    n = len(refs) - 1
    rows = speed_ref.shape[1]
    for distance in range(n):
        owner = lax.rem(me_ref[0] + (n - distance), n)

        def store(field, row, cell, values, owner=owner):
            out_ref[owner, row : row + TILE_ROWS, cell : cell + LANES] = values

        carry_piece(1, refs[distance], speed_ref.at[owner], back_ref.at[owner], store)


def carry_apart(me, speed, back_speed, received):
    n = len(received)
    levels, radii, width = speed.shape
    shape = (n, levels * radii // n, width)
    return pl.pallas_call(
        carry_apart_kernel,
        out_shape=jax.ShapeDtypeStruct(shape, jnp.float32),
        in_specs=[pl.BlockSpec(memory_space=pltpu.SMEM)] + [VMEM_SPEC] * (n + 2),
        out_specs=VMEM_SPEC,
        compiler_params=ROOMY,
        cost_estimate=pl.CostEstimate(
            flops=10 * speed.size, bytes_accessed=16 * speed.size, transcendentals=0
        ),
    )(me, speed.reshape(shape), back_speed.reshape(shape), *received).reshape(speed.shape)


def exchange(blocks):
    return lax.all_to_all(blocks, "az", split_axis=0, concat_axis=0, tiled=True)


def per_device(fields, velocity, shifts, block_inverse, coupling):
    n = lax.axis_size("az")
    nf, levels, radii, width = fields.shape
    rows = levels * radii // n
    me = lax.axis_index("az")

    me_scalar = me[None].astype(jnp.int32)
    blocked = fields.reshape(nf, n, rows, width)

    energy_blocks = send_apart(split(me_scalar, blocked))
    rest_blocks = exchange(blocked[: nf - 1].transpose(1, 0, 2, 3))

    own_shifts = lax.dynamic_slice_in_dim(shifts, (me * rows) % radii, rows)
    shift_rows = jnp.broadcast_to(own_shifts[:, None], (rows, LANES))
    edge_speed = lax.ppermute(velocity[:, :, -1], "az", [(i, (i + 1) % n) for i in range(n)])
    back_speed = jnp.concatenate([edge_speed[:, :, None], velocity[:, :, :-1]], axis=2)

    corners = jnp.stack(
        [
            block_inverse[:, 0, 0],
            block_inverse[:, 0, -1],
            block_inverse[:, -1, 0],
            block_inverse[:, -1, -1],
            coupling[:, 0],
        ],
        axis=1,
    )
    corner_all = lax.all_gather(corners, "rad", axis=1)
    energy_blocks, back_speed, corner_all = lax.optimization_barrier((energy_blocks, back_speed, corner_all))

    ordered = [energy_blocks[(n - m) % n] for m in range(n)]
    energy_turned = send_apart(turn_apart(shift_rows, ordered))
    rest_turned = exchange(turn(shift_rows, rest_blocks))

    energy = carry_apart(me_scalar, velocity, back_speed, energy_turned)
    local_part = jnp.einsum("zrl,zlp->zrp", block_inverse, energy, precision=lax.Precision.HIGHEST)
    ends = lax.all_gather(jnp.stack([local_part[:, 0, :], local_part[:, -1, :]], axis=0), "rad", axis=2)
    link_all = corner_all[..., 4]
    before, beyond = interface_solve(
        ends[0],
        ends[1],
        corner_all[..., 0],
        corner_all[..., 1],
        corner_all[..., 2],
        corner_all[..., 3],
        link_all,
    )
    band_index = lax.axis_index("rad")
    before_own = lax.dynamic_index_in_dim(before, band_index, 1, keepdims=False)
    beyond_own = lax.dynamic_index_in_dim(beyond, band_index, 1, keepdims=False)
    link_prev = jnp.concatenate([jnp.zeros_like(link_all[:, :1]), link_all[:, :-1]], axis=1)
    prev_own = lax.dynamic_index_in_dim(link_prev, band_index, 1, keepdims=False)
    link_own = coupling[:, 0]
    diffused = (
        local_part
        + (prev_own[:, None] * block_inverse[:, :, 0])[:, :, None] * before_own[:, None, :]
        + (link_own[:, None] * block_inverse[:, :, -1])[:, :, None] * beyond_own[:, None, :]
    )
    return carry(rest_turned, velocity, back_speed, diffused)


def solution(mesh):
    placed = (
        P(None, None, "rad", "az"),
        P(None, "rad", "az"),
        P("rad"),
        P(None, "rad", None),
        P(None, "rad"),
    )
    return jax.shard_map(
        per_device,
        mesh=mesh,
        in_specs=placed,
        out_specs=P(None, None, "rad", "az"),
        check_vma=False,
    )
```

time: 166 us -> 199 us (1.20)
  the two profiles are of different devices: /device:TPU:16 before, /device:TPU:0 now
where the time goes in v2:
time: 199 us; the launch traced here: 198 us
  waiting for transfers between devices  73.7 us (37%)
  starting transfers between devices  66.7 us (34%)
  local copies, waits for them, and re-layouts  32.8 us (16%)
  Pallas kernels  9.74 us (5%)
  blocking collectives  8.78 us (4%)
  other arithmetic  5.41 us (3%)
    ppermute x30, starting transfers between devices, send_apart(): lax.ppermute(blocks[distance], 'az', [(i, (i + distance) % n) for i in ra...  47.4 us
    all_to_all x2, waiting for transfers between devices, exchange(): return lax.all_to_all(blocks, 'az', split_axis=0, concat_axis=0, tiled=True)  41 us
    ppermute x1, waiting for transfers between devices, per_device(): lax.ppermute(velocity[:, :, -1], 'az', [(i, (i + 1) % n) for i in range(n)])  27.9 us
    unnamed x51, local copies, waits for them, and re-layouts  19 us
    all_to_all x2, starting transfers between devices, exchange(): return lax.all_to_all(blocks, 'az', split_axis=0, concat_axis=0, tiled=True)  18.8 us
    ppermute x30, waiting for transfers between devices, send_apart(): lax.ppermute(blocks[distance], 'az', [(i, (i + distance) % n) for i in ra...  4.84 us
    all_gather x1, blocking collectives, per_device(): lax.all_gather(jnp.stack([local_part[:, 0, :], local_part[:, -1, :]], axi...  4.44 us
    all_gather x1, blocking collectives, per_device(): corner_all = lax.all_gather(corners, 'rad', axis=1)  4.34 us
  transfers between devices with their start and end apart: 33, of which 8 were waited for; matrix products, arithmetic and copies ran while one was open for 10% of the time, Pallas kernels for 1%

profile of v2, /device:TPU:0, one launch (start us, length us, event | category | flops | bytes accessed | tf_op | source)
XLA Modules:
  0.0 198.0 jit_solution(10052035374605698831)
XLA Ops:
  0.0 1.6 slice-done
  1.6 1.6 copy.60
  3.2 7.5 %all-to-all-start = ((f32[16,4,32,256]{3,2,1,0:T(8,128)}), f32[16,4,32,256]{3,2,1,0:T(8,128)S(1)}, u32[]{:S(2)}, u32[]{:S(2)}) async-start(f32[16,4,32,256]{3,2,1,0:T(8,128)} %bitcast.59), calls=%async_computation | async-start | bytes 4194304 | tf_op jit(solution)/shard_map/all_to_all | solution.py:291
  10.8 41.0 %all-to-all-done.in_ref = f32[16,4,32,256]{3,2,1,0:T(8,128)S(1)} async-done(((f32[16,4,32,256]{3,2,1,0:T(8,128)}), f32[16,4,32,256]{3,2,1,0:T(8,128)S(1)}, u32[]{:S(2)}, u32[]{:S(2)}) %all-to-all-start) | async-done | bytes 2097184 | tf_op jit(solution)/shard_map/all_to_all | solution.py:291
  53.2 1.6 copy-done.3
  54.7 3.1 %shard_map.55 = f32[16,264,128]{2,1,0:T(8,128)S(1)} custom-call(s32[32,128]{1,0:T(8,128)S(1)} %broadcast_in_dim.6.shift_ref, f32[16,4,32,256]{3,2,1,0:T(8,128)S(1)} %copy-done.3), custom_call_target="tpu_custom_call" | custom-call | flops 5242880 | bytes 4194304 | tf_op jit(solution)/shard_map/pallas_call | solution.py:121
  59.2 11.3 %all-to-all-start.1 = ((f32[16,264,128]{2,1,0:T(8,128)}), f32[16,264,128]{2,1,0:T(8,128)S(1)}, u32[]{:S(2)}, u32[]{:S(2)}) async-start(f32[16,264,128]{2,1,0:T(8,128)} %copy-done), calls=%async_computation.1 | async-start | bytes 4325376 | tf_op jit(solution)/shard_map/all_to_all | solution.py:291
  71.2 1.7 copy-done.1
  73.0 1.6 shard_map.56
  74.6 1.7 collective-permute-start
  80.1 1.9 fusion.6
  83.2 27.9 %collective-permute-done.15 = f32[8,64]{1,0:T(8,128)S(1)} collective-permute-done((f32[8,64]{1,0:T(8,128)S(1)}, f32[8,64]{1,0:T(8,128)S(1)}, u32[]{:S(2)}, u32[]{:S(2)}) %collective-permute-start.15) | collective-permute-done | bytes 2080 | tf_op jit(solution)/shard_map/ppermute | solution.py:308
  112.6 8.6 %collective-permute-start.6 = (f32[32,256]{1,0:T(8,128)S(1)}, f32[32,256]{1,0:T(8,128)S(1)}, u32[]{:S(2)}, u32[]{:S(2)}) collective-permute-start(f32[32,256]{1,0:T(8,128)S(1)} %get-tuple-element.62), channel_id=1, source_target_pairs={{0,14},{2,16},{4,18},{6,20},{8,22},{10,24},{12,26},{14,28},{16,30}... | collective-permute-start | bytes 98312 | tf_op jit(solution)/shard_map/ppermute | solution.py:179
  121.2 2.4 %collective-permute-start.7 = (f32[32,256]{1,0:T(8,128)S(1)}, f32[32,256]{1,0:T(8,128)S(1)}, u32[]{:S(2)}, u32[]{:S(2)}) collective-permute-start(f32[32,256]{1,0:T(8,128)S(1)} %get-tuple-element.63), channel_id=1, source_target_pairs={{0,16},{2,18},{4,20},{6,22},{8,24},{10,26},{12,28},{14,30},{16,0},... | collective-permute-start | bytes 98312 | tf_op jit(solution)/shard_map/ppermute | solution.py:179
  123.6 2.3 %collective-permute-start.8 = (f32[32,256]{1,0:T(8,128)S(1)}, f32[32,256]{1,0:T(8,128)S(1)}, u32[]{:S(2)}, u32[]{:S(2)}) collective-permute-start(f32[32,256]{1,0:T(8,128)S(1)} %get-tuple-element.64), channel_id=1, source_target_pairs={{0,18},{2,20},{4,22},{6,24},{8,26},{10,28},{12,30},{14,0},{16,2},{... | collective-permute-start | bytes 98312 | tf_op jit(solution)/shard_map/ppermute | solution.py:179
  127.1 1.8 collective-permute-start.9
  130.1 4.3 %all-gather.2 = f32[2,5,8]{2,1,0:T(8,128)S(1)} all-gather(f32[1,5,8]{2,1,0:T(8,128)S(1)} %bitcast.61), channel_id=2, replica_groups=mesh['az'=16,'rad'=2] {'rad'}, dimensions={0}, use_global_device_ids=true | all-gather | bytes 480 | tf_op jit(solution)/shard_map/all_gather | solution.py:321
  135.2 1.7 copy.42
  137.7 3.0 %collective-permute-start.10 = (f32[32,256]{1,0:T(8,128)}, f32[32,256]{1,0:T(8,128)S(1)}, u32[]{:S(2)}, u32[]{:S(2)}) collective-permute-start(f32[32,256]{1,0:T(8,128)} %get-tuple-element.66), channel_id=1, source_target_pairs={{0,22},{2,24},{4,26},{6,28},{8,30},{10,0},{12,2},{14,4},{16,6},{18... | collective-permute-start | bytes 98312 | tf_op jit(solution)/shard_map/ppermute | solution.py:179
  140.7 1.8 collective-permute-start.12
  160.0 1.7 collective-permute-start.17
  162.2 2.0 collective-permute-start.19
  166.0 1.5 collective-permute-start.21
  167.5 2.0 collective-permute-start.22
  169.4 2.3 %collective-permute-start.23 = (f32[72,128]{1,0:T(8,128)S(1)}, f32[72,128]{1,0:T(8,128)S(1)}, u32[]{:S(2)}, u32[]{:S(2)}) collective-permute-start(f32[72,128]{1,0:T(8,128)S(1)} %get-tuple-element.96), channel_id=1, source_target_pairs={{0,16},{2,18},{4,20},{6,22},{8,24},{10,26},{12,28},{14,30},{16,0},... | collective-permute-start | bytes 110600 | tf_op jit(solution)/shard_map/ppermute | solution.py:179
  171.8 2.1 %collective-permute-start.25 = (f32[72,128]{1,0:T(8,128)S(1)}, f32[72,128]{1,0:T(8,128)S(1)}, u32[]{:S(2)}, u32[]{:S(2)}) collective-permute-start(f32[72,128]{1,0:T(8,128)S(1)} %get-tuple-element.98), channel_id=1, source_target_pairs={{0,20},{2,22},{4,24},{6,26},{8,28},{10,30},{12,0},{14,2},{16,4},{1... | collective-permute-start | bytes 110600 | tf_op jit(solution)/shard_map/ppermute | solution.py:179
  174.7 4.2 %collective-permute-start.26 = (f32[72,128]{1,0:T(8,128)S(1)}, f32[72,128]{1,0:T(8,128)S(1)}, u32[]{:S(2)}, u32[]{:S(2)}) collective-permute-start(f32[72,128]{1,0:T(8,128)S(1)} %get-tuple-element.99), channel_id=1, source_target_pairs={{0,22},{2,24},{4,26},{6,28},{8,30},{10,0},{12,2},{14,4},{16,6},{18... | collective-permute-start | bytes 110600 | tf_op jit(solution)/shard_map/ppermute | solution.py:179
  179.5 1.5 collective-permute-start.29
  181.0 1.6 collective-permute-start.30
  186.1 4.4 %all-gather.1 = f32[2,8,512]{2,0,1:T(2,128)S(1)} all-gather(f32[2,8,256]{2,0,1:T(2,128)S(1)} %pad_maximum_fusion.1), channel_id=3, replica_groups=mesh['az'=16,'rad'=2] {'rad'}, dimensions={2}, use_global_device_ids=true | all-gather | bytes 49152 | tf_op jit(solution)/shard_map/all_gather | solution.py:330
  190.8 2.1 %multiply_add_fusion.energy_ref = f32[8,64,256]{2,1,0:T(8,128)} fusion(f32[8,64,256]{2,1,0:T(8,128)} %copy-done.19, f32[8,256]{1,0:T(8,128)S(1)} %get-tuple-element.127, f32[8,64]{1,0:T(8,128)S(1)} %copy-done.20, f32[8,256]{1,0:T(8,128)S(1)} %get-tuple-element.126, f32[8,64]{1,0:T(8,128)S(1)} %multiply_bitcast_fusion.1), kind=kLoop, calls=%fused_computation.3 | loop fusion | flops 524288 | bytes 1069056 | tf_op jit(solution)/shard_map/add | solution.py:348
  193.9 4.1 %shard_map.59 = f32[5,8,64,256]{3,2,1,0:T(8,128)} custom-call(f32[16,264,128]{2,1,0:T(8,128)S(1)} %all-to-all-done.1.recv_ref, f32[8,64,256]{2,1,0:T(8,128)S(1)} %copy-done.4, f32[8,64,256]{2,1,0:T(8,128)S(1)} %pad_maximum_fusion.back_ref, f32[8,64,256]{2,1,0:T(8,128)S(1)} %copy-done.5), custom_call_target="tpu_custom_call" | custom-call | flops 5242880 | bytes 6291456 | tf_op jit(solution)/shard_map/pallas_call | solution.py:248
  (124 shorter events, 39.9 us)
Async XLA Ops:
  3.2 48.6 %all-to-all-start = ((f32[16,4,32,256]{3,2,1,0:T(8,128)}), f32[16,4,32,256]{3,2,1,0:T(8,128)S(1)}, u32[]{:S(2)}, u32[]{:S(2)}) async-start(f32[16,4,32,256]{3,2,1,0:T(8,128)} %bitcast.59), calls=%async_computation | async-start | bytes 4194304 | tf_op jit(solution)/shard_map/all_to_all | solution.py:291
  59.2 133.7 %all-to-all-start.1 = ((f32[16,264,128]{2,1,0:T(8,128)}), f32[16,264,128]{2,1,0:T(8,128)S(1)}, u32[]{:S(2)}, u32[]{:S(2)}) async-start(f32[16,264,128]{2,1,0:T(8,128)} %copy-done), calls=%async_computation.1 | async-start | bytes 4325376 | tf_op jit(solution)/shard_map/all_to_all | solution.py:291
  70.8 40.3 %collective-permute-start.15 = (f32[8,64]{1,0:T(8,128)S(1)}, f32[8,64]{1,0:T(8,128)S(1)}, u32[]{:S(2)}, u32[]{:S(2)}) collective-permute-start(f32[8,64]{1,0:T(8,128)S(1)} %bitcast.63), channel_id=1, source_target_pairs={{0,2},{2,4},{4,6},{6,8},{8,10},{10,12},{12,14},{14,16},{16,18},{18... | collective-permute-start | bytes 6152 | tf_op jit(solution)/shard_map/ppermute | solution.py:308
  74.6 37.2 %collective-permute-start = (f32[32,256]{1,0:T(8,128)S(1)}, f32[32,256]{1,0:T(8,128)S(1)}, u32[]{:S(2)}, u32[]{:S(2)}) collective-permute-start(f32[32,256]{1,0:T(8,128)S(1)} %get-tuple-element.56), channel_id=1, source_target_pairs={{0,2},{2,4},{4,6},{6,8},{8,10},{10,12},{12,14},{14,16},{16,18},{18... | collective-permute-start | bytes 98312 | tf_op jit(solution)/shard_map/ppermute | solution.py:179
  76.3 36.3 %collective-permute-start.1 = (f32[32,256]{1,0:T(8,128)S(1)}, f32[32,256]{1,0:T(8,128)S(1)}, u32[]{:S(2)}, u32[]{:S(2)}) collective-permute-start(f32[32,256]{1,0:T(8,128)S(1)} %get-tuple-element.57), channel_id=1, source_target_pairs={{0,4},{2,6},{4,8},{6,10},{8,12},{10,14},{12,16},{14,18},{16,20},{1... | collective-permute-start | bytes 98312 | tf_op jit(solution)/shard_map/ppermute | solution.py:179
  77.7 43.5 %collective-permute-start.2 = (f32[32,256]{1,0:T(8,128)S(1)}, f32[32,256]{1,0:T(8,128)S(1)}, u32[]{:S(2)}, u32[]{:S(2)}) collective-permute-start(f32[32,256]{1,0:T(8,128)S(1)} %get-tuple-element.58), channel_id=1, source_target_pairs={{0,6},{2,8},{4,10},{6,12},{8,14},{10,16},{12,18},{14,20},{16,22},{... | collective-permute-start | bytes 98312 | tf_op jit(solution)/shard_map/ppermute | solution.py:179
  78.7 44.9 %collective-permute-start.3 = (f32[32,256]{1,0:T(8,128)S(1)}, f32[32,256]{1,0:T(8,128)S(1)}, u32[]{:S(2)}, u32[]{:S(2)}) collective-permute-start(f32[32,256]{1,0:T(8,128)S(1)} %get-tuple-element.59), channel_id=1, source_target_pairs={{0,8},{2,10},{4,12},{6,14},{8,16},{10,18},{12,20},{14,22},{16,24},... | collective-permute-start | bytes 98312 | tf_op jit(solution)/shard_map/ppermute | solution.py:179
  111.1 16.1 %collective-permute-start.4 = (f32[32,256]{1,0:T(8,128)S(1)}, f32[32,256]{1,0:T(8,128)S(1)}, u32[]{:S(2)}, u32[]{:S(2)}) collective-permute-start(f32[32,256]{1,0:T(8,128)S(1)} %get-tuple-element.60), channel_id=1, source_target_pairs={{0,10},{2,12},{4,14},{6,16},{8,18},{10,20},{12,22},{14,24},{16,26}... | collective-permute-start | bytes 98312 | tf_op jit(solution)/shard_map/ppermute | solution.py:179
  111.8 26.0 %collective-permute-start.5 = (f32[32,256]{1,0:T(8,128)S(1)}, f32[32,256]{1,0:T(8,128)S(1)}, u32[]{:S(2)}, u32[]{:S(2)}) collective-permute-start(f32[32,256]{1,0:T(8,128)S(1)} %get-tuple-element.61), channel_id=1, source_target_pairs={{0,12},{2,14},{4,16},{6,18},{8,20},{10,22},{12,24},{14,26},{16,28}... | collective-permute-start | bytes 98312 | tf_op jit(solution)/shard_map/ppermute | solution.py:179
  112.6 28.1 %collective-permute-start.6 = (f32[32,256]{1,0:T(8,128)S(1)}, f32[32,256]{1,0:T(8,128)S(1)}, u32[]{:S(2)}, u32[]{:S(2)}) collective-permute-start(f32[32,256]{1,0:T(8,128)S(1)} %get-tuple-element.62), channel_id=1, source_target_pairs={{0,14},{2,16},{4,18},{6,20},{8,22},{10,24},{12,26},{14,28},{16,30}... | collective-permute-start | bytes 98312 | tf_op jit(solution)/shard_map/ppermute | solution.py:179
  121.2 19.5 %collective-permute-start.7 = (f32[32,256]{1,0:T(8,128)S(1)}, f32[32,256]{1,0:T(8,128)S(1)}, u32[]{:S(2)}, u32[]{:S(2)}) collective-permute-start(f32[32,256]{1,0:T(8,128)S(1)} %get-tuple-element.63), channel_id=1, source_target_pairs={{0,16},{2,18},{4,20},{6,22},{8,24},{10,26},{12,28},{14,30},{16,0},... | collective-permute-start | bytes 98312 | tf_op jit(solution)/shard_map/ppermute | solution.py:179
  123.6 18.9 %collective-permute-start.8 = (f32[32,256]{1,0:T(8,128)S(1)}, f32[32,256]{1,0:T(8,128)S(1)}, u32[]{:S(2)}, u32[]{:S(2)}) collective-permute-start(f32[32,256]{1,0:T(8,128)S(1)} %get-tuple-element.64), channel_id=1, source_target_pairs={{0,18},{2,20},{4,22},{6,24},{8,26},{10,28},{12,30},{14,0},{16,2},{... | collective-permute-start | bytes 98312 | tf_op jit(solution)/shard_map/ppermute | solution.py:179
  127.1 16.6 %collective-permute-start.9 = (f32[32,256]{1,0:T(8,128)S(1)}, f32[32,256]{1,0:T(8,128)S(1)}, u32[]{:S(2)}, u32[]{:S(2)}) collective-permute-start(f32[32,256]{1,0:T(8,128)S(1)} %get-tuple-element.65), channel_id=1, source_target_pairs={{0,20},{2,22},{4,24},{6,26},{8,28},{10,30},{12,0},{14,2},{16,4},{1... | collective-permute-start | bytes 98312 | tf_op jit(solution)/shard_map/ppermute | solution.py:179
  137.7 8.4 %collective-permute-start.10 = (f32[32,256]{1,0:T(8,128)}, f32[32,256]{1,0:T(8,128)S(1)}, u32[]{:S(2)}, u32[]{:S(2)}) collective-permute-start(f32[32,256]{1,0:T(8,128)} %get-tuple-element.66), channel_id=1, source_target_pairs={{0,22},{2,24},{4,26},{6,28},{8,30},{10,0},{12,2},{14,4},{16,6},{18... | collective-permute-start | bytes 98312 | tf_op jit(solution)/shard_map/ppermute | solution.py:179
  140.7 6.0 %collective-permute-start.11 = (f32[32,256]{1,0:T(8,128)}, f32[32,256]{1,0:T(8,128)S(1)}, u32[]{:S(2)}, u32[]{:S(2)}) collective-permute-start(f32[32,256]{1,0:T(8,128)} %get-tuple-element.67), channel_id=1, source_target_pairs={{0,24},{2,26},{4,28},{6,30},{8,0},{10,2},{12,4},{14,6},{16,8},{18,... | collective-permute-start | bytes 98312 | tf_op jit(solution)/shard_map/ppermute | solution.py:179
  140.7 6.6 %collective-permute-start.12 = (f32[32,256]{1,0:T(8,128)}, f32[32,256]{1,0:T(8,128)S(1)}, u32[]{:S(2)}, u32[]{:S(2)}) collective-permute-start(f32[32,256]{1,0:T(8,128)} %get-tuple-element.68), channel_id=1, source_target_pairs={{0,26},{2,28},{4,30},{6,0},{8,2},{10,4},{12,6},{14,8},{16,10},{18,... | collective-permute-start | bytes 98312 | tf_op jit(solution)/shard_map/ppermute | solution.py:179
  142.5 5.5 %collective-permute-start.13 = (f32[32,256]{1,0:T(8,128)}, f32[32,256]{1,0:T(8,128)S(1)}, u32[]{:S(2)}, u32[]{:S(2)}) collective-permute-start(f32[32,256]{1,0:T(8,128)} %get-tuple-element.69), channel_id=1, source_target_pairs={{0,28},{2,30},{4,0},{6,2},{8,4},{10,6},{12,8},{14,10},{16,12},{18,... | collective-permute-start | bytes 98312 | tf_op jit(solution)/shard_map/ppermute | solution.py:179
  144.3 4.2 %collective-permute-start.14 = (f32[32,256]{1,0:T(8,128)}, f32[32,256]{1,0:T(8,128)S(1)}, u32[]{:S(2)}, u32[]{:S(2)}) collective-permute-start(f32[32,256]{1,0:T(8,128)} %get-tuple-element.70), channel_id=1, source_target_pairs={{0,30},{2,0},{4,2},{6,4},{8,6},{10,8},{12,10},{14,12},{16,14},{18,... | collective-permute-start | bytes 98312 | tf_op jit(solution)/shard_map/ppermute | solution.py:179
  159.9 6.1 %collective-permute-start.16 = (f32[72,128]{1,0:T(8,128)S(1)}, f32[72,128]{1,0:T(8,128)S(1)}, u32[]{:S(2)}, u32[]{:S(2)}) collective-permute-start(f32[72,128]{1,0:T(8,128)S(1)} %get-tuple-element.89), channel_id=1, source_target_pairs={{0,2},{2,4},{4,6},{6,8},{8,10},{10,12},{12,14},{14,16},{16,18},{18... | collective-permute-start | bytes 110600 | tf_op jit(solution)/shard_map/ppermute | solution.py:179
  160.0 7.5 %collective-permute-start.17 = (f32[72,128]{1,0:T(8,128)S(1)}, f32[72,128]{1,0:T(8,128)S(1)}, u32[]{:S(2)}, u32[]{:S(2)}) collective-permute-start(f32[72,128]{1,0:T(8,128)S(1)} %get-tuple-element.90), channel_id=1, source_target_pairs={{0,4},{2,6},{4,8},{6,10},{8,12},{10,14},{12,16},{14,18},{16,20},{1... | collective-permute-start | bytes 110600 | tf_op jit(solution)/shard_map/ppermute | solution.py:179
  161.7 7.7 %collective-permute-start.18 = (f32[72,128]{1,0:T(8,128)S(1)}, f32[72,128]{1,0:T(8,128)S(1)}, u32[]{:S(2)}, u32[]{:S(2)}) collective-permute-start(f32[72,128]{1,0:T(8,128)S(1)} %get-tuple-element.91), channel_id=1, source_target_pairs={{0,6},{2,8},{4,10},{6,12},{8,14},{10,16},{12,18},{14,20},{16,22},{... | collective-permute-start | bytes 110600 | tf_op jit(solution)/shard_map/ppermute | solution.py:179
  162.2 9.6 %collective-permute-start.19 = (f32[72,128]{1,0:T(8,128)S(1)}, f32[72,128]{1,0:T(8,128)S(1)}, u32[]{:S(2)}, u32[]{:S(2)}) collective-permute-start(f32[72,128]{1,0:T(8,128)S(1)} %get-tuple-element.92), channel_id=1, source_target_pairs={{0,8},{2,10},{4,12},{6,14},{8,16},{10,18},{12,20},{14,22},{16,24},... | collective-permute-start | bytes 110600 | tf_op jit(solution)/shard_map/ppermute | solution.py:179
  164.2 7.6 %collective-permute-start.20 = (f32[72,128]{1,0:T(8,128)S(1)}, f32[72,128]{1,0:T(8,128)S(1)}, u32[]{:S(2)}, u32[]{:S(2)}) collective-permute-start(f32[72,128]{1,0:T(8,128)S(1)} %get-tuple-element.93), channel_id=1, source_target_pairs={{0,10},{2,12},{4,14},{6,16},{8,18},{10,20},{12,22},{14,24},{16,26}... | collective-permute-start | bytes 110600 | tf_op jit(solution)/shard_map/ppermute | solution.py:179
  166.0 8.7 %collective-permute-start.21 = (f32[72,128]{1,0:T(8,128)S(1)}, f32[72,128]{1,0:T(8,128)S(1)}, u32[]{:S(2)}, u32[]{:S(2)}) collective-permute-start(f32[72,128]{1,0:T(8,128)S(1)} %get-tuple-element.94), channel_id=1, source_target_pairs={{0,12},{2,14},{4,16},{6,18},{8,20},{10,22},{12,24},{14,26},{16,28}... | collective-permute-start | bytes 110600 | tf_op jit(solution)/shard_map/ppermute | solution.py:179
  167.5 11.4 %collective-permute-start.22 = (f32[72,128]{1,0:T(8,128)S(1)}, f32[72,128]{1,0:T(8,128)S(1)}, u32[]{:S(2)}, u32[]{:S(2)}) collective-permute-start(f32[72,128]{1,0:T(8,128)S(1)} %get-tuple-element.95), channel_id=1, source_target_pairs={{0,14},{2,16},{4,18},{6,20},{8,22},{10,24},{12,26},{14,28},{16,30}... | collective-permute-start | bytes 110600 | tf_op jit(solution)/shard_map/ppermute | solution.py:179
  169.4 9.4 %collective-permute-start.23 = (f32[72,128]{1,0:T(8,128)S(1)}, f32[72,128]{1,0:T(8,128)S(1)}, u32[]{:S(2)}, u32[]{:S(2)}) collective-permute-start(f32[72,128]{1,0:T(8,128)S(1)} %get-tuple-element.96), channel_id=1, source_target_pairs={{0,16},{2,18},{4,20},{6,22},{8,24},{10,26},{12,28},{14,30},{16,0},... | collective-permute-start | bytes 110600 | tf_op jit(solution)/shard_map/ppermute | solution.py:179
  171.8 7.7 %collective-permute-start.24 = (f32[72,128]{1,0:T(8,128)S(1)}, f32[72,128]{1,0:T(8,128)S(1)}, u32[]{:S(2)}, u32[]{:S(2)}) collective-permute-start(f32[72,128]{1,0:T(8,128)S(1)} %get-tuple-element.97), channel_id=1, source_target_pairs={{0,18},{2,20},{4,22},{6,24},{8,26},{10,28},{12,30},{14,0},{16,2},{... | collective-permute-start | bytes 110600 | tf_op jit(solution)/shard_map/ppermute | solution.py:179
  171.8 9.2 %collective-permute-start.25 = (f32[72,128]{1,0:T(8,128)S(1)}, f32[72,128]{1,0:T(8,128)S(1)}, u32[]{:S(2)}, u32[]{:S(2)}) collective-permute-start(f32[72,128]{1,0:T(8,128)S(1)} %get-tuple-element.98), channel_id=1, source_target_pairs={{0,20},{2,22},{4,24},{6,26},{8,28},{10,30},{12,0},{14,2},{16,4},{1... | collective-permute-start | bytes 110600 | tf_op jit(solution)/shard_map/ppermute | solution.py:179
  174.7 7.9 %collective-permute-start.26 = (f32[72,128]{1,0:T(8,128)S(1)}, f32[72,128]{1,0:T(8,128)S(1)}, u32[]{:S(2)}, u32[]{:S(2)}) collective-permute-start(f32[72,128]{1,0:T(8,128)S(1)} %get-tuple-element.99), channel_id=1, source_target_pairs={{0,22},{2,24},{4,26},{6,28},{8,30},{10,0},{12,2},{14,4},{16,6},{18... | collective-permute-start | bytes 110600 | tf_op jit(solution)/shard_map/ppermute | solution.py:179
  178.8 4.0 %collective-permute-start.27 = (f32[72,128]{1,0:T(8,128)S(1)}, f32[72,128]{1,0:T(8,128)S(1)}, u32[]{:S(2)}, u32[]{:S(2)}) collective-permute-start(f32[72,128]{1,0:T(8,128)S(1)} %get-tuple-element.100), channel_id=1, source_target_pairs={{0,24},{2,26},{4,28},{6,30},{8,0},{10,2},{12,4},{14,6},{16,8},{18,... | collective-permute-start | bytes 110600 | tf_op jit(solution)/shard_map/ppermute | solution.py:179
  178.9 4.0 %collective-permute-start.28 = (f32[72,128]{1,0:T(8,128)S(1)}, f32[72,128]{1,0:T(8,128)S(1)}, u32[]{:S(2)}, u32[]{:S(2)}) collective-permute-start(f32[72,128]{1,0:T(8,128)S(1)} %get-tuple-element.101), channel_id=1, source_target_pairs={{0,26},{2,28},{4,30},{6,0},{8,2},{10,4},{12,6},{14,8},{16,10},{18,... | collective-permute-start | bytes 110600 | tf_op jit(solution)/shard_map/ppermute | solution.py:179
  179.5 4.1 %collective-permute-start.29 = (f32[72,128]{1,0:T(8,128)S(1)}, f32[72,128]{1,0:T(8,128)S(1)}, u32[]{:S(2)}, u32[]{:S(2)}) collective-permute-start(f32[72,128]{1,0:T(8,128)S(1)} %get-tuple-element.102), channel_id=1, source_target_pairs={{0,28},{2,30},{4,0},{6,2},{8,4},{10,6},{12,8},{14,10},{16,12},{18,... | collective-permute-start | bytes 110600 | tf_op jit(solution)/shard_map/ppermute | solution.py:179
  (25 other events, 136.4 us)

commit v3 on v0

v3 whole, which is shorter than its diff:
```python
import functools

import jax
import jax.numpy as jnp
from jax import lax
from jax.experimental import pallas as pl
from jax.experimental.pallas import tpu as pltpu
from jax.sharding import PartitionSpec as P

LANES = 128
TILE_ROWS = 8
IN_VMEM = pl.BlockSpec(memory_space=pltpu.VMEM)
IN_HBM = pl.BlockSpec(memory_space=pltpu.HBM)
IN_SMEM = pl.BlockSpec(memory_space=pltpu.SMEM)
ROOMY = pltpu.CompilerParams(vmem_limit_bytes=40 * 1024 * 1024)


def cost(flops, moved):
    return pl.CostEstimate(flops=flops, bytes_accessed=4 * moved, transcendentals=0)


def copy_each(copies):
    for copy in copies:
        copy.start()
    for copy in copies:
        copy.wait()


def pack_kernel(in_ref, out_ref, sems):
    copy_each(
        [
            pltpu.make_async_copy(in_ref.at[field], out_ref.at[:, field], sems.at[field])
            for field in range(in_ref.shape[0])
        ]
    )


def pack(blocked):
    nf, n, rows, width = blocked.shape
    return pl.pallas_call(
        pack_kernel,
        out_shape=jax.ShapeDtypeStruct((n, nf, rows, width), jnp.float32),
        in_specs=[IN_HBM],
        out_specs=IN_HBM,
        scratch_shapes=[pltpu.SemaphoreType.DMA((nf,))],
        compiler_params=ROOMY,
        cost_estimate=cost(0, 2 * blocked.size),
    )(blocked)


def turn_kernel(shift_ref, in_ref, out_ref, held, sems):
    n, nf, rows, width = in_ref.shape
    per_block = width // LANES
    tiles = n * per_block
    groups = rows // TILE_ROWS
    field_rows = per_block * rows
    halo_row = nf * field_rows
    lane = lax.broadcasted_iota(jnp.int32, (TILE_ROWS, LANES), 1)

    def field_copy(field):
        part = pl.ds(pl.multiple_of(field * field_rows, TILE_ROWS), field_rows)
        return pltpu.make_async_copy(held.at[:, part, :], out_ref.at[:, part, :], sems.at[field])

    for block in range(n):
        held[block, halo_row : halo_row + TILE_ROWS, :] = jnp.zeros((TILE_ROWS, LANES), jnp.float32)

    def one_group(index, _):
        field = index // groups
        group = index % groups
        here = pl.ds(pl.multiple_of(group * TILE_ROWS, TILE_ROWS), TILE_ROWS)
        shift = shift_ref[here, :]
        cells = shift & (LANES - 1)
        whole = shift >> 7
        source = (lane - cells) & (LANES - 1)
        own = lane >= cells
        turned = []
        for tile in range(tiles):
            block, part = divmod(tile, per_block)
            values = in_ref[block, field, here, part * LANES : (part + 1) * LANES]
            turned.append(jnp.take_along_axis(values, source, axis=1, mode="promise_in_bounds"))
        circle = [jnp.where(own, turned[tile], turned[tile - 1]) for tile in range(tiles)]
        step = 1
        while step < tiles:
            wanted = (whole & step) != 0
            circle = [jnp.where(wanted, circle[(tile - step) % tiles], circle[tile]) for tile in range(tiles)]
            step *= 2
        for tile in range(tiles):
            block, part = divmod(tile, per_block)
            row = field * field_rows + part * rows + group * TILE_ROWS
            held[block, pl.ds(pl.multiple_of(row, TILE_ROWS), TILE_ROWS), :] = circle[tile]
        place = index * 2
        edge = (lane == place) | (lane == place + 1)
        for block in range(n):
            left = circle[(block * per_block - 1) % tiles]
            right = circle[((block + 1) * per_block) % tiles]
            both = pltpu.roll(jnp.where(lane == 0, right, left), place + 1, 1)
            target = held.at[block, halo_row : halo_row + TILE_ROWS, :]
            target[...] = jnp.where(edge, both, target[...])

        @pl.when(group == groups - 1)
        def _():
            field_copy(field).start()

        return 0

    lax.fori_loop(0, nf * groups, one_group, 0)
    halo = pl.ds(halo_row, TILE_ROWS)
    halo_copy = pltpu.make_async_copy(held.at[:, halo, :], out_ref.at[:, halo, :], sems.at[nf])
    halo_copy.start()
    for field in range(nf):
        field_copy(field).wait()
    halo_copy.wait()


def turn(shift_rows, gathered):
    n, nf, rows, width = gathered.shape
    shape = (n, nf * (width // LANES) * rows + TILE_ROWS, LANES)
    return pl.pallas_call(
        turn_kernel,
        out_shape=jax.ShapeDtypeStruct(shape, jnp.float32),
        in_specs=[IN_VMEM] * 2,
        out_specs=IN_HBM,
        scratch_shapes=[pltpu.VMEM(shape, jnp.float32), pltpu.SemaphoreType.DMA((nf + 1,))],
        compiler_params=ROOMY,
        cost_estimate=cost(10 * gathered.size, 2 * gathered.size),
    )(shift_rows, gathered)


def carry_piece(fields, halo_row, recv, speed, back, store):
    rows, width = speed.shape
    per_block = width // LANES
    groups = rows // TILE_ROWS
    lane = lax.broadcasted_iota(jnp.int32, (TILE_ROWS, LANES), 1)
    first = lane == 0
    last = lane == LANES - 1
    halo = recv[halo_row : halo_row + TILE_ROWS, :]
    for group in range(groups):
        at = slice(group * TILE_ROWS, (group + 1) * TILE_ROWS)
        rates = []
        for part in range(per_block):
            cut = (at, slice(part * LANES, (part + 1) * LANES))
            ahead_speed = speed[cut]
            back_speed = back[cut]
            rates.append(
                (
                    jnp.maximum(ahead_speed, 0.0),
                    jnp.minimum(ahead_speed, 0.0),
                    jnp.maximum(back_speed, 0.0),
                    jnp.minimum(back_speed, 0.0),
                )
            )
        for field in fields:
            values = []
            for part in range(per_block):
                row = (field * per_block + part) * rows + group * TILE_ROWS
                values.append(recv[row : row + TILE_ROWS, :])
            place = (field * groups + group) * 2
            up = [pltpu.roll(halo, (LANES - place) % LANES, 1)]
            up += [pltpu.roll(one, 1, 1) for one in values]
            down = [pltpu.roll(one, LANES - 1, 1) for one in values]
            down.append(pltpu.roll(halo, (LANES - 2 - place) % LANES, 1))
            for part in range(per_block):
                here = values[part]
                behind = jnp.where(first, up[part], up[part + 1])
                ahead = jnp.where(last, down[part + 1], down[part])
                plus, minus, back_plus, back_minus = rates[part]
                outflow = plus * here + minus * ahead
                inflow = back_plus * behind + back_minus * here
                store(field, group * TILE_ROWS, part * LANES, here - (outflow - inflow))


def energy_kernel(recv_ref, speed_ref, back_ref, inverse_ref, local_ref, ends_ref, moved):
    n, in_rows, _ = recv_ref.shape
    levels, radii, width = speed_ref.shape
    pieces = n // levels
    rows = radii // pieces
    field = (in_rows - TILE_ROWS) * LANES // (rows * width) - 1

    def one_level(level, _):
        for piece in range(pieces):
            part = pl.ds(piece * rows, rows)

            def store(_, row, cell, values, piece=piece):
                row += piece * rows
                moved[row : row + TILE_ROWS, cell : cell + LANES] = values

            carry_piece(
                [field],
                in_rows - TILE_ROWS,
                recv_ref.at[level * pieces + piece],
                speed_ref.at[level, part],
                back_ref.at[level, part],
                store,
            )
        local = jnp.dot(
            inverse_ref[level],
            moved[...],
            precision=lax.Precision.HIGHEST,
            preferred_element_type=jnp.float32,
        )
        local_ref[level] = local
        ends_ref[0, pl.ds(level, 1), :] = local[:1]
        ends_ref[1, pl.ds(level, 1), :] = local[-1:]
        return 0

    lax.fori_loop(0, levels, one_level, 0)


def energy_part(received, speed, back_speed, inverse):
    levels, radii, width = speed.shape
    return pl.pallas_call(
        energy_kernel,
        out_shape=[
            jax.ShapeDtypeStruct(speed.shape, jnp.float32),
            jax.ShapeDtypeStruct((2, levels, width), jnp.float32),
        ],
        in_specs=[IN_VMEM] * 4,
        out_specs=[IN_VMEM] * 2,
        scratch_shapes=[pltpu.VMEM((radii, width), jnp.float32)],
        compiler_params=ROOMY,
        cost_estimate=cost(2 * speed.size * radii, 4 * speed.size),
    )(received, speed, back_speed, inverse)


def carry_kernel(recv_ref, speed_ref, back_ref, out_ref, held, sems):
    n, in_rows, _ = recv_ref.shape
    levels, radii, width = speed_ref.shape
    pieces = n // levels
    rows = radii // pieces
    nf = held.shape[0]

    def level_copy(level):
        return pltpu.make_async_copy(held.at[:, level], out_ref.at[pl.ds(0, nf), level], sems.at[level])

    def one_level(level, _):
        for piece in range(pieces):
            part = pl.ds(piece * rows, rows)

            def store(field, row, cell, values, piece=piece):
                row += piece * rows
                held[field, level, row : row + TILE_ROWS, cell : cell + LANES] = values

            carry_piece(
                range(nf),
                in_rows - TILE_ROWS,
                recv_ref.at[level * pieces + piece],
                speed_ref.at[level, part],
                back_ref.at[level, part],
                store,
            )
        level_copy(level).start()
        return 0

    lax.fori_loop(0, levels, one_level, 0)
    for level in range(levels):
        level_copy(level).wait()


def carry(nf, received, speed, back_speed):
    levels, radii, width = speed.shape
    return pl.pallas_call(
        carry_kernel,
        out_shape=jax.ShapeDtypeStruct((nf,) + speed.shape, jnp.float32),
        in_specs=[IN_VMEM] * 3,
        out_specs=IN_HBM,
        scratch_shapes=[
            pltpu.VMEM((nf - 1,) + speed.shape, jnp.float32),
            pltpu.SemaphoreType.DMA((levels,)),
        ],
        compiler_params=ROOMY,
        cost_estimate=cost(10 * nf * speed.size, 2 * nf * speed.size),
    )(received, speed, back_speed)


def solve_interfaces(first_row, last_row, corner):
    bands = len(first_row)
    crossings = bands - 1
    nothing = jnp.zeros_like(first_row[0])
    carry_base = nothing
    carry_slope = jnp.zeros_like(corner[0][0])
    records = []
    for crossing in range(crossings):
        link = corner[crossing][4]
        steepness = link * corner[crossing][3]
        offset = last_row[crossing]
        if crossing > 0:
            back_link = corner[crossing - 1][4] * corner[crossing][2]
            steepness = back_link * carry_slope + steepness
            offset = offset + back_link * carry_base
        fore_link = link * corner[crossing + 1][0]
        next_link = jnp.zeros_like(link)
        if crossing + 1 < crossings:
            next_link = corner[crossing + 1][4] * corner[crossing + 1][1]
        denominator = 1.0 - fore_link * steepness
        upper_base = (first_row[crossing + 1] + fore_link * offset) / denominator
        upper_slope = next_link / denominator
        carry_base = offset + steepness * upper_base
        carry_slope = steepness * upper_slope
        records.append((carry_base, carry_slope, upper_base, upper_slope))
    lower_values = [nothing] * crossings
    upper_values = [nothing] * crossings
    follow = nothing
    for crossing in reversed(range(crossings)):
        carry_base, carry_slope, upper_base, upper_slope = records[crossing]
        lower_values[crossing] = carry_base + carry_slope * follow
        upper_values[crossing] = upper_base + upper_slope * follow
        follow = upper_values[crossing]
    return [nothing] + lower_values, upper_values + [nothing]


def diffuse_kernel(band_ref, corner_ref, local_ref, inverse_ref, *refs):
    end_refs, (_, out_ref, held, sems) = refs[:-4], refs[-4:]
    levels, radii, _ = local_ref.shape
    bands = corner_ref.shape[1] // 5
    band = band_ref[0]
    if len(end_refs) == 2:
        own, other = end_refs
        ends = [
            [jnp.where(band == j, own[side], other[side]) for j in range(bands)] for side in range(2)
        ]
    else:
        ends = [[end_refs[0][j, side] for j in range(bands)] for side in range(2)]
    corner = [[corner_ref[:, j * 5 + c : j * 5 + c + 1] for c in range(5)] for j in range(bands)]
    all_before, all_beyond = solve_interfaces(ends[0], ends[1], corner)
    before = beyond = jnp.zeros_like(ends[0][0])
    below = above = jnp.zeros_like(corner[0][4])
    for j in range(bands):
        mine = band == j
        before = jnp.where(mine, all_before[j], before)
        beyond = jnp.where(mine, all_beyond[j], beyond)
        above = jnp.where(mine, corner[j][4], above)
        if j > 0:
            below = jnp.where(mine, corner[j - 1][4], below)
    copies = []
    for level in range(levels):
        row = slice(level, level + 1)
        held[level] = (
            local_ref[level]
            + (below[row] * inverse_ref[level, :, :1]) * before[row]
            + (above[row] * inverse_ref[level, :, radii - 1 :]) * beyond[row]
        )
        copies.append(
            pltpu.make_async_copy(held.at[level], out_ref.at[out_ref.shape[0] - 1, level], sems.at[level])
        )
        copies[-1].start()
    for copy in copies:
        copy.wait()


def diffuse(band, corners, local_part, inverse, ends, result):
    levels = local_part.shape[0]
    return pl.pallas_call(
        diffuse_kernel,
        out_shape=jax.ShapeDtypeStruct(result.shape, jnp.float32),
        in_specs=[IN_SMEM] + [IN_VMEM] * (3 + len(ends)) + [IN_HBM],
        out_specs=IN_HBM,
        scratch_shapes=[pltpu.VMEM(local_part.shape, jnp.float32), pltpu.SemaphoreType.DMA((levels,))],
        input_output_aliases={4 + len(ends): 0},
        compiler_params=ROOMY,
        cost_estimate=cost(4 * local_part.size, 2 * local_part.size),
    )(band, corners, local_part, inverse, *ends, result)


def exchange(blocks):
    return lax.all_to_all(blocks, "az", split_axis=0, concat_axis=0, tiled=True)


def per_device(fields, velocity, shifts, block_inverse, coupling):
    n = lax.axis_size("az")
    bands = lax.axis_size("rad")
    nf, levels, radii, width = fields.shape
    rows = levels * radii // n
    me = lax.axis_index("az")
    band = lax.axis_index("rad")

    gathered = exchange(pack(fields.reshape(nf, n, rows, width)))

    own_shifts = lax.dynamic_slice_in_dim(shifts, (me * rows) % radii, rows)
    shift_rows = jnp.broadcast_to(own_shifts[:, None], (rows, LANES))
    edge_speed = lax.ppermute(velocity[:, :, -1], "az", [(i, (i + 1) % n) for i in range(n)])
    back_speed = jnp.concatenate([edge_speed[:, :, None], velocity[:, :, :-1]], axis=2)
    corners = jnp.stack(
        [
            block_inverse[:, 0, 0],
            block_inverse[:, 0, -1],
            block_inverse[:, -1, 0],
            block_inverse[:, -1, -1],
            coupling[:, 0],
        ],
        axis=1,
    )
    all_corners = lax.all_gather(corners, "rad", axis=1, tiled=True)
    gathered, back_speed, all_corners = lax.optimization_barrier((gathered, back_speed, all_corners))

    received = exchange(turn(shift_rows, gathered))

    local_part, ends = energy_part(received, velocity, back_speed, block_inverse)
    if bands == 2:
        all_ends = [ends, lax.ppermute(ends, "rad", [(0, 1), (1, 0)])]
    else:
        all_ends = [lax.all_gather(ends, "rad", axis=0)]
    result = carry(nf, received, velocity, back_speed)
    band_scalar = band[None].astype(jnp.int32)
    return diffuse(band_scalar, all_corners, local_part, block_inverse, all_ends, result)


def solution(mesh):
    placed = (
        P(None, None, "rad", "az"),
        P(None, "rad", "az"),
        P("rad"),
        P(None, "rad", None),
        P(None, "rad"),
    )
    return jax.shard_map(
        per_device,
        mesh=mesh,
        in_specs=placed,
        out_specs=P(None, None, "rad", "az"),
        check_vma=False,
    )
```

time: 393 us -> 154 us (0.39)
  the two profiles are of different devices: /device:TPU:20 before, /device:TPU:0 now
where the time goes in v3:
time: 154 us
  blocking collectives  81.3 us (53%)
  waiting for transfers between devices  40.8 us (26%)
  Pallas kernels  11.6 us (8%)
  starting transfers between devices  9.46 us (6%)
  local copies, waits for them, and re-layouts  8.3 us (5%)
  other arithmetic  1.95 us (1%)
    all_to_all x1, blocking collectives, exchange(): return lax.all_to_all(blocks, 'az', split_axis=0, concat_axis=0, tiled=True)  77 us
    ppermute x1, waiting for transfers between devices, per_device(): lax.ppermute(velocity[:, :, -1], 'az', [(i, (i + 1) % n) for i in range(n)])  40.8 us
    all_to_all x1, starting transfers between devices, exchange(): return lax.all_to_all(blocks, 'az', split_axis=0, concat_axis=0, tiled=True)  7.5 us
    unnamed x23, local copies, waits for them, and re-layouts  6.24 us
    all_gather x1, blocking collectives, per_device(): all_corners = lax.all_gather(corners, 'rad', axis=1, tiled=True)  4.34 us
    pallas_call x1, Pallas kernels, turn(): pl.pallas_call(turn_kernel, out_shape=jax.ShapeDtypeStruct(shape, jnp.flo...  4.32 us
  transfers between devices with their start and end apart: 3, of which 1 were waited for; matrix products, arithmetic and copies ran while one was open for 3% of the time, Pallas kernels for 2%

profile of v3, /device:TPU:0, one launch (start us, length us, event | category | flops | bytes accessed | tf_op | source)
XLA Modules:
  0.0 153.5 jit_solution(9716510501820144304)
XLA Ops:
  0.0 1.7 %copy-done.4 = f32[5,8,64,256]{3,2,1,0:T(8,128)S(1)} copy-done((f32[5,8,64,256]{3,2,1,0:T(8,128)S(1)}, f32[5,8,64,256]{3,2,1,0:T(8,128)}, u32[]{:S(2)}) %copy-start.4) | copy-done | bytes 2621464
  1.7 0.2 shard_map.55
  2.0 0.0 copy-start
  2.0 1.5 copy-done
  3.5 7.5 %all-to-all-start = ((f32[16,5,32,256]{3,2,1,0:T(8,128)}), f32[16,5,32,256]{3,2,1,0:T(8,128)S(1)}, u32[]{:S(2)}, u32[]{:S(2)}) async-start(f32[16,5,32,256]{3,2,1,0:T(8,128)} %copy-done), calls=%async_computation | async-start | bytes 5242880 | tf_op jit(solution)/shard_map/all_to_all | solution.py:365
  11.0 0.0 copy-done.1
  11.0 0.8 slice.18
  11.8 1.1 copy.16
  12.9 0.4 collective-permute-start
  13.3 0.0 copy-done.5
  13.3 0.2 slice_reduce_fusion
  13.6 0.0 copy-done.8
  13.6 4.3 %all-gather = f32[2,5,8]{2,1,0:T(8,128)S(1)} all-gather(f32[1,5,8]{2,1,0:T(8,128)S(1)} %bitcast.16), channel_id=1, replica_groups=mesh['az'=16,'rad'=2] {'rad'}, dimensions={0}, use_global_device_ids=true | all-gather | bytes 480 | tf_op jit(solution)/shard_map/all_gather | solution.py:392
  18.0 0.1 copy.15
  18.0 0.0 copy-done.9
  18.0 0.1 dynamic_slice.3
  18.1 40.8 %collective-permute-done = f32[8,64]{1,0:T(8,128)S(1)} collective-permute-done((f32[8,64]{1,0:T(8,128)S(1)}, f32[8,64]{1,0:T(8,128)S(1)}, u32[]{:S(2)}, u32[]{:S(2)}) %collective-permute-start) | collective-permute-done | bytes 2080 | tf_op jit(solution)/shard_map/ppermute | solution.py:380
  58.9 0.9 copy.13
  59.8 1.9 %pad_maximum_fusion.back_ref = f32[8,64,256]{2,1,0:T(8,128)} fusion(f32[8,64,255]{2,1,0:T(8,128)S(1)} %bitcast.13, f32[8,64,1]{2,1,0:T(8,128)} %copy.13), kind=kLoop, calls=%fused_computation | loop fusion | flops 131072 | bytes 1048576 | tf_op jit(solution)/shard_map/concatenate | solution.py:381
  61.7 0.0 all-to-all-done.in_ref
  61.7 0.1 broadcast_in_dim.14.shift_ref
  61.8 4.3 %shard_map.56 = f32[16,328,128]{2,1,0:T(8,128)S(1)} custom-call(s32[32,128]{1,0:T(8,128)S(1)} %broadcast_in_dim.14.shift_ref, f32[16,5,32,256]{3,2,1,0:T(8,128)S(1)} %all-to-all-done.in_ref), custom_call_target="tpu_custom_call" | custom-call | flops 6553600 | bytes 5242880 | tf_op jit(solution)/shard_map/pallas_call | solution.py:118
  66.1 0.0 copy-start.2
  66.1 77.0 %all_to_all.10.recv_ref = f32[16,328,128]{2,1,0:T(8,128)S(1)} all-to-all(f32[16,328,128]{2,1,0:T(8,128)S(1)} %shard_map.56), channel_id=1, replica_groups=mesh['az'=16,'rad'=2] {'az'}, dimensions={0} | all-to-all | bytes 5373952 | tf_op jit(solution)/shard_map/all_to_all | solution.py:365
  143.1 2.5 %shard_map.57 = (f32[8,64,256]{2,1,0:T(8,128)S(1)}, f32[2,8,256]{2,1,0:T(8,128)S(1)}) custom-call(f32[16,328,128]{2,1,0:T(8,128)S(1)} %all_to_all.10.recv_ref, f32[8,64,256]{2,1,0:T(8,128)S(1)} %copy-done.1, f32[8,64,256]{2,1,0:T(8,128)S(1)} %copy-done.2, f32[8,64,64]{2,1,0:T(8,128)S(1)} %copy-done.5), custom_call_target="tpu_custom_call" | custom-call | flops 16777216 | bytes 2097152 | tf_op jit(solution)/shard_map/pallas_call | solution.py:211
  145.6 0.0 copy-start.6
  145.6 0.8 copy-done.6
  146.4 1.5 collective-permute-start.1
  147.9 1.0 copy-done.3
  148.9 2.7 %shard_map.58.refs_2_ = f32[5,8,64,256]{3,2,1,0:T(8,128)} custom-call(f32[16,328,128]{2,1,0:T(8,128)S(1)} %all_to_all.10.recv_ref, f32[8,64,256]{2,1,0:T(8,128)S(1)} %copy-done.1, f32[8,64,256]{2,1,0:T(8,128)S(1)} %copy-done.3), custom_call_target="tpu_custom_call" | custom-call | flops 6553600 | bytes 5242880 | tf_op jit(solution)/shard_map/pallas_call | solution.py:261
  151.6 0.0 collective-permute-done.1.refs_1_
  151.7 1.9 %shard_map.59 = f32[5,8,64,256]{3,2,1,0:T(8,128)} custom-call(s32[1]{0:T(128)} %bitcast.band_ref, f32[8,10]{1,0:T(8,128)S(1)} %bitcast.15, f32[8,64,256]{2,1,0:T(8,128)S(1)} %copy-done.7, f32[8,64,64]{2,1,0:T(8,128)S(1)} %copy-done.5, f32[2,8,256]{2,1,0:T(8,128)S(1)} %get-tuple-element.14.refs_0_, ...), custom_call_target="tpu_custom_call", output_to_operand_aliasing={{}: (6, {})} | custom-call | flops 524288 | bytes 1048576 | tf_op jit(solution)/shard_map/pallas_call | solution.py:352
  (11 shorter events, 0.0 us)
Async XLA Ops:
  0.0 1.7 %copy-start.4 = (f32[5,8,64,256]{3,2,1,0:T(8,128)S(1)}, f32[5,8,64,256]{3,2,1,0:T(8,128)}, u32[]{:S(2)}) copy-start(f32[5,8,64,256]{3,2,1,0:T(8,128)} %param.5) | copy-start | bytes 7864324
  2.0 1.5 copy-start
  3.5 7.5 %copy-start.1 = (f32[8,64,256]{2,1,0:T(8,128)S(1)}, f32[8,64,256]{2,1,0:T(8,128)}, u32[]{:S(2)}) copy-start(f32[8,64,256]{2,1,0:T(8,128)} %speed_ref.3) | copy-start | bytes 1572868
  3.5 9.9 %copy-start.5 = (f32[8,64,64]{2,1,0:T(8,128)S(1)}, f32[8,64,64]{2,1,0:T(8,128)}, u32[]{:S(2)}) copy-start(f32[8,64,64]{2,1,0:T(8,128)} %inverse_ref.3) | copy-start | bytes 393220
  3.5 10.1 %copy-start.8 = (f32[8,1]{0,1:T(1,128)S(1)}, f32[8,1]{0,1:T(1,128)}, u32[]{:S(2)}) copy-start(f32[8,1]{0,1:T(1,128)} %param.9) | copy-start | bytes 100
  3.5 14.6 %copy-start.9 = (s32[64]{0:T(128)S(1)}, s32[64]{0:T(128)}, u32[]{:S(2)}) copy-start(s32[64]{0:T(128)} %param.7) | copy-start | bytes 772
  3.5 58.2 %all-to-all-start = ((f32[16,5,32,256]{3,2,1,0:T(8,128)}), f32[16,5,32,256]{3,2,1,0:T(8,128)S(1)}, u32[]{:S(2)}, u32[]{:S(2)}) async-start(f32[16,5,32,256]{3,2,1,0:T(8,128)} %copy-done), calls=%async_computation | async-start | bytes 5242880 | tf_op jit(solution)/shard_map/all_to_all | solution.py:365
  12.9 46.0 %collective-permute-start = (f32[8,64]{1,0:T(8,128)S(1)}, f32[8,64]{1,0:T(8,128)S(1)}, u32[]{:S(2)}, u32[]{:S(2)}) collective-permute-start(f32[8,64]{1,0:T(8,128)S(1)} %bitcast.17), channel_id=1, source_target_pairs={{0,2},{2,4},{4,6},{6,8},{8,10},{10,12},{12,14},{14,16},{16,18},{18... | collective-permute-start | bytes 6152 | tf_op jit(solution)/shard_map/ppermute | solution.py:380
  66.1 77.0 %copy-start.2 = (f32[8,64,256]{2,1,0:T(8,128)S(1)}, f32[8,64,256]{2,1,0:T(8,128)}, u32[]{:S(2)}) copy-start(f32[8,64,256]{2,1,0:T(8,128)} %pad_maximum_fusion.back_ref) | copy-start | bytes 1572868
  145.6 0.8 copy-start.6
  146.4 5.3 %collective-permute-start.1 = (f32[2,8,256]{2,1,0:T(8,128)S(1)}, f32[2,8,256]{2,1,0:T(8,128)S(1)}, u32[]{:S(2)}, u32[]{:S(2)}) collective-permute-start(f32[2,8,256]{2,1,0:T(8,128)S(1)} %get-tuple-element.14.refs_0_), channel_id=1, source_target_pairs={{0,1},{1,0},{2,3},{3,2},{4,5},{5,4},{6,7},{7,6},{8,9},{9,8},{10,11... | collective-permute-start | bytes 49160 | tf_op jit(solution)/shard_map/ppermute | solution.py:399
  147.9 1.0 copy-start.3
  148.9 2.7 %copy-start.7 = (f32[8,64,256]{2,1,0:T(8,128)S(1)}, f32[8,64,256]{2,1,0:T(8,128)}, u32[]{:S(2)}) copy-start(f32[8,64,256]{2,1,0:T(8,128)} %copy-done.6) | copy-start | bytes 1572868

commit v4 on v3

--- a/solution.py
+++ b/solution.py
@@ -11,45 +11,49 @@
 TILE_ROWS = 8
 IN_VMEM = pl.BlockSpec(memory_space=pltpu.VMEM)
 IN_HBM = pl.BlockSpec(memory_space=pltpu.HBM)
+IN_ANY = pl.BlockSpec(memory_space=pl.ANY)
 IN_SMEM = pl.BlockSpec(memory_space=pltpu.SMEM)
-ROOMY = pltpu.CompilerParams(vmem_limit_bytes=40 * 1024 * 1024)
+ROOMY = pltpu.CompilerParams(vmem_limit_bytes=20 * 1024 * 1024)
 
 
 def cost(flops, moved):
     return pl.CostEstimate(flops=flops, bytes_accessed=4 * moved, transcendentals=0)
 
 
-def copy_each(copies):
+def partner(me, step):
+    return lax.bitwise_xor(me, jnp.int32(step))
+
+
+def split_kernel(me_ref, in_ref, *rest):
+    outs, sems = rest[:-1], rest[-1]
+    copies = [
+        pltpu.make_async_copy(in_ref.at[:, partner(me_ref[0], step)], out, sems.at[step])
+        for step, out in enumerate(outs)
+    ]
     for copy in copies:
         copy.start()
     for copy in copies:
         copy.wait()
 
 
-def pack_kernel(in_ref, out_ref, sems):
-    copy_each(
-        [
-            pltpu.make_async_copy(in_ref.at[field], out_ref.at[:, field], sems.at[field])
-            for field in range(in_ref.shape[0])
-        ]
-    )
-
-
-def pack(blocked):
+def split(me, blocked):
     nf, n, rows, width = blocked.shape
     return pl.pallas_call(
-        pack_kernel,
-        out_shape=jax.ShapeDtypeStruct((n, nf, rows, width), jnp.float32),
-        in_specs=[IN_HBM],
-        out_specs=IN_HBM,
-        scratch_shapes=[pltpu.SemaphoreType.DMA((nf,))],
-        compiler_params=ROOMY,
+        split_kernel,
+        out_shape=[jax.ShapeDtypeStruct((nf, rows, width), jnp.float32)] * n,
+        in_specs=[IN_SMEM, IN_HBM],
+        out_specs=[IN_HBM] * n,
+        scratch_shapes=[pltpu.SemaphoreType.DMA((n,))],
+        compiler_params=pltpu.CompilerParams(vmem_limit_bytes=56 * 1024 * 1024),
         cost_estimate=cost(0, 2 * blocked.size),
-    )(blocked)
-
-
-def turn_kernel(shift_ref, in_ref, out_ref, held, sems):
-    n, nf, rows, width = in_ref.shape
+    )(me, blocked)
+
+
+def turn_kernel(me_ref, shift_ref, *refs):
+    circles, held, in_sems, out_sems = refs[-4:]
+    n, nf, rows, width = circles.shape
+    pieces, outs = refs[:n], refs[n : 2 * n]
+    me = me_ref[0]
     per_block = width // LANES
     tiles = n * per_block
     groups = rows // TILE_ROWS
@@ -57,10 +61,29 @@
     halo_row = nf * field_rows
     lane = lax.broadcasted_iota(jnp.int32, (TILE_ROWS, LANES), 1)
 
-    def field_copy(field):
-        part = pl.ds(pl.multiple_of(field * field_rows, TILE_ROWS), field_rows)
-        return pltpu.make_async_copy(held.at[:, part, :], out_ref.at[:, part, :], sems.at[field])
-
+    cuts = [pl.ds(0, 1), pl.ds(1, nf - 1)]
+    arrivals = [
+        [
+            pltpu.make_async_copy(
+                pieces[step].at[cut], circles.at[partner(me, step), cut], in_sems.at[half, step]
+            )
+            for step in range(n)
+        ]
+        for half, cut in enumerate(cuts)
+    ]
+    cuts = [pl.ds(0, halo_row - field_rows), pl.ds(halo_row - field_rows, field_rows + TILE_ROWS)]
+    leavings = [
+        [
+            pltpu.make_async_copy(
+                held.at[partner(me, step), cut, :], outs[step].at[cut, :], out_sems.at[half, step]
+            )
+            for step in range(n)
+        ]
+        for half, cut in enumerate(cuts)
+    ]
+    for half in arrivals:
+        for copy in half:
+            copy.start()
     for block in range(n):
         held[block, halo_row : halo_row + TILE_ROWS, :] = jnp.zeros((TILE_ROWS, LANES), jnp.float32)
 
@@ -76,7 +99,7 @@
         turned = []
         for tile in range(tiles):
             block, part = divmod(tile, per_block)
-            values = in_ref[block, field, here, part * LANES : (part + 1) * LANES]
+            values = circles[block, field, here, part * LANES : (part + 1) * LANES]
             turned.append(jnp.take_along_axis(values, source, axis=1, mode="promise_in_bounds"))
         circle = [jnp.where(own, turned[tile], turned[tile - 1]) for tile in range(tiles)]
         step = 1
@@ -96,34 +119,43 @@
             both = pltpu.roll(jnp.where(lane == 0, right, left), place + 1, 1)
             target = held.at[block, halo_row : halo_row + TILE_ROWS, :]
             target[...] = jnp.where(edge, both, target[...])
-
-        @pl.when(group == groups - 1)
-        def _():
-            field_copy(field).start()
-
         return 0
 
-    lax.fori_loop(0, nf * groups, one_group, 0)
-    halo = pl.ds(halo_row, TILE_ROWS)
-    halo_copy = pltpu.make_async_copy(held.at[:, halo, :], out_ref.at[:, halo, :], sems.at[nf])
-    halo_copy.start()
-    for field in range(nf):
-        field_copy(field).wait()
-    halo_copy.wait()
-
-
-def turn(shift_rows, gathered):
-    n, nf, rows, width = gathered.shape
-    shape = (n, nf * (width // LANES) * rows + TILE_ROWS, LANES)
+    for copy in arrivals[0]:
+        copy.wait()
+    lax.fori_loop(0, groups, one_group, 0)
+    for copy in arrivals[1]:
+        copy.wait()
+    lax.fori_loop(groups, (nf - 1) * groups, one_group, 0)
+    for copy in leavings[0]:
+        copy.start()
+    lax.fori_loop((nf - 1) * groups, nf * groups, one_group, 0)
+    for copy in leavings[1]:
+        copy.start()
+    for half in leavings:
+        for copy in half:
+            copy.wait()
+
+
+def turn(me, shift_rows, pieces):
+    n = len(pieces)
+    nf, rows, width = pieces[0].shape
+    shape = (nf * (width // LANES) * rows + TILE_ROWS, LANES)
+    size = n * nf * rows * width
     return pl.pallas_call(
         turn_kernel,
-        out_shape=jax.ShapeDtypeStruct(shape, jnp.float32),
-        in_specs=[IN_VMEM] * 2,
-        out_specs=IN_HBM,
-        scratch_shapes=[pltpu.VMEM(shape, jnp.float32), pltpu.SemaphoreType.DMA((nf + 1,))],
+        out_shape=[jax.ShapeDtypeStruct(shape, jnp.float32)] * n,
+        in_specs=[IN_SMEM, IN_VMEM] + [IN_ANY] * n,
+        out_specs=[IN_ANY] * n,
+        scratch_shapes=[
+            pltpu.VMEM((n, nf, rows, width), jnp.float32),
+            pltpu.VMEM((n,) + shape, jnp.float32),
+            pltpu.SemaphoreType.DMA((2, n)),
+            pltpu.SemaphoreType.DMA((2, n)),
+        ],
         compiler_params=ROOMY,
-        cost_estimate=cost(10 * gathered.size, 2 * gathered.size),
-    )(shift_rows, gathered)
+        cost_estimate=cost(10 * size, 2 * size),
+    )(me, shift_rows, *pieces)
 
 
 def carry_piece(fields, halo_row, recv, speed, back, store):
@@ -169,15 +201,35 @@
                 store(field, group * TILE_ROWS, part * LANES, here - (outflow - inflow))
 
 
-def energy_kernel(recv_ref, speed_ref, back_ref, inverse_ref, local_ref, ends_ref, moved):
+def energy_kernel(me_ref, speed_ref, back_ref, inverse_ref, *refs):
+    local_ref, ends_ref, recv_ref, moved, sems = refs[-5:]
     n, in_rows, _ = recv_ref.shape
+    pieces = refs[:n]
     levels, radii, width = speed_ref.shape
-    pieces = n // levels
-    rows = radii // pieces
-    field = (in_rows - TILE_ROWS) * LANES // (rows * width) - 1
+    per_level = n // levels
+    rows = radii // per_level
+    halo_row = in_rows - TILE_ROWS
+    field_rows = rows * width // LANES
+    field = halo_row // field_rows - 1
+
+    cuts = [pl.ds(halo_row - field_rows, field_rows + TILE_ROWS), pl.ds(0, halo_row - field_rows)]
+    copies = [
+        [
+            pltpu.make_async_copy(
+                pieces[step].at[cut, :], recv_ref.at[partner(me_ref[0], step), cut, :], sems.at[half, step]
+            )
+            for step in range(n)
+        ]
+        for half, cut in enumerate(cuts)
+    ]
+    for half in copies:
+        for copy in half:
+            copy.start()
+    for copy in copies[0]:
+        copy.wait()
 
     def one_level(level, _):
-        for piece in range(pieces):
+        for piece in range(per_level):
             part = pl.ds(piece * rows, rows)
 
             def store(_, row, cell, values, piece=piece):
@@ -186,8 +238,8 @@
 
             carry_piece(
                 [field],
-                in_rows - TILE_ROWS,
-                recv_ref.at[level * pieces + piece],
+                halo_row,
+                recv_ref.at[level * per_level + piece],
                 speed_ref.at[level, part],
                 back_ref.at[level, part],
                 store,
@@ -204,22 +256,26 @@
         return 0
 
     lax.fori_loop(0, levels, one_level, 0)
-
-
-def energy_part(received, speed, back_speed, inverse):
+    for copy in copies[1]:
+        copy.wait()
+
+
+def energy_part(me, pieces, speed, back_speed, inverse):
+    n = len(pieces)
     levels, radii, width = speed.shape
     return pl.pallas_call(
         energy_kernel,
         out_shape=[
             jax.ShapeDtypeStruct(speed.shape, jnp.float32),
             jax.ShapeDtypeStruct((2, levels, width), jnp.float32),
+            jax.ShapeDtypeStruct((n,) + pieces[0].shape, jnp.float32),
         ],
-        in_specs=[IN_VMEM] * 4,
-        out_specs=[IN_VMEM] * 2,
-        scratch_shapes=[pltpu.VMEM((radii, width), jnp.float32)],
+        in_specs=[IN_SMEM] + [IN_VMEM] * 3 + [IN_ANY] * n,
+        out_specs=[IN_VMEM] * 3,
+        scratch_shapes=[pltpu.VMEM((radii, width), jnp.float32), pltpu.SemaphoreType.DMA((2, n))],
         compiler_params=ROOMY,
         cost_estimate=cost(2 * speed.size * radii, 4 * speed.size),
-    )(received, speed, back_speed, inverse)
+    )(me, speed, back_speed, inverse, *pieces)
 
 
 def carry_kernel(recv_ref, speed_ref, back_ref, out_ref, held, sems):
@@ -361,8 +417,13 @@
     )(band, corners, local_part, inverse, *ends, result)
 
 
-def exchange(blocks):
-    return lax.all_to_all(blocks, "az", split_axis=0, concat_axis=0, tiled=True)
+def exchange(pieces):
+    n = len(pieces)
+    order = [step for pair in zip(range(n // 2, n), range(n // 2)) for step in pair if step > 0]
+    swapped = {0: pieces[0]}
+    for step in order:
+        swapped[step] = lax.ppermute(pieces[step], "az", [(i, i ^ step) for i in range(n)])
+    return [swapped[step] for step in range(n)]
 
 
 def per_device(fields, velocity, shifts, block_inverse, coupling):
@@ -373,7 +434,9 @@
     me = lax.axis_index("az")
     band = lax.axis_index("rad")
 
-    gathered = exchange(pack(fields.reshape(nf, n, rows, width)))
+    me_scalar = me[None].astype(jnp.int32)
+
+    gathered = exchange(split(me_scalar, fields.reshape(nf, n, rows, width)))
 
     own_shifts = lax.dynamic_slice_in_dim(shifts, (me * rows) % radii, rows)
     shift_rows = jnp.broadcast_to(own_shifts[:, None], (rows, LANES))
@@ -392,9 +455,9 @@
     all_corners = lax.all_gather(corners, "rad", axis=1, tiled=True)
     gathered, back_speed, all_corners = lax.optimization_barrier((gathered, back_speed, all_corners))
 
-    received = exchange(turn(shift_rows, gathered))
-
-    local_part, ends = energy_part(received, velocity, back_speed, block_inverse)
+    pieces = exchange(turn(me_scalar, shift_rows, gathered))
+
+    local_part, ends, received = energy_part(me_scalar, pieces, velocity, back_speed, block_inverse)
     if bands == 2:
         all_ends = [ends, lax.ppermute(ends, "rad", [(0, 1), (1, 0)])]
     else:

time: 154 us -> 255 us (1.66)
  the two profiles are of different devices: /device:TPU:0 before, /device:TPU:9 now
where the time goes in v4:
time: 255 us; the launch traced here: 254 us
  Pallas kernels  104 us (41%)
  waiting for transfers between devices  94 us (37%)
  starting transfers between devices  45.1 us (18%)
  local copies, waits for them, and re-layouts  6.8 us (3%)
  blocking collectives  3.19 us (1%)
    ppermute x30, waiting for transfers between devices, exchange(): lax.ppermute(pieces[step], 'az', [(i, i ^ step) for i in range(n)])  94 us
    pallas_call x1, Pallas kernels, split(): pl.pallas_call(split_kernel, out_shape=[jax.ShapeDtypeStruct((nf, rows, w...  80.7 us
    ppermute x30, starting transfers between devices, exchange(): lax.ppermute(pieces[step], 'az', [(i, i ^ step) for i in range(n)])  42 us
    pallas_call x1, Pallas kernels, turn(): pl.pallas_call(turn_kernel, out_shape=[jax.ShapeDtypeStruct(shape, jnp.fl...  12.1 us
    pallas_call x1, Pallas kernels, energy_part(): pl.pallas_call(energy_kernel, out_shape=[jax.ShapeDtypeStruct(speed.shape...  6.88 us
  transfers between devices with their start and end apart: 32, of which 19 were waited for; matrix products, arithmetic and copies ran while one was open for 1% of the time, Pallas kernels for 33%

profile of v4, /device:TPU:9, one launch (start us, length us, event | category | flops | bytes accessed | tf_op | source)
XLA Modules:
  0.0 254.5 jit_solution(16549228914668855161)
XLA Ops:
  1.3 1.8 collective-permute-start.15
  3.1 80.7 %shard_map.55 = (f32[5,32,256]{2,1,0:T(8,128)}, f32[5,32,256]{2,1,0:T(8,128)}, f32[5,32,256]{2,1,0:T(8,128)}, f32[5,32,256]{2,1,0:T(8,128)}, f32[5,32,256]{2,1,0...) custom-call(s32[1]{0:T(128)} %bitcast.1.me_ref, ...), custom_call_target="tpu_custom_call" | custom-call | bytes 5242880 | tf_op jit(solution)/shard_map/pallas_call | solution.py:41
  89.5 3.2 %collective-permute-start.6 = (f32[5,32,256]{2,1,0:T(8,128)}, f32[5,32,256]{2,1,0:T(8,128)S(1)}, u32[]{:S(2)}, u32[]{:S(2)}) collective-permute-start(f32[5,32,256]{2,1,0:T(8,128)} %get-tuple-element.65), channel_id=1, source_target_pairs={{0,14},{2,12},{4,10},{6,8},{8,6},{10,4},{12,2},{14,0},{16,30},{18,... | collective-permute-start | bytes 491528 | tf_op jit(solution)/shard_map/ppermute | solution.py:425
  93.9 2.3 collective-permute-start.7
  96.2 2.3 collective-permute-start.9
  98.4 6.1 %collective-permute-done.5.refs_6_ = f32[5,32,256]{2,1,0:T(8,128)S(1)} collective-permute-done((f32[5,32,256]{2,1,0:T(8,128)}, f32[5,32,256]{2,1,0:T(8,128)S(1)}, u32[]{:S(2)}, u32[]{:S(2)}) %collective-permute-start.5) | collective-permute-done | bytes 163872 | tf_op jit(solution)/shard_map/ppermute | solution.py:425
  104.6 3.7 %collective-permute-start.10 = (f32[5,32,256]{2,1,0:T(8,128)}, f32[5,32,256]{2,1,0:T(8,128)S(1)}, u32[]{:S(2)}, u32[]{:S(2)}) collective-permute-start(f32[5,32,256]{2,1,0:T(8,128)} %get-tuple-element.69), channel_id=1, source_target_pairs={{0,22},{2,20},{4,18},{6,16},{8,30},{10,28},{12,26},{14,24},{16,6},... | collective-permute-start | bytes 491528 | tf_op jit(solution)/shard_map/ppermute | solution.py:425
  110.4 14.7 %collective-permute-done.8.refs_9_ = f32[5,32,256]{2,1,0:T(8,128)S(1)} collective-permute-done((f32[5,32,256]{2,1,0:T(8,128)}, f32[5,32,256]{2,1,0:T(8,128)S(1)}, u32[]{:S(2)}, u32[]{:S(2)}) %collective-permute-start.8) | collective-permute-done | bytes 163872 | tf_op jit(solution)/shard_map/ppermute | solution.py:425
  125.1 3.5 %collective-permute-done.9.refs_10_ = f32[5,32,256]{2,1,0:T(8,128)S(1)} collective-permute-done((f32[5,32,256]{2,1,0:T(8,128)}, f32[5,32,256]{2,1,0:T(8,128)S(1)}, u32[]{:S(2)}, u32[]{:S(2)}) %collective-permute-start.9) | collective-permute-done | bytes 163872 | tf_op jit(solution)/shard_map/ppermute | solution.py:425
  129.2 3.2 %all-gather = f32[2,5,8]{2,1,0:T(8,128)S(1)} all-gather(f32[1,5,8]{2,1,0:T(8,128)S(1)} %bitcast.17), channel_id=1, replica_groups=mesh['az'=16,'rad'=2] {'rad'}, dimensions={0}, use_global_device_ids=true | all-gather | bytes 480 | tf_op jit(solution)/shard_map/all_gather | solution.py:455
  134.5 4.6 %collective-permute-done.10.refs_11_ = f32[5,32,256]{2,1,0:T(8,128)S(1)} collective-permute-done((f32[5,32,256]{2,1,0:T(8,128)}, f32[5,32,256]{2,1,0:T(8,128)S(1)}, u32[]{:S(2)}, u32[]{:S(2)}) %collective-permute-start.10) | collective-permute-done | bytes 163872 | tf_op jit(solution)/shard_map/ppermute | solution.py:425
  139.2 3.5 %collective-permute-done.11.refs_12_ = f32[5,32,256]{2,1,0:T(8,128)S(1)} collective-permute-done((f32[5,32,256]{2,1,0:T(8,128)}, f32[5,32,256]{2,1,0:T(8,128)S(1)}, u32[]{:S(2)}, u32[]{:S(2)}) %collective-permute-start.11) | collective-permute-done | bytes 163872 | tf_op jit(solution)/shard_map/ppermute | solution.py:425
  142.7 3.5 %collective-permute-done.12.refs_13_ = f32[5,32,256]{2,1,0:T(8,128)S(1)} collective-permute-done((f32[5,32,256]{2,1,0:T(8,128)}, f32[5,32,256]{2,1,0:T(8,128)S(1)}, u32[]{:S(2)}, u32[]{:S(2)}) %collective-permute-start.12) | collective-permute-done | bytes 163872 | tf_op jit(solution)/shard_map/ppermute | solution.py:425
  146.2 4.2 %collective-permute-done.13.refs_14_ = f32[5,32,256]{2,1,0:T(8,128)} collective-permute-done((f32[5,32,256]{2,1,0:T(8,128)}, f32[5,32,256]{2,1,0:T(8,128)}, u32[]{:S(2)}, u32[]{:S(2)}) %collective-permute-start.13) | collective-permute-done | bytes 163872 | tf_op jit(solution)/shard_map/ppermute | solution.py:425
  150.4 3.5 %collective-permute-done.14.refs_15_ = f32[5,32,256]{2,1,0:T(8,128)} collective-permute-done((f32[5,32,256]{2,1,0:T(8,128)}, f32[5,32,256]{2,1,0:T(8,128)}, u32[]{:S(2)}, u32[]{:S(2)}) %collective-permute-start.14) | collective-permute-done | bytes 163872 | tf_op jit(solution)/shard_map/ppermute | solution.py:425
  154.9 12.1 %shard_map.56 = (f32[328,128]{1,0:T(8,128)S(1)}, f32[328,128]{1,0:T(8,128)S(1)}, f32[328,128]{1,0:T(8,128)S(1)}, f32[328,128]{1,0:T(8,128)S(1)}, f32[328,128]{1,...) custom-call(s32[1]{0:T(128)} %bitcast.1.me_ref, ...), custom_call_target="tpu_custom_call" | custom-call | flops 6553600 | bytes 5242880 | tf_op jit(solution)/shard_map/pallas_call | solution.py:145
  169.2 1.8 collective-permute-start.20
  171.0 2.3 collective-permute-done.17.refs_2_
  173.6 3.8 %collective-permute-done.18.refs_3_ = f32[328,128]{1,0:T(8,128)S(1)} collective-permute-done((f32[328,128]{1,0:T(8,128)S(1)}, f32[328,128]{1,0:T(8,128)S(1)}, u32[]{:S(2)}, u32[]{:S(2)}) %collective-permute-start.18) | collective-permute-done | bytes 167968 | tf_op jit(solution)/shard_map/ppermute | solution.py:425
  178.1 1.8 collective-permute-start.24
  179.9 8.6 %collective-permute-start.25 = (f32[328,128]{1,0:T(8,128)S(1)}, f32[328,128]{1,0:T(8,128)S(1)}, u32[]{:S(2)}, u32[]{:S(2)}) collective-permute-start(f32[328,128]{1,0:T(8,128)S(1)} %get-tuple-element.102), channel_id=1, source_target_pairs={{0,20},{2,22},{4,16},{6,18},{8,28},{10,30},{12,24},{14,26},{16,4},... | collective-permute-start | bytes 503816 | tf_op jit(solution)/shard_map/ppermute | solution.py:425
  188.5 3.6 %collective-permute-start.26 = (f32[328,128]{1,0:T(8,128)S(1)}, f32[328,128]{1,0:T(8,128)S(1)}, u32[]{:S(2)}, u32[]{:S(2)}) collective-permute-start(f32[328,128]{1,0:T(8,128)S(1)} %get-tuple-element.103), channel_id=1, source_target_pairs={{0,22},{2,20},{4,18},{6,16},{8,30},{10,28},{12,26},{14,24},{16,6},... | collective-permute-start | bytes 503816 | tf_op jit(solution)/shard_map/ppermute | solution.py:425
  195.7 15.2 %collective-permute-done.25.refs_10_ = f32[328,128]{1,0:T(8,128)S(1)} collective-permute-done((f32[328,128]{1,0:T(8,128)S(1)}, f32[328,128]{1,0:T(8,128)S(1)}, u32[]{:S(2)}, u32[]{:S(2)}) %collective-permute-start.25) | collective-permute-done | bytes 167968 | tf_op jit(solution)/shard_map/ppermute | solution.py:425
  210.9 2.1 collective-permute-start.30
  213.1 8.7 %collective-permute-done.26.refs_11_ = f32[328,128]{1,0:T(8,128)S(1)} collective-permute-done((f32[328,128]{1,0:T(8,128)S(1)}, f32[328,128]{1,0:T(8,128)S(1)}, u32[]{:S(2)}, u32[]{:S(2)}) %collective-permute-start.26) | collective-permute-done | bytes 167968 | tf_op jit(solution)/shard_map/ppermute | solution.py:425
  221.7 4.7 %collective-permute-done.27.refs_12_ = f32[328,128]{1,0:T(8,128)S(1)} collective-permute-done((f32[328,128]{1,0:T(8,128)S(1)}, f32[328,128]{1,0:T(8,128)S(1)}, u32[]{:S(2)}, u32[]{:S(2)}) %collective-permute-start.27) | collective-permute-done | bytes 167968 | tf_op jit(solution)/shard_map/ppermute | solution.py:425
  226.4 3.8 %collective-permute-done.28.refs_13_ = f32[328,128]{1,0:T(8,128)S(1)} collective-permute-done((f32[328,128]{1,0:T(8,128)S(1)}, f32[328,128]{1,0:T(8,128)S(1)}, u32[]{:S(2)}, u32[]{:S(2)}) %collective-permute-start.28) | collective-permute-done | bytes 167968 | tf_op jit(solution)/shard_map/ppermute | solution.py:425
  230.2 4.7 %collective-permute-done.29.refs_14_ = f32[328,128]{1,0:T(8,128)S(1)} collective-permute-done((f32[328,128]{1,0:T(8,128)S(1)}, f32[328,128]{1,0:T(8,128)S(1)}, u32[]{:S(2)}, u32[]{:S(2)}) %collective-permute-start.29) | collective-permute-done | bytes 167968 | tf_op jit(solution)/shard_map/ppermute | solution.py:425
  234.9 3.6 %collective-permute-done.30.refs_15_ = f32[328,128]{1,0:T(8,128)S(1)} collective-permute-done((f32[328,128]{1,0:T(8,128)S(1)}, f32[328,128]{1,0:T(8,128)S(1)}, u32[]{:S(2)}, u32[]{:S(2)}) %collective-permute-start.30) | collective-permute-done | bytes 167968 | tf_op jit(solution)/shard_map/ppermute | solution.py:425
  238.5 6.9 %shard_map.57 = (f32[8,64,256]{2,1,0:T(8,128)S(1)}, f32[2,8,256]{2,1,0:T(8,128)S(1)}, f32[16,328,128]{2,1,0:T(8,128)S(1)}) custom-call(s32[1]{0:T(128)} %bitcast.1.me_ref, f32[8,64,256]{2,1,0:T(8,128)S(1)} %copy-done, f32[8,64,256]{2,1,0:T(8,128)S(1)} %pad_maximum_fusion.back_ref, f32[8,64,64]{2,1,0:T(8,128)S(1)} %copy-done.3, ...), custom_call_target="tpu_custom_call" | custom-call | flops 16777216 | bytes 2097152 | tf_op jit(solution)/shard_map/pallas_call | solution.py:266
  249.9 2.7 %shard_map.58.refs_2_ = f32[5,8,64,256]{3,2,1,0:T(8,128)} custom-call(f32[16,328,128]{2,1,0:T(8,128)S(1)} %copy-done.2, f32[8,64,256]{2,1,0:T(8,128)S(1)} %copy-done, f32[8,64,256]{2,1,0:T(8,128)S(1)} %pad_maximum_fusion.back_ref), custom_call_target="tpu_custom_call" | custom-call | flops 6553600 | bytes 5242880 | tf_op jit(solution)/shard_map/pallas_call | solution.py:317
  252.6 1.9 shard_map.59
  (62 shorter events, 25.2 us)
Async XLA Ops:
  1.3 84.8 %collective-permute-start.15 = (f32[8,64]{1,0:T(8,128)S(1)}, f32[8,64]{1,0:T(8,128)S(1)}, u32[]{:S(2)}, u32[]{:S(2)}) collective-permute-start(f32[8,64]{1,0:T(8,128)S(1)} %bitcast.19), channel_id=1, source_target_pairs={{0,2},{2,4},{4,6},{6,8},{8,10},{10,12},{12,14},{14,16},{16,18},{18... | collective-permute-start | bytes 6152 | tf_op jit(solution)/shard_map/ppermute | solution.py:443
  83.8 3.8 %collective-permute-start = (f32[5,32,256]{2,1,0:T(8,128)}, f32[5,32,256]{2,1,0:T(8,128)S(1)}, u32[]{:S(2)}, u32[]{:S(2)}) collective-permute-start(f32[5,32,256]{2,1,0:T(8,128)} %get-tuple-element.59), channel_id=1, source_target_pairs={{0,2},{2,0},{4,6},{6,4},{8,10},{10,8},{12,14},{14,12},{16,18},{18,... | collective-permute-start | bytes 491528 | tf_op jit(solution)/shard_map/ppermute | solution.py:425
  83.8 5.6 %collective-permute-start.1 = (f32[5,32,256]{2,1,0:T(8,128)}, f32[5,32,256]{2,1,0:T(8,128)S(1)}, u32[]{:S(2)}, u32[]{:S(2)}) collective-permute-start(f32[5,32,256]{2,1,0:T(8,128)} %get-tuple-element.60), channel_id=1, source_target_pairs={{0,4},{2,6},{4,0},{6,2},{8,12},{10,14},{12,8},{14,10},{16,20},{18,... | collective-permute-start | bytes 491528 | tf_op jit(solution)/shard_map/ppermute | solution.py:425
  85.2 8.7 %collective-permute-start.2 = (f32[5,32,256]{2,1,0:T(8,128)}, f32[5,32,256]{2,1,0:T(8,128)S(1)}, u32[]{:S(2)}, u32[]{:S(2)}) collective-permute-start(f32[5,32,256]{2,1,0:T(8,128)} %get-tuple-element.61), channel_id=1, source_target_pairs={{0,6},{2,4},{4,2},{6,0},{8,14},{10,12},{12,10},{14,8},{16,22},{18,... | collective-permute-start | bytes 491528 | tf_op jit(solution)/shard_map/ppermute | solution.py:425
  86.0 10.2 %collective-permute-start.3 = (f32[5,32,256]{2,1,0:T(8,128)}, f32[5,32,256]{2,1,0:T(8,128)S(1)}, u32[]{:S(2)}, u32[]{:S(2)}) collective-permute-start(f32[5,32,256]{2,1,0:T(8,128)} %get-tuple-element.62), channel_id=1, source_target_pairs={{0,8},{2,10},{4,12},{6,14},{8,0},{10,2},{12,4},{14,6},{16,24},{18,... | collective-permute-start | bytes 491528 | tf_op jit(solution)/shard_map/ppermute | solution.py:425
  86.1 10.0 %collective-permute-start.4 = (f32[5,32,256]{2,1,0:T(8,128)}, f32[5,32,256]{2,1,0:T(8,128)S(1)}, u32[]{:S(2)}, u32[]{:S(2)}) collective-permute-start(f32[5,32,256]{2,1,0:T(8,128)} %get-tuple-element.63), channel_id=1, source_target_pairs={{0,10},{2,8},{4,14},{6,12},{8,2},{10,0},{12,6},{14,4},{16,26},{18,... | collective-permute-start | bytes 491528 | tf_op jit(solution)/shard_map/ppermute | solution.py:425
  87.5 17.0 %collective-permute-start.5 = (f32[5,32,256]{2,1,0:T(8,128)}, f32[5,32,256]{2,1,0:T(8,128)S(1)}, u32[]{:S(2)}, u32[]{:S(2)}) collective-permute-start(f32[5,32,256]{2,1,0:T(8,128)} %get-tuple-element.64), channel_id=1, source_target_pairs={{0,12},{2,14},{4,8},{6,10},{8,4},{10,6},{12,0},{14,2},{16,28},{18,... | collective-permute-start | bytes 491528 | tf_op jit(solution)/shard_map/ppermute | solution.py:425
  89.5 18.8 %collective-permute-start.6 = (f32[5,32,256]{2,1,0:T(8,128)}, f32[5,32,256]{2,1,0:T(8,128)S(1)}, u32[]{:S(2)}, u32[]{:S(2)}) collective-permute-start(f32[5,32,256]{2,1,0:T(8,128)} %get-tuple-element.65), channel_id=1, source_target_pairs={{0,14},{2,12},{4,10},{6,8},{8,6},{10,4},{12,2},{14,0},{16,30},{18,... | collective-permute-start | bytes 491528 | tf_op jit(solution)/shard_map/ppermute | solution.py:425
  93.9 15.8 %collective-permute-start.7 = (f32[5,32,256]{2,1,0:T(8,128)}, f32[5,32,256]{2,1,0:T(8,128)S(1)}, u32[]{:S(2)}, u32[]{:S(2)}) collective-permute-start(f32[5,32,256]{2,1,0:T(8,128)} %get-tuple-element.66), channel_id=1, source_target_pairs={{0,16},{2,18},{4,20},{6,22},{8,24},{10,26},{12,28},{14,30},{16,0},... | collective-permute-start | bytes 491528 | tf_op jit(solution)/shard_map/ppermute | solution.py:425
  96.2 29.0 %collective-permute-start.8 = (f32[5,32,256]{2,1,0:T(8,128)}, f32[5,32,256]{2,1,0:T(8,128)S(1)}, u32[]{:S(2)}, u32[]{:S(2)}) collective-permute-start(f32[5,32,256]{2,1,0:T(8,128)} %get-tuple-element.67), channel_id=1, source_target_pairs={{0,18},{2,16},{4,22},{6,20},{8,26},{10,24},{12,30},{14,28},{16,2},... | collective-permute-start | bytes 491528 | tf_op jit(solution)/shard_map/ppermute | solution.py:425
  96.2 32.5 %collective-permute-start.9 = (f32[5,32,256]{2,1,0:T(8,128)}, f32[5,32,256]{2,1,0:T(8,128)S(1)}, u32[]{:S(2)}, u32[]{:S(2)}) collective-permute-start(f32[5,32,256]{2,1,0:T(8,128)} %get-tuple-element.68), channel_id=1, source_target_pairs={{0,20},{2,22},{4,16},{6,18},{8,28},{10,30},{12,24},{14,26},{16,4},... | collective-permute-start | bytes 491528 | tf_op jit(solution)/shard_map/ppermute | solution.py:425
  104.6 34.6 %collective-permute-start.10 = (f32[5,32,256]{2,1,0:T(8,128)}, f32[5,32,256]{2,1,0:T(8,128)S(1)}, u32[]{:S(2)}, u32[]{:S(2)}) collective-permute-start(f32[5,32,256]{2,1,0:T(8,128)} %get-tuple-element.69), channel_id=1, source_target_pairs={{0,22},{2,20},{4,18},{6,16},{8,30},{10,28},{12,26},{14,24},{16,6},... | collective-permute-start | bytes 491528 | tf_op jit(solution)/shard_map/ppermute | solution.py:425
  108.3 34.4 %collective-permute-start.11 = (f32[5,32,256]{2,1,0:T(8,128)}, f32[5,32,256]{2,1,0:T(8,128)S(1)}, u32[]{:S(2)}, u32[]{:S(2)}) collective-permute-start(f32[5,32,256]{2,1,0:T(8,128)} %get-tuple-element.70), channel_id=1, source_target_pairs={{0,24},{2,26},{4,28},{6,30},{8,16},{10,18},{12,20},{14,22},{16,8},... | collective-permute-start | bytes 491528 | tf_op jit(solution)/shard_map/ppermute | solution.py:425
  109.6 36.6 %collective-permute-start.12 = (f32[5,32,256]{2,1,0:T(8,128)}, f32[5,32,256]{2,1,0:T(8,128)S(1)}, u32[]{:S(2)}, u32[]{:S(2)}) collective-permute-start(f32[5,32,256]{2,1,0:T(8,128)} %get-tuple-element.71), channel_id=1, source_target_pairs={{0,26},{2,24},{4,30},{6,28},{8,18},{10,16},{12,22},{14,20},{16,10}... | collective-permute-start | bytes 491528 | tf_op jit(solution)/shard_map/ppermute | solution.py:425
  125.1 25.3 %collective-permute-start.13 = (f32[5,32,256]{2,1,0:T(8,128)}, f32[5,32,256]{2,1,0:T(8,128)}, u32[]{:S(2)}, u32[]{:S(2)}) collective-permute-start(f32[5,32,256]{2,1,0:T(8,128)} %get-tuple-element.72), channel_id=1, source_target_pairs={{0,28},{2,30},{4,24},{6,26},{8,20},{10,22},{12,16},{14,18},{16,12}... | collective-permute-start | bytes 491528 | tf_op jit(solution)/shard_map/ppermute | solution.py:425
  128.6 25.3 %collective-permute-start.14 = (f32[5,32,256]{2,1,0:T(8,128)}, f32[5,32,256]{2,1,0:T(8,128)}, u32[]{:S(2)}, u32[]{:S(2)}) collective-permute-start(f32[5,32,256]{2,1,0:T(8,128)} %get-tuple-element.73), channel_id=1, source_target_pairs={{0,30},{2,28},{4,26},{6,24},{8,22},{10,20},{12,18},{14,16},{16,14}... | collective-permute-start | bytes 491528 | tf_op jit(solution)/shard_map/ppermute | solution.py:425
  167.0 4.0 %collective-permute-start.16 = (f32[328,128]{1,0:T(8,128)S(1)}, f32[328,128]{1,0:T(8,128)S(1)}, u32[]{:S(2)}, u32[]{:S(2)}) collective-permute-start(f32[328,128]{1,0:T(8,128)S(1)} %get-tuple-element.93), channel_id=1, source_target_pairs={{0,2},{2,0},{4,6},{6,4},{8,10},{10,8},{12,14},{14,12},{16,18},{18,... | collective-permute-start | bytes 503816 | tf_op jit(solution)/shard_map/ppermute | solution.py:425
  167.5 5.8 %collective-permute-start.17 = (f32[328,128]{1,0:T(8,128)S(1)}, f32[328,128]{1,0:T(8,128)S(1)}, u32[]{:S(2)}, u32[]{:S(2)}) collective-permute-start(f32[328,128]{1,0:T(8,128)S(1)} %get-tuple-element.94), channel_id=1, source_target_pairs={{0,4},{2,6},{4,0},{6,2},{8,12},{10,14},{12,8},{14,10},{16,20},{18,... | collective-permute-start | bytes 503816 | tf_op jit(solution)/shard_map/ppermute | solution.py:425
  167.7 9.7 %collective-permute-start.18 = (f32[328,128]{1,0:T(8,128)S(1)}, f32[328,128]{1,0:T(8,128)S(1)}, u32[]{:S(2)}, u32[]{:S(2)}) collective-permute-start(f32[328,128]{1,0:T(8,128)S(1)} %get-tuple-element.95), channel_id=1, source_target_pairs={{0,6},{2,4},{4,2},{6,0},{8,14},{10,12},{12,10},{14,8},{16,22},{18,... | collective-permute-start | bytes 503816 | tf_op jit(solution)/shard_map/ppermute | solution.py:425
  169.2 8.9 %collective-permute-start.19 = (f32[328,128]{1,0:T(8,128)S(1)}, f32[328,128]{1,0:T(8,128)S(1)}, u32[]{:S(2)}, u32[]{:S(2)}) collective-permute-start(f32[328,128]{1,0:T(8,128)S(1)} %get-tuple-element.96), channel_id=1, source_target_pairs={{0,8},{2,10},{4,12},{6,14},{8,0},{10,2},{12,4},{14,6},{16,24},{18,... | collective-permute-start | bytes 503816 | tf_op jit(solution)/shard_map/ppermute | solution.py:425
  169.2 10.7 %collective-permute-start.20 = (f32[328,128]{1,0:T(8,128)S(1)}, f32[328,128]{1,0:T(8,128)S(1)}, u32[]{:S(2)}, u32[]{:S(2)}) collective-permute-start(f32[328,128]{1,0:T(8,128)S(1)} %get-tuple-element.97), channel_id=1, source_target_pairs={{0,10},{2,8},{4,14},{6,12},{8,2},{10,0},{12,6},{14,4},{16,26},{18,... | collective-permute-start | bytes 503816 | tf_op jit(solution)/shard_map/ppermute | solution.py:425
  171.0 17.5 %collective-permute-start.21 = (f32[328,128]{1,0:T(8,128)S(1)}, f32[328,128]{1,0:T(8,128)S(1)}, u32[]{:S(2)}, u32[]{:S(2)}) collective-permute-start(f32[328,128]{1,0:T(8,128)S(1)} %get-tuple-element.98), channel_id=1, source_target_pairs={{0,12},{2,14},{4,8},{6,10},{8,4},{10,6},{12,0},{14,2},{16,28},{18,... | collective-permute-start | bytes 503816 | tf_op jit(solution)/shard_map/ppermute | solution.py:425
  173.3 18.8 %collective-permute-start.22 = (f32[328,128]{1,0:T(8,128)S(1)}, f32[328,128]{1,0:T(8,128)S(1)}, u32[]{:S(2)}, u32[]{:S(2)}) collective-permute-start(f32[328,128]{1,0:T(8,128)S(1)} %get-tuple-element.99), channel_id=1, source_target_pairs={{0,14},{2,12},{4,10},{6,8},{8,6},{10,4},{12,2},{14,0},{16,30},{18,... | collective-permute-start | bytes 503816 | tf_op jit(solution)/shard_map/ppermute | solution.py:425
  177.4 15.3 %collective-permute-start.23 = (f32[328,128]{1,0:T(8,128)S(1)}, f32[328,128]{1,0:T(8,128)S(1)}, u32[]{:S(2)}, u32[]{:S(2)}) collective-permute-start(f32[328,128]{1,0:T(8,128)S(1)} %get-tuple-element.100), channel_id=1, source_target_pairs={{0,16},{2,18},{4,20},{6,22},{8,24},{10,26},{12,28},{14,30},{16,0},... | collective-permute-start | bytes 503816 | tf_op jit(solution)/shard_map/ppermute | solution.py:425
  178.1 16.7 %collective-permute-start.24 = (f32[328,128]{1,0:T(8,128)S(1)}, f32[328,128]{1,0:T(8,128)S(1)}, u32[]{:S(2)}, u32[]{:S(2)}) collective-permute-start(f32[328,128]{1,0:T(8,128)S(1)} %get-tuple-element.101), channel_id=1, source_target_pairs={{0,18},{2,16},{4,22},{6,20},{8,26},{10,24},{12,30},{14,28},{16,2},... | collective-permute-start | bytes 503816 | tf_op jit(solution)/shard_map/ppermute | solution.py:425
  179.9 31.1 %collective-permute-start.25 = (f32[328,128]{1,0:T(8,128)S(1)}, f32[328,128]{1,0:T(8,128)S(1)}, u32[]{:S(2)}, u32[]{:S(2)}) collective-permute-start(f32[328,128]{1,0:T(8,128)S(1)} %get-tuple-element.102), channel_id=1, source_target_pairs={{0,20},{2,22},{4,16},{6,18},{8,28},{10,30},{12,24},{14,26},{16,4},... | collective-permute-start | bytes 503816 | tf_op jit(solution)/shard_map/ppermute | solution.py:425
  188.5 33.2 %collective-permute-start.26 = (f32[328,128]{1,0:T(8,128)S(1)}, f32[328,128]{1,0:T(8,128)S(1)}, u32[]{:S(2)}, u32[]{:S(2)}) collective-permute-start(f32[328,128]{1,0:T(8,128)S(1)} %get-tuple-element.103), channel_id=1, source_target_pairs={{0,22},{2,20},{4,18},{6,16},{8,30},{10,28},{12,26},{14,24},{16,6},... | collective-permute-start | bytes 503816 | tf_op jit(solution)/shard_map/ppermute | solution.py:425
  192.2 34.2 %collective-permute-start.27 = (f32[328,128]{1,0:T(8,128)S(1)}, f32[328,128]{1,0:T(8,128)S(1)}, u32[]{:S(2)}, u32[]{:S(2)}) collective-permute-start(f32[328,128]{1,0:T(8,128)S(1)} %get-tuple-element.104), channel_id=1, source_target_pairs={{0,24},{2,26},{4,28},{6,30},{8,16},{10,18},{12,20},{14,22},{16,8},... | collective-permute-start | bytes 503816 | tf_op jit(solution)/shard_map/ppermute | solution.py:425
  192.7 37.4 %collective-permute-start.28 = (f32[328,128]{1,0:T(8,128)S(1)}, f32[328,128]{1,0:T(8,128)S(1)}, u32[]{:S(2)}, u32[]{:S(2)}) collective-permute-start(f32[328,128]{1,0:T(8,128)S(1)} %get-tuple-element.105), channel_id=1, source_target_pairs={{0,26},{2,24},{4,30},{6,28},{8,18},{10,16},{12,22},{14,20},{16,10}... | collective-permute-start | bytes 503816 | tf_op jit(solution)/shard_map/ppermute | solution.py:425
  194.8 40.1 %collective-permute-start.29 = (f32[328,128]{1,0:T(8,128)S(1)}, f32[328,128]{1,0:T(8,128)S(1)}, u32[]{:S(2)}, u32[]{:S(2)}) collective-permute-start(f32[328,128]{1,0:T(8,128)S(1)} %get-tuple-element.106), channel_id=1, source_target_pairs={{0,28},{2,30},{4,24},{6,26},{8,20},{10,22},{12,16},{14,18},{16,12}... | collective-permute-start | bytes 503816 | tf_op jit(solution)/shard_map/ppermute | solution.py:425
  210.9 27.6 %collective-permute-start.30 = (f32[328,128]{1,0:T(8,128)S(1)}, f32[328,128]{1,0:T(8,128)S(1)}, u32[]{:S(2)}, u32[]{:S(2)}) collective-permute-start(f32[328,128]{1,0:T(8,128)S(1)} %get-tuple-element.107), channel_id=1, source_target_pairs={{0,30},{2,28},{4,26},{6,24},{8,22},{10,20},{12,18},{14,16},{16,14}... | collective-permute-start | bytes 503816 | tf_op jit(solution)/shard_map/ppermute | solution.py:425
  246.9 5.7 %collective-permute-start.31 = (f32[2,8,256]{2,1,0:T(8,128)S(1)}, f32[2,8,256]{2,1,0:T(8,128)S(1)}, u32[]{:S(2)}, u32[]{:S(2)}) collective-permute-start(f32[2,8,256]{2,1,0:T(8,128)S(1)} %get-tuple-element.109.refs_0_), channel_id=1, source_target_pairs={{0,1},{1,0},{2,3},{3,2},{4,5},{5,4},{6,7},{7,6},{8,9},{9,8},{10,11... | collective-permute-start | bytes 49160 | tf_op jit(solution)/shard_map/ppermute | solution.py:462
  (7 other events, 528.0 us)

commit v5 on v3

--- a/solution.py
+++ b/solution.py
@@ -12,27 +12,32 @@
 IN_VMEM = pl.BlockSpec(memory_space=pltpu.VMEM)
 IN_HBM = pl.BlockSpec(memory_space=pltpu.HBM)
 IN_SMEM = pl.BlockSpec(memory_space=pltpu.SMEM)
-ROOMY = pltpu.CompilerParams(vmem_limit_bytes=40 * 1024 * 1024)
+ROOMY = pltpu.CompilerParams(vmem_limit_bytes=24 * 1024 * 1024)
 
 
 def cost(flops, moved):
     return pl.CostEstimate(flops=flops, bytes_accessed=4 * moved, transcendentals=0)
 
 
-def copy_each(copies):
-    for copy in copies:
+def pack_kernel(in_ref, out_ref, held, in_sems, out_sems):
+    nf, n = in_ref.shape[:2]
+    half = n // 2
+    arrivals, leavings = [], []
+    for piece in range(2 * nf):
+        field, part = piece // 2, pl.ds((piece % 2) * half, half)
+        arrivals.append(
+            pltpu.make_async_copy(in_ref.at[field, part], held.at[field, part], in_sems.at[piece])
+        )
+        leavings.append(
+            pltpu.make_async_copy(held.at[field, part], out_ref.at[part, field], out_sems.at[piece])
+        )
+    for copy in arrivals:
         copy.start()
-    for copy in copies:
+    for arrival, leaving in zip(arrivals, leavings):
+        arrival.wait()
+        leaving.start()
+    for copy in leavings:
         copy.wait()
-
-
-def pack_kernel(in_ref, out_ref, sems):
-    copy_each(
-        [
-            pltpu.make_async_copy(in_ref.at[field], out_ref.at[:, field], sems.at[field])
-            for field in range(in_ref.shape[0])
-        ]
-    )
 
 
 def pack(blocked):
@@ -42,13 +47,17 @@
         out_shape=jax.ShapeDtypeStruct((n, nf, rows, width), jnp.float32),
         in_specs=[IN_HBM],
         out_specs=IN_HBM,
-        scratch_shapes=[pltpu.SemaphoreType.DMA((nf,))],
-        compiler_params=ROOMY,
+        scratch_shapes=[
+            pltpu.VMEM(blocked.shape, jnp.float32),
+            pltpu.SemaphoreType.DMA((2 * nf,)),
+            pltpu.SemaphoreType.DMA((2 * nf,)),
+        ],
+        compiler_params=pltpu.CompilerParams(vmem_limit_bytes=58 * 1024 * 1024),
         cost_estimate=cost(0, 2 * blocked.size),
     )(blocked)
 
 
-def turn_kernel(shift_ref, in_ref, out_ref, held, sems):
+def turn_kernel(shift_ref, in_ref, out_ref):
     n, nf, rows, width = in_ref.shape
     per_block = width // LANES
     tiles = n * per_block
@@ -57,12 +66,8 @@
     halo_row = nf * field_rows
     lane = lax.broadcasted_iota(jnp.int32, (TILE_ROWS, LANES), 1)
 
-    def field_copy(field):
-        part = pl.ds(pl.multiple_of(field * field_rows, TILE_ROWS), field_rows)
-        return pltpu.make_async_copy(held.at[:, part, :], out_ref.at[:, part, :], sems.at[field])
-
     for block in range(n):
-        held[block, halo_row : halo_row + TILE_ROWS, :] = jnp.zeros((TILE_ROWS, LANES), jnp.float32)
+        out_ref[block, halo_row : halo_row + TILE_ROWS, :] = jnp.zeros((TILE_ROWS, LANES), jnp.float32)
 
     def one_group(index, _):
         field = index // groups
@@ -87,29 +92,19 @@
         for tile in range(tiles):
             block, part = divmod(tile, per_block)
             row = field * field_rows + part * rows + group * TILE_ROWS
-            held[block, pl.ds(pl.multiple_of(row, TILE_ROWS), TILE_ROWS), :] = circle[tile]
+            out_ref[block, pl.ds(pl.multiple_of(row, TILE_ROWS), TILE_ROWS), :] = circle[tile]
         place = index * 2
         edge = (lane == place) | (lane == place + 1)
         for block in range(n):
             left = circle[(block * per_block - 1) % tiles]
             right = circle[((block + 1) * per_block) % tiles]
             both = pltpu.roll(jnp.where(lane == 0, right, left), place + 1, 1)
-            target = held.at[block, halo_row : halo_row + TILE_ROWS, :]
+            target = out_ref.at[block, halo_row : halo_row + TILE_ROWS, :]
             target[...] = jnp.where(edge, both, target[...])
 
-        @pl.when(group == groups - 1)
-        def _():
-            field_copy(field).start()
-
         return 0
 
     lax.fori_loop(0, nf * groups, one_group, 0)
-    halo = pl.ds(halo_row, TILE_ROWS)
-    halo_copy = pltpu.make_async_copy(held.at[:, halo, :], out_ref.at[:, halo, :], sems.at[nf])
-    halo_copy.start()
-    for field in range(nf):
-        field_copy(field).wait()
-    halo_copy.wait()
 
 
 def turn(shift_rows, gathered):
@@ -119,8 +114,7 @@
         turn_kernel,
         out_shape=jax.ShapeDtypeStruct(shape, jnp.float32),
         in_specs=[IN_VMEM] * 2,
-        out_specs=IN_HBM,
-        scratch_shapes=[pltpu.VMEM(shape, jnp.float32), pltpu.SemaphoreType.DMA((nf + 1,))],
+        out_specs=IN_VMEM,
         compiler_params=ROOMY,
         cost_estimate=cost(10 * gathered.size, 2 * gathered.size),
     )(shift_rows, gathered)
@@ -176,13 +170,13 @@
     rows = radii // pieces
     field = (in_rows - TILE_ROWS) * LANES // (rows * width) - 1
 
-    def one_level(level, _):
+    def one_level(level):
         for piece in range(pieces):
             part = pl.ds(piece * rows, rows)
 
             def store(_, row, cell, values, piece=piece):
                 row += piece * rows
-                moved[row : row + TILE_ROWS, cell : cell + LANES] = values
+                moved[level, row : row + TILE_ROWS, cell : cell + LANES] = values
 
             carry_piece(
                 [field],
@@ -194,16 +188,16 @@
             )
         local = jnp.dot(
             inverse_ref[level],
-            moved[...],
+            moved[level],
             precision=lax.Precision.HIGHEST,
             preferred_element_type=jnp.float32,
         )
         local_ref[level] = local
-        ends_ref[0, pl.ds(level, 1), :] = local[:1]
-        ends_ref[1, pl.ds(level, 1), :] = local[-1:]
-        return 0
-
-    lax.fori_loop(0, levels, one_level, 0)
+        ends_ref[0, level : level + 1, :] = local[:1]
+        ends_ref[1, level : level + 1, :] = local[-1:]
+
+    for level in range(levels):
+        one_level(level)
 
 
 def energy_part(received, speed, back_speed, inverse):
@@ -216,7 +210,7 @@
         ],
         in_specs=[IN_VMEM] * 4,
         out_specs=[IN_VMEM] * 2,
-        scratch_shapes=[pltpu.VMEM((radii, width), jnp.float32)],
+        scratch_shapes=[pltpu.VMEM(speed.shape, jnp.float32)],
         compiler_params=ROOMY,
         cost_estimate=cost(2 * speed.size * radii, 4 * speed.size),
     )(received, speed, back_speed, inverse)
@@ -390,7 +384,10 @@
         axis=1,
     )
     all_corners = lax.all_gather(corners, "rad", axis=1, tiled=True)
-    gathered, back_speed, all_corners = lax.optimization_barrier((gathered, back_speed, all_corners))
+    band_scalar = band[None].astype(jnp.int32)
+    gathered, back_speed, all_corners, band_scalar, shift_rows = lax.optimization_barrier(
+        (gathered, back_speed, all_corners, band_scalar, shift_rows)
+    )
 
     received = exchange(turn(shift_rows, gathered))
 
@@ -400,7 +397,6 @@
     else:
         all_ends = [lax.all_gather(ends, "rad", axis=0)]
     result = carry(nf, received, velocity, back_speed)
-    band_scalar = band[None].astype(jnp.int32)
     return diffuse(band_scalar, all_corners, local_part, block_inverse, all_ends, result)
 
 

time: 154 us -> 149 us (0.968)
  local copies, waits for them, and re-layouts: 8.3 us -> 3.26 us
    unnamed x23 -> x13, local copies, waits for them, and re-layouts: 6.24 us -> 1.19 us
    pallas_call x1, Pallas kernels: 0.23 us -> 2.6 us  [pack(): pl.pallas_call(pack_kernel, out_shape=jax.ShapeDtypeStruct((n, nf, rows,...]
    pallas_call x1, Pallas kernels: 2.47 us -> 0.79 us  [energy_part(): pl.pallas_call(energy_kernel, out_shape=[jax.ShapeDtypeStruct(speed.shape...]
where the time goes in v5:
time: 149 us
  blocking collectives  81.3 us (55%)
  waiting for transfers between devices  40.8 us (27%)
  Pallas kernels  11.9 us (8%)
  starting transfers between devices  9.52 us (6%)
  local copies, waits for them, and re-layouts  3.26 us (2%)
  other arithmetic  1.94 us (1%)
    all_to_all x1, blocking collectives, exchange(): return lax.all_to_all(blocks, 'az', split_axis=0, concat_axis=0, tiled=True)  77 us
    ppermute x1, waiting for transfers between devices, per_device(): lax.ppermute(velocity[:, :, -1], 'az', [(i, (i + 1) % n) for i in range(n)])  40.8 us
    all_to_all x1, starting transfers between devices, exchange(): return lax.all_to_all(blocks, 'az', split_axis=0, concat_axis=0, tiled=True)  7.5 us
    all_gather x1, blocking collectives, per_device(): all_corners = lax.all_gather(corners, 'rad', axis=1, tiled=True)  4.34 us
    pallas_call x1, Pallas kernels, turn(): pl.pallas_call(turn_kernel, out_shape=jax.ShapeDtypeStruct(shape, jnp.flo...  3.95 us
  transfers between devices with their start and end apart: 3, of which 1 were waited for; matrix products, arithmetic and copies ran while one was open for 3% of the time, Pallas kernels for 2%

profile of v5, /device:TPU:0, one launch (start us, length us, event | category | flops | bytes accessed | tf_op | source)
XLA Modules:
  0.0 148.9 jit_solution(6279095770356847439)
XLA Ops:
  0.0 2.6 %shard_map.55 = f32[16,5,32,256]{3,2,1,0:T(8,128)} custom-call(f32[5,16,32,256]{3,2,1,0:T(8,128)} %bitcast.15), custom_call_target="tpu_custom_call" | custom-call | bytes 5242880 | tf_op jit(solution)/shard_map/pallas_call | solution.py:45
  2.6 0.0 copy-start
  2.6 0.0 copy-start.2
  2.6 0.0 copy-start.3
  2.6 0.0 copy-start.4
  2.7 7.5 %all-to-all-start = ((f32[16,5,32,256]{3,2,1,0:T(8,128)}), f32[16,5,32,256]{3,2,1,0:T(8,128)S(1)}, u32[]{:S(2)}, u32[]{:S(2)}) async-start(f32[16,5,32,256]{3,2,1,0:T(8,128)} %shard_map.55), calls=%async_computation | async-start | bytes 5242880 | tf_op jit(solution)/shard_map/all_to_all | solution.py:359
  10.2 0.0 copy-done
  10.2 0.8 slice.18
  11.0 1.1 copy.16
  12.1 0.4 collective-permute-start
  12.5 0.0 copy-done.2
  12.5 0.2 slice_reduce_fusion
  12.8 0.0 copy-done.3
  12.8 4.3 %all-gather = f32[2,5,8]{2,1,0:T(8,128)S(1)} all-gather(f32[1,5,8]{2,1,0:T(8,128)S(1)} %bitcast.16), channel_id=1, replica_groups=mesh['az'=16,'rad'=2] {'rad'}, dimensions={0}, use_global_device_ids=true | all-gather | bytes 480 | tf_op jit(solution)/shard_map/all_gather | solution.py:386
  17.1 0.1 copy.15
  17.2 0.0 copy-done.4
  17.2 0.1 dynamic_slice.3
  17.3 40.8 %collective-permute-done = f32[8,64]{1,0:T(8,128)S(1)} collective-permute-done((f32[8,64]{1,0:T(8,128)S(1)}, f32[8,64]{1,0:T(8,128)S(1)}, u32[]{:S(2)}, u32[]{:S(2)}) %collective-permute-start) | collective-permute-done | bytes 2080 | tf_op jit(solution)/shard_map/ppermute | solution.py:374
  58.1 0.9 copy.13
  58.9 1.9 %pad_maximum_fusion.back_ref = f32[8,64,256]{2,1,0:T(8,128)} fusion(f32[8,64,255]{2,1,0:T(8,128)S(1)} %bitcast.13, f32[8,64,1]{2,1,0:T(8,128)} %copy.13), kind=kLoop, calls=%fused_computation | loop fusion | flops 131072 | bytes 1048576 | tf_op jit(solution)/shard_map/concatenate | solution.py:375
  60.9 0.0 all-to-all-done.in_ref
  60.9 0.1 broadcast_in_dim.14.shift_ref
  61.0 4.0 %shard_map.56 = f32[16,328,128]{2,1,0:T(8,128)S(1)} custom-call(s32[32,128]{1,0:T(8,128)S(1)} %broadcast_in_dim.14.shift_ref, f32[16,5,32,256]{3,2,1,0:T(8,128)S(1)} %all-to-all-done.in_ref), custom_call_target="tpu_custom_call" | custom-call | flops 6553600 | bytes 5242880 | tf_op jit(solution)/shard_map/pallas_call | solution.py:113
  64.9 0.0 copy-start.1
  64.9 77.0 %all_to_all.10.recv_ref = f32[16,328,128]{2,1,0:T(8,128)S(1)} all-to-all(f32[16,328,128]{2,1,0:T(8,128)S(1)} %shard_map.56), channel_id=1, replica_groups=mesh['az'=16,'rad'=2] {'az'}, dimensions={0} | all-to-all | bytes 5373952 | tf_op jit(solution)/shard_map/all_to_all | solution.py:359
  141.9 0.0 copy-done.1
  141.9 0.8 shard_map.57
  142.7 1.6 %collective-permute-start.1 = (f32[2,8,256]{2,1,0:T(8,128)S(1)}, f32[2,8,256]{2,1,0:T(8,128)S(1)}, u32[]{:S(2)}, u32[]{:S(2)}) collective-permute-start(f32[2,8,256]{2,1,0:T(8,128)S(1)} %get-tuple-element.18.refs_0_), channel_id=1, source_target_pairs={{0,1},{1,0},{2,3},{3,2},{4,5},{5,4},{6,7},{7,6},{8,9},{9,8},{10,11... | collective-permute-start | bytes 49160 | tf_op jit(solution)/shard_map/ppermute | solution.py:396
  144.3 2.7 %shard_map.58.refs_2_ = f32[5,8,64,256]{3,2,1,0:T(8,128)} custom-call(f32[16,328,128]{2,1,0:T(8,128)S(1)} %all_to_all.10.recv_ref, f32[8,64,256]{2,1,0:T(8,128)S(1)} %copy-done, f32[8,64,256]{2,1,0:T(8,128)S(1)} %copy-done.1), custom_call_target="tpu_custom_call" | custom-call | flops 6553600 | bytes 5242880 | tf_op jit(solution)/shard_map/pallas_call | solution.py:255
  147.0 0.0 collective-permute-done.1.refs_1_
  147.0 1.9 %shard_map.59 = f32[5,8,64,256]{3,2,1,0:T(8,128)} custom-call(s32[1]{0:T(128)} %bitcast.6.band_ref, f32[8,10]{1,0:T(8,128)S(1)} %bitcast.14, f32[8,64,256]{2,1,0:T(8,128)S(1)} %get-tuple-element.17.local_ref, f32[8,64,64]{2,1,0:T(8,128)S(1)} %copy-done.2, f32[2,8,256]{2,1,0:T(8,128)S(1)} %get-tuple-element.18.refs_0_, ...), custom_call_target="tpu_custom_call", output_to_operand_aliasing={{}: (6, {})} | custom-call | flops 524288 | bytes 1048576 | tf_op jit(solution)/shard_map/pallas_call | solution.py:346
  (2 shorter events, 0.0 us)
Async XLA Ops:
  2.6 7.6 %copy-start = (f32[8,64,256]{2,1,0:T(8,128)S(1)}, f32[8,64,256]{2,1,0:T(8,128)}, u32[]{:S(2)}) copy-start(f32[8,64,256]{2,1,0:T(8,128)} %speed_ref.3) | copy-start | bytes 1572868
  2.6 9.9 %copy-start.2 = (f32[8,64,64]{2,1,0:T(8,128)S(1)}, f32[8,64,64]{2,1,0:T(8,128)}, u32[]{:S(2)}) copy-start(f32[8,64,64]{2,1,0:T(8,128)} %inverse_ref.3) | copy-start | bytes 393220
  2.6 10.1 %copy-start.3 = (f32[8,1]{0,1:T(1,128)S(1)}, f32[8,1]{0,1:T(1,128)}, u32[]{:S(2)}) copy-start(f32[8,1]{0,1:T(1,128)} %param.9) | copy-start | bytes 100
  2.6 14.6 %copy-start.4 = (s32[64]{0:T(128)S(1)}, s32[64]{0:T(128)}, u32[]{:S(2)}) copy-start(s32[64]{0:T(128)} %param.7) | copy-start | bytes 772
  2.7 58.2 %all-to-all-start = ((f32[16,5,32,256]{3,2,1,0:T(8,128)}), f32[16,5,32,256]{3,2,1,0:T(8,128)S(1)}, u32[]{:S(2)}, u32[]{:S(2)}) async-start(f32[16,5,32,256]{3,2,1,0:T(8,128)} %shard_map.55), calls=%async_computation | async-start | bytes 5242880 | tf_op jit(solution)/shard_map/all_to_all | solution.py:359
  12.1 46.0 %collective-permute-start = (f32[8,64]{1,0:T(8,128)S(1)}, f32[8,64]{1,0:T(8,128)S(1)}, u32[]{:S(2)}, u32[]{:S(2)}) collective-permute-start(f32[8,64]{1,0:T(8,128)S(1)} %bitcast.17), channel_id=1, source_target_pairs={{0,2},{2,4},{4,6},{6,8},{8,10},{10,12},{12,14},{14,16},{16,18},{18... | collective-permute-start | bytes 6152 | tf_op jit(solution)/shard_map/ppermute | solution.py:374
  64.9 77.0 %copy-start.1 = (f32[8,64,256]{2,1,0:T(8,128)S(1)}, f32[8,64,256]{2,1,0:T(8,128)}, u32[]{:S(2)}) copy-start(f32[8,64,256]{2,1,0:T(8,128)} %pad_maximum_fusion.back_ref) | copy-start | bytes 1572868
  142.7 4.3 %collective-permute-start.1 = (f32[2,8,256]{2,1,0:T(8,128)S(1)}, f32[2,8,256]{2,1,0:T(8,128)S(1)}, u32[]{:S(2)}, u32[]{:S(2)}) collective-permute-start(f32[2,8,256]{2,1,0:T(8,128)S(1)} %get-tuple-element.18.refs_0_), channel_id=1, source_target_pairs={{0,1},{1,0},{2,3},{3,2},{4,5},{5,4},{6,7},{7,6},{8,9},{9,8},{10,11... | collective-permute-start | bytes 49160 | tf_op jit(solution)/shard_map/ppermute | solution.py:396

commit v6 on v5

--- a/solution.py
+++ b/solution.py
@@ -21,10 +21,11 @@
 
 def pack_kernel(in_ref, out_ref, held, in_sems, out_sems):
     nf, n = in_ref.shape[:2]
-    half = n // 2
+    cuts = in_sems.shape[0] // nf
+    size = n // cuts
     arrivals, leavings = [], []
-    for piece in range(2 * nf):
-        field, part = piece // 2, pl.ds((piece % 2) * half, half)
+    for piece in range(cuts * nf):
+        field, part = piece // cuts, pl.ds((piece % cuts) * size, size)
         arrivals.append(
             pltpu.make_async_copy(in_ref.at[field, part], held.at[field, part], in_sems.at[piece])
         )
@@ -49,8 +50,8 @@
         out_specs=IN_HBM,
         scratch_shapes=[
             pltpu.VMEM(blocked.shape, jnp.float32),
-            pltpu.SemaphoreType.DMA((2 * nf,)),
-            pltpu.SemaphoreType.DMA((2 * nf,)),
+            pltpu.SemaphoreType.DMA((4 * nf,)),
+            pltpu.SemaphoreType.DMA((4 * nf,)),
         ],
         compiler_params=pltpu.CompilerParams(vmem_limit_bytes=58 * 1024 * 1024),
         cost_estimate=cost(0, 2 * blocked.size),
@@ -104,7 +105,7 @@
 
         return 0
 
-    lax.fori_loop(0, nf * groups, one_group, 0)
+    lax.fori_loop(0, nf * groups, one_group, 0, unroll=groups)
 
 
 def turn(shift_rows, gathered):
@@ -149,14 +150,12 @@
                 row = (field * per_block + part) * rows + group * TILE_ROWS
                 values.append(recv[row : row + TILE_ROWS, :])
             place = (field * groups + group) * 2
-            up = [pltpu.roll(halo, (LANES - place) % LANES, 1)]
-            up += [pltpu.roll(one, 1, 1) for one in values]
-            down = [pltpu.roll(one, LANES - 1, 1) for one in values]
-            down.append(pltpu.roll(halo, (LANES - 2 - place) % LANES, 1))
+            edges = pltpu.roll(halo, (2 * LANES - 1 - place) % LANES, 1)
+            circle = [edges] + values + [edges]
             for part in range(per_block):
-                here = values[part]
-                behind = jnp.where(first, up[part], up[part + 1])
-                ahead = jnp.where(last, down[part + 1], down[part])
+                before, here, after = circle[part : part + 3]
+                behind = pltpu.roll(jnp.where(last, before, here), 1, 1)
+                ahead = pltpu.roll(jnp.where(first, after, here), LANES - 1, 1)
                 plus, minus, back_plus, back_minus = rates[part]
                 outflow = plus * here + minus * ahead
                 inflow = back_plus * behind + back_minus * here
@@ -302,9 +301,9 @@
     return [nothing] + lower_values, upper_values + [nothing]
 
 
-def diffuse_kernel(band_ref, corner_ref, local_ref, inverse_ref, *refs):
+def diffuse_kernel(band_ref, corner_ref, local_ref, low_ref, high_ref, *refs):
     end_refs, (_, out_ref, held, sems) = refs[:-4], refs[-4:]
-    levels, radii, _ = local_ref.shape
+    levels, _, width = local_ref.shape
     bands = corner_ref.shape[1] // 5
     band = band_ref[0]
     if len(end_refs) == 2:
@@ -317,22 +316,18 @@
     corner = [[corner_ref[:, j * 5 + c : j * 5 + c + 1] for c in range(5)] for j in range(bands)]
     all_before, all_beyond = solve_interfaces(ends[0], ends[1], corner)
     before = beyond = jnp.zeros_like(ends[0][0])
-    below = above = jnp.zeros_like(corner[0][4])
     for j in range(bands):
-        mine = band == j
-        before = jnp.where(mine, all_before[j], before)
-        beyond = jnp.where(mine, all_beyond[j], beyond)
-        above = jnp.where(mine, corner[j][4], above)
-        if j > 0:
-            below = jnp.where(mine, corner[j - 1][4], below)
+        before = jnp.where(band == j, all_before[j], before)
+        beyond = jnp.where(band == j, all_beyond[j], beyond)
     copies = []
     for level in range(levels):
-        row = slice(level, level + 1)
-        held[level] = (
-            local_ref[level]
-            + (below[row] * inverse_ref[level, :, :1]) * before[row]
-            + (above[row] * inverse_ref[level, :, radii - 1 :]) * beyond[row]
-        )
+        for cell in range(0, width, LANES):
+            cut = slice(cell, cell + LANES)
+            held[level, :, cut] = (
+                local_ref[level, :, cut]
+                + low_ref[level] * before[level : level + 1, cut]
+                + high_ref[level] * beyond[level : level + 1, cut]
+            )
         copies.append(
             pltpu.make_async_copy(held.at[level], out_ref.at[out_ref.shape[0] - 1, level], sems.at[level])
         )
@@ -341,18 +336,18 @@
         copy.wait()
 
 
-def diffuse(band, corners, local_part, inverse, ends, result):
+def diffuse(band, corners, local_part, low, high, ends, result):
     levels = local_part.shape[0]
     return pl.pallas_call(
         diffuse_kernel,
         out_shape=jax.ShapeDtypeStruct(result.shape, jnp.float32),
-        in_specs=[IN_SMEM] + [IN_VMEM] * (3 + len(ends)) + [IN_HBM],
+        in_specs=[IN_SMEM] + [IN_VMEM] * (4 + len(ends)) + [IN_HBM],
         out_specs=IN_HBM,
         scratch_shapes=[pltpu.VMEM(local_part.shape, jnp.float32), pltpu.SemaphoreType.DMA((levels,))],
-        input_output_aliases={4 + len(ends): 0},
+        input_output_aliases={5 + len(ends): 0},
         compiler_params=ROOMY,
         cost_estimate=cost(4 * local_part.size, 2 * local_part.size),
-    )(band, corners, local_part, inverse, *ends, result)
+    )(band, corners, local_part, low, high, *ends, result)
 
 
 def exchange(blocks):
@@ -384,9 +379,14 @@
         axis=1,
     )
     all_corners = lax.all_gather(corners, "rad", axis=1, tiled=True)
+    links = all_corners.reshape(levels, bands, 5)[:, :, 4]
+    links_below = jnp.concatenate([jnp.zeros_like(links[:, :1]), links[:, :-1]], axis=1)
+    link_below = lax.dynamic_index_in_dim(links_below, band, 1, keepdims=True)
+    low = jnp.broadcast_to((link_below * block_inverse[:, :, 0])[:, :, None], (levels, radii, LANES))
+    high = jnp.broadcast_to((coupling * block_inverse[:, :, -1])[:, :, None], (levels, radii, LANES))
     band_scalar = band[None].astype(jnp.int32)
-    gathered, back_speed, all_corners, band_scalar, shift_rows = lax.optimization_barrier(
-        (gathered, back_speed, all_corners, band_scalar, shift_rows)
+    gathered, back_speed, all_corners, low, high, band_scalar, shift_rows = lax.optimization_barrier(
+        (gathered, back_speed, all_corners, low, high, band_scalar, shift_rows)
     )
 
     received = exchange(turn(shift_rows, gathered))
@@ -397,7 +397,7 @@
     else:
         all_ends = [lax.all_gather(ends, "rad", axis=0)]
     result = carry(nf, received, velocity, back_speed)
-    return diffuse(band_scalar, all_corners, local_part, block_inverse, all_ends, result)
+    return diffuse(band_scalar, all_corners, local_part, low, high, all_ends, result)
 
 
 def solution(mesh):

time: 149 us -> 150 us (level)
  local copies, waits for them, and re-layouts: 3.26 us -> 6.81 us
  waiting for transfers between devices: 40.8 us -> 37.4 us
    ppermute x1, waiting for transfers between devices: 40.8 us -> 37.3 us  [per_device(): lax.ppermute(velocity[:, :, -1], 'az', [(i, (i + 1) % n) for i in range(n)])]
    pallas_call x1, Pallas kernels: 2.71 us -> 5.6 us  [carry(): pl.pallas_call(carry_kernel, out_shape=jax.ShapeDtypeStruct((nf,) + speed...]
    unnamed x13 -> x15, local copies, waits for them, and re-layouts: 1.19 us -> 3.34 us
  transfers between devices with their start and end apart: 3 -> 3, of which waited for: 1 -> 1; matrix products, arithmetic and copies ran while one was open for 3% -> 6% of each run, Pallas kernels for 2% -> 4%
where the time goes in v6:
time: 150 us
  blocking collectives  81.3 us (54%)
  waiting for transfers between devices  37.4 us (25%)
  Pallas kernels  12.9 us (9%)
  starting transfers between devices  9.53 us (6%)
  local copies, waits for them, and re-layouts  6.81 us (5%)
  other arithmetic  2.08 us (1%)
    all_to_all x1, blocking collectives, exchange(): return lax.all_to_all(blocks, 'az', split_axis=0, concat_axis=0, tiled=True)  77 us
    ppermute x1, waiting for transfers between devices, per_device(): lax.ppermute(velocity[:, :, -1], 'az', [(i, (i + 1) % n) for i in range(n)])  37.3 us
    all_to_all x1, starting transfers between devices, exchange(): return lax.all_to_all(blocks, 'az', split_axis=0, concat_axis=0, tiled=True)  7.5 us
    pallas_call x1, Pallas kernels, carry(): pl.pallas_call(carry_kernel, out_shape=jax.ShapeDtypeStruct((nf,) + speed...  5.6 us
    all_gather x1, blocking collectives, per_device(): all_corners = lax.all_gather(corners, 'rad', axis=1, tiled=True)  4.34 us
    unnamed x15, local copies, waits for them, and re-layouts  3.34 us
  transfers between devices with their start and end apart: 3, of which 1 were waited for; matrix products, arithmetic and copies ran while one was open for 6% of the time, Pallas kernels for 4%

profile of v6, /device:TPU:0, one launch (start us, length us, event | category | flops | bytes accessed | tf_op | source)
XLA Modules:
  0.0 150.1 jit_solution(13253809046569372684)
XLA Ops:
  0.0 2.8 %shard_map.55 = f32[16,5,32,256]{3,2,1,0:T(8,128)} custom-call(f32[5,16,32,256]{3,2,1,0:T(8,128)} %bitcast.24), custom_call_target="tpu_custom_call" | custom-call | bytes 5242880 | tf_op jit(solution)/shard_map/pallas_call | solution.py:46
  2.8 0.0 copy-start
  2.8 0.0 copy-start.2
  2.8 0.0 copy-start.3
  2.9 7.5 %all-to-all-start = ((f32[16,5,32,256]{3,2,1,0:T(8,128)}), f32[16,5,32,256]{3,2,1,0:T(8,128)S(1)}, u32[]{:S(2)}, u32[]{:S(2)}) async-start(f32[16,5,32,256]{3,2,1,0:T(8,128)} %shard_map.55), calls=%async_computation | async-start | bytes 5242880 | tf_op jit(solution)/shard_map/all_to_all | solution.py:354
  10.4 0.8 slice.30
  11.2 1.1 copy.23
  12.3 0.4 collective-permute-start
  12.7 0.2 slice_reduce_fusion
  13.0 4.3 %all-gather = f32[2,5,8]{2,1,0:T(8,128)S(1)} all-gather(f32[1,5,8]{2,1,0:T(8,128)S(1)} %bitcast.25), channel_id=1, replica_groups=mesh['az'=16,'rad'=2] {'rad'}, dimensions={0}, use_global_device_ids=true | all-gather | bytes 480 | tf_op jit(solution)/shard_map/all_gather | solution.py:381
  17.3 0.1 copy.22
  17.4 0.1 reshape.20
  17.5 0.1 slice.40
  17.6 0.1 copy.19
  17.7 0.9 fusion.1
  18.5 1.1 copy.25
  19.6 1.1 copy.24
  20.7 0.1 multiply_bitcast_fusion
  20.8 0.1 multiply_bitcast_fusion.1
  20.9 0.1 dynamic_slice.8
  20.9 37.3 %collective-permute-done = f32[8,64]{1,0:T(8,128)S(1)} collective-permute-done((f32[8,64]{1,0:T(8,128)S(1)}, f32[8,64]{1,0:T(8,128)S(1)}, u32[]{:S(2)}, u32[]{:S(2)}) %collective-permute-start) | collective-permute-done | bytes 2080 | tf_op jit(solution)/shard_map/ppermute | solution.py:369
  58.3 0.9 copy.17
  59.1 1.9 %pad_maximum_fusion.back_ref = f32[8,64,256]{2,1,0:T(8,128)} fusion(f32[8,64,255]{2,1,0:T(8,128)S(1)} %bitcast.21, f32[8,64,1]{2,1,0:T(8,128)} %copy.17), kind=kLoop, calls=%fused_computation | loop fusion | flops 131072 | bytes 1048576 | tf_op jit(solution)/shard_map/concatenate | solution.py:370
  61.1 0.1 broadcast_in_dim.34.shift_ref
  61.1 0.1 broadcast_in_dim.30.low_ref
  61.3 0.1 broadcast_in_dim.32.high_ref
  61.4 2.5 %shard_map.56 = f32[16,328,128]{2,1,0:T(8,128)S(1)} custom-call(s32[32,128]{1,0:T(8,128)S(1)} %broadcast_in_dim.34.shift_ref, f32[16,5,32,256]{3,2,1,0:T(8,128)S(1)} %all-to-all-done.in_ref), custom_call_target="tpu_custom_call" | custom-call | flops 6553600 | bytes 5242880 | tf_op jit(solution)/shard_map/pallas_call | solution.py:114
  63.9 77.0 %all_to_all.10.recv_ref = f32[16,328,128]{2,1,0:T(8,128)S(1)} all-to-all(f32[16,328,128]{2,1,0:T(8,128)S(1)} %shard_map.56), channel_id=1, replica_groups=mesh['az'=16,'rad'=2] {'az'}, dimensions={0} | all-to-all | bytes 5373952 | tf_op jit(solution)/shard_map/all_to_all | solution.py:354
  140.9 1.0 shard_map.57
  141.8 1.6 %collective-permute-start.1 = (f32[2,8,256]{2,1,0:T(8,128)S(1)}, f32[2,8,256]{2,1,0:T(8,128)S(1)}, u32[]{:S(2)}, u32[]{:S(2)}) collective-permute-start(f32[2,8,256]{2,1,0:T(8,128)S(1)} %get-tuple-element.22.refs_0_), channel_id=1, source_target_pairs={{0,1},{1,0},{2,3},{3,2},{4,5},{5,4},{6,7},{7,6},{8,9},{9,8},{10,11... | collective-permute-start | bytes 49160 | tf_op jit(solution)/shard_map/ppermute | solution.py:396
  143.4 5.6 %shard_map.58.refs_2_ = f32[5,8,64,256]{3,2,1,0:T(8,128)} custom-call(f32[16,328,128]{2,1,0:T(8,128)S(1)} %all_to_all.10.recv_ref, f32[8,64,256]{2,1,0:T(8,128)S(1)} %copy-done, f32[8,64,256]{2,1,0:T(8,128)S(1)} %copy-done.1), custom_call_target="tpu_custom_call" | custom-call | flops 6553600 | bytes 5242880 | tf_op jit(solution)/shard_map/pallas_call | solution.py:254
  149.0 1.1 shard_map.59
  (13 shorter events, 0.1 us)
Async XLA Ops:
  2.8 7.6 %copy-start = (f32[8,64,256]{2,1,0:T(8,128)S(1)}, f32[8,64,256]{2,1,0:T(8,128)}, u32[]{:S(2)}) copy-start(f32[8,64,256]{2,1,0:T(8,128)} %speed_ref.3) | copy-start | bytes 1572868
  2.8 9.9 %copy-start.2 = (f32[8,64,64]{2,1,0:T(8,128)S(1)}, f32[8,64,64]{2,1,0:T(8,128)}, u32[]{:S(2)}) copy-start(f32[8,64,64]{2,1,0:T(8,128)} %inverse_ref.1) | copy-start | bytes 393220
  2.8 10.1 %copy-start.3 = (f32[8,1]{0,1:T(1,128)S(1)}, f32[8,1]{0,1:T(1,128)}, u32[]{:S(2)}) copy-start(f32[8,1]{0,1:T(1,128)} %param.9) | copy-start | bytes 100
  2.9 18.0 %copy-start.4 = (s32[64]{0:T(128)S(1)}, s32[64]{0:T(128)}, u32[]{:S(2)}) copy-start(s32[64]{0:T(128)} %param.7) | copy-start | bytes 772
  2.9 58.2 %all-to-all-start = ((f32[16,5,32,256]{3,2,1,0:T(8,128)}), f32[16,5,32,256]{3,2,1,0:T(8,128)S(1)}, u32[]{:S(2)}, u32[]{:S(2)}) async-start(f32[16,5,32,256]{3,2,1,0:T(8,128)} %shard_map.55), calls=%async_computation | async-start | bytes 5242880 | tf_op jit(solution)/shard_map/all_to_all | solution.py:354
  12.3 46.0 %collective-permute-start = (f32[8,64]{1,0:T(8,128)S(1)}, f32[8,64]{1,0:T(8,128)S(1)}, u32[]{:S(2)}, u32[]{:S(2)}) collective-permute-start(f32[8,64]{1,0:T(8,128)S(1)} %bitcast.26), channel_id=1, source_target_pairs={{0,2},{2,4},{4,6},{6,8},{8,10},{10,12},{12,14},{14,16},{16,18},{18... | collective-permute-start | bytes 6152 | tf_op jit(solution)/shard_map/ppermute | solution.py:369
  63.9 77.0 %copy-start.1 = (f32[8,64,256]{2,1,0:T(8,128)S(1)}, f32[8,64,256]{2,1,0:T(8,128)}, u32[]{:S(2)}) copy-start(f32[8,64,256]{2,1,0:T(8,128)} %pad_maximum_fusion.back_ref) | copy-start | bytes 1572868
  141.8 7.2 %collective-permute-start.1 = (f32[2,8,256]{2,1,0:T(8,128)S(1)}, f32[2,8,256]{2,1,0:T(8,128)S(1)}, u32[]{:S(2)}, u32[]{:S(2)}) collective-permute-start(f32[2,8,256]{2,1,0:T(8,128)S(1)} %get-tuple-element.22.refs_0_), channel_id=1, source_target_pairs={{0,1},{1,0},{2,3},{3,2},{4,5},{5,4},{6,7},{7,6},{8,9},{9,8},{10,11... | collective-permute-start | bytes 49160 | tf_op jit(solution)/shard_map/ppermute | solution.py:396

commit v7 on v6

--- a/solution.py
+++ b/solution.py
@@ -19,60 +19,17 @@
     return pl.CostEstimate(flops=flops, bytes_accessed=4 * moved, transcendentals=0)
 
 
-def pack_kernel(in_ref, out_ref, held, in_sems, out_sems):
-    nf, n = in_ref.shape[:2]
-    cuts = in_sems.shape[0] // nf
-    size = n // cuts
-    arrivals, leavings = [], []
-    for piece in range(cuts * nf):
-        field, part = piece // cuts, pl.ds((piece % cuts) * size, size)
-        arrivals.append(
-            pltpu.make_async_copy(in_ref.at[field, part], held.at[field, part], in_sems.at[piece])
-        )
-        leavings.append(
-            pltpu.make_async_copy(held.at[field, part], out_ref.at[part, field], out_sems.at[piece])
-        )
-    for copy in arrivals:
-        copy.start()
-    for arrival, leaving in zip(arrivals, leavings):
-        arrival.wait()
-        leaving.start()
-    for copy in leavings:
-        copy.wait()
-
-
-def pack(blocked):
-    nf, n, rows, width = blocked.shape
-    return pl.pallas_call(
-        pack_kernel,
-        out_shape=jax.ShapeDtypeStruct((n, nf, rows, width), jnp.float32),
-        in_specs=[IN_HBM],
-        out_specs=IN_HBM,
-        scratch_shapes=[
-            pltpu.VMEM(blocked.shape, jnp.float32),
-            pltpu.SemaphoreType.DMA((4 * nf,)),
-            pltpu.SemaphoreType.DMA((4 * nf,)),
-        ],
-        compiler_params=pltpu.CompilerParams(vmem_limit_bytes=58 * 1024 * 1024),
-        cost_estimate=cost(0, 2 * blocked.size),
-    )(blocked)
-
-
 def turn_kernel(shift_ref, in_ref, out_ref):
-    n, nf, rows, width = in_ref.shape
+    n, rows, width = in_ref.shape
     per_block = width // LANES
     tiles = n * per_block
     groups = rows // TILE_ROWS
-    field_rows = per_block * rows
-    halo_row = nf * field_rows
+    halo_row = per_block * rows
     lane = lax.broadcasted_iota(jnp.int32, (TILE_ROWS, LANES), 1)
-
     for block in range(n):
         out_ref[block, halo_row : halo_row + TILE_ROWS, :] = jnp.zeros((TILE_ROWS, LANES), jnp.float32)
 
-    def one_group(index, _):
-        field = index // groups
-        group = index % groups
+    def one_group(group, _):
         here = pl.ds(pl.multiple_of(group * TILE_ROWS, TILE_ROWS), TILE_ROWS)
         shift = shift_ref[here, :]
         cells = shift & (LANES - 1)
@@ -82,7 +39,7 @@
         turned = []
         for tile in range(tiles):
             block, part = divmod(tile, per_block)
-            values = in_ref[block, field, here, part * LANES : (part + 1) * LANES]
+            values = in_ref[block, here, part * LANES : (part + 1) * LANES]
             turned.append(jnp.take_along_axis(values, source, axis=1, mode="promise_in_bounds"))
         circle = [jnp.where(own, turned[tile], turned[tile - 1]) for tile in range(tiles)]
         step = 1
@@ -92,9 +49,9 @@
             step *= 2
         for tile in range(tiles):
             block, part = divmod(tile, per_block)
-            row = field * field_rows + part * rows + group * TILE_ROWS
-            out_ref[block, pl.ds(pl.multiple_of(row, TILE_ROWS), TILE_ROWS), :] = circle[tile]
-        place = index * 2
+            row = pl.multiple_of((group * per_block + part) * TILE_ROWS, TILE_ROWS)
+            out_ref[block, pl.ds(row, TILE_ROWS), :] = circle[tile]
+        place = group * 2
         edge = (lane == place) | (lane == place + 1)
         for block in range(n):
             left = circle[(block * per_block - 1) % tiles]
@@ -102,15 +59,14 @@
             both = pltpu.roll(jnp.where(lane == 0, right, left), place + 1, 1)
             target = out_ref.at[block, halo_row : halo_row + TILE_ROWS, :]
             target[...] = jnp.where(edge, both, target[...])
-
         return 0
 
-    lax.fori_loop(0, nf * groups, one_group, 0, unroll=groups)
+    lax.fori_loop(0, groups, one_group, 0, unroll=4 if groups % 4 == 0 else 2 if groups % 2 == 0 else 1)
 
 
 def turn(shift_rows, gathered):
-    n, nf, rows, width = gathered.shape
-    shape = (n, nf * (width // LANES) * rows + TILE_ROWS, LANES)
+    n, rows, width = gathered.shape
+    shape = (n, (width // LANES) * rows + TILE_ROWS, LANES)
     return pl.pallas_call(
         turn_kernel,
         out_shape=jax.ShapeDtypeStruct(shape, jnp.float32),
@@ -121,70 +77,74 @@
     )(shift_rows, gathered)
 
 
-def carry_piece(fields, halo_row, recv, speed, back, store):
-    rows, width = speed.shape
+def spread_kernel(low_ref, high_ref, low_out, high_out):
+    low_out[...] = jnp.broadcast_to(low_ref[...], low_out.shape)
+    high_out[...] = jnp.broadcast_to(high_ref[...], high_out.shape)
+
+
+def spread(low, high):
+    shape = low.shape[:-1] + (LANES,)
+    return pl.pallas_call(
+        spread_kernel,
+        out_shape=[jax.ShapeDtypeStruct(shape, jnp.float32)] * 2,
+        in_specs=[IN_VMEM] * 2,
+        out_specs=[IN_VMEM] * 2,
+        compiler_params=ROOMY,
+        cost_estimate=cost(low.size, 2 * low.size * LANES),
+    )(low, high)
+
+
+def carry_level(fields, level, recv_ref, speed_ref, back_ref, store):
+    levels, radii, width = speed_ref.shape
     per_block = width // LANES
-    groups = rows // TILE_ROWS
+    in_rows = recv_ref.shape[1]
+    halo_row = in_rows - TILE_ROWS
+    groups = halo_row // (per_block * TILE_ROWS)
     lane = lax.broadcasted_iota(jnp.int32, (TILE_ROWS, LANES), 1)
     first = lane == 0
     last = lane == LANES - 1
-    halo = recv[halo_row : halo_row + TILE_ROWS, :]
-    for group in range(groups):
-        at = slice(group * TILE_ROWS, (group + 1) * TILE_ROWS)
+    for row in range(0, radii, TILE_ROWS):
         rates = []
         for part in range(per_block):
-            cut = (at, slice(part * LANES, (part + 1) * LANES))
-            ahead_speed = speed[cut]
-            back_speed = back[cut]
+            cut = (level, slice(row, row + TILE_ROWS), slice(part * LANES, (part + 1) * LANES))
+            speed = speed_ref[cut]
+            back = back_ref[cut]
             rates.append(
                 (
-                    jnp.maximum(ahead_speed, 0.0),
-                    jnp.minimum(ahead_speed, 0.0),
-                    jnp.maximum(back_speed, 0.0),
-                    jnp.minimum(back_speed, 0.0),
+                    jnp.maximum(speed, 0.0),
+                    jnp.minimum(speed, 0.0),
+                    jnp.maximum(back, 0.0),
+                    jnp.minimum(back, 0.0),
                 )
             )
         for field in fields:
+            piece, group = divmod(((field * levels + level) * radii + row) // TILE_ROWS, groups)
+            halo = recv_ref[piece, halo_row : halo_row + TILE_ROWS, :]
             values = []
             for part in range(per_block):
-                row = (field * per_block + part) * rows + group * TILE_ROWS
-                values.append(recv[row : row + TILE_ROWS, :])
-            place = (field * groups + group) * 2
-            edges = pltpu.roll(halo, (2 * LANES - 1 - place) % LANES, 1)
-            circle = [edges] + values + [edges]
+                at = (group * per_block + part) * TILE_ROWS
+                values.append(recv_ref[piece, at : at + TILE_ROWS, :])
+            up = [pltpu.roll(halo, (LANES - 2 * group) % LANES, 1)]
+            up += [pltpu.roll(one, 1, 1) for one in values]
+            down = [pltpu.roll(one, LANES - 1, 1) for one in values]
+            down.append(pltpu.roll(halo, (LANES - 2 - 2 * group) % LANES, 1))
             for part in range(per_block):
-                before, here, after = circle[part : part + 3]
-                behind = pltpu.roll(jnp.where(last, before, here), 1, 1)
-                ahead = pltpu.roll(jnp.where(first, after, here), LANES - 1, 1)
+                here = values[part]
+                behind = jnp.where(first, up[part], up[part + 1])
+                ahead = jnp.where(last, down[part + 1], down[part])
                 plus, minus, back_plus, back_minus = rates[part]
                 outflow = plus * here + minus * ahead
                 inflow = back_plus * behind + back_minus * here
-                store(field, group * TILE_ROWS, part * LANES, here - (outflow - inflow))
-
-
-def energy_kernel(recv_ref, speed_ref, back_ref, inverse_ref, local_ref, ends_ref, moved):
-    n, in_rows, _ = recv_ref.shape
-    levels, radii, width = speed_ref.shape
-    pieces = n // levels
-    rows = radii // pieces
-    field = (in_rows - TILE_ROWS) * LANES // (rows * width) - 1
-
-    def one_level(level):
-        for piece in range(pieces):
-            part = pl.ds(piece * rows, rows)
-
-            def store(_, row, cell, values, piece=piece):
-                row += piece * rows
-                moved[level, row : row + TILE_ROWS, cell : cell + LANES] = values
-
-            carry_piece(
-                [field],
-                in_rows - TILE_ROWS,
-                recv_ref.at[level * pieces + piece],
-                speed_ref.at[level, part],
-                back_ref.at[level, part],
-                store,
-            )
+                store(field, row, part * LANES, here - (outflow - inflow))
+
+
+def energy_kernel(field, recv_ref, speed_ref, back_ref, inverse_ref, local_ref, ends_ref, moved):
+    for level in range(speed_ref.shape[0]):
+
+        def store(_, row, cell, values, level=level):
+            moved[level, row : row + TILE_ROWS, cell : cell + LANES] = values
+
+        carry_level([field], level, recv_ref, speed_ref, back_ref, store)
         local = jnp.dot(
             inverse_ref[level],
             moved[level],
@@ -195,14 +155,11 @@
         ends_ref[0, level : level + 1, :] = local[:1]
         ends_ref[1, level : level + 1, :] = local[-1:]
 
-    for level in range(levels):
-        one_level(level)
-
-
-def energy_part(received, speed, back_speed, inverse):
+
+def energy_part(field, received, speed, back_speed, inverse):
     levels, radii, width = speed.shape
     return pl.pallas_call(
-        energy_kernel,
+        functools.partial(energy_kernel, field),
         out_shape=[
             jax.ShapeDtypeStruct(speed.shape, jnp.float32),
             jax.ShapeDtypeStruct((2, levels, width), jnp.float32),
@@ -216,37 +173,20 @@
 
 
 def carry_kernel(recv_ref, speed_ref, back_ref, out_ref, held, sems):
-    n, in_rows, _ = recv_ref.shape
-    levels, radii, width = speed_ref.shape
-    pieces = n // levels
-    rows = radii // pieces
-    nf = held.shape[0]
-
-    def level_copy(level):
-        return pltpu.make_async_copy(held.at[:, level], out_ref.at[pl.ds(0, nf), level], sems.at[level])
-
-    def one_level(level, _):
-        for piece in range(pieces):
-            part = pl.ds(piece * rows, rows)
-
-            def store(field, row, cell, values, piece=piece):
-                row += piece * rows
-                held[field, level, row : row + TILE_ROWS, cell : cell + LANES] = values
-
-            carry_piece(
-                range(nf),
-                in_rows - TILE_ROWS,
-                recv_ref.at[level * pieces + piece],
-                speed_ref.at[level, part],
-                back_ref.at[level, part],
-                store,
-            )
-        level_copy(level).start()
-        return 0
-
-    lax.fori_loop(0, levels, one_level, 0)
+    nf, levels = held.shape[:2]
+    copies = []
     for level in range(levels):
-        level_copy(level).wait()
+
+        def store(field, row, cell, values, level=level):
+            held[field, level, row : row + TILE_ROWS, cell : cell + LANES] = values
+
+        carry_level(range(nf), level, recv_ref, speed_ref, back_ref, store)
+        copies.append(
+            pltpu.make_async_copy(held.at[:, level], out_ref.at[pl.ds(0, nf), level], sems.at[level])
+        )
+        copies[-1].start()
+    for copy in copies:
+        copy.wait()
 
 
 def carry(nf, received, speed, back_speed):
@@ -358,13 +298,14 @@
     n = lax.axis_size("az")
     bands = lax.axis_size("rad")
     nf, levels, radii, width = fields.shape
-    rows = levels * radii // n
+    rows = nf * levels * radii // n
     me = lax.axis_index("az")
     band = lax.axis_index("rad")
 
-    gathered = exchange(pack(fields.reshape(nf, n, rows, width)))
-
-    own_shifts = lax.dynamic_slice_in_dim(shifts, (me * rows) % radii, rows)
+    gathered = exchange(fields.reshape(n, rows, width))
+
+    all_shifts = jnp.tile(shifts, rows // radii + 2)
+    own_shifts = lax.dynamic_slice_in_dim(all_shifts, (me * rows) % radii, rows)
     shift_rows = jnp.broadcast_to(own_shifts[:, None], (rows, LANES))
     edge_speed = lax.ppermute(velocity[:, :, -1], "az", [(i, (i + 1) % n) for i in range(n)])
     back_speed = jnp.concatenate([edge_speed[:, :, None], velocity[:, :, :-1]], axis=2)
@@ -382,8 +323,9 @@
     links = all_corners.reshape(levels, bands, 5)[:, :, 4]
     links_below = jnp.concatenate([jnp.zeros_like(links[:, :1]), links[:, :-1]], axis=1)
     link_below = lax.dynamic_index_in_dim(links_below, band, 1, keepdims=True)
-    low = jnp.broadcast_to((link_below * block_inverse[:, :, 0])[:, :, None], (levels, radii, LANES))
-    high = jnp.broadcast_to((coupling * block_inverse[:, :, -1])[:, :, None], (levels, radii, LANES))
+    low, high = spread(
+        (link_below * block_inverse[:, :, 0])[:, :, None], (coupling * block_inverse[:, :, -1])[:, :, None]
+    )
     band_scalar = band[None].astype(jnp.int32)
     gathered, back_speed, all_corners, low, high, band_scalar, shift_rows = lax.optimization_barrier(
         (gathered, back_speed, all_corners, low, high, band_scalar, shift_rows)
@@ -391,7 +333,7 @@
 
     received = exchange(turn(shift_rows, gathered))
 
-    local_part, ends = energy_part(received, velocity, back_speed, block_inverse)
+    local_part, ends = energy_part(nf - 1, received, velocity, back_speed, block_inverse)
     if bands == 2:
         all_ends = [ends, lax.ppermute(ends, "rad", [(0, 1), (1, 0)])]
     else:

time: 150 us -> 144 us (0.960)
  Pallas kernels: 12.9 us -> 7.2 us
  local copies, waits for them, and re-layouts: 6.81 us -> 5.01 us
    pallas_call x1, Pallas kernels: 5.6 us -> 2.46 us  [carry(): pl.pallas_call(carry_kernel, out_shape=jax.ShapeDtypeStruct((nf,) + speed...]
    pallas_call x2, Pallas kernels: 3.76 us -> 1.03 us  [the longest x1 0.84 us: energy_part(): pl.pallas_call(functools.partial(energy_kernel, field), out_shape=[jax.Sh...]
    unnamed x15 -> x21, local copies, waits for them, and re-layouts: 3.34 us -> 2.58 us
  transfers between devices with their start and end apart: 3 -> 3, of which waited for: 1 -> 1; matrix products, arithmetic and copies ran while one was open for 6% -> 4% of each run, Pallas kernels for 4% -> 2%
where the time goes in v7:
time: 144 us
  blocking collectives  81.3 us (56%)
  waiting for transfers between devices  38.7 us (27%)
  starting transfers between devices  9.53 us (7%)
  Pallas kernels  7.2 us (5%)
  local copies, waits for them, and re-layouts  5.01 us (3%)
  other arithmetic  2.1 us (1%)
    all_to_all x1, blocking collectives, exchange(): return lax.all_to_all(blocks, 'az', split_axis=0, concat_axis=0, tiled=True)  77 us
    ppermute x1, waiting for transfers between devices, per_device(): lax.ppermute(velocity[:, :, -1], 'az', [(i, (i + 1) % n) for i in range(n)])  38.7 us
    all_to_all x1, starting transfers between devices, exchange(): return lax.all_to_all(blocks, 'az', split_axis=0, concat_axis=0, tiled=True)  7.51 us
    all_gather x1, blocking collectives, per_device(): all_corners = lax.all_gather(corners, 'rad', axis=1, tiled=True)  4.34 us
  transfers between devices with their start and end apart: 3, of which 1 were waited for; matrix products, arithmetic and copies ran while one was open for 4% of the time, Pallas kernels for 2%

profile of v7, /device:TPU:0, one launch (start us, length us, event | category | flops | bytes accessed | tf_op | source)
XLA Modules:
  0.0 144.0 jit_solution(16808914961189816653)
XLA Ops:
  0.0 7.5 %all-to-all-start = ((f32[16,160,256]{2,1,0:T(8,128)}), f32[16,160,256]{2,1,0:T(8,128)S(1)}, u32[]{:S(2)}, u32[]{:S(2)}) async-start(f32[16,160,256]{2,1,0:T(8,128)} %bitcast.20), calls=%async_computation | async-start | bytes 5242880 | tf_op jit(solution)/shard_map/all_to_all | solution.py:294
  7.5 0.8 slice.30
  8.4 1.1 copy.19
  9.4 0.4 collective-permute-start
  9.9 0.2 slice_reduce_fusion
  10.1 4.3 %all-gather = f32[2,5,8]{2,1,0:T(8,128)S(1)} all-gather(f32[1,5,8]{2,1,0:T(8,128)S(1)} %bitcast.21), channel_id=1, replica_groups=mesh['az'=16,'rad'=2] {'rad'}, dimensions={0}, use_global_device_ids=true | all-gather | bytes 480 | tf_op jit(solution)/shard_map/all_gather | solution.py:322
  14.5 0.1 copy.18
  14.6 0.1 reshape.21
  14.6 0.1 slice.40
  14.7 0.1 copy.17
  14.8 0.2 slice_multiply_fusion
  15.0 0.2 shard_map.55
  15.2 0.0 copy-start.3
  15.2 0.7 copy-done.3
  15.9 0.7 copy-done.5
  16.6 0.1 tile.10
  16.7 0.1 dynamic_slice.8
  16.8 38.7 %collective-permute-done = f32[8,64]{1,0:T(8,128)S(1)} collective-permute-done((f32[8,64]{1,0:T(8,128)S(1)}, f32[8,64]{1,0:T(8,128)S(1)}, u32[]{:S(2)}, u32[]{:S(2)}) %collective-permute-start) | collective-permute-done | bytes 2080 | tf_op jit(solution)/shard_map/ppermute | solution.py:310
  55.4 0.8 copy.15
  56.3 1.9 %pad_maximum_fusion.back_ref = f32[8,64,256]{2,1,0:T(8,128)} fusion(f32[8,64,255]{2,1,0:T(8,128)S(1)} %bitcast.17, f32[8,64,1]{2,1,0:T(8,128)} %copy.15), kind=kLoop, calls=%fused_computation | loop fusion | flops 131072 | bytes 1048576 | tf_op jit(solution)/shard_map/concatenate | solution.py:311
  58.2 0.0 all-to-all-done.in_ref
  58.2 0.1 broadcast_in_dim.16.shift_ref
  58.3 2.7 %shard_map.56 = f32[16,328,128]{2,1,0:T(8,128)S(1)} custom-call(s32[160,128]{1,0:T(8,128)S(1)} %broadcast_in_dim.16.shift_ref, f32[16,160,256]{2,1,0:T(8,128)S(1)} %all-to-all-done.in_ref), custom_call_target="tpu_custom_call" | custom-call | flops 6553600 | bytes 5242880 | tf_op jit(solution)/shard_map/pallas_call | solution.py:70
  61.0 0.0 copy-start.1
  61.0 77.0 %all_to_all.10.recv_ref = f32[16,328,128]{2,1,0:T(8,128)S(1)} all-to-all(f32[16,328,128]{2,1,0:T(8,128)S(1)} %shard_map.56), channel_id=1, replica_groups=mesh['az'=16,'rad'=2] {'az'}, dimensions={0} | all-to-all | bytes 5373952 | tf_op jit(solution)/shard_map/all_to_all | solution.py:294
  138.0 0.8 shard_map.57
  138.8 1.6 %collective-permute-start.1 = (f32[2,8,256]{2,1,0:T(8,128)S(1)}, f32[2,8,256]{2,1,0:T(8,128)S(1)}, u32[]{:S(2)}, u32[]{:S(2)}) collective-permute-start(f32[2,8,256]{2,1,0:T(8,128)S(1)} %get-tuple-element.26.refs_0_), channel_id=1, source_target_pairs={{0,1},{1,0},{2,3},{3,2},{4,5},{5,4},{6,7},{7,6},{8,9},{9,8},{10,11... | collective-permute-start | bytes 49160 | tf_op jit(solution)/shard_map/ppermute | solution.py:338
  140.4 2.5 %shard_map.58.refs_2_ = f32[5,8,64,256]{3,2,1,0:T(8,128)} custom-call(f32[16,328,128]{2,1,0:T(8,128)S(1)} %all_to_all.10.recv_ref, f32[8,64,256]{2,1,0:T(8,128)S(1)} %copy-done, f32[8,64,256]{2,1,0:T(8,128)S(1)} %copy-done.1), custom_call_target="tpu_custom_call" | custom-call | flops 6553600 | bytes 5242880 | tf_op jit(solution)/shard_map/pallas_call | solution.py:194
  142.9 0.0 collective-permute-done.1.refs_1_
  142.9 0.0 copy-done.4
  142.9 0.0 copy-done.6
  142.9 1.1 shard_map.59
  (17 shorter events, 0.1 us)
Async XLA Ops:
  0.0 7.5 %copy-start = (f32[8,64,256]{2,1,0:T(8,128)S(1)}, f32[8,64,256]{2,1,0:T(8,128)}, u32[]{:S(2)}) copy-start(f32[8,64,256]{2,1,0:T(8,128)} %speed_ref.3) | copy-start | bytes 1572868
  0.0 9.9 %copy-start.2 = (f32[8,64,64]{2,1,0:T(8,128)S(1)}, f32[8,64,64]{2,1,0:T(8,128)}, u32[]{:S(2)}) copy-start(f32[8,64,64]{2,1,0:T(8,128)} %inverse_ref.1) | copy-start | bytes 393220
  0.0 10.1 %copy-start.7 = (f32[8,1]{0,1:T(1,128)S(1)}, f32[8,1]{0,1:T(1,128)}, u32[]{:S(2)}) copy-start(f32[8,1]{0,1:T(1,128)} %param.9) | copy-start | bytes 100
  0.0 16.6 %copy-start.8 = (s32[64]{0:T(128)S(1)}, s32[64]{0:T(128)}, u32[]{:S(2)}) copy-start(s32[64]{0:T(128)} %param.7) | copy-start | bytes 772
  0.0 58.2 %all-to-all-start = ((f32[16,160,256]{2,1,0:T(8,128)}), f32[16,160,256]{2,1,0:T(8,128)S(1)}, u32[]{:S(2)}, u32[]{:S(2)}) async-start(f32[16,160,256]{2,1,0:T(8,128)} %bitcast.20), calls=%async_computation | async-start | bytes 5242880 | tf_op jit(solution)/shard_map/all_to_all | solution.py:294
  9.4 46.0 %collective-permute-start = (f32[8,64]{1,0:T(8,128)S(1)}, f32[8,64]{1,0:T(8,128)S(1)}, u32[]{:S(2)}, u32[]{:S(2)}) collective-permute-start(f32[8,64]{1,0:T(8,128)S(1)} %bitcast.22), channel_id=1, source_target_pairs={{0,2},{2,4},{4,6},{6,8},{8,10},{10,12},{12,14},{14,16},{16,18},{18... | collective-permute-start | bytes 6152 | tf_op jit(solution)/shard_map/ppermute | solution.py:310
  15.2 0.7 copy-start.3
  15.9 0.7 copy-start.5
  61.0 77.0 %copy-start.1 = (f32[8,64,256]{2,1,0:T(8,128)S(1)}, f32[8,64,256]{2,1,0:T(8,128)}, u32[]{:S(2)}) copy-start(f32[8,64,256]{2,1,0:T(8,128)} %pad_maximum_fusion.back_ref) | copy-start | bytes 1572868
  138.8 4.1 %copy-start.4 = (f32[8,64,128]{2,1,0:T(8,128)S(1)}, f32[8,64,128]{2,1,0:T(8,128)}, u32[]{:S(2)}) copy-start(f32[8,64,128]{2,1,0:T(8,128)} %copy-done.3) | copy-start | bytes 786436
  138.8 4.1 %copy-start.6 = (f32[8,64,128]{2,1,0:T(8,128)S(1)}, f32[8,64,128]{2,1,0:T(8,128)}, u32[]{:S(2)}) copy-start(f32[8,64,128]{2,1,0:T(8,128)} %copy-done.5) | copy-start | bytes 786436
  138.8 4.1 %collective-permute-start.1 = (f32[2,8,256]{2,1,0:T(8,128)S(1)}, f32[2,8,256]{2,1,0:T(8,128)S(1)}, u32[]{:S(2)}, u32[]{:S(2)}) collective-permute-start(f32[2,8,256]{2,1,0:T(8,128)S(1)} %get-tuple-element.26.refs_0_), channel_id=1, source_target_pairs={{0,1},{1,0},{2,3},{3,2},{4,5},{5,4},{6,7},{7,6},{8,9},{9,8},{10,11... | collective-permute-start | bytes 49160 | tf_op jit(solution)/shard_map/ppermute | solution.py:338

commit v8 on v7

--- a/solution.py
+++ b/solution.py
@@ -19,8 +19,14 @@
     return pl.CostEstimate(flops=flops, bytes_accessed=4 * moved, transcendentals=0)
 
 
+def group_order(n):
+    return [(place % 2) * (n // 2) + place // 2 for place in range(n)]
+
+
 def turn_kernel(shift_ref, in_ref, out_ref):
     n, rows, width = in_ref.shape
+    order = group_order(n)
+    places = [order.index(block) for block in range(n)]
     per_block = width // LANES
     tiles = n * per_block
     groups = rows // TILE_ROWS
@@ -39,7 +45,7 @@
         turned = []
         for tile in range(tiles):
             block, part = divmod(tile, per_block)
-            values = in_ref[block, here, part * LANES : (part + 1) * LANES]
+            values = in_ref[places[block], here, part * LANES : (part + 1) * LANES]
             turned.append(jnp.take_along_axis(values, source, axis=1, mode="promise_in_bounds"))
         circle = [jnp.where(own, turned[tile], turned[tile - 1]) for tile in range(tiles)]
         step = 1
@@ -50,14 +56,14 @@
         for tile in range(tiles):
             block, part = divmod(tile, per_block)
             row = pl.multiple_of((group * per_block + part) * TILE_ROWS, TILE_ROWS)
-            out_ref[block, pl.ds(row, TILE_ROWS), :] = circle[tile]
+            out_ref[places[block], pl.ds(row, TILE_ROWS), :] = circle[tile]
         place = group * 2
         edge = (lane == place) | (lane == place + 1)
         for block in range(n):
             left = circle[(block * per_block - 1) % tiles]
             right = circle[((block + 1) * per_block) % tiles]
             both = pltpu.roll(jnp.where(lane == 0, right, left), place + 1, 1)
-            target = out_ref.at[block, halo_row : halo_row + TILE_ROWS, :]
+            target = out_ref.at[places[block], halo_row : halo_row + TILE_ROWS, :]
             target[...] = jnp.where(edge, both, target[...])
         return 0
 
@@ -291,7 +297,8 @@
 
 
 def exchange(blocks):
-    return lax.all_to_all(blocks, "az", split_axis=0, concat_axis=0, tiled=True)
+    order = group_order(blocks.shape[0])
+    return lax.all_to_all(blocks, "az", split_axis=0, concat_axis=0, tiled=True, axis_index_groups=[order])
 
 
 def per_device(fields, velocity, shifts, block_inverse, coupling):
@@ -299,13 +306,15 @@
     bands = lax.axis_size("rad")
     nf, levels, radii, width = fields.shape
     rows = nf * levels * radii // n
-    me = lax.axis_index("az")
+    order = group_order(n)
+    places = jnp.array([order.index(block) for block in range(n)], jnp.int32)
+    place = places[lax.axis_index("az")]
     band = lax.axis_index("rad")
 
     gathered = exchange(fields.reshape(n, rows, width))
 
     all_shifts = jnp.tile(shifts, rows // radii + 2)
-    own_shifts = lax.dynamic_slice_in_dim(all_shifts, (me * rows) % radii, rows)
+    own_shifts = lax.dynamic_slice_in_dim(all_shifts, (place * rows) % radii, rows)
     shift_rows = jnp.broadcast_to(own_shifts[:, None], (rows, LANES))
     edge_speed = lax.ppermute(velocity[:, :, -1], "az", [(i, (i + 1) % n) for i in range(n)])
     back_speed = jnp.concatenate([edge_speed[:, :, None], velocity[:, :, :-1]], axis=2)

time: 144 us -> 146 us (1.014)
  waiting for transfers between devices: 38.7 us -> 46.9 us
  blocking collectives: 81.3 us -> 73.4 us
    all_to_all x1, waiting for transfers between devices: 0.01 us -> 9.77 us  [exchange(): lax.all_to_all(blocks, 'az', split_axis=0, concat_axis=0, tiled=True, axi...]
    all_to_all x1, blocking collectives: 77 us -> 69.1 us  [exchange(): lax.all_to_all(blocks, 'az', split_axis=0, concat_axis=0, tiled=True, axi...]
    ppermute x1, waiting for transfers between devices: 38.7 us -> 37.2 us  [per_device(): lax.ppermute(velocity[:, :, -1], 'az', [(i, (i + 1) % n) for i in range(n)])]
  transfers between devices with their start and end apart: 3 -> 3, of which waited for: 1 -> 2; matrix products, arithmetic and copies ran while one was open for 4% -> 4% of each run, Pallas kernels for 2% -> 2%
where the time goes in v8:
time: 146 us
  blocking collectives  73.4 us (50%)
  waiting for transfers between devices  46.9 us (32%)
  starting transfers between devices  9.54 us (7%)
  Pallas kernels  7.16 us (5%)
  local copies, waits for them, and re-layouts  5.61 us (4%)
  other arithmetic  2.1 us (1%)
    all_to_all x1, blocking collectives, exchange(): lax.all_to_all(blocks, 'az', split_axis=0, concat_axis=0, tiled=True, axi...  69.1 us
    ppermute x1, waiting for transfers between devices, per_device(): lax.ppermute(velocity[:, :, -1], 'az', [(i, (i + 1) % n) for i in range(n)])  37.2 us
    all_to_all x1, waiting for transfers between devices, exchange(): lax.all_to_all(blocks, 'az', split_axis=0, concat_axis=0, tiled=True, axi...  9.77 us
    all_to_all x1, starting transfers between devices, exchange(): lax.all_to_all(blocks, 'az', split_axis=0, concat_axis=0, tiled=True, axi...  7.52 us
    all_gather x1, blocking collectives, per_device(): all_corners = lax.all_gather(corners, 'rad', axis=1, tiled=True)  4.34 us
  transfers between devices with their start and end apart: 3, of which 2 were waited for; matrix products, arithmetic and copies ran while one was open for 4% of the time, Pallas kernels for 2%

profile of v8, /device:TPU:0, one launch (start us, length us, event | category | flops | bytes accessed | tf_op | source)
XLA Modules:
  0.0 145.6 jit_solution(9256124444748513876)
XLA Ops:
  0.0 7.5 %all-to-all-start = ((f32[16,160,256]{2,1,0:T(8,128)}), f32[16,160,256]{2,1,0:T(8,128)S(1)}, u32[]{:S(2)}, u32[]{:S(2)}) async-start(f32[16,160,256]{2,1,0:T(8,128)} %bitcast.21), calls=%async_computation | async-start | bytes 5242880 | tf_op jit(solution)/shard_map/all_to_all | solution.py:301
  7.5 0.0 copy-done
  7.6 0.8 slice.30
  8.4 1.1 copy.20
  9.5 0.4 collective-permute-start
  9.9 0.0 copy-done.2
  9.9 0.2 slice_reduce_fusion
  10.2 4.3 %all-gather = f32[2,5,8]{2,1,0:T(8,128)S(1)} all-gather(f32[1,5,8]{2,1,0:T(8,128)S(1)} %bitcast.22), channel_id=1, replica_groups=mesh['az'=16,'rad'=2] {'rad'}, dimensions={0}, use_global_device_ids=true | all-gather | bytes 480 | tf_op jit(solution)/shard_map/all_gather | solution.py:331
  14.5 0.1 copy.19
  14.6 0.1 reshape.23
  14.7 0.1 slice.40
  14.7 0.1 copy.18
  14.9 0.2 slice_multiply_fusion
  15.0 0.2 shard_map.64
  15.2 0.7 copy-done.3
  15.9 0.7 copy-done.5
  16.6 0.6 dynamic_slice.11
  17.9 0.1 tile.10
  18.0 0.1 dynamic_slice.12
  18.1 37.2 %collective-permute-done = f32[8,64]{1,0:T(8,128)S(1)} collective-permute-done((f32[8,64]{1,0:T(8,128)S(1)}, f32[8,64]{1,0:T(8,128)S(1)}, u32[]{:S(2)}, u32[]{:S(2)}) %collective-permute-start) | collective-permute-done | bytes 2080 | tf_op jit(solution)/shard_map/ppermute | solution.py:319
  55.2 0.9 copy.16
  56.1 1.9 %pad_maximum_fusion.back_ref = f32[8,64,256]{2,1,0:T(8,128)} fusion(f32[8,64,255]{2,1,0:T(8,128)S(1)} %bitcast.18, f32[8,64,1]{2,1,0:T(8,128)} %copy.16), kind=kLoop, calls=%fused_computation | loop fusion | flops 131072 | bytes 1048576 | tf_op jit(solution)/shard_map/concatenate | solution.py:320
  58.0 9.8 %all-to-all-done.in_ref = f32[16,160,256]{2,1,0:T(8,128)S(1)} async-done(((f32[16,160,256]{2,1,0:T(8,128)}), f32[16,160,256]{2,1,0:T(8,128)S(1)}, u32[]{:S(2)}, u32[]{:S(2)}) %all-to-all-start) | async-done | bytes 2621472 | tf_op jit(solution)/shard_map/all_to_all | solution.py:301
  67.8 0.1 broadcast_in_dim.16.shift_ref
  67.9 2.7 %shard_map.65 = f32[16,328,128]{2,1,0:T(8,128)S(1)} custom-call(s32[160,128]{1,0:T(8,128)S(1)} %broadcast_in_dim.16.shift_ref, f32[16,160,256]{2,1,0:T(8,128)S(1)} %all-to-all-done.in_ref), custom_call_target="tpu_custom_call" | custom-call | flops 6553600 | bytes 5242880 | tf_op jit(solution)/shard_map/pallas_call | solution.py:76
  70.5 0.0 copy-start.1
  70.6 69.1 %all_to_all.10.recv_ref = f32[16,328,128]{2,1,0:T(8,128)S(1)} all-to-all(f32[16,328,128]{2,1,0:T(8,128)S(1)} %shard_map.65), channel_id=1, replica_groups={{0,16,2,18,4,20,6,22,8,24,10,26,12,28,14,30},{1,17,3,19,5,21,7,23,9,25,..., dimensions={0} | all-to-all | bytes 5373952 | tf_op jit(solution)/shard_map/all_to_all | solution.py:301
  139.6 0.8 shard_map.66
  140.4 1.6 %collective-permute-start.1 = (f32[2,8,256]{2,1,0:T(8,128)S(1)}, f32[2,8,256]{2,1,0:T(8,128)S(1)}, u32[]{:S(2)}, u32[]{:S(2)}) collective-permute-start(f32[2,8,256]{2,1,0:T(8,128)S(1)} %get-tuple-element.26.refs_0_), channel_id=1, source_target_pairs={{0,1},{1,0},{2,3},{3,2},{4,5},{5,4},{6,7},{7,6},{8,9},{9,8},{10,11... | collective-permute-start | bytes 49160 | tf_op jit(solution)/shard_map/ppermute | solution.py:347
  142.0 2.4 %shard_map.67.refs_2_ = f32[5,8,64,256]{3,2,1,0:T(8,128)} custom-call(f32[16,328,128]{2,1,0:T(8,128)S(1)} %all_to_all.10.recv_ref, f32[8,64,256]{2,1,0:T(8,128)S(1)} %copy-done, f32[8,64,256]{2,1,0:T(8,128)S(1)} %copy-done.1), custom_call_target="tpu_custom_call" | custom-call | flops 6553600 | bytes 5242880 | tf_op jit(solution)/shard_map/pallas_call | solution.py:200
  144.5 0.0 collective-permute-done.1.refs_1_
  144.5 1.1 shard_map.68
  (20 shorter events, 0.1 us)
Async XLA Ops:
  0.0 7.5 %copy-start = (f32[8,64,256]{2,1,0:T(8,128)S(1)}, f32[8,64,256]{2,1,0:T(8,128)}, u32[]{:S(2)}) copy-start(f32[8,64,256]{2,1,0:T(8,128)} %speed_ref.3) | copy-start | bytes 1572868
  0.0 9.9 %copy-start.2 = (f32[8,64,64]{2,1,0:T(8,128)S(1)}, f32[8,64,64]{2,1,0:T(8,128)}, u32[]{:S(2)}) copy-start(f32[8,64,64]{2,1,0:T(8,128)} %inverse_ref.1) | copy-start | bytes 393220
  0.0 10.1 %copy-start.7 = (f32[8,1]{0,1:T(1,128)S(1)}, f32[8,1]{0,1:T(1,128)}, u32[]{:S(2)}) copy-start(f32[8,1]{0,1:T(1,128)} %param.10) | copy-start | bytes 100
  0.0 16.6 %copy-start.9 = (s32[16]{0:T(128)S(1)}, s32[16]{0:T(128)}, u32[]{:S(2)}) copy-start(s32[16]{0:T(128)} %constant.38.clone) | copy-start | bytes 196
  0.0 17.9 %copy-start.8 = (s32[64]{0:T(128)S(1)}, s32[64]{0:T(128)}, u32[]{:S(2)}) copy-start(s32[64]{0:T(128)} %param.8) | copy-start | bytes 772
  0.0 67.8 %all-to-all-start = ((f32[16,160,256]{2,1,0:T(8,128)}), f32[16,160,256]{2,1,0:T(8,128)S(1)}, u32[]{:S(2)}, u32[]{:S(2)}) async-start(f32[16,160,256]{2,1,0:T(8,128)} %bitcast.21), calls=%async_computation | async-start | bytes 5242880 | tf_op jit(solution)/shard_map/all_to_all | solution.py:301
  9.5 45.7 %collective-permute-start = (f32[8,64]{1,0:T(8,128)S(1)}, f32[8,64]{1,0:T(8,128)S(1)}, u32[]{:S(2)}, u32[]{:S(2)}) collective-permute-start(f32[8,64]{1,0:T(8,128)S(1)} %bitcast.23), channel_id=1, source_target_pairs={{0,2},{2,4},{4,6},{6,8},{8,10},{10,12},{12,14},{14,16},{16,18},{18... | collective-permute-start | bytes 6152 | tf_op jit(solution)/shard_map/ppermute | solution.py:319
  15.2 0.7 copy-start.3
  15.9 0.7 copy-start.5
  70.5 69.1 %copy-start.1 = (f32[8,64,256]{2,1,0:T(8,128)S(1)}, f32[8,64,256]{2,1,0:T(8,128)}, u32[]{:S(2)}) copy-start(f32[8,64,256]{2,1,0:T(8,128)} %pad_maximum_fusion.back_ref) | copy-start | bytes 1572868
  140.4 4.1 %copy-start.4 = (f32[8,64,128]{2,1,0:T(8,128)S(1)}, f32[8,64,128]{2,1,0:T(8,128)}, u32[]{:S(2)}) copy-start(f32[8,64,128]{2,1,0:T(8,128)} %copy-done.3) | copy-start | bytes 786436
  140.4 4.1 %copy-start.6 = (f32[8,64,128]{2,1,0:T(8,128)S(1)}, f32[8,64,128]{2,1,0:T(8,128)}, u32[]{:S(2)}) copy-start(f32[8,64,128]{2,1,0:T(8,128)} %copy-done.5) | copy-start | bytes 786436
  140.4 4.0 %collective-permute-start.1 = (f32[2,8,256]{2,1,0:T(8,128)S(1)}, f32[2,8,256]{2,1,0:T(8,128)S(1)}, u32[]{:S(2)}, u32[]{:S(2)}) collective-permute-start(f32[2,8,256]{2,1,0:T(8,128)S(1)} %get-tuple-element.26.refs_0_), channel_id=1, source_target_pairs={{0,1},{1,0},{2,3},{3,2},{4,5},{5,4},{6,7},{7,6},{8,9},{9,8},{10,11... | collective-permute-start | bytes 49160 | tf_op jit(solution)/shard_map/ppermute | solution.py:347

commit v9 on v7

--- a/solution.py
+++ b/solution.py
@@ -94,93 +94,125 @@
     )(low, high)
 
 
-def carry_level(fields, level, recv_ref, speed_ref, back_ref, store):
-    levels, radii, width = speed_ref.shape
+def speed_parts(level, row, speed_ref, back_ref):
+    rates = []
+    for cell in range(0, speed_ref.shape[2], LANES):
+        cut = (level, slice(row, row + TILE_ROWS), slice(cell, cell + LANES))
+        speed = speed_ref[cut]
+        back = back_ref[cut]
+        rates.append(
+            (
+                jnp.maximum(speed, 0.0),
+                jnp.minimum(speed, 0.0),
+                jnp.maximum(back, 0.0),
+                jnp.minimum(back, 0.0),
+            )
+        )
+    return rates
+
+
+def transport(values, left, right, rates):
+    lane = lax.broadcasted_iota(jnp.int32, (TILE_ROWS, LANES), 1)
+    up = [left] + [pltpu.roll(one, 1, 1) for one in values]
+    down = [pltpu.roll(one, LANES - 1, 1) for one in values] + [right]
+    moved = []
+    for part, (plus, minus, back_plus, back_minus) in enumerate(rates):
+        here = values[part]
+        behind = jnp.where(lane == 0, up[part], up[part + 1])
+        ahead = jnp.where(lane == LANES - 1, down[part + 1], down[part])
+        outflow = plus * here + minus * ahead
+        inflow = back_plus * behind + back_minus * here
+        moved.append(here - (outflow - inflow))
+    return moved
+
+
+def energy_kernel(me_ref, shift_ref, circle_ref, speed_ref, back_ref, inverse_ref, local_ref, ends_ref, moved):
+    n, _, radii, width = circle_ref.shape
     per_block = width // LANES
-    in_rows = recv_ref.shape[1]
-    halo_row = in_rows - TILE_ROWS
-    groups = halo_row // (per_block * TILE_ROWS)
+    tiles = n * per_block
     lane = lax.broadcasted_iota(jnp.int32, (TILE_ROWS, LANES), 1)
-    first = lane == 0
-    last = lane == LANES - 1
     for row in range(0, radii, TILE_ROWS):
-        rates = []
-        for part in range(per_block):
-            cut = (level, slice(row, row + TILE_ROWS), slice(part * LANES, (part + 1) * LANES))
-            speed = speed_ref[cut]
-            back = back_ref[cut]
-            rates.append(
-                (
-                    jnp.maximum(speed, 0.0),
-                    jnp.minimum(speed, 0.0),
-                    jnp.maximum(back, 0.0),
-                    jnp.minimum(back, 0.0),
-                )
-            )
-        for field in fields:
-            piece, group = divmod(((field * levels + level) * radii + row) // TILE_ROWS, groups)
-            halo = recv_ref[piece, halo_row : halo_row + TILE_ROWS, :]
-            values = []
-            for part in range(per_block):
-                at = (group * per_block + part) * TILE_ROWS
-                values.append(recv_ref[piece, at : at + TILE_ROWS, :])
-            up = [pltpu.roll(halo, (LANES - 2 * group) % LANES, 1)]
-            up += [pltpu.roll(one, 1, 1) for one in values]
-            down = [pltpu.roll(one, LANES - 1, 1) for one in values]
-            down.append(pltpu.roll(halo, (LANES - 2 - 2 * group) % LANES, 1))
-            for part in range(per_block):
-                here = values[part]
-                behind = jnp.where(first, up[part], up[part + 1])
-                ahead = jnp.where(last, down[part + 1], down[part])
-                plus, minus, back_plus, back_minus = rates[part]
-                outflow = plus * here + minus * ahead
-                inflow = back_plus * behind + back_minus * here
-                store(field, row, part * LANES, here - (outflow - inflow))
-
-
-def energy_kernel(field, recv_ref, speed_ref, back_ref, inverse_ref, local_ref, ends_ref, moved):
-    for level in range(speed_ref.shape[0]):
-
-        def store(_, row, cell, values, level=level):
-            moved[level, row : row + TILE_ROWS, cell : cell + LANES] = values
-
-        carry_level([field], level, recv_ref, speed_ref, back_ref, store)
-        local = jnp.dot(
-            inverse_ref[level],
-            moved[level],
-            precision=lax.Precision.HIGHEST,
-            preferred_element_type=jnp.float32,
-        )
-        local_ref[level] = local
-        ends_ref[0, level : level + 1, :] = local[:1]
-        ends_ref[1, level : level + 1, :] = local[-1:]
-
-
-def energy_part(field, received, speed, back_speed, inverse):
+        here = slice(row, row + TILE_ROWS)
+        start = (me_ref[0] * width - shift_ref[here, :]) & (tiles * LANES - 1)
+        offset = start & (LANES - 1)
+        base = ((start >> 7) - 1) & (tiles - 1)
+        found = []
+        for tile in range(tiles):
+            block, part = divmod(tile, per_block)
+            found.append(circle_ref[block, 0, here, part * LANES : (part + 1) * LANES])
+        step = tiles // 2
+        while step > 0:
+            count = min(len(found), step + per_block + 1)
+            high = (base & step) != 0
+            found = [
+                jnp.where(high, found[(tile + step) % len(found)], found[tile]) for tile in range(count)
+            ]
+            step //= 2
+        source = (lane + offset) & (LANES - 1)
+        found = [jnp.take_along_axis(one, source, axis=1, mode="promise_in_bounds") for one in found]
+        fits = lane < LANES - offset
+        window = [jnp.where(fits, found[k], found[k + 1]) for k in range(per_block + 1)]
+        left = pltpu.roll(window[0], 1, 1)
+        right = pltpu.roll(found[per_block + 1], LANES - 1, 1)
+        results = transport(window[1:], left, right, speed_parts(0, row, speed_ref, back_ref))
+        for part, values in enumerate(results):
+            moved[here, part * LANES : (part + 1) * LANES] = values
+    local = jnp.dot(
+        inverse_ref[0], moved[...], precision=lax.Precision.HIGHEST, preferred_element_type=jnp.float32
+    )
+    local_ref[0] = local
+    level = pl.ds(pl.program_id(0), 1)
+    ends_ref[0, level, :] = local[:1]
+    ends_ref[1, level, :] = local[-1:]
+
+
+def energy_part(me, shift_rows, circles, speed, back_speed, inverse):
     levels, radii, width = speed.shape
+    n = circles.shape[0]
+    plane = pl.BlockSpec((1, radii, width), lambda level: (level, 0, 0))
     return pl.pallas_call(
-        functools.partial(energy_kernel, field),
+        energy_kernel,
+        grid=(levels,),
         out_shape=[
             jax.ShapeDtypeStruct(speed.shape, jnp.float32),
             jax.ShapeDtypeStruct((2, levels, width), jnp.float32),
         ],
-        in_specs=[IN_VMEM] * 4,
-        out_specs=[IN_VMEM] * 2,
-        scratch_shapes=[pltpu.VMEM(speed.shape, jnp.float32)],
+        in_specs=[
+            IN_SMEM,
+            pl.BlockSpec((radii, LANES), lambda level: (0, 0)),
+            pl.BlockSpec((n, 1, radii, width), lambda level: (0, level, 0, 0)),
+            plane,
+            plane,
+            pl.BlockSpec((1, radii, radii), lambda level: (level, 0, 0)),
+        ],
+        out_specs=[plane, pl.BlockSpec((2, levels, width), lambda level: (0, 0, 0))],
+        scratch_shapes=[pltpu.VMEM((radii, width), jnp.float32)],
         compiler_params=ROOMY,
-        cost_estimate=cost(2 * speed.size * radii, 4 * speed.size),
-    )(received, speed, back_speed, inverse)
-
-
-def carry_kernel(recv_ref, speed_ref, back_ref, out_ref, held, sems):
-    nf, levels = held.shape[:2]
-    copies = []
+        cost_estimate=cost(2 * speed.size * radii, (n + 4) * speed.size),
+    )(me, shift_rows, circles, speed, back_speed, inverse)
+
+
+def carry_kernel(recv_ref, speed_ref, back_ref, energy_ref, out_ref, held, sems):
+    nf, levels, radii, width = held.shape
+    per_block = width // LANES
+    halo_row = recv_ref.shape[1] - TILE_ROWS
+    groups = halo_row // (per_block * TILE_ROWS)
+    copies = [pltpu.make_async_copy(energy_ref, out_ref.at[nf], sems.at[levels])]
+    copies[0].start()
     for level in range(levels):
-
-        def store(field, row, cell, values, level=level):
-            held[field, level, row : row + TILE_ROWS, cell : cell + LANES] = values
-
-        carry_level(range(nf), level, recv_ref, speed_ref, back_ref, store)
+        for row in range(0, radii, TILE_ROWS):
+            rates = speed_parts(level, row, speed_ref, back_ref)
+            for field in range(nf):
+                piece, group = divmod(((field * levels + level) * radii + row) // TILE_ROWS, groups)
+                halo = recv_ref[piece, halo_row : halo_row + TILE_ROWS, :]
+                values = []
+                for part in range(per_block):
+                    at = (group * per_block + part) * TILE_ROWS
+                    values.append(recv_ref[piece, at : at + TILE_ROWS, :])
+                left = pltpu.roll(halo, (LANES - 2 * group) % LANES, 1)
+                right = pltpu.roll(halo, (LANES - 2 - 2 * group) % LANES, 1)
+                for part, result in enumerate(transport(values, left, right, rates)):
+                    held[field, level, row : row + TILE_ROWS, part * LANES : (part + 1) * LANES] = result
         copies.append(
             pltpu.make_async_copy(held.at[:, level], out_ref.at[pl.ds(0, nf), level], sems.at[level])
         )
@@ -189,20 +221,22 @@
         copy.wait()
 
 
-def carry(nf, received, speed, back_speed):
+def carry(received, speed, back_speed, energy):
+    n, in_rows, _ = received.shape
     levels, radii, width = speed.shape
+    nf = n * (in_rows - TILE_ROWS) * LANES // speed.size
     return pl.pallas_call(
         carry_kernel,
-        out_shape=jax.ShapeDtypeStruct((nf,) + speed.shape, jnp.float32),
-        in_specs=[IN_VMEM] * 3,
+        out_shape=jax.ShapeDtypeStruct((nf + 1,) + speed.shape, jnp.float32),
+        in_specs=[IN_VMEM] * 4,
         out_specs=IN_HBM,
         scratch_shapes=[
-            pltpu.VMEM((nf - 1,) + speed.shape, jnp.float32),
-            pltpu.SemaphoreType.DMA((levels,)),
+            pltpu.VMEM((nf,) + speed.shape, jnp.float32),
+            pltpu.SemaphoreType.DMA((levels + 1,)),
         ],
         compiler_params=ROOMY,
         cost_estimate=cost(10 * nf * speed.size, 2 * nf * speed.size),
-    )(received, speed, back_speed)
+    )(received, speed, back_speed, energy)
 
 
 def solve_interfaces(first_row, last_row, corner):
@@ -242,7 +276,7 @@
 
 
 def diffuse_kernel(band_ref, corner_ref, local_ref, low_ref, high_ref, *refs):
-    end_refs, (_, out_ref, held, sems) = refs[:-4], refs[-4:]
+    end_refs, out_ref = refs[:-1], refs[-1]
     levels, _, width = local_ref.shape
     bands = corner_ref.shape[1] // 5
     band = band_ref[0]
@@ -259,35 +293,25 @@
     for j in range(bands):
         before = jnp.where(band == j, all_before[j], before)
         beyond = jnp.where(band == j, all_beyond[j], beyond)
-    copies = []
     for level in range(levels):
         for cell in range(0, width, LANES):
             cut = slice(cell, cell + LANES)
-            held[level, :, cut] = (
+            out_ref[level, :, cut] = (
                 local_ref[level, :, cut]
                 + low_ref[level] * before[level : level + 1, cut]
                 + high_ref[level] * beyond[level : level + 1, cut]
             )
-        copies.append(
-            pltpu.make_async_copy(held.at[level], out_ref.at[out_ref.shape[0] - 1, level], sems.at[level])
-        )
-        copies[-1].start()
-    for copy in copies:
-        copy.wait()
-
-
-def diffuse(band, corners, local_part, low, high, ends, result):
-    levels = local_part.shape[0]
+
+
+def diffuse(band, corners, local_part, low, high, ends):
     return pl.pallas_call(
         diffuse_kernel,
-        out_shape=jax.ShapeDtypeStruct(result.shape, jnp.float32),
-        in_specs=[IN_SMEM] + [IN_VMEM] * (4 + len(ends)) + [IN_HBM],
-        out_specs=IN_HBM,
-        scratch_shapes=[pltpu.VMEM(local_part.shape, jnp.float32), pltpu.SemaphoreType.DMA((levels,))],
-        input_output_aliases={5 + len(ends): 0},
+        out_shape=jax.ShapeDtypeStruct(local_part.shape, jnp.float32),
+        in_specs=[IN_SMEM] + [IN_VMEM] * (4 + len(ends)),
+        out_specs=IN_VMEM,
         compiler_params=ROOMY,
         cost_estimate=cost(4 * local_part.size, 2 * local_part.size),
-    )(band, corners, local_part, low, high, *ends, result)
+    )(band, corners, local_part, low, high, *ends)
 
 
 def exchange(blocks):
@@ -298,11 +322,12 @@
     n = lax.axis_size("az")
     bands = lax.axis_size("rad")
     nf, levels, radii, width = fields.shape
-    rows = nf * levels * radii // n
+    rows = (nf - 1) * levels * radii // n
     me = lax.axis_index("az")
     band = lax.axis_index("rad")
 
-    gathered = exchange(fields.reshape(n, rows, width))
+    circles = lax.all_gather(fields[nf - 1], "az", axis=0)
+    gathered = exchange(fields[: nf - 1].reshape(n, rows, width))
 
     all_shifts = jnp.tile(shifts, rows // radii + 2)
     own_shifts = lax.dynamic_slice_in_dim(all_shifts, (me * rows) % radii, rows)
@@ -327,19 +352,35 @@
         (link_below * block_inverse[:, :, 0])[:, :, None], (coupling * block_inverse[:, :, -1])[:, :, None]
     )
     band_scalar = band[None].astype(jnp.int32)
-    gathered, back_speed, all_corners, low, high, band_scalar, shift_rows = lax.optimization_barrier(
-        (gathered, back_speed, all_corners, low, high, band_scalar, shift_rows)
-    )
-
-    received = exchange(turn(shift_rows, gathered))
-
-    local_part, ends = energy_part(nf - 1, received, velocity, back_speed, block_inverse)
+    me_scalar = me[None].astype(jnp.int32)
+    all_shift_rows = jnp.broadcast_to(shifts[:, None], (radii, LANES))
+    gathered, back_speed, all_corners, low, high, band_scalar, me_scalar, shift_rows, all_shift_rows = (
+        lax.optimization_barrier(
+            (
+                gathered,
+                back_speed,
+                all_corners,
+                low,
+                high,
+                band_scalar,
+                me_scalar,
+                shift_rows,
+                all_shift_rows,
+            )
+        )
+    )
+
+    turned = turn(shift_rows, gathered)
+    turned, circles = lax.optimization_barrier((turned, circles))
+    received = exchange(turned)
+
+    local_part, ends = energy_part(me_scalar, all_shift_rows, circles, velocity, back_speed, block_inverse)
     if bands == 2:
         all_ends = [ends, lax.ppermute(ends, "rad", [(0, 1), (1, 0)])]
     else:
         all_ends = [lax.all_gather(ends, "rad", axis=0)]
-    result = carry(nf, received, velocity, back_speed)
-    return diffuse(band_scalar, all_corners, local_part, low, high, all_ends, result)
+    energy = diffuse(band_scalar, all_corners, local_part, low, high, all_ends)
+    return carry(received, velocity, back_speed, energy)
 
 
 def solution(mesh):

time: 144 us -> 184 us (1.28)
  the two profiles are of different devices: /device:TPU:0 before, /device:TPU:11 now
where the time goes in v9:
time: 184 us
  waiting for transfers between devices  126 us (68%)
  starting transfers between devices  15.7 us (9%)
  local copies, waits for them, and re-layouts  14.4 us (8%)
  between operations  13.5 us (7%)
  Pallas kernels  9.14 us (5%)
  blocking collectives  3.5 us (2%)
    ppermute x1, waiting for transfers between devices, per_device(): lax.ppermute(velocity[:, :, -1], 'az', [(i, (i + 1) % n) for i in range(n)])  67.8 us
    all_to_all x2, waiting for transfers between devices, exchange(): return lax.all_to_all(blocks, 'az', split_axis=0, concat_axis=0, tiled=True)  40.5 us
    all_gather x1, waiting for transfers between devices, per_device(): circles = lax.all_gather(fields[nf - 1], 'az', axis=0)  16.3 us
    all_to_all x2, starting transfers between devices, exchange(): return lax.all_to_all(blocks, 'az', split_axis=0, concat_axis=0, tiled=True)  13 us
    unnamed x27, local copies, waits for them, and re-layouts  7.51 us
    pallas_call x1, Pallas kernels, energy_part(): pl.pallas_call(energy_kernel, grid=(levels,), out_shape=[jax.ShapeDtypeSt...  4.13 us
  transfers between devices with their start and end apart: 5, of which 5 were waited for; matrix products, arithmetic and copies ran while one was open for 4% of the time, Pallas kernels for 4%

profile of v9, /device:TPU:11, one launch (start us, length us, event | category | flops | bytes accessed | tf_op | source)
XLA Modules:
  0.0 183.7 jit_solution(5886789088450122849)
XLA Ops:
  6.5 1.9 %slice.47 = f32[1,8,64,256]{3,2,1,0:T(8,128)} slice(f32[5,8,64,256]{3,2,1,0:T(8,128)} %param.5), slice={[4:5], [0:8], [0:64], [0:256]} | slice | bytes 1048576 | tf_op jit(solution)/shard_map/slice | solution.py:329
  8.5 3.1 %slice.36 = f32[4,8,64,256]{3,2,1,0:T(8,128)} slice(f32[5,8,64,256]{3,2,1,0:T(8,128)} %param.5), slice={[0:4], [0:8], [0:64], [0:256]} | slice | bytes 4194304 | tf_op jit(solution)/shard_map/slice | solution.py:330
  11.6 6.7 %all-to-all-start = ((f32[16,128,256]{2,1,0:T(8,128)}), f32[16,128,256]{2,1,0:T(8,128)S(1)}, u32[]{:S(2)}, u32[]{:S(2)}) async-start(f32[16,128,256]{2,1,0:T(8,128)} %bitcast.21), calls=%async_computation | async-start | bytes 4194304 | tf_op jit(solution)/shard_map/all_to_all | solution.py:318
  18.3 0.1 slice.37
  18.4 0.1 copy.18
  18.6 1.5 collective-permute-start
  20.0 0.2 slice_reduce_fusion
  20.3 3.5 %all-gather = f32[2,5,8]{2,1,0:T(8,128)S(1)} all-gather(f32[1,5,8]{2,1,0:T(8,128)S(1)} %bitcast.22), channel_id=1, replica_groups=mesh['az'=16,'rad'=2] {'rad'}, dimensions={0}, use_global_device_ids=true | all-gather | bytes 480 | tf_op jit(solution)/shard_map/all_gather | solution.py:347
  23.8 0.1 copy.17
  23.9 0.1 reshape.22
  24.0 0.1 copy.16
  24.2 0.2 slice_multiply_fusion
  24.3 0.2 shard_map.55
  24.5 0.7 copy-done.6
  25.3 0.1 tile.10
  25.4 67.8 %collective-permute-done = f32[8,64]{1,0:T(8,128)S(1)} collective-permute-done((f32[8,64]{1,0:T(8,128)S(1)}, f32[8,64]{1,0:T(8,128)S(1)}, u32[]{:S(2)}, u32[]{:S(2)}) %collective-permute-start) | collective-permute-done | bytes 2080 | tf_op jit(solution)/shard_map/ppermute | solution.py:335
  93.2 0.9 copy.14
  94.1 1.1 pad_maximum_fusion.back_ref
  95.2 3.1 %all-to-all-done.in_ref = f32[16,128,256]{2,1,0:T(8,128)S(1)} async-done(((f32[16,128,256]{2,1,0:T(8,128)}), f32[16,128,256]{2,1,0:T(8,128)S(1)}, u32[]{:S(2)}, u32[]{:S(2)}) %all-to-all-start) | async-done | bytes 2097184 | tf_op jit(solution)/shard_map/all_to_all | solution.py:318
  98.5 2.1 %shard_map.56 = f32[16,264,128]{2,1,0:T(8,128)S(1)} custom-call(s32[128,128]{1,0:T(8,128)S(1)} %broadcast_in_dim.26.shift_ref, f32[16,128,256]{2,1,0:T(8,128)S(1)} %all-to-all-done.in_ref), custom_call_target="tpu_custom_call" | custom-call | flops 5242880 | bytes 4194304 | tf_op jit(solution)/shard_map/pallas_call | solution.py:70
  100.6 1.3 copy-done
  102.0 16.3 %all-gather.3.cloned.1.call-done.circle_ref = f32[16,8,64,256]{3,2,1,0:T(8,128)} async-done(((f32[1,8,64,256]{3,2,1,0:T(8,128)}), f32[16,8,64,256]{3,2,1,0:T(8,128)}) %all-gather.3.cloned.1.call-update) | async-done | bytes 8388624 | tf_op jit(solution)/shard_map/all_gather | solution.py:329
  118.3 6.3 %all-to-all-start.1 = ((f32[16,264,128]{2,1,0:T(8,128)}), f32[16,264,128]{2,1,0:T(8,128)S(1)}, u32[]{:S(2)}, u32[]{:S(2)}) async-start(f32[16,264,128]{2,1,0:T(8,128)} %copy-done), calls=%async_computation.1 | async-start | bytes 4325376 | tf_op jit(solution)/shard_map/all_to_all | solution.py:318
  124.5 3.4 %copy-done.1 = f32[16,8,64,256]{3,2,1,0:T(8,128)S(1)} copy-done((f32[16,8,64,256]{3,2,1,0:T(8,128)S(1)}, f32[16,8,64,256]{3,2,1,0:T(8,128)}, u32[]{:S(2)}) %copy-start.1) | copy-done | bytes 8388632
  127.9 4.1 %shard_map.57 = (f32[8,64,256]{2,1,0:T(8,128)S(1)}, f32[2,8,256]{2,1,0:T(8,128)S(1)}) custom-call(s32[1]{0:T(128)} %bitcast.10.me_ref, s32[64,128]{1,0:T(8,128)S(1)} %broadcast_in_dim.27.shift_ref, f32[16,8,64,256]{3,2,1,0:T(8,128)S(1)} %copy-done.1, f32[8,64,256]{2,1,0:T(8,128)S(1)} %copy-done.2, f32[8,64,256]{2,1,0:T(8,128)S(1)} %pad_maximum_fusion.back_ref, ...), custom_call_target="tpu_custom_call" | custom-call | flops 16777216 | bytes 10485760 | tf_op jit(solution)/shard_map/pallas_call | solution.py:173
  132.1 1.3 collective-permute-start.1
  133.4 1.7 collective-permute-done.1.refs_1_
  135.0 0.2 shard_map.58.energy_ref
  135.3 0.8 copy-done.4
  136.1 37.3 %all-to-all-done.1.recv_ref = f32[16,264,128]{2,1,0:T(8,128)S(1)} async-done(((f32[16,264,128]{2,1,0:T(8,128)}), f32[16,264,128]{2,1,0:T(8,128)S(1)}, u32[]{:S(2)}, u32[]{:S(2)}) %all-to-all-start.1) | async-done | bytes 2162720 | tf_op jit(solution)/shard_map/all_to_all | solution.py:318
  173.4 1.0 copy-done.5
  174.4 2.5 %shard_map.59 = f32[5,8,64,256]{3,2,1,0:T(8,128)} custom-call(f32[16,264,128]{2,1,0:T(8,128)S(1)} %all-to-all-done.1.recv_ref, f32[8,64,256]{2,1,0:T(8,128)S(1)} %copy-done.2, f32[8,64,256]{2,1,0:T(8,128)S(1)} %pad_maximum_fusion.back_ref, f32[8,64,256]{2,1,0:T(8,128)S(1)} %copy-done.5), custom_call_target="tpu_custom_call" | custom-call | flops 5242880 | bytes 4194304 | tf_op jit(solution)/shard_map/pallas_call | solution.py:228
  (30 shorter events, 0.4 us)
Async XLA Ops:
  6.5 111.7 %all-gather.3.cloned.1.call-start = ((), (), s32[]{:S(2)}) async-start(), calls=%async_computation.2 | async-start | bytes 8912896 | tf_op jit(solution)/shard_map/all_gather | solution.py:329
  11.6 6.7 %copy-start.2 = (f32[8,64,256]{2,1,0:T(8,128)S(1)}, f32[8,64,256]{2,1,0:T(8,128)}, u32[]{:S(2)}) copy-start(f32[8,64,256]{2,1,0:T(8,128)} %speed_ref.3) | copy-start | bytes 1572868
  11.6 8.4 %copy-start.3 = (f32[8,64,64]{2,1,0:T(8,128)S(1)}, f32[8,64,64]{2,1,0:T(8,128)}, u32[]{:S(2)}) copy-start(f32[8,64,64]{2,1,0:T(8,128)} %inverse_ref.1) | copy-start | bytes 393220
  11.6 8.7 %copy-start.10 = (f32[8,1]{0,1:T(1,128)S(1)}, f32[8,1]{0,1:T(1,128)}, u32[]{:S(2)}) copy-start(f32[8,1]{0,1:T(1,128)} %param.9) | copy-start | bytes 100
  11.6 86.7 %all-to-all-start = ((f32[16,128,256]{2,1,0:T(8,128)}), f32[16,128,256]{2,1,0:T(8,128)S(1)}, u32[]{:S(2)}, u32[]{:S(2)}) async-start(f32[16,128,256]{2,1,0:T(8,128)} %bitcast.21), calls=%async_computation | async-start | bytes 4194304 | tf_op jit(solution)/shard_map/all_to_all | solution.py:318
  18.3 6.9 %copy-start.11 = (s32[64]{0:T(128)S(1)}, s32[64]{0:T(128)}, u32[]{:S(2)}) copy-start(s32[64]{0:T(128)} %param.7) | copy-start | bytes 772
  18.6 74.6 %collective-permute-start = (f32[8,64]{1,0:T(8,128)S(1)}, f32[8,64]{1,0:T(8,128)S(1)}, u32[]{:S(2)}, u32[]{:S(2)}) collective-permute-start(f32[8,64]{1,0:T(8,128)S(1)} %bitcast.23), channel_id=1, source_target_pairs={{0,2},{2,4},{4,6},{6,8},{8,10},{10,12},{12,14},{14,16},{16,18},{18... | collective-permute-start | bytes 6152 | tf_op jit(solution)/shard_map/ppermute | solution.py:335
  24.5 0.7 copy-start.6
  25.2 68.8 %copy-start.8 = (f32[8,64,128]{2,1,0:T(8,128)}, f32[8,64,128]{2,1,0:T(8,128)S(1)}, u32[]{:S(2)}) copy-start(f32[8,64,128]{2,1,0:T(8,128)S(1)} %get-tuple-element.33.high_ref) | copy-start | bytes 786436
  100.6 1.3 copy-start
  118.3 55.1 %all-to-all-start.1 = ((f32[16,264,128]{2,1,0:T(8,128)}), f32[16,264,128]{2,1,0:T(8,128)S(1)}, u32[]{:S(2)}, u32[]{:S(2)}) async-start(f32[16,264,128]{2,1,0:T(8,128)} %copy-done), calls=%async_computation.1 | async-start | bytes 4325376 | tf_op jit(solution)/shard_map/all_to_all | solution.py:318
  124.5 3.4 %copy-start.1 = (f32[16,8,64,256]{3,2,1,0:T(8,128)S(1)}, f32[16,8,64,256]{3,2,1,0:T(8,128)}, u32[]{:S(2)}) copy-start(f32[16,8,64,256]{3,2,1,0:T(8,128)} %all-gather.3.cloned.1.call-done.circle_ref) | copy-start | bytes 25165828
  127.9 7.1 %copy-start.7 = (f32[8,64,128]{2,1,0:T(8,128)S(1)}, f32[8,64,128]{2,1,0:T(8,128)}, u32[]{:S(2)}) copy-start(f32[8,64,128]{2,1,0:T(8,128)} %copy-done.6) | copy-start | bytes 786436
  127.9 7.1 %copy-start.9 = (f32[8,64,128]{2,1,0:T(8,128)S(1)}, f32[8,64,128]{2,1,0:T(8,128)}, u32[]{:S(2)}) copy-start(f32[8,64,128]{2,1,0:T(8,128)} %copy-done.8) | copy-start | bytes 786436
  132.1 2.9 %collective-permute-start.1 = (f32[2,8,256]{2,1,0:T(8,128)S(1)}, f32[2,8,256]{2,1,0:T(8,128)S(1)}, u32[]{:S(2)}, u32[]{:S(2)}) collective-permute-start(f32[2,8,256]{2,1,0:T(8,128)S(1)} %get-tuple-element.34.refs_0_), channel_id=1, source_target_pairs={{0,1},{1,0},{2,3},{3,2},{4,5},{5,4},{6,7},{7,6},{8,9},{9,8},{10,11... | collective-permute-start | bytes 49160 | tf_op jit(solution)/shard_map/ppermute | solution.py:379
  135.3 0.8 copy-start.4
  173.4 1.0 copy-start.5
Sparse Core Ops, SparseCore 0:
  9.5 108.6 all-gather.2

commit v10 on v7

--- a/solution.py
+++ b/solution.py
@@ -29,8 +29,8 @@
     for block in range(n):
         out_ref[block, halo_row : halo_row + TILE_ROWS, :] = jnp.zeros((TILE_ROWS, LANES), jnp.float32)
 
-    def one_group(group, _):
-        here = pl.ds(pl.multiple_of(group * TILE_ROWS, TILE_ROWS), TILE_ROWS)
+    def one_group(group):
+        here = pl.ds(group * TILE_ROWS, TILE_ROWS)
         shift = shift_ref[here, :]
         cells = shift & (LANES - 1)
         whole = shift >> 7
@@ -49,7 +49,7 @@
             step *= 2
         for tile in range(tiles):
             block, part = divmod(tile, per_block)
-            row = pl.multiple_of((group * per_block + part) * TILE_ROWS, TILE_ROWS)
+            row = (group * per_block + part) * TILE_ROWS
             out_ref[block, pl.ds(row, TILE_ROWS), :] = circle[tile]
         place = group * 2
         edge = (lane == place) | (lane == place + 1)
@@ -59,9 +59,9 @@
             both = pltpu.roll(jnp.where(lane == 0, right, left), place + 1, 1)
             target = out_ref.at[block, halo_row : halo_row + TILE_ROWS, :]
             target[...] = jnp.where(edge, both, target[...])
-        return 0
-
-    lax.fori_loop(0, groups, one_group, 0, unroll=4 if groups % 4 == 0 else 2 if groups % 2 == 0 else 1)
+
+    for group in range(groups):
+        one_group(group)
 
 
 def turn(shift_rows, gathered):
@@ -104,19 +104,13 @@
     first = lane == 0
     last = lane == LANES - 1
     for row in range(0, radii, TILE_ROWS):
-        rates = []
-        for part in range(per_block):
-            cut = (level, slice(row, row + TILE_ROWS), slice(part * LANES, (part + 1) * LANES))
-            speed = speed_ref[cut]
-            back = back_ref[cut]
-            rates.append(
-                (
-                    jnp.maximum(speed, 0.0),
-                    jnp.minimum(speed, 0.0),
-                    jnp.maximum(back, 0.0),
-                    jnp.minimum(back, 0.0),
-                )
-            )
+        cuts = [
+            (level, slice(row, row + TILE_ROWS), slice(part * LANES, (part + 1) * LANES))
+            for part in range(per_block)
+        ]
+        rates = [(jnp.maximum(speed_ref[cut], 0.0), jnp.minimum(speed_ref[cut], 0.0)) for cut in cuts]
+        back_plus = jnp.maximum(back_ref[cuts[0]], 0.0)
+        back_minus = jnp.minimum(back_ref[cuts[0]], 0.0)
         for field in fields:
             piece, group = divmod(((field * levels + level) * radii + row) // TILE_ROWS, groups)
             halo = recv_ref[piece, halo_row : halo_row + TILE_ROWS, :]
@@ -124,18 +118,18 @@
             for part in range(per_block):
                 at = (group * per_block + part) * TILE_ROWS
                 values.append(recv_ref[piece, at : at + TILE_ROWS, :])
-            up = [pltpu.roll(halo, (LANES - 2 * group) % LANES, 1)]
-            up += [pltpu.roll(one, 1, 1) for one in values]
+            edge = pltpu.roll(halo, (LANES - 2 * group) % LANES, 1)
+            inflow = [back_plus * edge + back_minus * values[0]]
             down = [pltpu.roll(one, LANES - 1, 1) for one in values]
             down.append(pltpu.roll(halo, (LANES - 2 - 2 * group) % LANES, 1))
+            outflow = []
+            for part, (plus, minus) in enumerate(rates):
+                ahead = jnp.where(last, down[part + 1], down[part])
+                outflow.append(plus * values[part] + minus * ahead)
+                inflow.append(pltpu.roll(outflow[part], 1, 1))
             for part in range(per_block):
-                here = values[part]
-                behind = jnp.where(first, up[part], up[part + 1])
-                ahead = jnp.where(last, down[part + 1], down[part])
-                plus, minus, back_plus, back_minus = rates[part]
-                outflow = plus * here + minus * ahead
-                inflow = back_plus * behind + back_minus * here
-                store(field, row, part * LANES, here - (outflow - inflow))
+                behind = jnp.where(first, inflow[part], inflow[part + 1])
+                store(field, row, part * LANES, values[part] - (outflow[part] - behind))
 
 
 def energy_kernel(field, recv_ref, speed_ref, back_ref, inverse_ref, local_ref, ends_ref, moved):

time: 144 us -> 160 us (1.11)
  Pallas kernels: 7.2 us -> 23 us
    pallas_call x1, Pallas kernels: 2.46 us -> 18.3 us  [carry(): pl.pallas_call(carry_kernel, out_shape=jax.ShapeDtypeStruct((nf,) + speed...]
  transfers between devices with their start and end apart: 3 -> 3, of which waited for: 1 -> 1; matrix products, arithmetic and copies ran while one was open for 4% -> 4% of each run, Pallas kernels for 2% -> 12%
where the time goes in v10:
time: 160 us
  blocking collectives  81.3 us (51%)
  waiting for transfers between devices  38.7 us (24%)
  Pallas kernels  23 us (14%)
  starting transfers between devices  9.54 us (6%)
  local copies, waits for them, and re-layouts  5.01 us (3%)
  other arithmetic  2.1 us (1%)
    all_to_all x1, blocking collectives, exchange(): return lax.all_to_all(blocks, 'az', split_axis=0, concat_axis=0, tiled=True)  77 us
    ppermute x1, waiting for transfers between devices, per_device(): lax.ppermute(velocity[:, :, -1], 'az', [(i, (i + 1) % n) for i in range(n)])  38.7 us
    pallas_call x1, Pallas kernels, carry(): pl.pallas_call(carry_kernel, out_shape=jax.ShapeDtypeStruct((nf,) + speed...  18.3 us
    all_to_all x1, starting transfers between devices, exchange(): return lax.all_to_all(blocks, 'az', split_axis=0, concat_axis=0, tiled=True)  7.51 us
    all_gather x1, blocking collectives, per_device(): all_corners = lax.all_gather(corners, 'rad', axis=1, tiled=True)  4.34 us
  transfers between devices with their start and end apart: 3, of which 1 were waited for; matrix products, arithmetic and copies ran while one was open for 4% of the time, Pallas kernels for 12%

profile of v10, /device:TPU:0, one launch (start us, length us, event | category | flops | bytes accessed | tf_op | source)
XLA Modules:
  0.0 159.7 jit_solution(15560234938511989306)
XLA Ops:
  0.0 7.5 %all-to-all-start = ((f32[16,160,256]{2,1,0:T(8,128)}), f32[16,160,256]{2,1,0:T(8,128)S(1)}, u32[]{:S(2)}, u32[]{:S(2)}) async-start(f32[16,160,256]{2,1,0:T(8,128)} %bitcast.20), calls=%async_computation | async-start | bytes 5242880 | tf_op jit(solution)/shard_map/all_to_all | solution.py:288
  7.5 0.0 copy-done
  7.5 0.8 slice.30
  8.4 1.1 copy.19
  9.4 0.4 collective-permute-start
  9.9 0.0 copy-done.2
  9.9 0.2 slice_reduce_fusion
  10.1 4.3 %all-gather = f32[2,5,8]{2,1,0:T(8,128)S(1)} all-gather(f32[1,5,8]{2,1,0:T(8,128)S(1)} %bitcast.21), channel_id=1, replica_groups=mesh['az'=16,'rad'=2] {'rad'}, dimensions={0}, use_global_device_ids=true | all-gather | bytes 480 | tf_op jit(solution)/shard_map/all_gather | solution.py:316
  14.5 0.1 copy.18
  14.6 0.1 reshape.21
  14.6 0.1 slice.40
  14.7 0.1 copy.17
  14.8 0.2 slice_multiply_fusion
  15.0 0.2 shard_map.55
  15.2 0.0 copy-start.3
  15.2 0.7 copy-done.3
  15.9 0.7 copy-done.5
  16.6 0.1 tile.10
  16.7 0.1 dynamic_slice.8
  16.8 38.7 %collective-permute-done = f32[8,64]{1,0:T(8,128)S(1)} collective-permute-done((f32[8,64]{1,0:T(8,128)S(1)}, f32[8,64]{1,0:T(8,128)S(1)}, u32[]{:S(2)}, u32[]{:S(2)}) %collective-permute-start) | collective-permute-done | bytes 2080 | tf_op jit(solution)/shard_map/ppermute | solution.py:304
  55.4 0.8 copy.15
  56.3 1.9 %pad_maximum_fusion.back_ref = f32[8,64,256]{2,1,0:T(8,128)} fusion(f32[8,64,255]{2,1,0:T(8,128)S(1)} %bitcast.17, f32[8,64,1]{2,1,0:T(8,128)} %copy.15), kind=kLoop, calls=%fused_computation | loop fusion | flops 131072 | bytes 1048576 | tf_op jit(solution)/shard_map/concatenate | solution.py:305
  58.2 0.0 all-to-all-done.in_ref
  58.2 0.1 broadcast_in_dim.16.shift_ref
  58.3 2.5 %shard_map.56 = f32[16,328,128]{2,1,0:T(8,128)S(1)} custom-call(s32[160,128]{1,0:T(8,128)S(1)} %broadcast_in_dim.16.shift_ref, f32[16,160,256]{2,1,0:T(8,128)S(1)} %all-to-all-done.in_ref), custom_call_target="tpu_custom_call" | custom-call | flops 6553600 | bytes 5242880 | tf_op jit(solution)/shard_map/pallas_call | solution.py:70
  60.8 0.0 copy-start.1
  60.8 77.0 %all_to_all.10.recv_ref = f32[16,328,128]{2,1,0:T(8,128)S(1)} all-to-all(f32[16,328,128]{2,1,0:T(8,128)S(1)} %shard_map.56), channel_id=1, replica_groups=mesh['az'=16,'rad'=2] {'az'}, dimensions={0} | all-to-all | bytes 5373952 | tf_op jit(solution)/shard_map/all_to_all | solution.py:288
  137.8 0.9 shard_map.57
  138.7 1.6 collective-permute-start.1
  140.3 18.3 %shard_map.58.refs_2_ = f32[5,8,64,256]{3,2,1,0:T(8,128)} custom-call(f32[16,328,128]{2,1,0:T(8,128)S(1)} %all_to_all.10.recv_ref, f32[8,64,256]{2,1,0:T(8,128)S(1)} %copy-done, f32[8,64,256]{2,1,0:T(8,128)S(1)} %copy-done.1), custom_call_target="tpu_custom_call" | custom-call | flops 6553600 | bytes 5242880 | tf_op jit(solution)/shard_map/pallas_call | solution.py:188
  158.7 0.0 collective-permute-done.1.refs_1_
  158.7 1.1 shard_map.59
  (17 shorter events, 0.1 us)
Async XLA Ops:
  0.0 7.5 %copy-start = (f32[8,64,256]{2,1,0:T(8,128)S(1)}, f32[8,64,256]{2,1,0:T(8,128)}, u32[]{:S(2)}) copy-start(f32[8,64,256]{2,1,0:T(8,128)} %speed_ref.3) | copy-start | bytes 1572868
  0.0 9.9 %copy-start.2 = (f32[8,64,64]{2,1,0:T(8,128)S(1)}, f32[8,64,64]{2,1,0:T(8,128)}, u32[]{:S(2)}) copy-start(f32[8,64,64]{2,1,0:T(8,128)} %inverse_ref.1) | copy-start | bytes 393220
  0.0 10.1 %copy-start.7 = (f32[8,1]{0,1:T(1,128)S(1)}, f32[8,1]{0,1:T(1,128)}, u32[]{:S(2)}) copy-start(f32[8,1]{0,1:T(1,128)} %param.9) | copy-start | bytes 100
  0.0 16.6 %copy-start.8 = (s32[64]{0:T(128)S(1)}, s32[64]{0:T(128)}, u32[]{:S(2)}) copy-start(s32[64]{0:T(128)} %param.7) | copy-start | bytes 772
  0.0 58.2 %all-to-all-start = ((f32[16,160,256]{2,1,0:T(8,128)}), f32[16,160,256]{2,1,0:T(8,128)S(1)}, u32[]{:S(2)}, u32[]{:S(2)}) async-start(f32[16,160,256]{2,1,0:T(8,128)} %bitcast.20), calls=%async_computation | async-start | bytes 5242880 | tf_op jit(solution)/shard_map/all_to_all | solution.py:288
  9.4 46.0 %collective-permute-start = (f32[8,64]{1,0:T(8,128)S(1)}, f32[8,64]{1,0:T(8,128)S(1)}, u32[]{:S(2)}, u32[]{:S(2)}) collective-permute-start(f32[8,64]{1,0:T(8,128)S(1)} %bitcast.22), channel_id=1, source_target_pairs={{0,2},{2,4},{4,6},{6,8},{8,10},{10,12},{12,14},{14,16},{16,18},{18... | collective-permute-start | bytes 6152 | tf_op jit(solution)/shard_map/ppermute | solution.py:304
  15.2 0.7 copy-start.3
  15.9 0.7 copy-start.5
  60.8 77.0 %copy-start.1 = (f32[8,64,256]{2,1,0:T(8,128)S(1)}, f32[8,64,256]{2,1,0:T(8,128)}, u32[]{:S(2)}) copy-start(f32[8,64,256]{2,1,0:T(8,128)} %pad_maximum_fusion.back_ref) | copy-start | bytes 1572868
  138.7 20.0 %copy-start.4 = (f32[8,64,128]{2,1,0:T(8,128)S(1)}, f32[8,64,128]{2,1,0:T(8,128)}, u32[]{:S(2)}) copy-start(f32[8,64,128]{2,1,0:T(8,128)} %copy-done.3) | copy-start | bytes 786436
  138.7 20.0 %copy-start.6 = (f32[8,64,128]{2,1,0:T(8,128)S(1)}, f32[8,64,128]{2,1,0:T(8,128)}, u32[]{:S(2)}) copy-start(f32[8,64,128]{2,1,0:T(8,128)} %copy-done.5) | copy-start | bytes 786436
  138.7 19.9 %collective-permute-start.1 = (f32[2,8,256]{2,1,0:T(8,128)S(1)}, f32[2,8,256]{2,1,0:T(8,128)S(1)}, u32[]{:S(2)}, u32[]{:S(2)}) collective-permute-start(f32[2,8,256]{2,1,0:T(8,128)S(1)} %get-tuple-element.26.refs_0_), channel_id=1, source_target_pairs={{0,1},{1,0},{2,3},{3,2},{4,5},{5,4},{6,7},{7,6},{8,9},{9,8},{10,11... | collective-permute-start | bytes 49160 | tf_op jit(solution)/shard_map/ppermute | solution.py:332

commit v11 on v7

--- a/solution.py
+++ b/solution.py
@@ -19,8 +19,13 @@
     return pl.CostEstimate(flops=flops, bytes_accessed=4 * moved, transcendentals=0)
 
 
+def place_of(device, n):
+    return (device + n - n // 4) % n
+
+
 def turn_kernel(shift_ref, in_ref, out_ref):
     n, rows, width = in_ref.shape
+    places = [place_of(block, n) for block in range(n)]
     per_block = width // LANES
     tiles = n * per_block
     groups = rows // TILE_ROWS
@@ -29,8 +34,8 @@
     for block in range(n):
         out_ref[block, halo_row : halo_row + TILE_ROWS, :] = jnp.zeros((TILE_ROWS, LANES), jnp.float32)
 
-    def one_group(group, _):
-        here = pl.ds(pl.multiple_of(group * TILE_ROWS, TILE_ROWS), TILE_ROWS)
+    def one_group(group):
+        here = pl.ds(group * TILE_ROWS, TILE_ROWS)
         shift = shift_ref[here, :]
         cells = shift & (LANES - 1)
         whole = shift >> 7
@@ -39,7 +44,7 @@
         turned = []
         for tile in range(tiles):
             block, part = divmod(tile, per_block)
-            values = in_ref[block, here, part * LANES : (part + 1) * LANES]
+            values = in_ref[places[block], here, part * LANES : (part + 1) * LANES]
             turned.append(jnp.take_along_axis(values, source, axis=1, mode="promise_in_bounds"))
         circle = [jnp.where(own, turned[tile], turned[tile - 1]) for tile in range(tiles)]
         step = 1
@@ -49,19 +54,19 @@
             step *= 2
         for tile in range(tiles):
             block, part = divmod(tile, per_block)
-            row = pl.multiple_of((group * per_block + part) * TILE_ROWS, TILE_ROWS)
-            out_ref[block, pl.ds(row, TILE_ROWS), :] = circle[tile]
+            row = (group * per_block + part) * TILE_ROWS
+            out_ref[places[block], pl.ds(row, TILE_ROWS), :] = circle[tile]
         place = group * 2
         edge = (lane == place) | (lane == place + 1)
         for block in range(n):
             left = circle[(block * per_block - 1) % tiles]
             right = circle[((block + 1) * per_block) % tiles]
             both = pltpu.roll(jnp.where(lane == 0, right, left), place + 1, 1)
-            target = out_ref.at[block, halo_row : halo_row + TILE_ROWS, :]
+            target = out_ref.at[places[block], halo_row : halo_row + TILE_ROWS, :]
             target[...] = jnp.where(edge, both, target[...])
-        return 0
-
-    lax.fori_loop(0, groups, one_group, 0, unroll=4 if groups % 4 == 0 else 2 if groups % 2 == 0 else 1)
+
+    for group in range(groups):
+        one_group(group)
 
 
 def turn(shift_rows, gathered):
@@ -94,7 +99,7 @@
     )(low, high)
 
 
-def carry_level(fields, level, recv_ref, speed_ref, back_ref, store):
+def carry_level(fields, level, recv_ref, speed_ref, back_ref, known, store):
     levels, radii, width = speed_ref.shape
     per_block = width // LANES
     in_rows = recv_ref.shape[1]
@@ -103,6 +108,13 @@
     lane = lax.broadcasted_iota(jnp.int32, (TILE_ROWS, LANES), 1)
     first = lane == 0
     last = lane == LANES - 1
+
+    def edges(piece, group):
+        key = (piece, group)
+        if key not in known:
+            known[key] = pltpu.roll(recv_ref[piece, halo_row:in_rows, :], (LANES - 2 * group) % LANES, 1)
+        return known[key]
+
     for row in range(0, radii, TILE_ROWS):
         rates = []
         for part in range(per_block):
@@ -119,15 +131,14 @@
             )
         for field in fields:
             piece, group = divmod(((field * levels + level) * radii + row) // TILE_ROWS, groups)
-            halo = recv_ref[piece, halo_row : halo_row + TILE_ROWS, :]
             values = []
             for part in range(per_block):
                 at = (group * per_block + part) * TILE_ROWS
                 values.append(recv_ref[piece, at : at + TILE_ROWS, :])
-            up = [pltpu.roll(halo, (LANES - 2 * group) % LANES, 1)]
+            up = [edges(piece, group)]
             up += [pltpu.roll(one, 1, 1) for one in values]
             down = [pltpu.roll(one, LANES - 1, 1) for one in values]
-            down.append(pltpu.roll(halo, (LANES - 2 - 2 * group) % LANES, 1))
+            down.append(edges(piece, group + 1))
             for part in range(per_block):
                 here = values[part]
                 behind = jnp.where(first, up[part], up[part + 1])
@@ -139,12 +150,13 @@
 
 
 def energy_kernel(field, recv_ref, speed_ref, back_ref, inverse_ref, local_ref, ends_ref, moved):
+    known = {}
     for level in range(speed_ref.shape[0]):
 
         def store(_, row, cell, values, level=level):
             moved[level, row : row + TILE_ROWS, cell : cell + LANES] = values
 
-        carry_level([field], level, recv_ref, speed_ref, back_ref, store)
+        carry_level([field], level, recv_ref, speed_ref, back_ref, known, store)
         local = jnp.dot(
             inverse_ref[level],
             moved[level],
@@ -175,12 +187,13 @@
 def carry_kernel(recv_ref, speed_ref, back_ref, out_ref, held, sems):
     nf, levels = held.shape[:2]
     copies = []
+    known = {}
     for level in range(levels):
 
         def store(field, row, cell, values, level=level):
             held[field, level, row : row + TILE_ROWS, cell : cell + LANES] = values
 
-        carry_level(range(nf), level, recv_ref, speed_ref, back_ref, store)
+        carry_level(range(nf), level, recv_ref, speed_ref, back_ref, known, store)
         copies.append(
             pltpu.make_async_copy(held.at[:, level], out_ref.at[pl.ds(0, nf), level], sems.at[level])
         )
@@ -189,7 +202,7 @@
         copy.wait()
 
 
-def carry(nf, received, speed, back_speed):
+def carry(nf, count, received, speed, back_speed):
     levels, radii, width = speed.shape
     return pl.pallas_call(
         carry_kernel,
@@ -197,11 +210,11 @@
         in_specs=[IN_VMEM] * 3,
         out_specs=IN_HBM,
         scratch_shapes=[
-            pltpu.VMEM((nf - 1,) + speed.shape, jnp.float32),
+            pltpu.VMEM((count,) + speed.shape, jnp.float32),
             pltpu.SemaphoreType.DMA((levels,)),
         ],
         compiler_params=ROOMY,
-        cost_estimate=cost(10 * nf * speed.size, 2 * nf * speed.size),
+        cost_estimate=cost(10 * count * speed.size, 2 * count * speed.size),
     )(received, speed, back_speed)
 
 
@@ -241,8 +254,10 @@
     return [nothing] + lower_values, upper_values + [nothing]
 
 
-def diffuse_kernel(band_ref, corner_ref, local_ref, low_ref, high_ref, *refs):
+def finish_kernel(band_ref, corner_ref, local_ref, low_ref, high_ref, recv_ref, speed_ref, back_ref, *refs):
     end_refs, (_, out_ref, held, sems) = refs[:-4], refs[-4:]
+    nf = out_ref.shape[0]
+    begin = nf - held.shape[0]
     levels, _, width = local_ref.shape
     bands = corner_ref.shape[1] // 5
     band = band_ref[0]
@@ -260,38 +275,51 @@
         before = jnp.where(band == j, all_before[j], before)
         beyond = jnp.where(band == j, all_beyond[j], beyond)
     copies = []
+    known = {}
     for level in range(levels):
+
+        def store(field, row, cell, values, level=level):
+            held[field - begin, level, row : row + TILE_ROWS, cell : cell + LANES] = values
+
         for cell in range(0, width, LANES):
             cut = slice(cell, cell + LANES)
-            held[level, :, cut] = (
+            held[nf - 1 - begin, level, :, cut] = (
                 local_ref[level, :, cut]
                 + low_ref[level] * before[level : level + 1, cut]
                 + high_ref[level] * beyond[level : level + 1, cut]
             )
+        carry_level(range(begin, nf - 1), level, recv_ref, speed_ref, back_ref, known, store)
         copies.append(
-            pltpu.make_async_copy(held.at[level], out_ref.at[out_ref.shape[0] - 1, level], sems.at[level])
+            pltpu.make_async_copy(
+                held.at[:, level], out_ref.at[pl.ds(begin, nf - begin), level], sems.at[level]
+            )
         )
         copies[-1].start()
     for copy in copies:
         copy.wait()
 
 
-def diffuse(band, corners, local_part, low, high, ends, result):
+def finish(count, band, corners, local_part, low, high, received, speed, back_speed, ends, result):
     levels = local_part.shape[0]
     return pl.pallas_call(
-        diffuse_kernel,
+        finish_kernel,
         out_shape=jax.ShapeDtypeStruct(result.shape, jnp.float32),
-        in_specs=[IN_SMEM] + [IN_VMEM] * (4 + len(ends)) + [IN_HBM],
+        in_specs=[IN_SMEM] + [IN_VMEM] * (7 + len(ends)) + [IN_HBM],
         out_specs=IN_HBM,
-        scratch_shapes=[pltpu.VMEM(local_part.shape, jnp.float32), pltpu.SemaphoreType.DMA((levels,))],
-        input_output_aliases={5 + len(ends): 0},
+        scratch_shapes=[
+            pltpu.VMEM((count,) + local_part.shape, jnp.float32),
+            pltpu.SemaphoreType.DMA((levels,)),
+        ],
+        input_output_aliases={8 + len(ends): 0},
         compiler_params=ROOMY,
-        cost_estimate=cost(4 * local_part.size, 2 * local_part.size),
-    )(band, corners, local_part, low, high, *ends, result)
+        cost_estimate=cost(10 * count * local_part.size, 2 * count * local_part.size),
+    )(band, corners, local_part, low, high, received, speed, back_speed, *ends, result)
 
 
 def exchange(blocks):
-    return lax.all_to_all(blocks, "az", split_axis=0, concat_axis=0, tiled=True)
+    n = blocks.shape[0]
+    order = sorted(range(n), key=lambda device: place_of(device, n))
+    return lax.all_to_all(blocks, "az", split_axis=0, concat_axis=0, tiled=True, axis_index_groups=[order])
 
 
 def per_device(fields, velocity, shifts, block_inverse, coupling):
@@ -305,7 +333,7 @@
     gathered = exchange(fields.reshape(n, rows, width))
 
     all_shifts = jnp.tile(shifts, rows // radii + 2)
-    own_shifts = lax.dynamic_slice_in_dim(all_shifts, (me * rows) % radii, rows)
+    own_shifts = lax.dynamic_slice_in_dim(all_shifts, (place_of(me, n) * rows) % radii, rows)
     shift_rows = jnp.broadcast_to(own_shifts[:, None], (rows, LANES))
     edge_speed = lax.ppermute(velocity[:, :, -1], "az", [(i, (i + 1) % n) for i in range(n)])
     back_speed = jnp.concatenate([edge_speed[:, :, None], velocity[:, :, :-1]], axis=2)
@@ -338,8 +366,21 @@
         all_ends = [ends, lax.ppermute(ends, "rad", [(0, 1), (1, 0)])]
     else:
         all_ends = [lax.all_gather(ends, "rad", axis=0)]
-    result = carry(nf, received, velocity, back_speed)
-    return diffuse(band_scalar, all_corners, local_part, low, high, all_ends, result)
+    first = nf // 2
+    result = carry(nf, first, received, velocity, back_speed)
+    return finish(
+        nf - first,
+        band_scalar,
+        all_corners,
+        local_part,
+        low,
+        high,
+        received,
+        velocity,
+        back_speed,
+        all_ends,
+        result,
+    )
 
 
 def solution(mesh):

time: 144 us -> 142 us (0.986)
  transfers between devices with their start and end apart: 3 -> 3, of which waited for: 1 -> 2; matrix products, arithmetic and copies ran while one was open for 4% -> 4% of each run, Pallas kernels for 2% -> 1%
where the time goes in v11:
time: 142 us
  blocking collectives  80.4 us (57%)
  waiting for transfers between devices  38.3 us (27%)
  starting transfers between devices  9.75 us (7%)
  Pallas kernels  6.5 us (5%)
  local copies, waits for them, and re-layouts  5.01 us (4%)
  other arithmetic  2.1 us (1%)
    all_to_all x1, blocking collectives, exchange(): lax.all_to_all(blocks, 'az', split_axis=0, concat_axis=0, tiled=True, axi...  76.1 us
    ppermute x1, waiting for transfers between devices, per_device(): lax.ppermute(velocity[:, :, -1], 'az', [(i, (i + 1) % n) for i in range(n)])  37.6 us
    all_to_all x1, starting transfers between devices, exchange(): lax.all_to_all(blocks, 'az', split_axis=0, concat_axis=0, tiled=True, axi...  7.99 us
    all_gather x1, blocking collectives, per_device(): all_corners = lax.all_gather(corners, 'rad', axis=1, tiled=True)  4.34 us
  transfers between devices with their start and end apart: 3, of which 2 were waited for; matrix products, arithmetic and copies ran while one was open for 4% of the time, Pallas kernels for 1%

profile of v11, /device:TPU:0, one launch (start us, length us, event | category | flops | bytes accessed | tf_op | source)
XLA Modules:
  0.0 142.2 jit_solution(9690886084122084349)
XLA Ops:
  0.0 8.0 %all-to-all-start = ((f32[16,160,256]{2,1,0:T(8,128)}), f32[16,160,256]{2,1,0:T(8,128)S(1)}, u32[]{:S(2)}, u32[]{:S(2)}) async-start(f32[16,160,256]{2,1,0:T(8,128)} %bitcast.20), calls=%async_computation | async-start | bytes 5242880 | tf_op jit(solution)/shard_map/all_to_all | solution.py:322
  8.0 0.0 copy-done
  8.0 0.8 slice.30
  8.8 1.1 copy.19
  9.9 0.2 collective-permute-start
  10.1 0.0 copy-done.2
  10.1 0.2 slice_reduce_fusion
  10.4 4.3 %all-gather = f32[2,5,8]{2,1,0:T(8,128)S(1)} all-gather(f32[1,5,8]{2,1,0:T(8,128)S(1)} %bitcast.21), channel_id=1, replica_groups=mesh['az'=16,'rad'=2] {'rad'}, dimensions={0}, use_global_device_ids=true | all-gather | bytes 480 | tf_op jit(solution)/shard_map/all_gather | solution.py:350
  14.7 0.1 copy.18
  14.8 0.1 reshape.21
  14.9 0.1 slice.40
  14.9 0.1 copy.17
  15.1 0.2 slice_multiply_fusion
  15.2 0.2 shard_map.55
  15.4 0.7 copy-done.3
  16.1 0.7 copy-done.5
  16.8 0.0 copy-done.8
  16.8 0.1 tile.10
  16.9 0.1 dynamic_slice.8
  17.0 37.6 %collective-permute-done = f32[8,64]{1,0:T(8,128)S(1)} collective-permute-done((f32[8,64]{1,0:T(8,128)S(1)}, f32[8,64]{1,0:T(8,128)S(1)}, u32[]{:S(2)}, u32[]{:S(2)}) %collective-permute-start) | collective-permute-done | bytes 2080 | tf_op jit(solution)/shard_map/ppermute | solution.py:338
  54.5 0.8 copy.15
  55.4 1.9 %pad_maximum_fusion.back_ref = f32[8,64,256]{2,1,0:T(8,128)} fusion(f32[8,64,255]{2,1,0:T(8,128)S(1)} %bitcast.17, f32[8,64,1]{2,1,0:T(8,128)} %copy.15), kind=kLoop, calls=%fused_computation | loop fusion | flops 131072 | bytes 1048576 | tf_op jit(solution)/shard_map/concatenate | solution.py:339
  57.3 0.0 all-to-all-done.in_ref
  57.3 0.1 broadcast_in_dim.16.shift_ref
  57.4 2.5 %shard_map.56 = f32[16,328,128]{2,1,0:T(8,128)S(1)} custom-call(s32[160,128]{1,0:T(8,128)S(1)} %broadcast_in_dim.16.shift_ref, f32[16,160,256]{2,1,0:T(8,128)S(1)} %all-to-all-done.in_ref), custom_call_target="tpu_custom_call" | custom-call | flops 6553600 | bytes 5242880 | tf_op jit(solution)/shard_map/pallas_call | solution.py:75
  59.9 0.0 copy-start.1
  59.9 76.1 %all_to_all.10.recv_ref = f32[16,328,128]{2,1,0:T(8,128)S(1)} all-to-all(f32[16,328,128]{2,1,0:T(8,128)S(1)} %shard_map.56), channel_id=1, replica_groups={{8,10,12,14,16,18,20,22,24,26,28,30,0,2,4,6},{9,11,13,15,17,19,21,23,25..., dimensions={0} | all-to-all | bytes 5373952 | tf_op jit(solution)/shard_map/all_to_all | solution.py:322
  136.0 0.8 shard_map.57
  136.8 1.6 %collective-permute-start.1 = (f32[2,8,256]{2,1,0:T(8,128)S(1)}, f32[2,8,256]{2,1,0:T(8,128)S(1)}, u32[]{:S(2)}, u32[]{:S(2)}) collective-permute-start(f32[2,8,256]{2,1,0:T(8,128)S(1)} %get-tuple-element.26.refs_0_), channel_id=1, source_target_pairs={{0,1},{1,0},{2,3},{3,2},{4,5},{5,4},{6,7},{7,6},{8,9},{9,8},{10,11... | collective-permute-start | bytes 49160 | tf_op jit(solution)/shard_map/ppermute | solution.py:366
  138.4 1.5 %shard_map.58.refs_2_ = f32[5,8,64,256]{3,2,1,0:T(8,128)} custom-call(f32[16,328,128]{2,1,0:T(8,128)S(1)} %all_to_all.10.recv_ref, f32[8,64,256]{2,1,0:T(8,128)S(1)} %copy-done, f32[8,64,256]{2,1,0:T(8,128)S(1)} %copy-done.1), custom_call_target="tpu_custom_call" | custom-call | flops 2621440 | bytes 2097152 | tf_op jit(solution)/shard_map/pallas_call | solution.py:207
  139.9 0.7 collective-permute-done.1.refs_1_
  140.6 1.6 %shard_map.59 = f32[5,8,64,256]{3,2,1,0:T(8,128)} custom-call(s32[1]{0:T(128)} %bitcast.9.band_ref, f32[8,10]{1,0:T(8,128)S(1)} %bitcast.19, f32[8,64,256]{2,1,0:T(8,128)S(1)} %get-tuple-element.23.local_ref, f32[8,64,128]{2,1,0:T(8,128)S(1)} %copy-done.4, f32[8,64,128]{2,1,0:T(8,128)S(1)} %copy-done.6, ...), custom_call_target="tpu_custom_call", output_to_operand_aliasing={{}: (10, {})} | custom-call | flops 3932160 | bytes 3145728 | tf_op jit(solution)/shard_map/pallas_call | solution.py:304
  (17 shorter events, 0.1 us)
Async XLA Ops:
  0.0 8.0 %copy-start = (f32[8,64,256]{2,1,0:T(8,128)S(1)}, f32[8,64,256]{2,1,0:T(8,128)}, u32[]{:S(2)}) copy-start(f32[8,64,256]{2,1,0:T(8,128)} %speed_ref.5) | copy-start | bytes 1572868
  0.0 10.1 %copy-start.2 = (f32[8,64,64]{2,1,0:T(8,128)S(1)}, f32[8,64,64]{2,1,0:T(8,128)}, u32[]{:S(2)}) copy-start(f32[8,64,64]{2,1,0:T(8,128)} %inverse_ref.1) | copy-start | bytes 393220
  0.0 10.3 %copy-start.7 = (f32[8,1]{0,1:T(1,128)S(1)}, f32[8,1]{0,1:T(1,128)}, u32[]{:S(2)}) copy-start(f32[8,1]{0,1:T(1,128)} %param.9) | copy-start | bytes 100
  0.0 16.8 %copy-start.8 = (s32[64]{0:T(128)S(1)}, s32[64]{0:T(128)}, u32[]{:S(2)}) copy-start(s32[64]{0:T(128)} %param.7) | copy-start | bytes 772
  0.0 57.3 %all-to-all-start = ((f32[16,160,256]{2,1,0:T(8,128)}), f32[16,160,256]{2,1,0:T(8,128)S(1)}, u32[]{:S(2)}, u32[]{:S(2)}) async-start(f32[16,160,256]{2,1,0:T(8,128)} %bitcast.20), calls=%async_computation | async-start | bytes 5242880 | tf_op jit(solution)/shard_map/all_to_all | solution.py:322
  9.9 44.6 %collective-permute-start = (f32[8,64]{1,0:T(8,128)S(1)}, f32[8,64]{1,0:T(8,128)S(1)}, u32[]{:S(2)}, u32[]{:S(2)}) collective-permute-start(f32[8,64]{1,0:T(8,128)S(1)} %bitcast.22), channel_id=1, source_target_pairs={{0,2},{2,4},{4,6},{6,8},{8,10},{10,12},{12,14},{14,16},{16,18},{18... | collective-permute-start | bytes 6152 | tf_op jit(solution)/shard_map/ppermute | solution.py:338
  15.4 0.7 copy-start.3
  16.1 0.7 copy-start.5
  59.9 76.1 %copy-start.1 = (f32[8,64,256]{2,1,0:T(8,128)S(1)}, f32[8,64,256]{2,1,0:T(8,128)}, u32[]{:S(2)}) copy-start(f32[8,64,256]{2,1,0:T(8,128)} %pad_maximum_fusion.back_ref) | copy-start | bytes 1572868
  136.8 3.8 %copy-start.4 = (f32[8,64,128]{2,1,0:T(8,128)S(1)}, f32[8,64,128]{2,1,0:T(8,128)}, u32[]{:S(2)}) copy-start(f32[8,64,128]{2,1,0:T(8,128)} %copy-done.3) | copy-start | bytes 786436
  136.8 3.8 %copy-start.6 = (f32[8,64,128]{2,1,0:T(8,128)S(1)}, f32[8,64,128]{2,1,0:T(8,128)}, u32[]{:S(2)}) copy-start(f32[8,64,128]{2,1,0:T(8,128)} %copy-done.5) | copy-start | bytes 786436
  136.8 3.8 %collective-permute-start.1 = (f32[2,8,256]{2,1,0:T(8,128)S(1)}, f32[2,8,256]{2,1,0:T(8,128)S(1)}, u32[]{:S(2)}, u32[]{:S(2)}) collective-permute-start(f32[2,8,256]{2,1,0:T(8,128)S(1)} %get-tuple-element.26.refs_0_), channel_id=1, source_target_pairs={{0,1},{1,0},{2,3},{3,2},{4,5},{5,4},{6,7},{7,6},{8,9},{9,8},{10,11... | collective-permute-start | bytes 49160 | tf_op jit(solution)/shard_map/ppermute | solution.py:366

commit v12 on v11

--- a/solution.py
+++ b/solution.py
@@ -149,23 +149,23 @@
                 store(field, row, part * LANES, here - (outflow - inflow))
 
 
-def energy_kernel(field, recv_ref, speed_ref, back_ref, inverse_ref, local_ref, ends_ref, moved):
+def energy_kernel(field, recv_ref, speed_ref, back_ref, inverse_ref, moved_ref, ends_ref):
+    levels, radii, _ = speed_ref.shape
     known = {}
-    for level in range(speed_ref.shape[0]):
+    for level in range(levels):
 
         def store(_, row, cell, values, level=level):
-            moved[level, row : row + TILE_ROWS, cell : cell + LANES] = values
+            moved_ref[level, row : row + TILE_ROWS, cell : cell + LANES] = values
 
         carry_level([field], level, recv_ref, speed_ref, back_ref, known, store)
-        local = jnp.dot(
-            inverse_ref[level],
-            moved[level],
-            precision=lax.Precision.HIGHEST,
-            preferred_element_type=jnp.float32,
-        )
-        local_ref[level] = local
-        ends_ref[0, level : level + 1, :] = local[:1]
-        ends_ref[1, level : level + 1, :] = local[-1:]
+        outer = jnp.concatenate([inverse_ref[level, :TILE_ROWS], inverse_ref[level, radii - TILE_ROWS :]])
+        ends = exact_product(outer, moved_ref[level])
+        ends_ref[0, level : level + 1, :] = ends[:1]
+        ends_ref[1, level : level + 1, :] = ends[-1:]
+
+
+def exact_product(left, right):
+    return jnp.dot(left, right, precision=lax.Precision.HIGHEST, preferred_element_type=jnp.float32)
 
 
 def energy_part(field, received, speed, back_speed, inverse):
@@ -178,10 +178,25 @@
         ],
         in_specs=[IN_VMEM] * 4,
         out_specs=[IN_VMEM] * 2,
-        scratch_shapes=[pltpu.VMEM(speed.shape, jnp.float32)],
-        compiler_params=ROOMY,
-        cost_estimate=cost(2 * speed.size * radii, 4 * speed.size),
+        compiler_params=ROOMY,
+        cost_estimate=cost(60 * speed.size, 4 * speed.size),
     )(received, speed, back_speed, inverse)
+
+
+def product_kernel(inverse_ref, moved_ref, local_ref):
+    for level in range(moved_ref.shape[0]):
+        local_ref[level] = exact_product(inverse_ref[level], moved_ref[level])
+
+
+def product(inverse, moved):
+    return pl.pallas_call(
+        product_kernel,
+        out_shape=jax.ShapeDtypeStruct(moved.shape, jnp.float32),
+        in_specs=[IN_VMEM] * 2,
+        out_specs=IN_VMEM,
+        compiler_params=ROOMY,
+        cost_estimate=cost(2 * moved.size * moved.shape[1], 2 * moved.size),
+    )(inverse, moved)
 
 
 def carry_kernel(recv_ref, speed_ref, back_ref, out_ref, held, sems):
@@ -254,10 +269,8 @@
     return [nothing] + lower_values, upper_values + [nothing]
 
 
-def finish_kernel(band_ref, corner_ref, local_ref, low_ref, high_ref, recv_ref, speed_ref, back_ref, *refs):
+def finish_kernel(band_ref, corner_ref, local_ref, low_ref, high_ref, *refs):
     end_refs, (_, out_ref, held, sems) = refs[:-4], refs[-4:]
-    nf = out_ref.shape[0]
-    begin = nf - held.shape[0]
     levels, _, width = local_ref.shape
     bands = corner_ref.shape[1] // 5
     band = band_ref[0]
@@ -275,45 +288,34 @@
         before = jnp.where(band == j, all_before[j], before)
         beyond = jnp.where(band == j, all_beyond[j], beyond)
     copies = []
-    known = {}
     for level in range(levels):
-
-        def store(field, row, cell, values, level=level):
-            held[field - begin, level, row : row + TILE_ROWS, cell : cell + LANES] = values
-
         for cell in range(0, width, LANES):
             cut = slice(cell, cell + LANES)
-            held[nf - 1 - begin, level, :, cut] = (
+            held[level, :, cut] = (
                 local_ref[level, :, cut]
                 + low_ref[level] * before[level : level + 1, cut]
                 + high_ref[level] * beyond[level : level + 1, cut]
             )
-        carry_level(range(begin, nf - 1), level, recv_ref, speed_ref, back_ref, known, store)
         copies.append(
-            pltpu.make_async_copy(
-                held.at[:, level], out_ref.at[pl.ds(begin, nf - begin), level], sems.at[level]
-            )
+            pltpu.make_async_copy(held.at[level], out_ref.at[out_ref.shape[0] - 1, level], sems.at[level])
         )
         copies[-1].start()
     for copy in copies:
         copy.wait()
 
 
-def finish(count, band, corners, local_part, low, high, received, speed, back_speed, ends, result):
+def finish(band, corners, local_part, low, high, ends, result):
     levels = local_part.shape[0]
     return pl.pallas_call(
         finish_kernel,
         out_shape=jax.ShapeDtypeStruct(result.shape, jnp.float32),
-        in_specs=[IN_SMEM] + [IN_VMEM] * (7 + len(ends)) + [IN_HBM],
+        in_specs=[IN_SMEM] + [IN_VMEM] * (4 + len(ends)) + [IN_HBM],
         out_specs=IN_HBM,
-        scratch_shapes=[
-            pltpu.VMEM((count,) + local_part.shape, jnp.float32),
-            pltpu.SemaphoreType.DMA((levels,)),
-        ],
-        input_output_aliases={8 + len(ends): 0},
-        compiler_params=ROOMY,
-        cost_estimate=cost(10 * count * local_part.size, 2 * count * local_part.size),
-    )(band, corners, local_part, low, high, received, speed, back_speed, *ends, result)
+        scratch_shapes=[pltpu.VMEM(local_part.shape, jnp.float32), pltpu.SemaphoreType.DMA((levels,))],
+        input_output_aliases={5 + len(ends): 0},
+        compiler_params=ROOMY,
+        cost_estimate=cost(4 * local_part.size, 2 * local_part.size),
+    )(band, corners, local_part, low, high, *ends, result)
 
 
 def exchange(blocks):
@@ -361,26 +363,14 @@
 
     received = exchange(turn(shift_rows, gathered))
 
-    local_part, ends = energy_part(nf - 1, received, velocity, back_speed, block_inverse)
+    moved, ends = energy_part(nf - 1, received, velocity, back_speed, block_inverse)
     if bands == 2:
         all_ends = [ends, lax.ppermute(ends, "rad", [(0, 1), (1, 0)])]
     else:
         all_ends = [lax.all_gather(ends, "rad", axis=0)]
-    first = nf // 2
-    result = carry(nf, first, received, velocity, back_speed)
-    return finish(
-        nf - first,
-        band_scalar,
-        all_corners,
-        local_part,
-        low,
-        high,
-        received,
-        velocity,
-        back_speed,
-        all_ends,
-        result,
-    )
+    local_part = product(block_inverse, moved)
+    result = carry(nf, nf - 1, received, velocity, back_speed)
+    return finish(band_scalar, all_corners, local_part, low, high, all_ends, result)
 
 
 def solution(mesh):

time: 142 us -> 142 us (level)
  transfers between devices with their start and end apart: 3 -> 3, of which waited for: 2 -> 1; matrix products, arithmetic and copies ran while one was open for 4% -> 4% of each run, Pallas kernels for 1% -> 2%
where the time goes in v12:
time: 142 us
  blocking collectives  80.4 us (57%)
  waiting for transfers between devices  37.6 us (26%)
  starting transfers between devices  9.75 us (7%)
  Pallas kernels  7.14 us (5%)
  local copies, waits for them, and re-layouts  5.01 us (4%)
  other arithmetic  2.1 us (1%)
    all_to_all x1, blocking collectives, exchange(): lax.all_to_all(blocks, 'az', split_axis=0, concat_axis=0, tiled=True, axi...  76.1 us
    ppermute x1, waiting for transfers between devices, per_device(): lax.ppermute(velocity[:, :, -1], 'az', [(i, (i + 1) % n) for i in range(n)])  37.6 us
    all_to_all x1, starting transfers between devices, exchange(): lax.all_to_all(blocks, 'az', split_axis=0, concat_axis=0, tiled=True, axi...  7.99 us
    all_gather x1, blocking collectives, per_device(): all_corners = lax.all_gather(corners, 'rad', axis=1, tiled=True)  4.34 us
  transfers between devices with their start and end apart: 3, of which 1 were waited for; matrix products, arithmetic and copies ran while one was open for 4% of the time, Pallas kernels for 2%

profile of v12, /device:TPU:0, one launch (start us, length us, event | category | flops | bytes accessed | tf_op | source)
XLA Modules:
  0.0 142.1 jit_solution(9970675800842965721)
XLA Ops:
  0.0 8.0 %all-to-all-start = ((f32[16,160,256]{2,1,0:T(8,128)}), f32[16,160,256]{2,1,0:T(8,128)S(1)}, u32[]{:S(2)}, u32[]{:S(2)}) async-start(f32[16,160,256]{2,1,0:T(8,128)} %bitcast.20), calls=%async_computation | async-start | bytes 5242880 | tf_op jit(solution)/shard_map/all_to_all | solution.py:324
  8.0 0.0 copy-done
  8.0 0.8 slice.30
  8.8 1.1 copy.19
  9.9 0.2 collective-permute-start
  10.1 0.0 copy-done.2
  10.1 0.2 slice_reduce_fusion
  10.4 4.3 %all-gather = f32[2,5,8]{2,1,0:T(8,128)S(1)} all-gather(f32[1,5,8]{2,1,0:T(8,128)S(1)} %bitcast.21), channel_id=1, replica_groups=mesh['az'=16,'rad'=2] {'rad'}, dimensions={0}, use_global_device_ids=true | all-gather | bytes 480 | tf_op jit(solution)/shard_map/all_gather | solution.py:352
  14.7 0.1 copy.18
  14.8 0.1 reshape.21
  14.9 0.1 slice.40
  14.9 0.1 copy.17
  15.1 0.2 slice_multiply_fusion
  15.2 0.2 shard_map.55
  15.4 0.7 copy-done.3
  16.1 0.7 copy-done.5
  16.8 0.1 tile.10
  16.9 0.1 dynamic_slice.8
  17.0 37.6 %collective-permute-done = f32[8,64]{1,0:T(8,128)S(1)} collective-permute-done((f32[8,64]{1,0:T(8,128)S(1)}, f32[8,64]{1,0:T(8,128)S(1)}, u32[]{:S(2)}, u32[]{:S(2)}) %collective-permute-start) | collective-permute-done | bytes 2080 | tf_op jit(solution)/shard_map/ppermute | solution.py:340
  54.5 0.8 copy.15
  55.4 1.9 %pad_maximum_fusion.back_ref = f32[8,64,256]{2,1,0:T(8,128)} fusion(f32[8,64,255]{2,1,0:T(8,128)S(1)} %bitcast.17, f32[8,64,1]{2,1,0:T(8,128)} %copy.15), kind=kLoop, calls=%fused_computation | loop fusion | flops 131072 | bytes 1048576 | tf_op jit(solution)/shard_map/concatenate | solution.py:341
  57.3 0.0 all-to-all-done.in_ref
  57.3 0.1 broadcast_in_dim.16.shift_ref
  57.4 2.5 %shard_map.56 = f32[16,328,128]{2,1,0:T(8,128)S(1)} custom-call(s32[160,128]{1,0:T(8,128)S(1)} %broadcast_in_dim.16.shift_ref, f32[16,160,256]{2,1,0:T(8,128)S(1)} %all-to-all-done.in_ref), custom_call_target="tpu_custom_call" | custom-call | flops 6553600 | bytes 5242880 | tf_op jit(solution)/shard_map/pallas_call | solution.py:75
  59.9 0.0 copy-start.1
  59.9 76.1 %all_to_all.10.recv_ref = f32[16,328,128]{2,1,0:T(8,128)S(1)} all-to-all(f32[16,328,128]{2,1,0:T(8,128)S(1)} %shard_map.56), channel_id=1, replica_groups={{8,10,12,14,16,18,20,22,24,26,28,30,0,2,4,6},{9,11,13,15,17,19,21,23,25..., dimensions={0} | all-to-all | bytes 5373952 | tf_op jit(solution)/shard_map/all_to_all | solution.py:324
  136.0 0.7 shard_map.57
  136.7 1.6 %collective-permute-start.1 = (f32[2,8,256]{2,1,0:T(8,128)S(1)}, f32[2,8,256]{2,1,0:T(8,128)S(1)}, u32[]{:S(2)}, u32[]{:S(2)}) collective-permute-start(f32[2,8,256]{2,1,0:T(8,128)S(1)} %get-tuple-element.26.refs_0_), channel_id=1, source_target_pairs={{0,1},{1,0},{2,3},{3,2},{4,5},{5,4},{6,7},{7,6},{8,9},{9,8},{10,11... | collective-permute-start | bytes 49160 | tf_op jit(solution)/shard_map/ppermute | solution.py:368
  138.3 2.2 %shard_map.59.refs_2_ = f32[5,8,64,256]{3,2,1,0:T(8,128)} custom-call(f32[16,328,128]{2,1,0:T(8,128)S(1)} %all_to_all.10.recv_ref, f32[8,64,256]{2,1,0:T(8,128)S(1)} %copy-done, f32[8,64,256]{2,1,0:T(8,128)S(1)} %copy-done.1), custom_call_target="tpu_custom_call" | custom-call | flops 5242880 | bytes 4194304 | tf_op jit(solution)/shard_map/pallas_call | solution.py:222
  140.5 0.6 shard_map.58.local_ref
  141.0 0.0 collective-permute-done.1.refs_1_
  141.1 1.1 shard_map.60
  (18 shorter events, 0.1 us)
Async XLA Ops:
  0.0 8.0 %copy-start = (f32[8,64,256]{2,1,0:T(8,128)S(1)}, f32[8,64,256]{2,1,0:T(8,128)}, u32[]{:S(2)}) copy-start(f32[8,64,256]{2,1,0:T(8,128)} %speed_ref.3) | copy-start | bytes 1572868
  0.0 10.1 %copy-start.2 = (f32[8,64,64]{2,1,0:T(8,128)S(1)}, f32[8,64,64]{2,1,0:T(8,128)}, u32[]{:S(2)}) copy-start(f32[8,64,64]{2,1,0:T(8,128)} %inverse_ref.3) | copy-start | bytes 393220
  0.0 10.3 %copy-start.7 = (f32[8,1]{0,1:T(1,128)S(1)}, f32[8,1]{0,1:T(1,128)}, u32[]{:S(2)}) copy-start(f32[8,1]{0,1:T(1,128)} %param.9) | copy-start | bytes 100
  0.0 16.8 %copy-start.8 = (s32[64]{0:T(128)S(1)}, s32[64]{0:T(128)}, u32[]{:S(2)}) copy-start(s32[64]{0:T(128)} %param.7) | copy-start | bytes 772
  0.0 57.3 %all-to-all-start = ((f32[16,160,256]{2,1,0:T(8,128)}), f32[16,160,256]{2,1,0:T(8,128)S(1)}, u32[]{:S(2)}, u32[]{:S(2)}) async-start(f32[16,160,256]{2,1,0:T(8,128)} %bitcast.20), calls=%async_computation | async-start | bytes 5242880 | tf_op jit(solution)/shard_map/all_to_all | solution.py:324
  9.9 44.6 %collective-permute-start = (f32[8,64]{1,0:T(8,128)S(1)}, f32[8,64]{1,0:T(8,128)S(1)}, u32[]{:S(2)}, u32[]{:S(2)}) collective-permute-start(f32[8,64]{1,0:T(8,128)S(1)} %bitcast.22), channel_id=1, source_target_pairs={{0,2},{2,4},{4,6},{6,8},{8,10},{10,12},{12,14},{14,16},{16,18},{18... | collective-permute-start | bytes 6152 | tf_op jit(solution)/shard_map/ppermute | solution.py:340
  15.4 0.7 copy-start.3
  16.1 0.7 copy-start.5
  59.9 76.1 %copy-start.1 = (f32[8,64,256]{2,1,0:T(8,128)S(1)}, f32[8,64,256]{2,1,0:T(8,128)}, u32[]{:S(2)}) copy-start(f32[8,64,256]{2,1,0:T(8,128)} %pad_maximum_fusion.back_ref) | copy-start | bytes 1572868
  136.7 4.4 %copy-start.4 = (f32[8,64,128]{2,1,0:T(8,128)S(1)}, f32[8,64,128]{2,1,0:T(8,128)}, u32[]{:S(2)}) copy-start(f32[8,64,128]{2,1,0:T(8,128)} %copy-done.3) | copy-start | bytes 786436
  136.7 4.4 %copy-start.6 = (f32[8,64,128]{2,1,0:T(8,128)S(1)}, f32[8,64,128]{2,1,0:T(8,128)}, u32[]{:S(2)}) copy-start(f32[8,64,128]{2,1,0:T(8,128)} %copy-done.5) | copy-start | bytes 786436
  136.7 4.4 %collective-permute-start.1 = (f32[2,8,256]{2,1,0:T(8,128)S(1)}, f32[2,8,256]{2,1,0:T(8,128)S(1)}, u32[]{:S(2)}, u32[]{:S(2)}) collective-permute-start(f32[2,8,256]{2,1,0:T(8,128)S(1)} %get-tuple-element.26.refs_0_), channel_id=1, source_target_pairs={{0,1},{1,0},{2,3},{3,2},{4,5},{5,4},{6,7},{7,6},{8,9},{9,8},{10,11... | collective-permute-start | bytes 49160 | tf_op jit(solution)/shard_map/ppermute | solution.py:368

commit v13 on v12

--- a/solution.py
+++ b/solution.py
@@ -82,25 +82,30 @@
     )(shift_rows, gathered)
 
 
-def spread_kernel(low_ref, high_ref, low_out, high_out):
+def prepare_kernel(low_ref, high_ref, speed_ref, back_ref, low_out, high_out, weights_out):
     low_out[...] = jnp.broadcast_to(low_ref[...], low_out.shape)
     high_out[...] = jnp.broadcast_to(high_ref[...], high_out.shape)
-
-
-def spread(low, high):
-    shape = low.shape[:-1] + (LANES,)
-    return pl.pallas_call(
-        spread_kernel,
-        out_shape=[jax.ShapeDtypeStruct(shape, jnp.float32)] * 2,
-        in_specs=[IN_VMEM] * 2,
-        out_specs=[IN_VMEM] * 2,
-        compiler_params=ROOMY,
-        cost_estimate=cost(low.size, 2 * low.size * LANES),
-    )(low, high)
-
-
-def carry_level(fields, level, recv_ref, speed_ref, back_ref, known, store):
-    levels, radii, width = speed_ref.shape
+    speed = speed_ref[...]
+    back = back_ref[...]
+    weights_out[0] = 1.0 - jnp.maximum(speed, 0.0) + jnp.minimum(back, 0.0)
+    weights_out[1] = jnp.maximum(back, 0.0)
+    weights_out[2] = -jnp.minimum(speed, 0.0)
+
+
+def prepare(low, high, speed, back_speed):
+    column = jax.ShapeDtypeStruct(low.shape[:-1] + (LANES,), jnp.float32)
+    return pl.pallas_call(
+        prepare_kernel,
+        out_shape=[column, column, jax.ShapeDtypeStruct((3,) + speed.shape, jnp.float32)],
+        in_specs=[IN_VMEM] * 4,
+        out_specs=[IN_VMEM] * 3,
+        compiler_params=ROOMY,
+        cost_estimate=cost(6 * speed.size, 6 * speed.size),
+    )(low, high, speed, back_speed)
+
+
+def carry_level(fields, level, recv_ref, weights_ref, known, store):
+    _, levels, radii, width = weights_ref.shape
     per_block = width // LANES
     in_rows = recv_ref.shape[1]
     halo_row = in_rows - TILE_ROWS
@@ -116,19 +121,13 @@
         return known[key]
 
     for row in range(0, radii, TILE_ROWS):
-        rates = []
-        for part in range(per_block):
-            cut = (level, slice(row, row + TILE_ROWS), slice(part * LANES, (part + 1) * LANES))
-            speed = speed_ref[cut]
-            back = back_ref[cut]
-            rates.append(
-                (
-                    jnp.maximum(speed, 0.0),
-                    jnp.minimum(speed, 0.0),
-                    jnp.maximum(back, 0.0),
-                    jnp.minimum(back, 0.0),
-                )
-            )
+        weights = [
+            [
+                weights_ref[side, level, row : row + TILE_ROWS, part * LANES : (part + 1) * LANES]
+                for side in range(3)
+            ]
+            for part in range(per_block)
+        ]
         for field in fields:
             piece, group = divmod(((field * levels + level) * radii + row) // TILE_ROWS, groups)
             values = []
@@ -143,21 +142,20 @@
                 here = values[part]
                 behind = jnp.where(first, up[part], up[part + 1])
                 ahead = jnp.where(last, down[part + 1], down[part])
-                plus, minus, back_plus, back_minus = rates[part]
-                outflow = plus * here + minus * ahead
-                inflow = back_plus * behind + back_minus * here
-                store(field, row, part * LANES, here - (outflow - inflow))
-
-
-def energy_kernel(field, recv_ref, speed_ref, back_ref, inverse_ref, moved_ref, ends_ref):
-    levels, radii, _ = speed_ref.shape
+                keep, from_behind, from_ahead = weights[part]
+                result = keep * here + from_behind * behind + from_ahead * ahead
+                store(field, row, part * LANES, result)
+
+
+def energy_kernel(field, recv_ref, weights_ref, inverse_ref, moved_ref, ends_ref):
+    levels, radii, _ = moved_ref.shape
     known = {}
     for level in range(levels):
 
         def store(_, row, cell, values, level=level):
             moved_ref[level, row : row + TILE_ROWS, cell : cell + LANES] = values
 
-        carry_level([field], level, recv_ref, speed_ref, back_ref, known, store)
+        carry_level([field], level, recv_ref, weights_ref, known, store)
         outer = jnp.concatenate([inverse_ref[level, :TILE_ROWS], inverse_ref[level, radii - TILE_ROWS :]])
         ends = exact_product(outer, moved_ref[level])
         ends_ref[0, level : level + 1, :] = ends[:1]
@@ -168,19 +166,20 @@
     return jnp.dot(left, right, precision=lax.Precision.HIGHEST, preferred_element_type=jnp.float32)
 
 
-def energy_part(field, received, speed, back_speed, inverse):
-    levels, radii, width = speed.shape
+def energy_part(field, received, weights, inverse):
+    _, levels, radii, width = weights.shape
+    shape = (levels, radii, width)
     return pl.pallas_call(
         functools.partial(energy_kernel, field),
         out_shape=[
-            jax.ShapeDtypeStruct(speed.shape, jnp.float32),
+            jax.ShapeDtypeStruct(shape, jnp.float32),
             jax.ShapeDtypeStruct((2, levels, width), jnp.float32),
         ],
-        in_specs=[IN_VMEM] * 4,
+        in_specs=[IN_VMEM] * 3,
         out_specs=[IN_VMEM] * 2,
         compiler_params=ROOMY,
-        cost_estimate=cost(60 * speed.size, 4 * speed.size),
-    )(received, speed, back_speed, inverse)
+        cost_estimate=cost(20 * weights.size, 2 * weights.size),
+    )(received, weights, inverse)
 
 
 def product_kernel(inverse_ref, moved_ref, local_ref):
@@ -199,7 +198,7 @@
     )(inverse, moved)
 
 
-def carry_kernel(recv_ref, speed_ref, back_ref, out_ref, held, sems):
+def carry_kernel(recv_ref, weights_ref, out_ref, held, sems):
     nf, levels = held.shape[:2]
     copies = []
     known = {}
@@ -208,7 +207,7 @@
         def store(field, row, cell, values, level=level):
             held[field, level, row : row + TILE_ROWS, cell : cell + LANES] = values
 
-        carry_level(range(nf), level, recv_ref, speed_ref, back_ref, known, store)
+        carry_level(range(nf), level, recv_ref, weights_ref, known, store)
         copies.append(
             pltpu.make_async_copy(held.at[:, level], out_ref.at[pl.ds(0, nf), level], sems.at[level])
         )
@@ -217,20 +216,20 @@
         copy.wait()
 
 
-def carry(nf, count, received, speed, back_speed):
-    levels, radii, width = speed.shape
+def carry(nf, count, received, weights):
+    shape = weights.shape[1:]
     return pl.pallas_call(
         carry_kernel,
-        out_shape=jax.ShapeDtypeStruct((nf,) + speed.shape, jnp.float32),
-        in_specs=[IN_VMEM] * 3,
+        out_shape=jax.ShapeDtypeStruct((nf,) + shape, jnp.float32),
+        in_specs=[IN_VMEM] * 2,
         out_specs=IN_HBM,
         scratch_shapes=[
-            pltpu.VMEM((count,) + speed.shape, jnp.float32),
-            pltpu.SemaphoreType.DMA((levels,)),
+            pltpu.VMEM((count,) + shape, jnp.float32),
+            pltpu.SemaphoreType.DMA((shape[0],)),
         ],
         compiler_params=ROOMY,
-        cost_estimate=cost(10 * count * speed.size, 2 * count * speed.size),
-    )(received, speed, back_speed)
+        cost_estimate=cost(2 * count * weights.size, count * weights.size),
+    )(received, weights)
 
 
 def solve_interfaces(first_row, last_row, corner):
@@ -353,23 +352,26 @@
     links = all_corners.reshape(levels, bands, 5)[:, :, 4]
     links_below = jnp.concatenate([jnp.zeros_like(links[:, :1]), links[:, :-1]], axis=1)
     link_below = lax.dynamic_index_in_dim(links_below, band, 1, keepdims=True)
-    low, high = spread(
-        (link_below * block_inverse[:, :, 0])[:, :, None], (coupling * block_inverse[:, :, -1])[:, :, None]
+    low, high, weights = prepare(
+        (link_below * block_inverse[:, :, 0])[:, :, None],
+        (coupling * block_inverse[:, :, -1])[:, :, None],
+        velocity,
+        back_speed,
     )
     band_scalar = band[None].astype(jnp.int32)
-    gathered, back_speed, all_corners, low, high, band_scalar, shift_rows = lax.optimization_barrier(
-        (gathered, back_speed, all_corners, low, high, band_scalar, shift_rows)
+    gathered, weights, all_corners, low, high, band_scalar, shift_rows = lax.optimization_barrier(
+        (gathered, weights, all_corners, low, high, band_scalar, shift_rows)
     )
 
     received = exchange(turn(shift_rows, gathered))
 
-    moved, ends = energy_part(nf - 1, received, velocity, back_speed, block_inverse)
+    moved, ends = energy_part(nf - 1, received, weights, block_inverse)
     if bands == 2:
         all_ends = [ends, lax.ppermute(ends, "rad", [(0, 1), (1, 0)])]
     else:
         all_ends = [lax.all_gather(ends, "rad", axis=0)]
     local_part = product(block_inverse, moved)
-    result = carry(nf, nf - 1, received, velocity, back_speed)
+    result = carry(nf, nf - 1, received, weights)
     return finish(band_scalar, all_corners, local_part, low, high, all_ends, result)
 
 

time: 142 us -> 146 us (1.028)
  local copies, waits for them, and re-layouts: 5.01 us -> 8.08 us
    unnamed x21 -> x27, local copies, waits for them, and re-layouts: 2.58 us -> 5.62 us
where the time goes in v13:
time: 146 us
  blocking collectives  80.4 us (55%)
  waiting for transfers between devices  38.4 us (26%)
  starting transfers between devices  9.75 us (7%)
  local copies, waits for them, and re-layouts  8.08 us (6%)
  Pallas kernels  7.29 us (5%)
  other arithmetic  2.04 us (1%)
    all_to_all x1, blocking collectives, exchange(): lax.all_to_all(blocks, 'az', split_axis=0, concat_axis=0, tiled=True, axi...  76.1 us
    ppermute x1, waiting for transfers between devices, per_device(): lax.ppermute(velocity[:, :, -1], 'az', [(i, (i + 1) % n) for i in range(n)])  38.4 us
    all_to_all x1, starting transfers between devices, exchange(): lax.all_to_all(blocks, 'az', split_axis=0, concat_axis=0, tiled=True, axi...  7.99 us
    unnamed x27, local copies, waits for them, and re-layouts  5.62 us
    all_gather x1, blocking collectives, per_device(): all_corners = lax.all_gather(corners, 'rad', axis=1, tiled=True)  4.34 us
  transfers between devices with their start and end apart: 3, of which 1 were waited for; matrix products, arithmetic and copies ran while one was open for 4% of the time, Pallas kernels for 2%

profile of v13, /device:TPU:0, one launch (start us, length us, event | category | flops | bytes accessed | tf_op | source)
XLA Modules:
  0.0 146.1 jit_solution(6555249764051579905)
XLA Ops:
  0.0 8.0 %all-to-all-start = ((f32[16,160,256]{2,1,0:T(8,128)}), f32[16,160,256]{2,1,0:T(8,128)S(1)}, u32[]{:S(2)}, u32[]{:S(2)}) async-start(f32[16,160,256]{2,1,0:T(8,128)} %bitcast.20), calls=%async_computation | async-start | bytes 5242880 | tf_op jit(solution)/shard_map/all_to_all | solution.py:323
  8.0 0.8 slice.38
  8.8 1.1 copy.19
  9.9 0.2 collective-permute-start
  10.1 0.2 slice_reduce_fusion
  10.4 4.3 %all-gather = f32[2,5,8]{2,1,0:T(8,128)S(1)} all-gather(f32[1,5,8]{2,1,0:T(8,128)S(1)} %bitcast.21), channel_id=1, replica_groups=mesh['az'=16,'rad'=2] {'rad'}, dimensions={0}, use_global_device_ids=true | all-gather | bytes 480 | tf_op jit(solution)/shard_map/all_gather | solution.py:351
  14.7 0.1 copy.18
  14.8 0.1 reshape.21
  14.9 0.1 slice.40
  14.9 0.1 copy.15
  15.1 0.9 slice_multiply_fusion
  15.9 0.1 tile.10
  16.0 0.1 dynamic_slice.8
  16.1 38.4 %collective-permute-done = f32[8,64]{1,0:T(8,128)S(1)} collective-permute-done((f32[8,64]{1,0:T(8,128)S(1)}, f32[8,64]{1,0:T(8,128)S(1)}, u32[]{:S(2)}, u32[]{:S(2)}) %collective-permute-start) | collective-permute-done | bytes 2080 | tf_op jit(solution)/shard_map/ppermute | solution.py:339
  54.5 0.9 copy.17
  55.4 1.1 pad_maximum_fusion.back_ref
  56.6 0.9 copy-done.4
  57.5 0.9 copy-done.5
  58.5 0.4 shard_map.55
  58.8 0.0 copy-start
  58.9 1.1 copy-done
  60.0 0.7 copy-done.6
  60.7 0.7 copy-done.8
  61.4 0.1 broadcast_in_dim.16.shift_ref
  61.5 2.5 %shard_map.56 = f32[16,328,128]{2,1,0:T(8,128)S(1)} custom-call(s32[160,128]{1,0:T(8,128)S(1)} %broadcast_in_dim.16.shift_ref, f32[16,160,256]{2,1,0:T(8,128)S(1)} %all-to-all-done.in_ref), custom_call_target="tpu_custom_call" | custom-call | flops 6553600 | bytes 5242880 | tf_op jit(solution)/shard_map/pallas_call | solution.py:75
  64.0 0.0 copy-start.1
  64.0 76.1 %all_to_all.10.recv_ref = f32[16,328,128]{2,1,0:T(8,128)S(1)} all-to-all(f32[16,328,128]{2,1,0:T(8,128)S(1)} %shard_map.56), channel_id=1, replica_groups={{8,10,12,14,16,18,20,22,24,26,28,30,0,2,4,6},{9,11,13,15,17,19,21,23,25..., dimensions={0} | all-to-all | bytes 5373952 | tf_op jit(solution)/shard_map/all_to_all | solution.py:323
  140.1 0.6 shard_map.57
  140.7 1.6 %collective-permute-start.1 = (f32[2,8,256]{2,1,0:T(8,128)S(1)}, f32[2,8,256]{2,1,0:T(8,128)S(1)}, u32[]{:S(2)}, u32[]{:S(2)}) collective-permute-start(f32[2,8,256]{2,1,0:T(8,128)S(1)} %get-tuple-element.28.refs_0_), channel_id=1, source_target_pairs={{0,1},{1,0},{2,3},{3,2},{4,5},{5,4},{6,7},{7,6},{8,9},{9,8},{10,11... | collective-permute-start | bytes 49160 | tf_op jit(solution)/shard_map/ppermute | solution.py:370
  142.3 2.2 %shard_map.59.refs_2_ = f32[5,8,64,256]{3,2,1,0:T(8,128)} custom-call(f32[16,328,128]{2,1,0:T(8,128)S(1)} %all_to_all.10.recv_ref, f32[3,8,64,256]{3,2,1,0:T(8,128)S(1)} %copy-done.1), custom_call_target="tpu_custom_call" | custom-call | flops 3145728 | bytes 6291456 | tf_op jit(solution)/shard_map/pallas_call | solution.py:221
  144.5 0.6 shard_map.58.local_ref
  145.1 1.1 shard_map.60
  (24 shorter events, 0.1 us)
Async XLA Ops:
  0.0 8.0 %copy-start.3 = (f32[8,64,256]{2,1,0:T(8,128)S(1)}, f32[8,64,256]{2,1,0:T(8,128)}, u32[]{:S(2)}) copy-start(f32[8,64,256]{2,1,0:T(8,128)} %speed_ref.1) | copy-start | bytes 1572868
  0.0 10.1 %copy-start.2 = (f32[8,64,64]{2,1,0:T(8,128)S(1)}, f32[8,64,64]{2,1,0:T(8,128)}, u32[]{:S(2)}) copy-start(f32[8,64,64]{2,1,0:T(8,128)} %inverse_ref.3) | copy-start | bytes 393220
  0.0 10.3 %copy-start.10 = (f32[8,1]{0,1:T(1,128)S(1)}, f32[8,1]{0,1:T(1,128)}, u32[]{:S(2)}) copy-start(f32[8,1]{0,1:T(1,128)} %param.9) | copy-start | bytes 100
  0.0 15.9 %copy-start.11 = (s32[64]{0:T(128)S(1)}, s32[64]{0:T(128)}, u32[]{:S(2)}) copy-start(s32[64]{0:T(128)} %param.7) | copy-start | bytes 772
  0.0 61.4 %all-to-all-start = ((f32[16,160,256]{2,1,0:T(8,128)}), f32[16,160,256]{2,1,0:T(8,128)S(1)}, u32[]{:S(2)}, u32[]{:S(2)}) async-start(f32[16,160,256]{2,1,0:T(8,128)} %bitcast.20), calls=%async_computation | async-start | bytes 5242880 | tf_op jit(solution)/shard_map/all_to_all | solution.py:323
  9.9 44.6 %collective-permute-start = (f32[8,64]{1,0:T(8,128)S(1)}, f32[8,64]{1,0:T(8,128)S(1)}, u32[]{:S(2)}, u32[]{:S(2)}) collective-permute-start(f32[8,64]{1,0:T(8,128)S(1)} %bitcast.22), channel_id=1, source_target_pairs={{0,2},{2,4},{4,6},{6,8},{8,10},{10,12},{12,14},{14,16},{16,18},{18... | collective-permute-start | bytes 6152 | tf_op jit(solution)/shard_map/ppermute | solution.py:339
  56.6 1.0 copy-start.4
  57.5 0.9 copy-start.5
  58.8 1.1 copy-start
  60.0 0.7 copy-start.6
  60.7 0.7 copy-start.8
  64.0 76.1 %copy-start.1 = (f32[3,8,64,256]{3,2,1,0:T(8,128)S(1)}, f32[3,8,64,256]{3,2,1,0:T(8,128)}, u32[]{:S(2)}) copy-start(f32[3,8,64,256]{3,2,1,0:T(8,128)} %copy-done) | copy-start | bytes 4718596
  140.7 4.4 %copy-start.7 = (f32[8,64,128]{2,1,0:T(8,128)S(1)}, f32[8,64,128]{2,1,0:T(8,128)}, u32[]{:S(2)}) copy-start(f32[8,64,128]{2,1,0:T(8,128)} %copy-done.6) | copy-start | bytes 786436
  140.7 4.4 %copy-start.9 = (f32[8,64,128]{2,1,0:T(8,128)S(1)}, f32[8,64,128]{2,1,0:T(8,128)}, u32[]{:S(2)}) copy-start(f32[8,64,128]{2,1,0:T(8,128)} %copy-done.8) | copy-start | bytes 786436
  140.7 4.4 %collective-permute-start.1 = (f32[2,8,256]{2,1,0:T(8,128)S(1)}, f32[2,8,256]{2,1,0:T(8,128)S(1)}, u32[]{:S(2)}, u32[]{:S(2)}) collective-permute-start(f32[2,8,256]{2,1,0:T(8,128)S(1)} %get-tuple-element.28.refs_0_), channel_id=1, source_target_pairs={{0,1},{1,0},{2,3},{3,2},{4,5},{5,4},{6,7},{7,6},{8,9},{9,8},{10,11... | collective-permute-start | bytes 49160 | tf_op jit(solution)/shard_map/ppermute | solution.py:370

commit v14 on v12

--- a/solution.py
+++ b/solution.py
@@ -23,7 +23,7 @@
     return (device + n - n // 4) % n
 
 
-def turn_kernel(shift_ref, in_ref, out_ref):
+def turn_kernel(shift_ref, edge_ref, in_ref, out_ref):
     n, rows, width = in_ref.shape
     places = [place_of(block, n) for block in range(n)]
     per_block = width // LANES
@@ -32,7 +32,7 @@
     halo_row = per_block * rows
     lane = lax.broadcasted_iota(jnp.int32, (TILE_ROWS, LANES), 1)
     for block in range(n):
-        out_ref[block, halo_row : halo_row + TILE_ROWS, :] = jnp.zeros((TILE_ROWS, LANES), jnp.float32)
+        out_ref[block, halo_row : halo_row + TILE_ROWS, :] = edge_ref[...]
 
     def one_group(group):
         here = pl.ds(group * TILE_ROWS, TILE_ROWS)
@@ -69,17 +69,17 @@
         one_group(group)
 
 
-def turn(shift_rows, gathered):
+def turn(shift_rows, edge_tile, gathered):
     n, rows, width = gathered.shape
     shape = (n, (width // LANES) * rows + TILE_ROWS, LANES)
     return pl.pallas_call(
         turn_kernel,
         out_shape=jax.ShapeDtypeStruct(shape, jnp.float32),
-        in_specs=[IN_VMEM] * 2,
+        in_specs=[IN_VMEM] * 3,
         out_specs=IN_VMEM,
         compiler_params=ROOMY,
         cost_estimate=cost(10 * gathered.size, 2 * gathered.size),
-    )(shift_rows, gathered)
+    )(shift_rows, edge_tile, gathered)
 
 
 def spread_kernel(low_ref, high_ref, low_out, high_out):
@@ -149,10 +149,24 @@
                 store(field, row, part * LANES, here - (outflow - inflow))
 
 
-def energy_kernel(field, recv_ref, speed_ref, back_ref, inverse_ref, moved_ref, ends_ref):
-    levels, radii, _ = speed_ref.shape
+def energy_kernel(
+    field, left_ref, recv_ref, speed_ref, inverse_ref, moved_ref, ends_ref, back_ref, columns
+):
+    levels, radii, width = speed_ref.shape
+    in_rows = recv_ref.shape[1]
+    tile = recv_ref[left_ref[0], in_rows - TILE_ROWS :, :]
+    columns[...] = jnp.transpose(jnp.concatenate([tile] * (LANES // TILE_ROWS), axis=0))
+    first = lax.broadcasted_iota(jnp.int32, (TILE_ROWS, LANES), 1) == 0
     known = {}
     for level in range(levels):
+        for row in range(0, radii, TILE_ROWS):
+            here = slice(row, row + TILE_ROWS)
+            column = columns[LANES - radii + row : LANES - radii + row + TILE_ROWS, level : level + 1]
+            before = jnp.broadcast_to(column, (TILE_ROWS, LANES))
+            for cell in range(0, width, LANES):
+                behind = pltpu.roll(speed_ref[level, here, cell : cell + LANES], 1, 1)
+                back_ref[level, here, cell : cell + LANES] = jnp.where(first, before, behind)
+                before = behind
 
         def store(_, row, cell, values, level=level):
             moved_ref[level, row : row + TILE_ROWS, cell : cell + LANES] = values
@@ -168,19 +182,18 @@
     return jnp.dot(left, right, precision=lax.Precision.HIGHEST, preferred_element_type=jnp.float32)
 
 
-def energy_part(field, received, speed, back_speed, inverse):
+def energy_part(field, left, received, speed, inverse):
     levels, radii, width = speed.shape
+    plane = jax.ShapeDtypeStruct(speed.shape, jnp.float32)
     return pl.pallas_call(
         functools.partial(energy_kernel, field),
-        out_shape=[
-            jax.ShapeDtypeStruct(speed.shape, jnp.float32),
-            jax.ShapeDtypeStruct((2, levels, width), jnp.float32),
-        ],
-        in_specs=[IN_VMEM] * 4,
-        out_specs=[IN_VMEM] * 2,
-        compiler_params=ROOMY,
-        cost_estimate=cost(60 * speed.size, 4 * speed.size),
-    )(received, speed, back_speed, inverse)
+        out_shape=[plane, jax.ShapeDtypeStruct((2, levels, width), jnp.float32), plane],
+        in_specs=[IN_SMEM] + [IN_VMEM] * 3,
+        out_specs=[IN_VMEM] * 3,
+        scratch_shapes=[pltpu.VMEM((LANES, LANES), jnp.float32)],
+        compiler_params=ROOMY,
+        cost_estimate=cost(60 * speed.size, 5 * speed.size),
+    )(left, received, speed, inverse)
 
 
 def product_kernel(inverse_ref, moved_ref, local_ref):
@@ -337,8 +350,8 @@
     all_shifts = jnp.tile(shifts, rows // radii + 2)
     own_shifts = lax.dynamic_slice_in_dim(all_shifts, (place_of(me, n) * rows) % radii, rows)
     shift_rows = jnp.broadcast_to(own_shifts[:, None], (rows, LANES))
-    edge_speed = lax.ppermute(velocity[:, :, -1], "az", [(i, (i + 1) % n) for i in range(n)])
-    back_speed = jnp.concatenate([edge_speed[:, :, None], velocity[:, :, :-1]], axis=2)
+    edge_tile = jnp.pad(velocity[:, :, -1], ((0, 0), (LANES - radii, 0)))
+    left_scalar = place_of((me + n - 1) % n, n)[None].astype(jnp.int32)
     corners = jnp.stack(
         [
             block_inverse[:, 0, 0],
@@ -357,13 +370,13 @@
         (link_below * block_inverse[:, :, 0])[:, :, None], (coupling * block_inverse[:, :, -1])[:, :, None]
     )
     band_scalar = band[None].astype(jnp.int32)
-    gathered, back_speed, all_corners, low, high, band_scalar, shift_rows = lax.optimization_barrier(
-        (gathered, back_speed, all_corners, low, high, band_scalar, shift_rows)
+    gathered, edge_tile, all_corners, low, high, band_scalar, left_scalar, shift_rows = lax.optimization_barrier(
+        (gathered, edge_tile, all_corners, low, high, band_scalar, left_scalar, shift_rows)
     )
 
-    received = exchange(turn(shift_rows, gathered))
-
-    moved, ends = energy_part(nf - 1, received, velocity, back_speed, block_inverse)
+    received = exchange(turn(shift_rows, edge_tile, gathered))
+
+    moved, ends, back_speed = energy_part(nf - 1, left_scalar, received, velocity, block_inverse)
     if bands == 2:
         all_ends = [ends, lax.ppermute(ends, "rad", [(0, 1), (1, 0)])]
     else:

time: 142 us -> 140 us (0.986)
  waiting for transfers between devices: 37.6 us -> 40 us
  other arithmetic: 2.1 us -> 0.15 us
  blocking collectives: 80.4 us -> 78.9 us
    all_to_all x1, waiting for transfers between devices: 0.01 us -> 40 us  [exchange(): lax.all_to_all(blocks, 'az', split_axis=0, concat_axis=0, tiled=True, axi...]
    ppermute x1 -> x0, waiting for transfers between devices: 37.6 us -> none  [per_device(): lax.ppermute(velocity[:, :, -1], 'az', [(i, (i + 1) % n) for i in range(n)])]
    concatenate x1 -> x0, other arithmetic: 1.95 us -> none  [per_device(): jnp.concatenate([edge_speed[:, :, None], velocity[:, :, :-1]], axis=2)]
    all_to_all x1, blocking collectives: 76.1 us -> 74.5 us  [exchange(): lax.all_to_all(blocks, 'az', split_axis=0, concat_axis=0, tiled=True, axi...]
  transfers between devices with their start and end apart: 3 -> 2, of which waited for: 1 -> 1; matrix products, arithmetic and copies ran while one was open for 4% -> 2% of each run, Pallas kernels for 2% -> 2%
where the time goes in v14:
time: 140 us
  blocking collectives  78.9 us (56%)
  waiting for transfers between devices  40 us (29%)
  starting transfers between devices  9.52 us (7%)
  Pallas kernels  7.36 us (5%)
  local copies, waits for them, and re-layouts  4.21 us (3%)
    all_to_all x1, blocking collectives, exchange(): lax.all_to_all(blocks, 'az', split_axis=0, concat_axis=0, tiled=True, axi...  74.5 us
    all_to_all x1, waiting for transfers between devices, exchange(): lax.all_to_all(blocks, 'az', split_axis=0, concat_axis=0, tiled=True, axi...  40 us
    all_to_all x1, starting transfers between devices, exchange(): lax.all_to_all(blocks, 'az', split_axis=0, concat_axis=0, tiled=True, axi...  7.99 us
    all_gather x1, blocking collectives, per_device(): all_corners = lax.all_gather(corners, 'rad', axis=1, tiled=True)  4.34 us
  transfers between devices with their start and end apart: 2, of which 1 were waited for; matrix products, arithmetic and copies ran while one was open for 2% of the time, Pallas kernels for 2%

profile of v14, /device:TPU:0, one launch (start us, length us, event | category | flops | bytes accessed | tf_op | source)
XLA Modules:
  0.0 140.2 jit_solution(890930184135702621)
XLA Ops:
  0.0 8.0 %all-to-all-start = ((f32[16,160,256]{2,1,0:T(8,128)}), f32[16,160,256]{2,1,0:T(8,128)S(1)}, u32[]{:S(2)}, u32[]{:S(2)}) async-start(f32[16,160,256]{2,1,0:T(8,128)} %bitcast.18), calls=%async_computation | async-start | bytes 5242880 | tf_op jit(solution)/shard_map/all_to_all | solution.py:337
  8.0 0.0 copy-done
  8.0 0.2 slice_reduce_fusion
  8.2 0.0 copy-done.6
  8.3 4.3 %all-gather = f32[2,5,8]{2,1,0:T(8,128)S(1)} all-gather(f32[1,5,8]{2,1,0:T(8,128)S(1)} %bitcast.20), channel_id=1, replica_groups=mesh['az'=16,'rad'=2] {'rad'}, dimensions={0}, use_global_device_ids=true | all-gather | bytes 480 | tf_op jit(solution)/shard_map/all_gather | solution.py:365
  12.6 0.1 copy.16
  12.7 0.1 reshape.21
  12.8 0.1 slice.36
  12.8 0.1 copy.15
  13.0 0.2 slice_multiply_fusion
  13.1 0.2 shard_map.55
  13.3 0.0 copy-start.2
  13.3 0.7 copy-done.2
  14.0 0.7 copy-done.4
  14.7 0.0 copy-done.7
  14.7 0.1 tile.10
  14.8 0.0 copy-done.1
  14.8 0.8 slice.27
  15.6 1.1 copy.17
  16.7 0.1 dynamic_slice.8
  16.8 0.1 pad.5.edge_ref
  16.9 40.0 %all-to-all-done.in_ref = f32[16,160,256]{2,1,0:T(8,128)S(1)} async-done(((f32[16,160,256]{2,1,0:T(8,128)}), f32[16,160,256]{2,1,0:T(8,128)S(1)}, u32[]{:S(2)}, u32[]{:S(2)}) %all-to-all-start) | async-done | bytes 2621472 | tf_op jit(solution)/shard_map/all_to_all | solution.py:337
  56.9 0.1 broadcast_in_dim.16.shift_ref
  56.9 2.5 %shard_map.56 = f32[16,328,128]{2,1,0:T(8,128)S(1)} custom-call(s32[160,128]{1,0:T(8,128)S(1)} %broadcast_in_dim.16.shift_ref, f32[8,128]{1,0:T(8,128)S(1)} %pad.5.edge_ref, f32[16,160,256]{2,1,0:T(8,128)S(1)} %all-to-all-done.in_ref), custom_call_target="tpu_custom_call" | custom-call | flops 6553600 | bytes 5242880 | tf_op jit(solution)/shard_map/pallas_call | solution.py:75
  59.4 74.5 %all_to_all.10.recv_ref = f32[16,328,128]{2,1,0:T(8,128)S(1)} all-to-all(f32[16,328,128]{2,1,0:T(8,128)S(1)} %shard_map.56), channel_id=1, replica_groups={{8,10,12,14,16,18,20,22,24,26,28,30,0,2,4,6},{9,11,13,15,17,19,21,23,25..., dimensions={0} | all-to-all | bytes 5373952 | tf_op jit(solution)/shard_map/all_to_all | solution.py:337
  134.0 0.9 shard_map.57
  134.9 1.5 %collective-permute-start = (f32[2,8,256]{2,1,0:T(8,128)S(1)}, f32[2,8,256]{2,1,0:T(8,128)S(1)}, u32[]{:S(2)}, u32[]{:S(2)}) collective-permute-start(f32[2,8,256]{2,1,0:T(8,128)S(1)} %get-tuple-element.29.refs_0_), channel_id=1, source_target_pairs={{0,1},{1,0},{2,3},{3,2},{4,5},{5,4},{6,7},{7,6},{8,9},{9,8},{10,11... | collective-permute-start | bytes 49160 | tf_op jit(solution)/shard_map/ppermute | solution.py:381
  136.4 2.2 %shard_map.59.refs_2_ = f32[5,8,64,256]{3,2,1,0:T(8,128)} custom-call(f32[16,328,128]{2,1,0:T(8,128)S(1)} %all_to_all.10.recv_ref, f32[8,64,256]{2,1,0:T(8,128)S(1)} %copy-done.1, f32[8,64,256]{2,1,0:T(8,128)S(1)} %get-tuple-element.30.back_ref), custom_call_target="tpu_custom_call" | custom-call | flops 5242880 | bytes 4194304 | tf_op jit(solution)/shard_map/pallas_call | solution.py:235
  138.6 0.6 shard_map.58.local_ref
  139.2 0.0 collective-permute-done.refs_1_
  139.2 0.0 copy-done.3
  139.2 1.1 shard_map.60
  (13 shorter events, 0.1 us)
Async XLA Ops:
  0.0 8.0 %copy-start = (f32[8,64,64]{2,1,0:T(8,128)S(1)}, f32[8,64,64]{2,1,0:T(8,128)}, u32[]{:S(2)}) copy-start(f32[8,64,64]{2,1,0:T(8,128)} %inverse_ref.3) | copy-start | bytes 393220
  0.0 8.2 %copy-start.6 = (f32[8,1]{0,1:T(1,128)S(1)}, f32[8,1]{0,1:T(1,128)}, u32[]{:S(2)}) copy-start(f32[8,1]{0,1:T(1,128)} %param.9) | copy-start | bytes 100
  0.0 14.7 %copy-start.7 = (s32[64]{0:T(128)S(1)}, s32[64]{0:T(128)}, u32[]{:S(2)}) copy-start(s32[64]{0:T(128)} %param.7) | copy-start | bytes 772
  0.0 14.8 %copy-start.1 = (f32[8,64,256]{2,1,0:T(8,128)S(1)}, f32[8,64,256]{2,1,0:T(8,128)}, u32[]{:S(2)}) copy-start(f32[8,64,256]{2,1,0:T(8,128)} %speed_ref.3) | copy-start | bytes 1572868
  0.0 56.8 %all-to-all-start = ((f32[16,160,256]{2,1,0:T(8,128)}), f32[16,160,256]{2,1,0:T(8,128)S(1)}, u32[]{:S(2)}, u32[]{:S(2)}) async-start(f32[16,160,256]{2,1,0:T(8,128)} %bitcast.18), calls=%async_computation | async-start | bytes 5242880 | tf_op jit(solution)/shard_map/all_to_all | solution.py:337
  13.3 0.7 copy-start.2
  14.0 0.7 copy-start.4
  134.9 4.3 %collective-permute-start = (f32[2,8,256]{2,1,0:T(8,128)S(1)}, f32[2,8,256]{2,1,0:T(8,128)S(1)}, u32[]{:S(2)}, u32[]{:S(2)}) collective-permute-start(f32[2,8,256]{2,1,0:T(8,128)S(1)} %get-tuple-element.29.refs_0_), channel_id=1, source_target_pairs={{0,1},{1,0},{2,3},{3,2},{4,5},{5,4},{6,7},{7,6},{8,9},{9,8},{10,11... | collective-permute-start | bytes 49160 | tf_op jit(solution)/shard_map/ppermute | solution.py:381
  136.4 2.8 %copy-start.3 = (f32[8,64,128]{2,1,0:T(8,128)S(1)}, f32[8,64,128]{2,1,0:T(8,128)}, u32[]{:S(2)}) copy-start(f32[8,64,128]{2,1,0:T(8,128)} %copy-done.2) | copy-start | bytes 786436
  136.4 2.8 %copy-start.5 = (f32[8,64,128]{2,1,0:T(8,128)S(1)}, f32[8,64,128]{2,1,0:T(8,128)}, u32[]{:S(2)}) copy-start(f32[8,64,128]{2,1,0:T(8,128)} %copy-done.4) | copy-start | bytes 786436

commit v15 on v14

--- a/solution.py
+++ b/solution.py
@@ -20,7 +20,7 @@
 
 
 def place_of(device, n):
-    return (device + n - n // 4) % n
+    return (device + n // 2) % n
 
 
 def turn_kernel(shift_ref, edge_ref, in_ref, out_ref):
@@ -196,27 +196,12 @@
     )(left, received, speed, inverse)
 
 
-def product_kernel(inverse_ref, moved_ref, local_ref):
-    for level in range(moved_ref.shape[0]):
-        local_ref[level] = exact_product(inverse_ref[level], moved_ref[level])
-
-
-def product(inverse, moved):
-    return pl.pallas_call(
-        product_kernel,
-        out_shape=jax.ShapeDtypeStruct(moved.shape, jnp.float32),
-        in_specs=[IN_VMEM] * 2,
-        out_specs=IN_VMEM,
-        compiler_params=ROOMY,
-        cost_estimate=cost(2 * moved.size * moved.shape[1], 2 * moved.size),
-    )(inverse, moved)
-
-
-def carry_kernel(recv_ref, speed_ref, back_ref, out_ref, held, sems):
+def carry_kernel(recv_ref, speed_ref, back_ref, inverse_ref, moved_ref, out_ref, local_ref, held, sems):
     nf, levels = held.shape[:2]
     copies = []
     known = {}
     for level in range(levels):
+        local_ref[level] = exact_product(inverse_ref[level], moved_ref[level])
 
         def store(field, row, cell, values, level=level):
             held[field, level, row : row + TILE_ROWS, cell : cell + LANES] = values
@@ -230,20 +215,23 @@
         copy.wait()
 
 
-def carry(nf, count, received, speed, back_speed):
+def carry(nf, count, received, speed, back_speed, inverse, moved):
     levels, radii, width = speed.shape
     return pl.pallas_call(
         carry_kernel,
-        out_shape=jax.ShapeDtypeStruct((nf,) + speed.shape, jnp.float32),
-        in_specs=[IN_VMEM] * 3,
-        out_specs=IN_HBM,
+        out_shape=[
+            jax.ShapeDtypeStruct((nf,) + speed.shape, jnp.float32),
+            jax.ShapeDtypeStruct(speed.shape, jnp.float32),
+        ],
+        in_specs=[IN_VMEM] * 5,
+        out_specs=[IN_HBM, IN_VMEM],
         scratch_shapes=[
             pltpu.VMEM((count,) + speed.shape, jnp.float32),
             pltpu.SemaphoreType.DMA((levels,)),
         ],
         compiler_params=ROOMY,
         cost_estimate=cost(10 * count * speed.size, 2 * count * speed.size),
-    )(received, speed, back_speed)
+    )(received, speed, back_speed, inverse, moved)
 
 
 def solve_interfaces(first_row, last_row, corner):
@@ -381,8 +369,7 @@
         all_ends = [ends, lax.ppermute(ends, "rad", [(0, 1), (1, 0)])]
     else:
         all_ends = [lax.all_gather(ends, "rad", axis=0)]
-    local_part = product(block_inverse, moved)
-    result = carry(nf, nf - 1, received, velocity, back_speed)
+    result, local_part = carry(nf, nf - 1, received, velocity, back_speed, block_inverse, moved)
     return finish(band_scalar, all_corners, local_part, low, high, all_ends, result)
 
 

time: 140 us -> 139 us (level)
  no operation moved by 1% of the time
where the time goes in v15:
time: 139 us
  blocking collectives  79.1 us (57%)
  waiting for transfers between devices  39 us (28%)
  starting transfers between devices  9.57 us (7%)
  Pallas kernels  6.95 us (5%)
  local copies, waits for them, and re-layouts  4.22 us (3%)
    all_to_all x1, blocking collectives, exchange(): lax.all_to_all(blocks, 'az', split_axis=0, concat_axis=0, tiled=True, axi...  74.8 us
    all_to_all x1, waiting for transfers between devices, exchange(): lax.all_to_all(blocks, 'az', split_axis=0, concat_axis=0, tiled=True, axi...  39 us
    all_to_all x1, starting transfers between devices, exchange(): lax.all_to_all(blocks, 'az', split_axis=0, concat_axis=0, tiled=True, axi...  7.99 us
    all_gather x1, blocking collectives, per_device(): all_corners = lax.all_gather(corners, 'rad', axis=1, tiled=True)  4.34 us
  transfers between devices with their start and end apart: 2, of which 1 were waited for; matrix products, arithmetic and copies ran while one was open for 2% of the time, Pallas kernels for 2%

profile of v15, /device:TPU:0, one launch (start us, length us, event | category | flops | bytes accessed | tf_op | source)
XLA Modules:
  0.0 139.2 jit_solution(18019593877576235829)
XLA Ops:
  0.0 8.0 %all-to-all-start = ((f32[16,160,256]{2,1,0:T(8,128)}), f32[16,160,256]{2,1,0:T(8,128)S(1)}, u32[]{:S(2)}, u32[]{:S(2)}) async-start(f32[16,160,256]{2,1,0:T(8,128)} %bitcast.18), calls=%async_computation | async-start | bytes 5242880 | tf_op jit(solution)/shard_map/all_to_all | solution.py:325
  8.0 0.0 copy-done
  8.0 0.2 slice_reduce_fusion
  8.2 0.0 copy-done.6
  8.3 4.3 %all-gather = f32[2,5,8]{2,1,0:T(8,128)S(1)} all-gather(f32[1,5,8]{2,1,0:T(8,128)S(1)} %bitcast.20), channel_id=1, replica_groups=mesh['az'=16,'rad'=2] {'rad'}, dimensions={0}, use_global_device_ids=true | all-gather | bytes 480 | tf_op jit(solution)/shard_map/all_gather | solution.py:353
  12.6 0.1 copy.16
  12.7 0.1 reshape.21
  12.8 0.1 slice.36
  12.8 0.1 copy.15
  13.0 0.2 slice_multiply_fusion
  13.1 0.2 shard_map.55
  13.3 0.0 copy-start.2
  13.3 0.7 copy-done.2
  14.0 0.7 copy-done.4
  14.7 0.0 copy-done.7
  14.7 0.1 tile.10
  14.8 0.0 copy-done.1
  14.8 0.8 slice.27
  15.6 1.1 copy.17
  16.7 0.1 dynamic_slice.8
  16.8 0.1 pad.5.edge_ref
  16.9 39.0 %all-to-all-done.in_ref = f32[16,160,256]{2,1,0:T(8,128)S(1)} async-done(((f32[16,160,256]{2,1,0:T(8,128)}), f32[16,160,256]{2,1,0:T(8,128)S(1)}, u32[]{:S(2)}, u32[]{:S(2)}) %all-to-all-start) | async-done | bytes 2621472 | tf_op jit(solution)/shard_map/all_to_all | solution.py:325
  55.9 0.1 broadcast_in_dim.16.shift_ref
  56.0 2.5 %shard_map.56 = f32[16,328,128]{2,1,0:T(8,128)S(1)} custom-call(s32[160,128]{1,0:T(8,128)S(1)} %broadcast_in_dim.16.shift_ref, f32[8,128]{1,0:T(8,128)S(1)} %pad.5.edge_ref, f32[16,160,256]{2,1,0:T(8,128)S(1)} %all-to-all-done.in_ref), custom_call_target="tpu_custom_call" | custom-call | flops 6553600 | bytes 5242880 | tf_op jit(solution)/shard_map/pallas_call | solution.py:75
  58.5 74.8 %all_to_all.10.recv_ref = f32[16,328,128]{2,1,0:T(8,128)S(1)} all-to-all(f32[16,328,128]{2,1,0:T(8,128)S(1)} %shard_map.56), channel_id=1, replica_groups={{16,18,20,22,24,26,28,30,0,2,4,6,8,10,12,14},{17,19,21,23,25,27,29,31,1..., dimensions={0} | all-to-all | bytes 5373952 | tf_op jit(solution)/shard_map/all_to_all | solution.py:325
  133.3 0.9 shard_map.57
  134.2 0.0 copy-start.5
  134.2 1.6 %collective-permute-start = (f32[2,8,256]{2,1,0:T(8,128)S(1)}, f32[2,8,256]{2,1,0:T(8,128)S(1)}, u32[]{:S(2)}, u32[]{:S(2)}) collective-permute-start(f32[2,8,256]{2,1,0:T(8,128)S(1)} %get-tuple-element.33.refs_0_), channel_id=1, source_target_pairs={{0,1},{1,0},{2,3},{3,2},{4,5},{5,4},{6,7},{7,6},{8,9},{9,8},{10,11... | collective-permute-start | bytes 49160 | tf_op jit(solution)/shard_map/ppermute | solution.py:369
  135.8 2.3 %shard_map.58 = (f32[5,8,64,256]{3,2,1,0:T(8,128)}, f32[8,64,256]{2,1,0:T(8,128)S(1)}) custom-call(f32[16,328,128]{2,1,0:T(8,128)S(1)} %all_to_all.10.recv_ref, f32[8,64,256]{2,1,0:T(8,128)S(1)} %copy-done.1, f32[8,64,256]{2,1,0:T(8,128)S(1)} %get-tuple-element.28.back_ref, f32[8,64,64]{2,1,0:T(8,128)S(1)} %copy-done, ...), custom_call_target="tpu_custom_call" | custom-call | flops 5242880 | bytes 4194304 | tf_op jit(solution)/shard_map/pallas_call | solution.py:220
  138.1 0.0 collective-permute-done.refs_1_
  138.1 0.0 copy-done.3
  138.1 1.1 shard_map.59
  (12 shorter events, 0.1 us)
Async XLA Ops:
  0.0 8.0 %copy-start = (f32[8,64,64]{2,1,0:T(8,128)S(1)}, f32[8,64,64]{2,1,0:T(8,128)}, u32[]{:S(2)}) copy-start(f32[8,64,64]{2,1,0:T(8,128)} %inverse_ref.3) | copy-start | bytes 393220
  0.0 8.2 %copy-start.6 = (f32[8,1]{0,1:T(1,128)S(1)}, f32[8,1]{0,1:T(1,128)}, u32[]{:S(2)}) copy-start(f32[8,1]{0,1:T(1,128)} %param.9) | copy-start | bytes 100
  0.0 14.7 %copy-start.7 = (s32[64]{0:T(128)S(1)}, s32[64]{0:T(128)}, u32[]{:S(2)}) copy-start(s32[64]{0:T(128)} %param.7) | copy-start | bytes 772
  0.0 14.8 %copy-start.1 = (f32[8,64,256]{2,1,0:T(8,128)S(1)}, f32[8,64,256]{2,1,0:T(8,128)}, u32[]{:S(2)}) copy-start(f32[8,64,256]{2,1,0:T(8,128)} %speed_ref.3) | copy-start | bytes 1572868
  0.0 55.9 %all-to-all-start = ((f32[16,160,256]{2,1,0:T(8,128)}), f32[16,160,256]{2,1,0:T(8,128)S(1)}, u32[]{:S(2)}, u32[]{:S(2)}) async-start(f32[16,160,256]{2,1,0:T(8,128)} %bitcast.18), calls=%async_computation | async-start | bytes 5242880 | tf_op jit(solution)/shard_map/all_to_all | solution.py:325
  13.3 0.7 copy-start.2
  14.0 0.7 copy-start.4
  134.2 4.0 %copy-start.3 = (f32[8,64,128]{2,1,0:T(8,128)S(1)}, f32[8,64,128]{2,1,0:T(8,128)}, u32[]{:S(2)}) copy-start(f32[8,64,128]{2,1,0:T(8,128)} %copy-done.2) | copy-start | bytes 786436
  134.2 4.0 %copy-start.5 = (f32[8,64,128]{2,1,0:T(8,128)S(1)}, f32[8,64,128]{2,1,0:T(8,128)}, u32[]{:S(2)}) copy-start(f32[8,64,128]{2,1,0:T(8,128)} %copy-done.4) | copy-start | bytes 786436
  134.2 3.9 %collective-permute-start = (f32[2,8,256]{2,1,0:T(8,128)S(1)}, f32[2,8,256]{2,1,0:T(8,128)S(1)}, u32[]{:S(2)}, u32[]{:S(2)}) collective-permute-start(f32[2,8,256]{2,1,0:T(8,128)S(1)} %get-tuple-element.33.refs_0_), channel_id=1, source_target_pairs={{0,1},{1,0},{2,3},{3,2},{4,5},{5,4},{6,7},{7,6},{8,9},{9,8},{10,11... | collective-permute-start | bytes 49160 | tf_op jit(solution)/shard_map/ppermute | solution.py:369

commit v16 on v15

--- a/solution.py
+++ b/solution.py
@@ -20,7 +20,8 @@
 
 
 def place_of(device, n):
-    return (device + n // 2) % n
+    blocks = n // 4
+    return (device % 4) * blocks + (device // 4 + blocks // 2) % blocks
 
 
 def turn_kernel(shift_ref, edge_ref, in_ref, out_ref):

time: 139 us -> 140 us (level)
  waiting for transfers between devices: 39 us -> 48.9 us
  blocking collectives: 79.1 us -> 69.5 us
    all_to_all x1, waiting for transfers between devices: 39 us -> 48.9 us  [exchange(): lax.all_to_all(blocks, 'az', split_axis=0, concat_axis=0, tiled=True, axi...]
    all_to_all x1, blocking collectives: 74.8 us -> 65.2 us  [exchange(): lax.all_to_all(blocks, 'az', split_axis=0, concat_axis=0, tiled=True, axi...]
where the time goes in v16:
time: 140 us; the launch traced here: 139 us
  blocking collectives  69.5 us (50%)
  waiting for transfers between devices  48.9 us (35%)
  starting transfers between devices  9.57 us (7%)
  Pallas kernels  6.95 us (5%)
  local copies, waits for them, and re-layouts  4.23 us (3%)
    all_to_all x1, blocking collectives, exchange(): lax.all_to_all(blocks, 'az', split_axis=0, concat_axis=0, tiled=True, axi...  65.2 us
    all_to_all x1, waiting for transfers between devices, exchange(): lax.all_to_all(blocks, 'az', split_axis=0, concat_axis=0, tiled=True, axi...  48.9 us
    all_to_all x1, starting transfers between devices, exchange(): lax.all_to_all(blocks, 'az', split_axis=0, concat_axis=0, tiled=True, axi...  7.98 us
    all_gather x1, blocking collectives, per_device(): all_corners = lax.all_gather(corners, 'rad', axis=1, tiled=True)  4.34 us
  transfers between devices with their start and end apart: 2, of which 1 were waited for; matrix products, arithmetic and copies ran while one was open for 2% of the time, Pallas kernels for 2%

profile of v16, /device:TPU:0, one launch (start us, length us, event | category | flops | bytes accessed | tf_op | source)
XLA Modules:
  0.0 139.4 jit_solution(10623040687777491309)
XLA Ops:
  0.0 8.0 %all-to-all-start = ((f32[16,160,256]{2,1,0:T(8,128)}), f32[16,160,256]{2,1,0:T(8,128)S(1)}, u32[]{:S(2)}, u32[]{:S(2)}) async-start(f32[16,160,256]{2,1,0:T(8,128)} %bitcast.18), calls=%async_computation | async-start | bytes 5242880 | tf_op jit(solution)/shard_map/all_to_all | solution.py:326
  8.0 0.0 copy-done
  8.0 0.2 slice_reduce_fusion
  8.2 0.0 copy-done.6
  8.3 4.3 %all-gather = f32[2,5,8]{2,1,0:T(8,128)S(1)} all-gather(f32[1,5,8]{2,1,0:T(8,128)S(1)} %bitcast.20), channel_id=1, replica_groups=mesh['az'=16,'rad'=2] {'rad'}, dimensions={0}, use_global_device_ids=true | all-gather | bytes 480 | tf_op jit(solution)/shard_map/all_gather | solution.py:354
  12.6 0.1 copy.16
  12.7 0.1 reshape.21
  12.8 0.1 slice.36
  12.8 0.1 copy.15
  13.0 0.2 slice_multiply_fusion
  13.1 0.2 shard_map.55
  13.3 0.0 copy-start.2
  13.3 0.7 copy-done.2
  14.0 0.7 copy-done.4
  14.7 0.0 copy-done.7
  14.7 0.1 tile.10
  14.8 0.0 copy-done.1
  14.8 0.8 slice.27
  15.6 1.1 copy.17
  16.7 0.1 dynamic_slice.8
  16.8 0.1 pad.5.edge_ref
  16.9 48.9 %all-to-all-done.in_ref = f32[16,160,256]{2,1,0:T(8,128)S(1)} async-done(((f32[16,160,256]{2,1,0:T(8,128)}), f32[16,160,256]{2,1,0:T(8,128)S(1)}, u32[]{:S(2)}, u32[]{:S(2)}) %all-to-all-start) | async-done | bytes 2621472 | tf_op jit(solution)/shard_map/all_to_all | solution.py:326
  65.8 0.1 broadcast_in_dim.16.shift_ref
  65.9 2.5 %shard_map.56 = f32[16,328,128]{2,1,0:T(8,128)S(1)} custom-call(s32[160,128]{1,0:T(8,128)S(1)} %broadcast_in_dim.16.shift_ref, f32[8,128]{1,0:T(8,128)S(1)} %pad.5.edge_ref, f32[16,160,256]{2,1,0:T(8,128)S(1)} %all-to-all-done.in_ref), custom_call_target="tpu_custom_call" | custom-call | flops 6553600 | bytes 5242880 | tf_op jit(solution)/shard_map/pallas_call | solution.py:76
  68.4 65.2 %all_to_all.10.recv_ref = f32[16,328,128]{2,1,0:T(8,128)S(1)} all-to-all(f32[16,328,128]{2,1,0:T(8,128)S(1)} %shard_map.56), channel_id=1, replica_groups={{16,24,0,8,18,26,2,10,20,28,4,12,22,30,6,14},{17,25,1,9,19,27,3,11,21,2..., dimensions={0} | all-to-all | bytes 5373952 | tf_op jit(solution)/shard_map/all_to_all | solution.py:326
  133.5 0.9 shard_map.57
  134.4 0.0 copy-start.5
  134.4 1.6 %collective-permute-start = (f32[2,8,256]{2,1,0:T(8,128)S(1)}, f32[2,8,256]{2,1,0:T(8,128)S(1)}, u32[]{:S(2)}, u32[]{:S(2)}) collective-permute-start(f32[2,8,256]{2,1,0:T(8,128)S(1)} %get-tuple-element.33.refs_0_), channel_id=1, source_target_pairs={{0,1},{1,0},{2,3},{3,2},{4,5},{5,4},{6,7},{7,6},{8,9},{9,8},{10,11... | collective-permute-start | bytes 49160 | tf_op jit(solution)/shard_map/ppermute | solution.py:370
  136.0 2.3 %shard_map.58 = (f32[5,8,64,256]{3,2,1,0:T(8,128)}, f32[8,64,256]{2,1,0:T(8,128)S(1)}) custom-call(f32[16,328,128]{2,1,0:T(8,128)S(1)} %all_to_all.10.recv_ref, f32[8,64,256]{2,1,0:T(8,128)S(1)} %copy-done.1, f32[8,64,256]{2,1,0:T(8,128)S(1)} %get-tuple-element.28.back_ref, f32[8,64,64]{2,1,0:T(8,128)S(1)} %copy-done, ...), custom_call_target="tpu_custom_call" | custom-call | flops 5242880 | bytes 4194304 | tf_op jit(solution)/shard_map/pallas_call | solution.py:221
  138.4 0.0 collective-permute-done.refs_1_
  138.4 0.0 copy-done.3
  138.4 1.1 shard_map.59
  (12 shorter events, 0.1 us)
Async XLA Ops:
  0.0 8.0 %copy-start = (f32[8,64,64]{2,1,0:T(8,128)S(1)}, f32[8,64,64]{2,1,0:T(8,128)}, u32[]{:S(2)}) copy-start(f32[8,64,64]{2,1,0:T(8,128)} %inverse_ref.3) | copy-start | bytes 393220
  0.0 8.2 %copy-start.6 = (f32[8,1]{0,1:T(1,128)S(1)}, f32[8,1]{0,1:T(1,128)}, u32[]{:S(2)}) copy-start(f32[8,1]{0,1:T(1,128)} %param.9) | copy-start | bytes 100
  0.0 14.7 %copy-start.7 = (s32[64]{0:T(128)S(1)}, s32[64]{0:T(128)}, u32[]{:S(2)}) copy-start(s32[64]{0:T(128)} %param.7) | copy-start | bytes 772
  0.0 14.8 %copy-start.1 = (f32[8,64,256]{2,1,0:T(8,128)S(1)}, f32[8,64,256]{2,1,0:T(8,128)}, u32[]{:S(2)}) copy-start(f32[8,64,256]{2,1,0:T(8,128)} %speed_ref.3) | copy-start | bytes 1572868
  0.0 65.8 %all-to-all-start = ((f32[16,160,256]{2,1,0:T(8,128)}), f32[16,160,256]{2,1,0:T(8,128)S(1)}, u32[]{:S(2)}, u32[]{:S(2)}) async-start(f32[16,160,256]{2,1,0:T(8,128)} %bitcast.18), calls=%async_computation | async-start | bytes 5242880 | tf_op jit(solution)/shard_map/all_to_all | solution.py:326
  13.3 0.7 copy-start.2
  14.0 0.7 copy-start.4
  134.4 4.0 %copy-start.3 = (f32[8,64,128]{2,1,0:T(8,128)S(1)}, f32[8,64,128]{2,1,0:T(8,128)}, u32[]{:S(2)}) copy-start(f32[8,64,128]{2,1,0:T(8,128)} %copy-done.2) | copy-start | bytes 786436
  134.4 4.0 %copy-start.5 = (f32[8,64,128]{2,1,0:T(8,128)S(1)}, f32[8,64,128]{2,1,0:T(8,128)}, u32[]{:S(2)}) copy-start(f32[8,64,128]{2,1,0:T(8,128)} %copy-done.4) | copy-start | bytes 786436
  134.4 3.9 %collective-permute-start = (f32[2,8,256]{2,1,0:T(8,128)S(1)}, f32[2,8,256]{2,1,0:T(8,128)S(1)}, u32[]{:S(2)}, u32[]{:S(2)}) collective-permute-start(f32[2,8,256]{2,1,0:T(8,128)S(1)} %get-tuple-element.33.refs_0_), channel_id=1, source_target_pairs={{0,1},{1,0},{2,3},{3,2},{4,5},{5,4},{6,7},{7,6},{8,9},{9,8},{10,11... | collective-permute-start | bytes 49160 | tf_op jit(solution)/shard_map/ppermute | solution.py:370

commit v17 on v15

--- a/solution.py
+++ b/solution.py
@@ -82,21 +82,37 @@
     )(shift_rows, edge_tile, gathered)
 
 
-def spread_kernel(low_ref, high_ref, low_out, high_out):
+def spread_kernel(low_ref, high_ref, speed_ref, low_out, high_out, back_out):
     low_out[...] = jnp.broadcast_to(low_ref[...], low_out.shape)
     high_out[...] = jnp.broadcast_to(high_ref[...], high_out.shape)
-
-
-def spread(low, high):
-    shape = low.shape[:-1] + (LANES,)
+    levels, radii, width = speed_ref.shape
+    first = lax.broadcasted_iota(jnp.int32, (TILE_ROWS, LANES), 1) == 0
+
+    def one_level(level, _):
+        for row in range(0, radii, TILE_ROWS):
+            here = slice(row, row + TILE_ROWS)
+            before = None
+            for cell in range(0, width, LANES):
+                behind = pltpu.roll(speed_ref[level, here, cell : cell + LANES], 1, 1)
+                back_out[level, here, cell : cell + LANES] = (
+                    behind if before is None else jnp.where(first, before, behind)
+                )
+                before = behind
+        return 0
+
+    lax.fori_loop(0, levels, one_level, 0)
+
+
+def spread(low, high, speed):
+    column = jax.ShapeDtypeStruct(low.shape[:-1] + (LANES,), jnp.float32)
     return pl.pallas_call(
         spread_kernel,
-        out_shape=[jax.ShapeDtypeStruct(shape, jnp.float32)] * 2,
-        in_specs=[IN_VMEM] * 2,
-        out_specs=[IN_VMEM] * 2,
+        out_shape=[column, column, jax.ShapeDtypeStruct(speed.shape, jnp.float32)],
+        in_specs=[IN_VMEM] * 3,
+        out_specs=[IN_VMEM] * 3,
         compiler_params=ROOMY,
-        cost_estimate=cost(low.size, 2 * low.size * LANES),
-    )(low, high)
+        cost_estimate=cost(2 * speed.size, 3 * speed.size),
+    )(low, high, speed)
 
 
 def carry_level(fields, level, recv_ref, speed_ref, back_ref, known, store):
@@ -150,7 +166,7 @@
 
 
 def energy_kernel(
-    field, left_ref, recv_ref, speed_ref, inverse_ref, moved_ref, ends_ref, back_ref, columns
+    field, left_ref, recv_ref, speed_ref, shifted_ref, inverse_ref, moved_ref, ends_ref, back_ref, columns
 ):
     levels, radii, width = speed_ref.shape
     in_rows = recv_ref.shape[1]
@@ -163,10 +179,9 @@
             here = slice(row, row + TILE_ROWS)
             column = columns[LANES - radii + row : LANES - radii + row + TILE_ROWS, level : level + 1]
             before = jnp.broadcast_to(column, (TILE_ROWS, LANES))
-            for cell in range(0, width, LANES):
-                behind = pltpu.roll(speed_ref[level, here, cell : cell + LANES], 1, 1)
-                back_ref[level, here, cell : cell + LANES] = jnp.where(first, before, behind)
-                before = behind
+            back_ref[level, here, :LANES] = jnp.where(first, before, shifted_ref[level, here, :LANES])
+            for cell in range(LANES, width, LANES):
+                back_ref[level, here, cell : cell + LANES] = shifted_ref[level, here, cell : cell + LANES]
 
         def store(_, row, cell, values, level=level):
             moved_ref[level, row : row + TILE_ROWS, cell : cell + LANES] = values
@@ -182,18 +197,18 @@
     return jnp.dot(left, right, precision=lax.Precision.HIGHEST, preferred_element_type=jnp.float32)
 
 
-def energy_part(field, left, received, speed, inverse):
+def energy_part(field, left, received, speed, shifted, inverse):
     levels, radii, width = speed.shape
     plane = jax.ShapeDtypeStruct(speed.shape, jnp.float32)
     return pl.pallas_call(
         functools.partial(energy_kernel, field),
         out_shape=[plane, jax.ShapeDtypeStruct((2, levels, width), jnp.float32), plane],
-        in_specs=[IN_SMEM] + [IN_VMEM] * 3,
+        in_specs=[IN_SMEM] + [IN_VMEM] * 4,
         out_specs=[IN_VMEM] * 3,
         scratch_shapes=[pltpu.VMEM((LANES, LANES), jnp.float32)],
         compiler_params=ROOMY,
         cost_estimate=cost(60 * speed.size, 5 * speed.size),
-    )(left, received, speed, inverse)
+    )(left, received, speed, shifted, inverse)
 
 
 def carry_kernel(recv_ref, speed_ref, back_ref, inverse_ref, moved_ref, out_ref, local_ref, held, sems):
@@ -354,17 +369,23 @@
     links = all_corners.reshape(levels, bands, 5)[:, :, 4]
     links_below = jnp.concatenate([jnp.zeros_like(links[:, :1]), links[:, :-1]], axis=1)
     link_below = lax.dynamic_index_in_dim(links_below, band, 1, keepdims=True)
-    low, high = spread(
-        (link_below * block_inverse[:, :, 0])[:, :, None], (coupling * block_inverse[:, :, -1])[:, :, None]
+    low, high, shifted = spread(
+        (link_below * block_inverse[:, :, 0])[:, :, None],
+        (coupling * block_inverse[:, :, -1])[:, :, None],
+        velocity,
     )
     band_scalar = band[None].astype(jnp.int32)
-    gathered, edge_tile, all_corners, low, high, band_scalar, left_scalar, shift_rows = lax.optimization_barrier(
-        (gathered, edge_tile, all_corners, low, high, band_scalar, left_scalar, shift_rows)
+    gathered, edge_tile, shifted, all_corners, low, high, band_scalar, left_scalar, shift_rows = (
+        lax.optimization_barrier(
+            (gathered, edge_tile, shifted, all_corners, low, high, band_scalar, left_scalar, shift_rows)
+        )
     )
 
     received = exchange(turn(shift_rows, edge_tile, gathered))
 
-    moved, ends, back_speed = energy_part(nf - 1, left_scalar, received, velocity, block_inverse)
+    moved, ends, back_speed = energy_part(
+        nf - 1, left_scalar, received, velocity, shifted, block_inverse
+    )
     if bands == 2:
         all_ends = [ends, lax.ppermute(ends, "rad", [(0, 1), (1, 0)])]
     else:

time: 139 us -> 139 us (level)
  waiting for transfers between devices: 39 us -> 37.5 us
    all_to_all x1, waiting for transfers between devices: 39 us -> 37.5 us  [exchange(): lax.all_to_all(blocks, 'az', split_axis=0, concat_axis=0, tiled=True, axi...]
    unnamed x19 -> x23, local copies, waits for them, and re-layouts: 2.57 us -> 3.37 us
where the time goes in v17:
time: 139 us
  blocking collectives  79.3 us (57%)
  waiting for transfers between devices  37.5 us (27%)
  starting transfers between devices  9.56 us (7%)
  Pallas kernels  7.52 us (5%)
  local copies, waits for them, and re-layouts  5.02 us (4%)
    all_to_all x1, blocking collectives, exchange(): lax.all_to_all(blocks, 'az', split_axis=0, concat_axis=0, tiled=True, axi...  74.9 us
    all_to_all x1, waiting for transfers between devices, exchange(): lax.all_to_all(blocks, 'az', split_axis=0, concat_axis=0, tiled=True, axi...  37.5 us
    all_to_all x1, starting transfers between devices, exchange(): lax.all_to_all(blocks, 'az', split_axis=0, concat_axis=0, tiled=True, axi...  7.98 us
    all_gather x1, blocking collectives, per_device(): all_corners = lax.all_gather(corners, 'rad', axis=1, tiled=True)  4.34 us
    unnamed x23, local copies, waits for them, and re-layouts  3.37 us
  transfers between devices with their start and end apart: 2, of which 1 were waited for; matrix products, arithmetic and copies ran while one was open for 2% of the time, Pallas kernels for 2%

profile of v17, /device:TPU:0, one launch (start us, length us, event | category | flops | bytes accessed | tf_op | source)
XLA Modules:
  0.0 139.2 jit_solution(2228045840729455600)
XLA Ops:
  0.0 8.0 %all-to-all-start = ((f32[16,160,256]{2,1,0:T(8,128)}), f32[16,160,256]{2,1,0:T(8,128)S(1)}, u32[]{:S(2)}, u32[]{:S(2)}) async-start(f32[16,160,256]{2,1,0:T(8,128)} %bitcast.18), calls=%async_computation | async-start | bytes 5242880 | tf_op jit(solution)/shard_map/all_to_all | solution.py:340
  8.0 0.0 copy-done.1
  8.0 0.2 slice_reduce_fusion
  8.2 0.0 copy-done.8
  8.3 4.3 %all-gather = f32[2,5,8]{2,1,0:T(8,128)S(1)} all-gather(f32[1,5,8]{2,1,0:T(8,128)S(1)} %bitcast.20), channel_id=1, replica_groups=mesh['az'=16,'rad'=2] {'rad'}, dimensions={0}, use_global_device_ids=true | all-gather | bytes 480 | tf_op jit(solution)/shard_map/all_gather | solution.py:368
  12.6 0.1 copy.16
  12.7 0.1 reshape.21
  12.8 0.1 slice.36
  12.8 0.1 copy.15
  13.0 0.2 slice_multiply_fusion
  13.1 0.0 copy-done
  13.1 0.9 shard_map.55
  14.0 0.0 copy-start.2
  14.0 0.8 copy-done.2
  14.8 0.7 copy-done.4
  15.5 0.7 copy-done.6
  16.2 0.8 slice.27
  17.0 0.0 copy-done.9
  17.0 0.1 tile.10
  17.1 1.1 copy.17
  18.2 0.1 dynamic_slice.8
  18.3 0.1 pad.5.edge_ref
  18.4 37.5 %all-to-all-done.in_ref = f32[16,160,256]{2,1,0:T(8,128)S(1)} async-done(((f32[16,160,256]{2,1,0:T(8,128)}), f32[16,160,256]{2,1,0:T(8,128)S(1)}, u32[]{:S(2)}, u32[]{:S(2)}) %all-to-all-start) | async-done | bytes 2621472 | tf_op jit(solution)/shard_map/all_to_all | solution.py:340
  55.9 0.1 broadcast_in_dim.16.shift_ref
  56.0 2.5 %shard_map.56 = f32[16,328,128]{2,1,0:T(8,128)S(1)} custom-call(s32[160,128]{1,0:T(8,128)S(1)} %broadcast_in_dim.16.shift_ref, f32[8,128]{1,0:T(8,128)S(1)} %pad.5.edge_ref, f32[16,160,256]{2,1,0:T(8,128)S(1)} %all-to-all-done.in_ref), custom_call_target="tpu_custom_call" | custom-call | flops 6553600 | bytes 5242880 | tf_op jit(solution)/shard_map/pallas_call | solution.py:75
  58.5 0.0 copy-start.3
  58.5 74.9 %all_to_all.10.recv_ref = f32[16,328,128]{2,1,0:T(8,128)S(1)} all-to-all(f32[16,328,128]{2,1,0:T(8,128)S(1)} %shard_map.56), channel_id=1, replica_groups={{16,18,20,22,24,26,28,30,0,2,4,6,8,10,12,14},{17,19,21,23,25,27,29,31,1..., dimensions={0} | all-to-all | bytes 5373952 | tf_op jit(solution)/shard_map/all_to_all | solution.py:340
  133.4 0.8 shard_map.57
  134.2 1.6 %collective-permute-start = (f32[2,8,256]{2,1,0:T(8,128)S(1)}, f32[2,8,256]{2,1,0:T(8,128)S(1)}, u32[]{:S(2)}, u32[]{:S(2)}) collective-permute-start(f32[2,8,256]{2,1,0:T(8,128)S(1)} %get-tuple-element.37.refs_0_), channel_id=1, source_target_pairs={{0,1},{1,0},{2,3},{3,2},{4,5},{5,4},{6,7},{7,6},{8,9},{9,8},{10,11... | collective-permute-start | bytes 49160 | tf_op jit(solution)/shard_map/ppermute | solution.py:390
  135.8 2.3 %shard_map.58 = (f32[5,8,64,256]{3,2,1,0:T(8,128)}, f32[8,64,256]{2,1,0:T(8,128)S(1)}) custom-call(f32[16,328,128]{2,1,0:T(8,128)S(1)} %all_to_all.10.recv_ref, f32[8,64,256]{2,1,0:T(8,128)S(1)} %copy-done, f32[8,64,256]{2,1,0:T(8,128)S(1)} %get-tuple-element.32.back_ref, f32[8,64,64]{2,1,0:T(8,128)S(1)} %copy-done.1, ...), custom_call_target="tpu_custom_call" | custom-call | flops 5242880 | bytes 4194304 | tf_op jit(solution)/shard_map/pallas_call | solution.py:235
  138.2 0.0 collective-permute-done.refs_1_
  138.2 1.1 shard_map.59
  (16 shorter events, 0.1 us)
Async XLA Ops:
  0.0 8.0 %copy-start.1 = (f32[8,64,64]{2,1,0:T(8,128)S(1)}, f32[8,64,64]{2,1,0:T(8,128)}, u32[]{:S(2)}) copy-start(f32[8,64,64]{2,1,0:T(8,128)} %inverse_ref.3) | copy-start | bytes 393220
  0.0 8.2 %copy-start.8 = (f32[8,1]{0,1:T(1,128)S(1)}, f32[8,1]{0,1:T(1,128)}, u32[]{:S(2)}) copy-start(f32[8,1]{0,1:T(1,128)} %param.9) | copy-start | bytes 100
  0.0 13.1 %copy-start = (f32[8,64,256]{2,1,0:T(8,128)S(1)}, f32[8,64,256]{2,1,0:T(8,128)}, u32[]{:S(2)}) copy-start(f32[8,64,256]{2,1,0:T(8,128)} %speed_ref.5) | copy-start | bytes 1572868
  0.0 55.9 %all-to-all-start = ((f32[16,160,256]{2,1,0:T(8,128)}), f32[16,160,256]{2,1,0:T(8,128)S(1)}, u32[]{:S(2)}, u32[]{:S(2)}) async-start(f32[16,160,256]{2,1,0:T(8,128)} %bitcast.18), calls=%async_computation | async-start | bytes 5242880 | tf_op jit(solution)/shard_map/all_to_all | solution.py:340
  8.0 9.1 %copy-start.9 = (s32[64]{0:T(128)S(1)}, s32[64]{0:T(128)}, u32[]{:S(2)}) copy-start(s32[64]{0:T(128)} %param.7) | copy-start | bytes 772
  14.0 0.8 copy-start.2
  14.8 0.7 copy-start.4
  15.5 0.7 copy-start.6
  58.5 75.0 %copy-start.3 = (f32[8,64,256]{2,1,0:T(8,128)S(1)}, f32[8,64,256]{2,1,0:T(8,128)}, u32[]{:S(2)}) copy-start(f32[8,64,256]{2,1,0:T(8,128)} %copy-done.2) | copy-start | bytes 1572868
  134.2 4.0 %copy-start.5 = (f32[8,64,128]{2,1,0:T(8,128)S(1)}, f32[8,64,128]{2,1,0:T(8,128)}, u32[]{:S(2)}) copy-start(f32[8,64,128]{2,1,0:T(8,128)} %copy-done.4) | copy-start | bytes 786436
  134.2 4.0 %copy-start.7 = (f32[8,64,128]{2,1,0:T(8,128)S(1)}, f32[8,64,128]{2,1,0:T(8,128)}, u32[]{:S(2)}) copy-start(f32[8,64,128]{2,1,0:T(8,128)} %copy-done.6) | copy-start | bytes 786436
  134.2 3.9 %collective-permute-start = (f32[2,8,256]{2,1,0:T(8,128)S(1)}, f32[2,8,256]{2,1,0:T(8,128)S(1)}, u32[]{:S(2)}, u32[]{:S(2)}) collective-permute-start(f32[2,8,256]{2,1,0:T(8,128)S(1)} %get-tuple-element.37.refs_0_), channel_id=1, source_target_pairs={{0,1},{1,0},{2,3},{3,2},{4,5},{5,4},{6,7},{7,6},{8,9},{9,8},{10,11... | collective-permute-start | bytes 49160 | tf_op jit(solution)/shard_map/ppermute | solution.py:390

commit v18 on v17

--- a/solution.py
+++ b/solution.py
@@ -40,18 +40,18 @@
         cells = shift & (LANES - 1)
         whole = shift >> 7
         source = (lane - cells) & (LANES - 1)
-        own = lane >= cells
-        turned = []
+        stays = lane < LANES - cells
+        circle = []
         for tile in range(tiles):
             block, part = divmod(tile, per_block)
-            values = in_ref[places[block], here, part * LANES : (part + 1) * LANES]
-            turned.append(jnp.take_along_axis(values, source, axis=1, mode="promise_in_bounds"))
-        circle = [jnp.where(own, turned[tile], turned[tile - 1]) for tile in range(tiles)]
+            circle.append(in_ref[places[block], here, part * LANES : (part + 1) * LANES])
         step = 1
         while step < tiles:
             wanted = (whole & step) != 0
             circle = [jnp.where(wanted, circle[(tile - step) % tiles], circle[tile]) for tile in range(tiles)]
             step *= 2
+        joined = [jnp.where(stays, circle[tile], circle[tile - 1]) for tile in range(tiles)]
+        circle = [jnp.take_along_axis(one, source, axis=1, mode="promise_in_bounds") for one in joined]
         for tile in range(tiles):
             block, part = divmod(tile, per_block)
             row = (group * per_block + part) * TILE_ROWS

time: 139 us -> 139 us (level)
  no operation moved by 1% of the time
where the time goes in v18:
time: 139 us
  blocking collectives  79.3 us (57%)
  waiting for transfers between devices  37.5 us (27%)
  starting transfers between devices  9.56 us (7%)
  Pallas kernels  7.47 us (5%)
  local copies, waits for them, and re-layouts  5.02 us (4%)
    all_to_all x1, blocking collectives, exchange(): lax.all_to_all(blocks, 'az', split_axis=0, concat_axis=0, tiled=True, axi...  74.9 us
    all_to_all x1, waiting for transfers between devices, exchange(): lax.all_to_all(blocks, 'az', split_axis=0, concat_axis=0, tiled=True, axi...  37.5 us
    all_to_all x1, starting transfers between devices, exchange(): lax.all_to_all(blocks, 'az', split_axis=0, concat_axis=0, tiled=True, axi...  7.98 us
    all_gather x1, blocking collectives, per_device(): all_corners = lax.all_gather(corners, 'rad', axis=1, tiled=True)  4.34 us
    unnamed x23, local copies, waits for them, and re-layouts  3.37 us
  transfers between devices with their start and end apart: 2, of which 1 were waited for; matrix products, arithmetic and copies ran while one was open for 2% of the time, Pallas kernels for 2%

profile of v18, /device:TPU:0, one launch (start us, length us, event | category | flops | bytes accessed | tf_op | source)
XLA Modules:
  0.0 139.2 jit_solution(17165097237333592125)
XLA Ops:
  0.0 8.0 %all-to-all-start = ((f32[16,160,256]{2,1,0:T(8,128)}), f32[16,160,256]{2,1,0:T(8,128)S(1)}, u32[]{:S(2)}, u32[]{:S(2)}) async-start(f32[16,160,256]{2,1,0:T(8,128)} %bitcast.18), calls=%async_computation | async-start | bytes 5242880 | tf_op jit(solution)/shard_map/all_to_all | solution.py:340
  8.0 0.0 copy-done.1
  8.0 0.2 slice_reduce_fusion
  8.2 0.0 copy-done.8
  8.3 4.3 %all-gather = f32[2,5,8]{2,1,0:T(8,128)S(1)} all-gather(f32[1,5,8]{2,1,0:T(8,128)S(1)} %bitcast.20), channel_id=1, replica_groups=mesh['az'=16,'rad'=2] {'rad'}, dimensions={0}, use_global_device_ids=true | all-gather | bytes 480 | tf_op jit(solution)/shard_map/all_gather | solution.py:368
  12.6 0.1 copy.16
  12.7 0.1 reshape.21
  12.8 0.1 slice.36
  12.8 0.1 copy.15
  13.0 0.2 slice_multiply_fusion
  13.1 0.0 copy-done
  13.1 0.9 shard_map.55
  14.0 0.0 copy-start.2
  14.0 0.8 copy-done.2
  14.8 0.7 copy-done.4
  15.5 0.7 copy-done.6
  16.2 0.8 slice.27
  17.0 0.1 tile.10
  17.1 1.1 copy.17
  18.2 0.1 dynamic_slice.8
  18.3 0.1 pad.5.edge_ref
  18.4 37.5 %all-to-all-done.in_ref = f32[16,160,256]{2,1,0:T(8,128)S(1)} async-done(((f32[16,160,256]{2,1,0:T(8,128)}), f32[16,160,256]{2,1,0:T(8,128)S(1)}, u32[]{:S(2)}, u32[]{:S(2)}) %all-to-all-start) | async-done | bytes 2621472 | tf_op jit(solution)/shard_map/all_to_all | solution.py:340
  55.9 0.1 broadcast_in_dim.16.shift_ref
  56.0 2.4 %shard_map.56 = f32[16,328,128]{2,1,0:T(8,128)S(1)} custom-call(s32[160,128]{1,0:T(8,128)S(1)} %broadcast_in_dim.16.shift_ref, f32[8,128]{1,0:T(8,128)S(1)} %pad.5.edge_ref, f32[16,160,256]{2,1,0:T(8,128)S(1)} %all-to-all-done.in_ref), custom_call_target="tpu_custom_call" | custom-call | flops 6553600 | bytes 5242880 | tf_op jit(solution)/shard_map/pallas_call | solution.py:75
  58.4 0.0 copy-start.3
  58.4 74.9 %all_to_all.10.recv_ref = f32[16,328,128]{2,1,0:T(8,128)S(1)} all-to-all(f32[16,328,128]{2,1,0:T(8,128)S(1)} %shard_map.56), channel_id=1, replica_groups={{16,18,20,22,24,26,28,30,0,2,4,6,8,10,12,14},{17,19,21,23,25,27,29,31,1..., dimensions={0} | all-to-all | bytes 5373952 | tf_op jit(solution)/shard_map/all_to_all | solution.py:340
  133.4 0.8 shard_map.57
  134.2 0.0 copy-start.7
  134.2 1.6 %collective-permute-start = (f32[2,8,256]{2,1,0:T(8,128)S(1)}, f32[2,8,256]{2,1,0:T(8,128)S(1)}, u32[]{:S(2)}, u32[]{:S(2)}) collective-permute-start(f32[2,8,256]{2,1,0:T(8,128)S(1)} %get-tuple-element.37.refs_0_), channel_id=1, source_target_pairs={{0,1},{1,0},{2,3},{3,2},{4,5},{5,4},{6,7},{7,6},{8,9},{9,8},{10,11... | collective-permute-start | bytes 49160 | tf_op jit(solution)/shard_map/ppermute | solution.py:390
  135.8 2.3 %shard_map.58 = (f32[5,8,64,256]{3,2,1,0:T(8,128)}, f32[8,64,256]{2,1,0:T(8,128)S(1)}) custom-call(f32[16,328,128]{2,1,0:T(8,128)S(1)} %all_to_all.10.recv_ref, f32[8,64,256]{2,1,0:T(8,128)S(1)} %copy-done, f32[8,64,256]{2,1,0:T(8,128)S(1)} %get-tuple-element.32.back_ref, f32[8,64,64]{2,1,0:T(8,128)S(1)} %copy-done.1, ...), custom_call_target="tpu_custom_call" | custom-call | flops 5242880 | bytes 4194304 | tf_op jit(solution)/shard_map/pallas_call | solution.py:235
  138.1 0.0 collective-permute-done.refs_1_
  138.1 1.1 shard_map.59
  (16 shorter events, 0.1 us)
Async XLA Ops:
  0.0 8.0 %copy-start.1 = (f32[8,64,64]{2,1,0:T(8,128)S(1)}, f32[8,64,64]{2,1,0:T(8,128)}, u32[]{:S(2)}) copy-start(f32[8,64,64]{2,1,0:T(8,128)} %inverse_ref.3) | copy-start | bytes 393220
  0.0 8.2 %copy-start.8 = (f32[8,1]{0,1:T(1,128)S(1)}, f32[8,1]{0,1:T(1,128)}, u32[]{:S(2)}) copy-start(f32[8,1]{0,1:T(1,128)} %param.9) | copy-start | bytes 100
  0.0 13.1 %copy-start = (f32[8,64,256]{2,1,0:T(8,128)S(1)}, f32[8,64,256]{2,1,0:T(8,128)}, u32[]{:S(2)}) copy-start(f32[8,64,256]{2,1,0:T(8,128)} %speed_ref.5) | copy-start | bytes 1572868
  0.0 55.9 %all-to-all-start = ((f32[16,160,256]{2,1,0:T(8,128)}), f32[16,160,256]{2,1,0:T(8,128)S(1)}, u32[]{:S(2)}, u32[]{:S(2)}) async-start(f32[16,160,256]{2,1,0:T(8,128)} %bitcast.18), calls=%async_computation | async-start | bytes 5242880 | tf_op jit(solution)/shard_map/all_to_all | solution.py:340
  8.0 9.1 %copy-start.9 = (s32[64]{0:T(128)S(1)}, s32[64]{0:T(128)}, u32[]{:S(2)}) copy-start(s32[64]{0:T(128)} %param.7) | copy-start | bytes 772
  14.0 0.8 copy-start.2
  14.8 0.7 copy-start.4
  15.5 0.7 copy-start.6
  58.4 75.0 %copy-start.3 = (f32[8,64,256]{2,1,0:T(8,128)S(1)}, f32[8,64,256]{2,1,0:T(8,128)}, u32[]{:S(2)}) copy-start(f32[8,64,256]{2,1,0:T(8,128)} %copy-done.2) | copy-start | bytes 1572868
  134.2 4.0 %copy-start.5 = (f32[8,64,128]{2,1,0:T(8,128)S(1)}, f32[8,64,128]{2,1,0:T(8,128)}, u32[]{:S(2)}) copy-start(f32[8,64,128]{2,1,0:T(8,128)} %copy-done.4) | copy-start | bytes 786436
  134.2 4.0 %copy-start.7 = (f32[8,64,128]{2,1,0:T(8,128)S(1)}, f32[8,64,128]{2,1,0:T(8,128)}, u32[]{:S(2)}) copy-start(f32[8,64,128]{2,1,0:T(8,128)} %copy-done.6) | copy-start | bytes 786436
  134.2 3.9 %collective-permute-start = (f32[2,8,256]{2,1,0:T(8,128)S(1)}, f32[2,8,256]{2,1,0:T(8,128)S(1)}, u32[]{:S(2)}, u32[]{:S(2)}) collective-permute-start(f32[2,8,256]{2,1,0:T(8,128)S(1)} %get-tuple-element.37.refs_0_), channel_id=1, source_target_pairs={{0,1},{1,0},{2,3},{3,2},{4,5},{5,4},{6,7},{7,6},{8,9},{9,8},{10,11... | collective-permute-start | bytes 49160 | tf_op jit(solution)/shard_map/ppermute | solution.py:390

commit v19 on v18

--- a/solution.py
+++ b/solution.py
@@ -20,7 +20,8 @@
 
 
 def place_of(device, n):
-    return (device + n // 2) % n
+    blocks = n // 4
+    return (device % 4) * blocks + (device // 4 + blocks // 2) % blocks
 
 
 def turn_kernel(shift_ref, edge_ref, in_ref, out_ref):

time: 139 us -> 140 us (level)
  waiting for transfers between devices: 37.5 us -> 47.4 us
  blocking collectives: 79.3 us -> 69.6 us
    all_to_all x1, waiting for transfers between devices: 37.5 us -> 47.4 us  [exchange(): lax.all_to_all(blocks, 'az', split_axis=0, concat_axis=0, tiled=True, axi...]
    all_to_all x1, blocking collectives: 74.9 us -> 65.3 us  [exchange(): lax.all_to_all(blocks, 'az', split_axis=0, concat_axis=0, tiled=True, axi...]
where the time goes in v19:
time: 140 us; the launch traced here: 139 us
  blocking collectives  69.6 us (50%)
  waiting for transfers between devices  47.4 us (34%)
  starting transfers between devices  9.56 us (7%)
  Pallas kernels  7.48 us (5%)
  local copies, waits for them, and re-layouts  5.03 us (4%)
    all_to_all x1, blocking collectives, exchange(): lax.all_to_all(blocks, 'az', split_axis=0, concat_axis=0, tiled=True, axi...  65.3 us
    all_to_all x1, waiting for transfers between devices, exchange(): lax.all_to_all(blocks, 'az', split_axis=0, concat_axis=0, tiled=True, axi...  47.4 us
    all_to_all x1, starting transfers between devices, exchange(): lax.all_to_all(blocks, 'az', split_axis=0, concat_axis=0, tiled=True, axi...  7.97 us
    all_gather x1, blocking collectives, per_device(): all_corners = lax.all_gather(corners, 'rad', axis=1, tiled=True)  4.34 us
    unnamed x23, local copies, waits for them, and re-layouts  3.37 us
  transfers between devices with their start and end apart: 2, of which 1 were waited for; matrix products, arithmetic and copies ran while one was open for 2% of the time, Pallas kernels for 2%

profile of v19, /device:TPU:0, one launch (start us, length us, event | category | flops | bytes accessed | tf_op | source)
XLA Modules:
  0.0 139.4 jit_solution(4207198950911735334)
XLA Ops:
  0.0 8.0 %all-to-all-start = ((f32[16,160,256]{2,1,0:T(8,128)}), f32[16,160,256]{2,1,0:T(8,128)S(1)}, u32[]{:S(2)}, u32[]{:S(2)}) async-start(f32[16,160,256]{2,1,0:T(8,128)} %bitcast.18), calls=%async_computation | async-start | bytes 5242880 | tf_op jit(solution)/shard_map/all_to_all | solution.py:341
  8.0 0.0 copy-done.1
  8.0 0.2 slice_reduce_fusion
  8.2 0.0 copy-done.8
  8.3 4.3 %all-gather = f32[2,5,8]{2,1,0:T(8,128)S(1)} all-gather(f32[1,5,8]{2,1,0:T(8,128)S(1)} %bitcast.20), channel_id=1, replica_groups=mesh['az'=16,'rad'=2] {'rad'}, dimensions={0}, use_global_device_ids=true | all-gather | bytes 480 | tf_op jit(solution)/shard_map/all_gather | solution.py:369
  12.6 0.1 copy.16
  12.7 0.1 reshape.21
  12.8 0.1 slice.36
  12.8 0.1 copy.15
  13.0 0.2 slice_multiply_fusion
  13.1 0.0 copy-done
  13.1 0.9 shard_map.55
  14.0 0.0 copy-start.2
  14.0 0.8 copy-done.2
  14.8 0.7 copy-done.4
  15.5 0.7 copy-done.6
  16.2 0.8 slice.27
  17.0 0.0 copy-done.9
  17.0 0.1 tile.10
  17.1 1.1 copy.17
  18.2 0.1 dynamic_slice.8
  18.3 0.1 pad.5.edge_ref
  18.3 47.4 %all-to-all-done.in_ref = f32[16,160,256]{2,1,0:T(8,128)S(1)} async-done(((f32[16,160,256]{2,1,0:T(8,128)}), f32[16,160,256]{2,1,0:T(8,128)S(1)}, u32[]{:S(2)}, u32[]{:S(2)}) %all-to-all-start) | async-done | bytes 2621472 | tf_op jit(solution)/shard_map/all_to_all | solution.py:341
  65.8 0.1 broadcast_in_dim.16.shift_ref
  65.8 2.4 %shard_map.56 = f32[16,328,128]{2,1,0:T(8,128)S(1)} custom-call(s32[160,128]{1,0:T(8,128)S(1)} %broadcast_in_dim.16.shift_ref, f32[8,128]{1,0:T(8,128)S(1)} %pad.5.edge_ref, f32[16,160,256]{2,1,0:T(8,128)S(1)} %all-to-all-done.in_ref), custom_call_target="tpu_custom_call" | custom-call | flops 6553600 | bytes 5242880 | tf_op jit(solution)/shard_map/pallas_call | solution.py:76
  68.3 0.0 copy-start.3
  68.3 65.3 %all_to_all.10.recv_ref = f32[16,328,128]{2,1,0:T(8,128)S(1)} all-to-all(f32[16,328,128]{2,1,0:T(8,128)S(1)} %shard_map.56), channel_id=1, replica_groups={{16,24,0,8,18,26,2,10,20,28,4,12,22,30,6,14},{17,25,1,9,19,27,3,11,21,2..., dimensions={0} | all-to-all | bytes 5373952 | tf_op jit(solution)/shard_map/all_to_all | solution.py:341
  133.6 0.8 shard_map.57
  134.4 1.6 %collective-permute-start = (f32[2,8,256]{2,1,0:T(8,128)S(1)}, f32[2,8,256]{2,1,0:T(8,128)S(1)}, u32[]{:S(2)}, u32[]{:S(2)}) collective-permute-start(f32[2,8,256]{2,1,0:T(8,128)S(1)} %get-tuple-element.37.refs_0_), channel_id=1, source_target_pairs={{0,1},{1,0},{2,3},{3,2},{4,5},{5,4},{6,7},{7,6},{8,9},{9,8},{10,11... | collective-permute-start | bytes 49160 | tf_op jit(solution)/shard_map/ppermute | solution.py:391
  136.0 2.3 %shard_map.58 = (f32[5,8,64,256]{3,2,1,0:T(8,128)}, f32[8,64,256]{2,1,0:T(8,128)S(1)}) custom-call(f32[16,328,128]{2,1,0:T(8,128)S(1)} %all_to_all.10.recv_ref, f32[8,64,256]{2,1,0:T(8,128)S(1)} %copy-done, f32[8,64,256]{2,1,0:T(8,128)S(1)} %get-tuple-element.32.back_ref, f32[8,64,64]{2,1,0:T(8,128)S(1)} %copy-done.1, ...), custom_call_target="tpu_custom_call" | custom-call | flops 5242880 | bytes 4194304 | tf_op jit(solution)/shard_map/pallas_call | solution.py:236
  138.3 0.0 collective-permute-done.refs_1_
  138.4 1.1 shard_map.59
  (16 shorter events, 0.1 us)
Async XLA Ops:
  0.0 8.0 %copy-start.1 = (f32[8,64,64]{2,1,0:T(8,128)S(1)}, f32[8,64,64]{2,1,0:T(8,128)}, u32[]{:S(2)}) copy-start(f32[8,64,64]{2,1,0:T(8,128)} %inverse_ref.3) | copy-start | bytes 393220
  0.0 8.2 %copy-start.8 = (f32[8,1]{0,1:T(1,128)S(1)}, f32[8,1]{0,1:T(1,128)}, u32[]{:S(2)}) copy-start(f32[8,1]{0,1:T(1,128)} %param.9) | copy-start | bytes 100
  0.0 13.1 %copy-start = (f32[8,64,256]{2,1,0:T(8,128)S(1)}, f32[8,64,256]{2,1,0:T(8,128)}, u32[]{:S(2)}) copy-start(f32[8,64,256]{2,1,0:T(8,128)} %speed_ref.5) | copy-start | bytes 1572868
  0.0 65.8 %all-to-all-start = ((f32[16,160,256]{2,1,0:T(8,128)}), f32[16,160,256]{2,1,0:T(8,128)S(1)}, u32[]{:S(2)}, u32[]{:S(2)}) async-start(f32[16,160,256]{2,1,0:T(8,128)} %bitcast.18), calls=%async_computation | async-start | bytes 5242880 | tf_op jit(solution)/shard_map/all_to_all | solution.py:341
  8.0 9.1 %copy-start.9 = (s32[64]{0:T(128)S(1)}, s32[64]{0:T(128)}, u32[]{:S(2)}) copy-start(s32[64]{0:T(128)} %param.7) | copy-start | bytes 772
  14.0 0.8 copy-start.2
  14.8 0.7 copy-start.4
  15.5 0.7 copy-start.6
  68.3 65.3 %copy-start.3 = (f32[8,64,256]{2,1,0:T(8,128)S(1)}, f32[8,64,256]{2,1,0:T(8,128)}, u32[]{:S(2)}) copy-start(f32[8,64,256]{2,1,0:T(8,128)} %copy-done.2) | copy-start | bytes 1572868
  134.4 4.0 %copy-start.5 = (f32[8,64,128]{2,1,0:T(8,128)S(1)}, f32[8,64,128]{2,1,0:T(8,128)}, u32[]{:S(2)}) copy-start(f32[8,64,128]{2,1,0:T(8,128)} %copy-done.4) | copy-start | bytes 786436
  134.4 4.0 %copy-start.7 = (f32[8,64,128]{2,1,0:T(8,128)S(1)}, f32[8,64,128]{2,1,0:T(8,128)}, u32[]{:S(2)}) copy-start(f32[8,64,128]{2,1,0:T(8,128)} %copy-done.6) | copy-start | bytes 786436
  134.4 3.9 %collective-permute-start = (f32[2,8,256]{2,1,0:T(8,128)S(1)}, f32[2,8,256]{2,1,0:T(8,128)S(1)}, u32[]{:S(2)}, u32[]{:S(2)}) collective-permute-start(f32[2,8,256]{2,1,0:T(8,128)S(1)} %get-tuple-element.37.refs_0_), channel_id=1, source_target_pairs={{0,1},{1,0},{2,3},{3,2},{4,5},{5,4},{6,7},{7,6},{8,9},{9,8},{10,11... | collective-permute-start | bytes 49160 | tf_op jit(solution)/shard_map/ppermute | solution.py:391
